TPU v7x, 256 devices: a whole 4x4x8 slice. The times are simulated.
256 devices in a mesh: gossip: 4 (over x_lo, core), fsdp: 64 (over z, x_hi, y).
Axes of the slice: x: 4 (x_hi: 2, x_lo: 2; x = x_hi * 2 + x_lo), y: 4, z: 8, core: 2. Of those that a mesh axis runs over, the one named last changes fastest.
Arguments:
- tokens: bfloat16 [4, 1280, 5120], P('gossip', 'fsdp'), may hold values from -6 to 6
- cotangent: bfloat16 [4, 1280, 5120], P('gossip', 'fsdp'), may hold values from -6 to 6
- gate_num: float32 [4, 7168, 5120], P('gossip', 'fsdp'), may hold values from -6 to 6
- push_weight: float32 [4], P('gossip'), may hold values from 0.5 to 2
- stale_num: float32 [4, 7168, 5120], P('gossip', 'fsdp'), may hold values from -3 to 3
- stale_weight: float32 [4], P('gossip'), may hold values from 0.25 to 1
- up_weight: bfloat16 [7168, 5120], P('fsdp'), may hold values from -0.078125 to 0.078125
- down_weight: bfloat16 [7168, 5120], P('fsdp')
- step: int32 [1], replicated, may hold values from 0 to 999999
Outputs:
- new_num: float32 [4, 7168, 5120], P('gossip', 'fsdp')
- new_weight: float32 [4], P('gossip')
- next_num: float32 [4, 7168, 5120], P('gossip', 'fsdp')
- next_weight: float32 [4], P('gossip')
All inputs are finite; a program needn't handle non-finite values.
Results may differ from a plain program's by a relative error of at most 0.0003.
Values may be sent and summed in bfloat16 or wider, within the bound.
No kernel may reach another device: no remote copies, remote signals or barrier semaphores. Data moves between devices by JAX's collectives and lax.ppermute only.
A program may use at most 192 MiB of HBM per device.

v0:
```python
from functools import partial
import math

import jax
import jax.numpy as jnp
from jax import lax
from jax.sharding import PartitionSpec as P

D = 5120
FFW = 7168


eps = 1e-06


def passed_along(value, axis, steps):
    count = lax.axis_size(axis)
    pairs = [(source, (source + steps) % count) for source in range(count)]
    return lax.ppermute(value, axis, pairs)


def silu_slope(preact):
    sigmoid_val = jax.nn.sigmoid(preact)
    return sigmoid_val * (1.0 + preact * (1.0 - sigmoid_val))


def plan_rate(step):
    phase = (step[0] % 1000).astype(jnp.float32) / 1000.0
    return 0.4 + 1.8 * (1.0 + jnp.cos(math.pi * phase))


def send_stale(offset, message):
    return passed_along((message[0], message[1]), "gossip", offset)


def deliver(stale_num, stale_weight, step):
    distances = lax.axis_size("gossip").bit_length() - 1
    branches = [partial(send_stale, 1 << level) for level in range(distances)]
    return lax.switch(step[0] % distances, branches, (stale_num, stale_weight))


def shards(
    tokens, cotangent, gate_num, push_weight, stale_num, stale_weight, up_weight, down_weight, step
):
    width_scale = D ** (-0.5)
    max_norm = 0.05 * math.sqrt(D * FFW)
    rate = plan_rate(step)
    numerator = gate_num[0]
    params = (numerator / push_weight[0]).astype(jnp.bfloat16)
    rows_in, rows_grad = (
        lax.all_gather(tokens[0], "fsdp", axis=0, tiled=True),
        lax.all_gather(cotangent[0], "fsdp", axis=0, tiled=True),
    )
    preact = jnp.dot(rows_in, params.T, preferred_element_type=jnp.float32) * width_scale
    up_proj = jnp.dot(rows_in, up_weight.T, preferred_element_type=jnp.float32)
    hidden_grad = jnp.dot(rows_grad, down_weight.T, preferred_element_type=jnp.float32)
    pre_grad = (hidden_grad * up_proj * silu_slope(preact)).astype(jnp.bfloat16)
    gate_grad = jnp.dot(pre_grad.T, rows_in, preferred_element_type=jnp.float32) * width_scale
    norm_sq = lax.psum(jnp.sum(gate_grad * gate_grad), "fsdp")
    clip_factor = jnp.minimum(1.0, max_norm / jnp.sqrt(norm_sq + eps))
    kept_half = (0.5 * (numerator - rate * clip_factor * gate_grad))[None]
    kept_weight = 0.5 * push_weight
    received = deliver(stale_num, stale_weight, step)
    new_num = kept_half + received[0]
    new_weight = kept_weight + received[1]
    return (new_num, new_weight, kept_half, kept_weight)


def solution(mesh):
    in_specs = (
        P("gossip", "fsdp", None),
        P("gossip", "fsdp", None),
        P("gossip", "fsdp", None),
        P("gossip"),
        P("gossip", "fsdp", None),
        P("gossip"),
        P("fsdp", None),
        P("fsdp", None),
        P(),
    )
    out_specs = (P("gossip", "fsdp", None), P("gossip"), P("gossip", "fsdp", None), P("gossip"))
    return jax.shard_map(shards, mesh=mesh, in_specs=in_specs, out_specs=out_specs, check_vma=False)
```

profile of v0, /device:TPU:2, one launch (start us, length us, event | category | flops | bytes accessed | tf_op | source)
XLA Modules:
  0.0 812.3 jit_solution(6278882357737719140)
XLA Ops:
  7.2 0.0 copy-start
  7.2 0.0 all-gather.7.cloned.1.call-start
  7.2 2.1 copy.16
  9.3 0.0 all-gather.7.cloned.1.call-update
  9.3 0.0 all-gather.5.cloned.1.call-start
  9.4 2.0 copy.15
  11.4 0.0 all-gather.5.cloned.1.call-update
  12.9 55.0 %conditional.1 = (f32[1,112,5120]{2,1,0:T(8,128)}, f32[1]{0:T(128)}) conditional(s32[]{:T(128)} %clamp.3, (f32[1,112,5120]{2,1,0:T(8,128)}, f32[1]{0:T(128)}) %tuple.16, (f32[1,112,5120]{2,1,0:T(8,128)}, f32[1]{0:T(128)}) %tuple.16), branch_computations={%region_2.3_spmd, %region_3.4_spmd} | conditional | bytes 9175152 | solution.py:39
  12.9 2.4 collective-permute-start.2
  15.2 0.1 collective-permute-start.3
  15.3 52.5 %collective-permute-done.3 = f32[1]{0:T(128)} collective-permute-done((f32[1]{0:T(128)}, f32[1]{0:T(128)}, u32[]{:S(2)}, u32[]{:S(2)}) %collective-permute-start.3) | collective-permute-done | bytes 36 | tf_op jit(solution)/shard_map/cond/branch_1_fun/ppermute | solution.py:19
  67.9 0.0 collective-permute-done.2
  68.4 229.3 %all-gather.7.cloned.1.call-done = bf16[1,1280,5120]{2,0,1:T(2,128)(2,1)} async-done(((bf16[1,20,5120]{2,0,1:T(2,128)(2,1)}), bf16[1,1280,5120]{2,0,1:T(2,128)(2,1)}) %all-gather.7.cloned.1.call-update) | async-done | bytes 13107216 | tf_op jit(solution)/shard_map/all_gather | solution.py:51
  297.7 0.0 copy-start.3
  297.7 14.8 %fusion.12 = f32[1280,112]{0,1:T(8,128)} fusion(f32[1,112,5120]{2,1,0:T(8,128)} %param.13, f32[]{:T(128)} %bitcast.46, bf16[1,1280,5120]{2,0,1:T(2,128)(2,1)} %all-gather.7.cloned.1.call-done), kind=kOutput, calls=%fused_computation.10 | convolution fusion | flops 1469296640 | bytes 15974404 | tf_op jit(solution)/shard_map/dot_general | solution.py:54
  312.5 0.0 copy-done.3
  312.5 14.2 %fusion.4 = f32[1280,112]{0,1:T(8,128)} fusion(bf16[112,5120]{1,0:T(8,128)(2,1)S(1)} %copy-done.3, bf16[1,1280,5120]{2,0,1:T(2,128)(2,1)} %all-gather.7.cloned.1.call-done), kind=kOutput, calls=%fused_computation.4 | convolution fusion | flops 1468006400 | bytes 14827520 | tf_op jit(solution)/shard_map/dot_general | solution.py:55
  326.7 0.0 copy-start.2
  326.7 253.9 %all-gather.5.cloned.1.call-done = bf16[1,1280,5120]{2,0,1:T(2,128)(2,1)} async-done(((bf16[1,20,5120]{2,0,1:T(2,128)(2,1)}), bf16[1,1280,5120]{2,0,1:T(2,128)(2,1)}) %all-gather.5.cloned.1.call-update) | async-done | bytes 13107216 | tf_op jit(solution)/shard_map/all_gather | solution.py:52
  580.5 0.0 copy-done
  580.6 35.5 %multiply_reduce_fusion = (f32[]{:T(128)}, f32[112,5120]{1,0:T(8,128)}) fusion(bf16[1,1280,5120]{2,0,1:T(2,128)(2,1)} %all-gather.7.cloned.1.call-done, f32[1280,112]{0,1:T(8,128)} %fusion.4, bf16[112,5120]{1,0:T(8,128)(2,1)S(1)} %copy-done, bf16[1,1280,5120]{2,0,1:T(2,128)(2,1)} %all-gather.5.cloned.1.call-done, f32[1280,112]{0,1:T(8,128)} %fusion.12), kind=kOutput, calls=%fused_computation.19 | convolution fusion | flops 2939166720 | bytes 30801924 | tf_op jit(solution)/shard_map/dot_general | solution.py:58
  616.0 181.3 %psum.7 = f32[]{:T(128)} all-reduce(f32[]{:T(128)} %get-tuple-element.22), channel_id=1, replica_groups=mesh['gossip'=4,'fsdp'=64] {'fsdp'}, use_global_device_ids=true, to_apply=%region_1.2 | all-reduce | flops 1 | bytes 8 | tf_op jit(solution)/shard_map/psum | solution.py:59
  798.1 0.0 copy-done.2
  798.1 0.0 copy-start.1
  798.1 5.1 fusion.44
  803.2 0.0 copy-done.1
Async XLA Ops:
  7.2 573.4 %copy-start = (bf16[112,5120]{1,0:T(8,128)(2,1)S(1)}, bf16[112,5120]{1,0:T(8,128)(2,1)}, u32[]{:S(2)}) copy-start(bf16[112,5120]{1,0:T(8,128)(2,1)} %param.18) | copy-start | bytes 3440644
  7.2 290.6 %all-gather.7.cloned.1.call-start = ((), (), s32[]{:S(2)}) async-start(), calls=%async_computation.1 | async-start | bytes 26624000 | tf_op jit(solution)/shard_map/all_gather | solution.py:51
  9.3 571.2 %all-gather.5.cloned.1.call-start = ((), (), s32[]{:S(2)}) async-start(), calls=%async_computation | async-start | bytes 26624000 | tf_op jit(solution)/shard_map/all_gather | solution.py:52
  12.9 55.0 %collective-permute-start.2 = (f32[1,112,5120]{2,1,0:T(8,128)}, f32[1,112,5120]{2,1,0:T(8,128)}, u32[]{:S(2)}, u32[]{:S(2)}) collective-permute-start(f32[1,112,5120]{2,1,0:T(8,128)} %get-tuple-element.10), channel_id=1, source_target_pairs={{0,128},{64,192},{128,0},{192,64},{1,129},{65,193},{129,1},{193,65... | collective-permute-start | bytes 6881288 | tf_op jit(solution)/shard_map/cond/branch_1_fun/ppermute | solution.py:19
  15.2 52.6 %collective-permute-start.3 = (f32[1]{0:T(128)}, f32[1]{0:T(128)}, u32[]{:S(2)}, u32[]{:S(2)}) collective-permute-start(f32[1]{0:T(128)} %get-tuple-element.11), channel_id=1, source_target_pairs={{0,128},{64,192},{128,0},{192,64},{1,129},{65,193},{129,1},{193,65... | collective-permute-start | bytes 20 | tf_op jit(solution)/shard_map/cond/branch_1_fun/ppermute | solution.py:19
  297.7 14.8 %copy-start.3 = (bf16[112,5120]{1,0:T(8,128)(2,1)S(1)}, bf16[112,5120]{1,0:T(8,128)(2,1)}, u32[]{:S(2)}) copy-start(bf16[112,5120]{1,0:T(8,128)(2,1)} %param.17) | copy-start | bytes 3440644
  326.7 471.4 %copy-start.2 = (f32[1,112,5120]{2,1,0:T(8,128)S(1)}, f32[1,112,5120]{2,1,0:T(8,128)}, u32[]{:S(2)}) copy-start(f32[1,112,5120]{2,1,0:T(8,128)} %param.13) | copy-start | bytes 6881284
  798.1 5.1 copy-start.1
Sparse Core Ops, SparseCore 0:
  12.1 285.6 all-gather.6
  301.2 279.3 all-gather.4
where the time goes:
time: 813 us; the launch traced here: 812 us
  waiting for transfers between devices  536 us (66%)
  blocking collectives  181 us (22%)
  matrix products  64.4 us (8%)
  between operations  19 us (2%)
    all_gather x1, waiting for transfers between devices, shards(): lax.all_gather(cotangent[0], 'fsdp', axis=0, tiled=True)  254 us
    all_gather x1, waiting for transfers between devices, shards(): lax.all_gather(tokens[0], 'fsdp', axis=0, tiled=True)  229 us
    psum x1, blocking collectives, shards(): norm_sq = lax.psum(jnp.sum(gate_grad * gate_grad), 'fsdp')  181 us
    ppermute x2, waiting for transfers between devices, passed_along(): return lax.ppermute(value, axis, pairs)  52.5 us
    dot_general x1, matrix products, shards(): jnp.dot(pre_grad.T, rows_in, preferred_element_type=jnp.float32)  35.5 us
  transfers between devices with their start and end apart: 4, of which 3 were waited for; matrix products, arithmetic and copies ran while one was open for 4% of the time, Pallas kernels for 0%

commit v1 on v0

v1 whole, which is shorter than its diff:
```python
import math

import jax
import jax.numpy as jnp
import numpy as np
from jax import lax
from jax.sharding import Mesh, PartitionSpec as P

D = 5120
FFW = 7168

eps = 1e-06

SIZES = {"x_lo": 2, "core": 2, "z": 8, "x_hi": 2, "y": 4}
GOSSIP = ("x_lo", "core")
FSDP = ("z", "x_hi", "y")


def shifted(value, axis, steps):
    count = SIZES[axis]
    pairs = [((place + steps) % count, place) for place in range(count)]
    return lax.ppermute(value, axis, pairs)


def transposed(value):
    pairs = [(2 * x_hi + core, 2 * core + x_hi) for x_hi in range(2) for core in range(2)]
    return lax.ppermute(value, ("core", "x_hi"), pairs)


def silu_slope(preact):
    sigmoid_val = jax.nn.sigmoid(preact)
    return sigmoid_val * (1.0 + preact * (1.0 - sigmoid_val))


def plan_rate(step):
    phase = (step[0] % 1000).astype(jnp.float32) / 1000.0
    return 0.4 + 1.8 * (1.0 + jnp.cos(math.pi * phase))


def deliver(stale, step):
    two_before = shifted(stale, "x_lo", 1)
    payload = jnp.where(lax.axis_index("core") == 1, two_before, stale)
    one_before = shifted(payload, "core", 1)
    return jnp.where(step[0] % 2 == 0, one_before, two_before)


def dot_t(rows, weights):
    return lax.dot_general(
        rows, weights, (((1,), (1,)), ((), ())), preferred_element_type=jnp.float32
    )


def gather_tokens(block):
    near = [block] + [shifted(block, "y", d) for d in (1, 3, 2)]
    return lax.all_gather(jnp.concatenate(near, axis=0), "z", axis=0, tiled=True)


def hidden_of(block, down):
    up_way, down_way = [block], [block]
    for _ in range(4):
        up_way.append(shifted(up_way[-1], "z", 1))
    for _ in range(3):
        down_way.append(shifted(down_way[-1], "z", 7))
    column = jnp.concatenate(up_way + down_way[:0:-1], axis=0)
    after = shifted(column, "y", 1)
    before = shifted(column, "y", 3)
    half = column.shape[0] // 2
    far = [shifted(after[:half], "y", 1), shifted(before[half:], "y", 3)]
    hidden = jnp.concatenate([dot_t(part, down) for part in (column, after, before, *far)], axis=0)
    width = hidden.shape[1]
    hidden = hidden.reshape(4, 8, -1, width).transpose(1, 0, 2, 3).reshape(-1, width)
    start = (8 - lax.axis_index("z")) % 8 * (hidden.shape[0] // 8)
    return lax.dynamic_slice_in_dim(
        jnp.concatenate([hidden, hidden], axis=0), start, hidden.shape[0], axis=0
    )


def shards(
    tokens, cotangent, gate_num, push_weight, stale_num, stale_weight, up_weight, down_weight, step
):
    width_scale = D ** (-0.5)
    max_norm = 0.05 * math.sqrt(D * FFW)
    rate = plan_rate(step)
    numerator = gate_num[0]

    rows_in, rows_grad = transposed(tokens[0]), transposed(cotangent[0])
    params = transposed((numerator / push_weight[0]).astype(jnp.bfloat16))
    up, down = transposed(up_weight), transposed(down_weight)
    params, up, down = (
        jnp.concatenate([value, shifted(value, "core", 1)], axis=0) for value in (params, up, down)
    )
    hidden_grad = hidden_of(rows_grad, down)
    rows_in = gather_tokens(rows_in)
    preact = dot_t(rows_in, params) * width_scale
    up_proj = dot_t(rows_in, up)
    pre_grad = (hidden_grad * up_proj * silu_slope(preact)).astype(jnp.bfloat16)
    partial = (
        lax.dot_general(
            pre_grad, rows_in, (((0,), (0,)), ((), ())), preferred_element_type=jnp.float32
        )
        * width_scale
    )
    half = partial.shape[0] // 2
    gate_grad = partial[:half] + shifted(partial[half:], "core", 1)
    norm_sq = jnp.sum(gate_grad * gate_grad)
    for axes in ("z", "y", "core"):
        norm_sq = lax.psum(norm_sq, axes)
    gate_grad, norm_sq = transposed(gate_grad), transposed(norm_sq)

    clip_factor = jnp.minimum(1.0, max_norm / jnp.sqrt(norm_sq + eps))
    kept_half = (0.5 * (numerator - rate * clip_factor * gate_grad))[None]
    kept_weight = 0.5 * push_weight
    new_num = kept_half + deliver(stale_num, step)
    new_weight = kept_weight + deliver(stale_weight, step)
    return (new_num, new_weight, kept_half, kept_weight)


def solution(mesh):
    named = Mesh(np.asarray(mesh.devices).reshape(tuple(SIZES.values())), tuple(SIZES))
    groups = P(GOSSIP, FSDP, None)
    in_specs = (
        groups,
        groups,
        groups,
        P(GOSSIP),
        groups,
        P(GOSSIP),
        P(FSDP, None),
        P(FSDP, None),
        P(),
    )
    out_specs = (groups, P(GOSSIP), groups, P(GOSSIP))
    return jax.shard_map(shards, mesh=named, in_specs=in_specs, out_specs=out_specs, check_vma=False)
```

time: 813 us -> 307 us (0.38)
  the two profiles are of different devices: /device:TPU:2 before, /device:TPU:1 now
where the time goes in v1:
time: 307 us; the launch traced here: 303 us
  waiting for transfers between devices  114 us (37%)
  starting transfers between devices  62.7 us (20%)
  local copies, waits for them, and re-layouts  34.1 us (11%)
  matrix products  29.2 us (10%)
  blocking collectives  26.5 us (9%)
  between operations  21.3 us (7%)
  other arithmetic  15.4 us (5%)
    ppermute x22, waiting for transfers between devices, shifted(): return lax.ppermute(value, axis, pairs)  103 us
    ppermute x7, starting transfers between devices, transposed(): return lax.ppermute(value, ('core', 'x_hi'), pairs)  33.1 us
    ppermute x22, starting transfers between devices, shifted(): return lax.ppermute(value, axis, pairs)  29.6 us
    psum x3, blocking collectives, shards(): norm_sq = lax.psum(norm_sq, axes)  26.5 us
    concatenate x1, local copies, waits for them, and re-layouts, hidden_of(): column = jnp.concatenate(up_way + down_way[:0:-1], axis=0)  22.8 us
    dot_general x6, matrix products, dot_t(): lax.dot_general(rows, weights, (((1,), (1,)), ((), ())), preferred_elemen...  16.4 us
    dot_general x1, matrix products, shards(): lax.dot_general(pre_grad, rows_in, (((0,), (0,)), ((), ())), preferred_el...  12.8 us
    ppermute x7, waiting for transfers between devices, transposed(): return lax.ppermute(value, ('core', 'x_hi'), pairs)  10.7 us
  transfers between devices with their start and end apart: 30, of which 13 were waited for; matrix products, arithmetic and copies ran while one was open for 24% of the time, Pallas kernels for 0%

profile of v1, /device:TPU:1, one launch (start us, length us, event | category | flops | bytes accessed | tf_op | source)
XLA Modules:
  0.0 302.7 jit_solution(15582395797997602615)
XLA Ops:
  7.2 6.2 %collective-permute-start.14 = (bf16[20,5120]{1,0:T(8,128)(2,1)}, bf16[20,5120]{1,0:T(8,128)(2,1)S(1)}, u32[]{:S(2)}, u32[]{:S(2)}) collective-permute-start(bf16[20,5120]{1,0:T(8,128)(2,1)} %bitcast.39), channel_id=1, source_target_pairs={{0,0},{4,64},{64,4},{68,68},{1,1},{5,65},{65,5},{69,69},{2,2},{6,6... | collective-permute-start | bytes 614408 | tf_op jit(solution)/shard_map/ppermute | solution.py:27
  13.4 4.1 %collective-permute-done.14 = bf16[20,5120]{1,0:T(8,128)(2,1)S(1)} collective-permute-done((bf16[20,5120]{1,0:T(8,128)(2,1)}, bf16[20,5120]{1,0:T(8,128)(2,1)S(1)}, u32[]{:S(2)}, u32[]{:S(2)}) %collective-permute-start.14) | collective-permute-done | bytes 204832 | tf_op jit(solution)/shard_map/ppermute | solution.py:27
  17.5 2.7 collective-permute-start.15
  20.2 1.6 collective-permute-start.17
  21.9 1.8 collective-permute-done.15
  23.7 5.4 %collective-permute-done.16 = bf16[20,5120]{1,0:T(8,128)(2,1)S(1)} collective-permute-done((bf16[20,5120]{1,0:T(8,128)(2,1)S(1)}, bf16[20,5120]{1,0:T(8,128)(2,1)S(1)}, u32[]{:S(2)}, u32[]{:S(2)}) %collective-permute-start.16) | collective-permute-done | bytes 204832 | tf_op jit(solution)/shard_map/ppermute | solution.py:22
  29.1 1.1 pad_maximum_fusion
  30.2 6.6 %collective-permute-start = (bf16[20,5120]{1,0:T(8,128)(2,1)S(1)}, bf16[20,5120]{1,0:T(8,128)(2,1)S(1)}, u32[]{:S(2)}, u32[]{:S(2)}) collective-permute-start(bf16[20,5120]{1,0:T(8,128)(2,1)S(1)} %bitcast.40), channel_id=1, source_target_pairs={{0,0},{4,64},{64,4},{68,68},{1,1},{5,65},{65,5},{69,69},{2,2},{6,6... | collective-permute-start | bytes 614408 | tf_op jit(solution)/shard_map/ppermute | solution.py:27
  36.8 3.9 %collective-permute-done = bf16[20,5120]{1,0:T(8,128)(2,1)S(1)} collective-permute-done((bf16[20,5120]{1,0:T(8,128)(2,1)S(1)}, bf16[20,5120]{1,0:T(8,128)(2,1)S(1)}, u32[]{:S(2)}, u32[]{:S(2)}) %collective-permute-start) | collective-permute-done | bytes 204832 | tf_op jit(solution)/shard_map/ppermute | solution.py:27
  40.7 5.6 %collective-permute-start.1 = (bf16[20,5120]{1,0:T(8,128)(2,1)S(1)}, bf16[20,5120]{1,0:T(8,128)(2,1)S(1)}, u32[]{:S(2)}, u32[]{:S(2)}) collective-permute-start(bf16[20,5120]{1,0:T(8,128)(2,1)S(1)} %collective-permute-done), channel_id=1, source_target_pairs={{8,0},{16,8},{24,16},{32,24},{40,32},{48,40},{56,48},{0,56},{9,1},... | collective-permute-start | bytes 614408 | tf_op jit(solution)/shard_map/ppermute | solution.py:22
  46.3 11.0 %collective-permute-done.1 = bf16[20,5120]{1,0:T(8,128)(2,1)S(1)} collective-permute-done((bf16[20,5120]{1,0:T(8,128)(2,1)S(1)}, bf16[20,5120]{1,0:T(8,128)(2,1)S(1)}, u32[]{:S(2)}, u32[]{:S(2)}) %collective-permute-start.1) | collective-permute-done | bytes 204832 | tf_op jit(solution)/shard_map/ppermute | solution.py:22
  57.3 3.5 %collective-permute-start.2 = (bf16[20,5120]{1,0:T(8,128)(2,1)S(1)}, bf16[20,5120]{1,0:T(8,128)(2,1)S(1)}, u32[]{:S(2)}, u32[]{:S(2)}) collective-permute-start(bf16[20,5120]{1,0:T(8,128)(2,1)S(1)} %collective-permute-done.1), channel_id=1, source_target_pairs={{8,0},{16,8},{24,16},{32,24},{40,32},{48,40},{56,48},{0,56},{9,1},... | collective-permute-start | bytes 614408 | tf_op jit(solution)/shard_map/ppermute | solution.py:22
  60.8 10.7 %collective-permute-done.2 = bf16[20,5120]{1,0:T(8,128)(2,1)S(1)} collective-permute-done((bf16[20,5120]{1,0:T(8,128)(2,1)S(1)}, bf16[20,5120]{1,0:T(8,128)(2,1)S(1)}, u32[]{:S(2)}, u32[]{:S(2)}) %collective-permute-start.2) | collective-permute-done | bytes 204832 | tf_op jit(solution)/shard_map/ppermute | solution.py:22
  71.5 3.5 %collective-permute-start.3 = (bf16[20,5120]{1,0:T(8,128)(2,1)S(1)}, bf16[20,5120]{1,0:T(8,128)(2,1)S(1)}, u32[]{:S(2)}, u32[]{:S(2)}) collective-permute-start(bf16[20,5120]{1,0:T(8,128)(2,1)S(1)} %collective-permute-done.2), channel_id=1, source_target_pairs={{8,0},{16,8},{24,16},{32,24},{40,32},{48,40},{56,48},{0,56},{9,1},... | collective-permute-start | bytes 614408 | tf_op jit(solution)/shard_map/ppermute | solution.py:22
  75.1 3.5 %collective-permute-start.8 = (bf16[112,5120]{1,0:T(8,128)(2,1)}, bf16[112,5120]{1,0:T(8,128)(2,1)S(1)}, u32[]{:S(2)}, u32[]{:S(2)}) collective-permute-start(bf16[112,5120]{1,0:T(8,128)(2,1)} %param.16), channel_id=1, source_target_pairs={{0,0},{4,64},{64,4},{68,68},{1,1},{5,65},{65,5},{69,69},{2,2},{6,6... | collective-permute-start | bytes 3440648 | tf_op jit(solution)/shard_map/ppermute | solution.py:27
  79.2 0.1 collective-permute-start.7
  79.3 4.1 %collective-permute-done.3 = bf16[20,5120]{1,0:T(8,128)(2,1)S(1)} collective-permute-done((bf16[20,5120]{1,0:T(8,128)(2,1)S(1)}, bf16[20,5120]{1,0:T(8,128)(2,1)S(1)}, u32[]{:S(2)}, u32[]{:S(2)}) %collective-permute-start.3) | collective-permute-done | bytes 204832 | tf_op jit(solution)/shard_map/ppermute | solution.py:22
  83.4 3.5 %collective-permute-start.4 = (bf16[20,5120]{1,0:T(8,128)(2,1)S(1)}, bf16[20,5120]{1,0:T(8,128)(2,1)}, u32[]{:S(2)}, u32[]{:S(2)}) collective-permute-start(bf16[20,5120]{1,0:T(8,128)(2,1)S(1)} %collective-permute-done.3), channel_id=1, source_target_pairs={{8,0},{16,8},{24,16},{32,24},{40,32},{48,40},{56,48},{0,56},{9,1},... | collective-permute-start | bytes 614408 | tf_op jit(solution)/shard_map/ppermute | solution.py:22
  86.9 1.2 fusion.8
  88.1 4.2 %collective-permute-start.20 = (bf16[112,5120]{1,0:T(8,128)(2,1)}, bf16[112,5120]{1,0:T(8,128)(2,1)}, u32[]{:S(2)}, u32[]{:S(2)}) collective-permute-start(bf16[112,5120]{1,0:T(8,128)(2,1)} %fusion.8), channel_id=1, source_target_pairs={{0,0},{4,64},{64,4},{68,68},{1,1},{5,65},{65,5},{69,69},{2,2},{6,6... | collective-permute-start | bytes 3440648 | tf_op jit(solution)/shard_map/ppermute | solution.py:27
  92.4 2.8 collective-permute-start.18
  95.2 0.1 collective-permute-start.9
  95.4 0.7 copy-done.9
  96.1 22.8 %concatenate.21 = bf16[160,5120]{1,0:T(8,128)(2,1)} concatenate(bf16[20,5120]{1,0:T(8,128)(2,1)} %copy-done.3, bf16[20,5120]{1,0:T(8,128)(2,1)} %copy-done.4, bf16[20,5120]{1,0:T(8,128)(2,1)} %copy-done.6, bf16[20,5120]{1,0:T(8,128)(2,1)} %copy-done.8, bf16[20,5120]{1,0:T(8,128)(2,1)} %collective-permute-done.4, bf16[20,5120]{1,0:T(8,128)(2,1)} %copy-done.9, ...), dimensions={0} | concatenate | bytes 3276800 | tf_op jit(solution)/shard_map/concatenate | solution.py:64
  118.8 0.7 collective-permute-start.10
  119.5 0.8 collective-permute-start.11
  120.3 0.1 constant_dynamic-update-slice_fusion.1
  120.4 0.1 collective-permute-start.25
  120.5 1.3 collective-permute-start.21
  121.8 0.1 collective-permute-start.19
  121.9 1.3 constant_dynamic-update-slice_fusion
  123.3 32.8 %collective-permute-done.10 = bf16[160,5120]{1,0:T(8,128)(2,1)} collective-permute-done((bf16[160,5120]{1,0:T(8,128)(2,1)}, bf16[160,5120]{1,0:T(8,128)(2,1)}, u32[]{:S(2)}, u32[]{:S(2)}) %collective-permute-start.10) | collective-permute-done | bytes 1638432 | tf_op jit(solution)/shard_map/ppermute | solution.py:22
  156.0 1.2 slice.16
  157.2 1.9 collective-permute-start.12
  159.2 1.6 convolution_dynamic-update-slice_fusion.2
  160.7 1.2 slice.17
  161.9 0.1 collective-permute-start.13
  162.0 3.1 %convolution_dynamic-update-slice_fusion.1 = f32[640,224]{1,0:T(8,128)} fusion(f32[640,224]{1,0:T(8,128)} %convolution_dynamic-update-slice_fusion.2, bf16[160,5120]{1,0:T(8,128)(2,1)} %collective-permute-done.10, bf16[224,5120]{1,0:T(8,128)(2,1)S(1)} %constant_dynamic-update-slice_fusion), kind=kOutput, calls=%fused_computation.22 | convolution fusion | flops 367001600 | bytes 4096000 | tf_op jit(solution)/shard_map/dot_general | solution.py:48
  165.1 3.0 %convolution_dynamic-update-slice_fusion = f32[640,224]{1,0:T(8,128)} fusion(f32[640,224]{1,0:T(8,128)} %convolution_dynamic-update-slice_fusion.1, bf16[160,5120]{1,0:T(8,128)(2,1)} %collective-permute-done.11, bf16[224,5120]{1,0:T(8,128)(2,1)S(1)} %constant_dynamic-update-slice_fusion), kind=kOutput, calls=%fused_computation.21 | convolution fusion | flops 367001600 | bytes 4096000 | tf_op jit(solution)/shard_map/dot_general | solution.py:48
  168.1 7.6 %collective-permute-done.12 = bf16[80,5120]{1,0:T(8,128)(2,1)S(1)} collective-permute-done((bf16[80,5120]{1,0:T(8,128)(2,1)S(1)}, bf16[80,5120]{1,0:T(8,128)(2,1)S(1)}, u32[]{:S(2)}, u32[]{:S(2)}) %collective-permute-start.12) | collective-permute-done | bytes 819232 | tf_op jit(solution)/shard_map/ppermute | solution.py:22
  175.7 1.5 convolution_dynamic-update-slice_fusion.4
  177.2 4.1 %collective-permute-done.13 = bf16[80,5120]{1,0:T(8,128)(2,1)S(1)} collective-permute-done((bf16[80,5120]{1,0:T(8,128)(2,1)S(1)}, bf16[80,5120]{1,0:T(8,128)(2,1)S(1)}, u32[]{:S(2)}, u32[]{:S(2)}) %collective-permute-start.13) | collective-permute-done | bytes 819232 | tf_op jit(solution)/shard_map/ppermute | solution.py:22
  181.3 1.5 convolution_dynamic-update-slice_fusion.3
  182.8 1.2 reshape.16
  184.0 1.0 copy.14
  184.9 1.2 reshape.17
  186.1 0.2 copy.15
  186.4 5.7 %fusion.11 = f32[640,224]{0,1:T(8,128)S(1)} fusion(bf16[640,5120]{1,0:T(8,128)(2,1)} %all-gather.2.cloned.1.call-done, bf16[112,5120]{1,0:T(8,128)(2,1)} %collective-permute-done.21, bf16[112,5120]{1,0:T(8,128)(2,1)} %collective-permute-done.20), kind=kOutput, calls=%fused_computation.17 | convolution fusion | flops 1472737280 | bytes 9420800 | tf_op jit(solution)/shard_map/dot_general | solution.py:48
  192.1 12.8 %convolution_multiply_fusion = f32[224,5120]{1,0:T(8,128)} fusion(bf16[640,5120]{1,0:T(8,128)(2,1)} %all-gather.2.cloned.1.call-done, bf16[112,5120]{1,0:T(8,128)(2,1)} %collective-permute-done.19, bf16[112,5120]{1,0:T(8,128)(2,1)} %collective-permute-done.18, s32[]{:T(128)S(6)} %select_n.50, f32[640,224]{0,1:T(8,128)S(1)} %copy.15, f32[640,224]{0,1:T(8,128)S(1)} %fusion.11), kind=kOutput, calls=%fused_computation | convolution fusion | flops 2943324160 | bytes 21135364 | tf_op jit(solution)/shard_map/dot_general | solution.py:98
  205.0 3.2 %slice.19 = f32[112,5120]{1,0:T(8,128)} slice(f32[224,5120]{1,0:T(8,128)} %convolution_multiply_fusion), slice={[112:224], [0:5120]} | slice | bytes 4587520 | tf_op jit(solution)/shard_map/slice | solution.py:104
  208.2 2.6 collective-permute-start.22
  210.8 3.5 %broadcast_select_fusion = f32[1,112,5120]{2,1,0:T(8,128)} fusion(f32[1,112,5120]{2,1,0:T(8,128)} %collective-permute-done.25, f32[1,112,5120]{2,1,0:T(8,128)} %param.13, pred[]{:T(512)} %eq.14), kind=kLoop, calls=%fused_computation.26 | loop fusion | flops 573440 | bytes 6881281 | tf_op jit(solution)/shard_map/jit(_where)/select_n | solution.py:42
  214.2 0.9 collective-permute-done.22
  215.2 4.3 %multiply_reduce_fusion = (f32[]{:T(128)}, f32[112,5120]{1,0:T(8,128)}) fusion(f32[112,5120]{1,0:T(8,128)} %collective-permute-done.22, f32[224,5120]{1,0:T(8,128)S(1)} %copy-done.2), kind=kLoop, calls=%fused_computation.16 | loop fusion | flops 1720319 | bytes 6881284 | tf_op jit(solution)/shard_map/reduce_sum | solution.py:105
  219.5 6.1 %collective-permute-start.24 = (f32[112,5120]{1,0:T(8,128)}, f32[112,5120]{1,0:T(8,128)}, u32[]{:S(2)}, u32[]{:S(2)}) collective-permute-start(f32[112,5120]{1,0:T(8,128)} %get-tuple-element.7), channel_id=1, source_target_pairs={{0,0},{4,64},{64,4},{68,68},{1,1},{5,65},{65,5},{69,69},{2,2},{6,6... | collective-permute-start | bytes 6881288 | tf_op jit(solution)/shard_map/ppermute | solution.py:27
  225.5 0.4 collective-permute-start.27
  227.3 24.3 %collective-permute-done.27 = f32[1]{0:T(128)} collective-permute-done((f32[1]{0:T(128)}, f32[1]{0:T(128)}, u32[]{:S(2)}, u32[]{:S(2)}) %collective-permute-start.27) | collective-permute-done | bytes 36 | tf_op jit(solution)/shard_map/ppermute | solution.py:22
  252.3 0.9 collective-permute-start.28
  253.2 11.5 %psum.21 = f32[]{:T(128)} all-reduce(f32[]{:T(128)} %get-tuple-element.6), channel_id=1, replica_groups=mesh['x_lo'=2,'core'=2,'z'=8,'x_hi'=2,'y'=4] {'z'}, use_global_device_ids=true, to_apply=%region_1.2 | all-reduce | flops 1 | bytes 8 | tf_op jit(solution)/shard_map/psum | solution.py:107
  266.0 6.7 %psum.22 = f32[]{:T(128)} all-reduce(f32[]{:T(128)} %psum.21), channel_id=1, replica_groups=mesh['x_lo'=2,'core'=2,'z'=8,'x_hi'=2,'y'=4] {'y'}, use_global_device_ids=true, to_apply=%region_2.3 | all-reduce | flops 1 | bytes 8 | tf_op jit(solution)/shard_map/psum | solution.py:107
  272.7 8.2 %psum.23 = f32[]{:T(128)} all-reduce(f32[]{:T(128)} %psum.22), channel_id=1, replica_groups=mesh['x_lo'=2,'core'=2,'z'=8,'x_hi'=2,'y'=4] {'core'}, use_global_device_ids=true, to_apply=%region_3.4 | all-reduce | flops 1 | bytes 8 | tf_op jit(solution)/shard_map/psum | solution.py:107
  280.9 3.8 %collective-permute-start.23 = (f32[]{:T(128)}, f32[]{:T(128)}, u32[]{:S(2)}, u32[]{:S(2)}) collective-permute-start(f32[]{:T(128)} %psum.23), channel_id=1, source_target_pairs={{0,0},{4,64},{64,4},{68,68},{1,1},{5,65},{65,5},{69,69},{2,2},{6,6... | collective-permute-start | bytes 20 | tf_op jit(solution)/shard_map/ppermute | solution.py:27
  284.7 2.7 collective-permute-done.23
  288.2 5.4 %select_add_fusion = (f32[1,112,5120]{2,1,0:T(8,128)}, f32[1,112,5120]{2,1,0:T(8,128)}) fusion(f32[1,112,5120]{2,1,0:T(8,128)} %collective-permute-done.26, f32[1,112,5120]{2,1,0:T(8,128)} %collective-permute-done.25, pred[]{:T(512)} %eq.13, f32[112,5120]{1,0:T(8,128)} %collective-permute-done.24, f32[]{:T(128)S(6)} %mul.58, f32[1,112,5120]{2,1,0:T(8,128)S(1)} %copy-done), kind=kLoop, calls=%fused_computation.15 | loop fusion | flops 2867200 | bytes 13762565 | tf_op jit(solution)/shard_map/add | solution.py:113
  (44 shorter events, 0.2 us)
Async XLA Ops:
  7.2 23.1 %copy-start.10 = (bf16[1,20,5120]{2,1,0:T(8,128)(2,1)S(1)}, bf16[1,20,5120]{2,1,0:T(8,128)(2,1)}, u32[]{:S(2)}) copy-start(bf16[1,20,5120]{2,1,0:T(8,128)(2,1)} %param.10) | copy-start | bytes 614404
  7.2 79.8 %copy-start = (f32[1,112,5120]{2,1,0:T(8,128)S(1)}, f32[1,112,5120]{2,1,0:T(8,128)}, u32[]{:S(2)}) copy-start(f32[1,112,5120]{2,1,0:T(8,128)} %param.11) | copy-start | bytes 6881284
  7.2 179.2 %all-gather.2.cloned.1.call-start = ((), (), s32[]{:S(2)}) async-start(), calls=%async_computation | async-start | bytes 7372800 | tf_op jit(solution)/shard_map/all_gather | solution.py:55
  7.2 10.3 %collective-permute-start.14 = (bf16[20,5120]{1,0:T(8,128)(2,1)}, bf16[20,5120]{1,0:T(8,128)(2,1)S(1)}, u32[]{:S(2)}, u32[]{:S(2)}) collective-permute-start(bf16[20,5120]{1,0:T(8,128)(2,1)} %bitcast.39), channel_id=1, source_target_pairs={{0,0},{4,64},{64,4},{68,68},{1,1},{5,65},{65,5},{69,69},{2,2},{6,6... | collective-permute-start | bytes 614408 | tf_op jit(solution)/shard_map/ppermute | solution.py:27
  17.5 6.2 %collective-permute-start.15 = (bf16[20,5120]{1,0:T(8,128)(2,1)S(1)}, bf16[20,5120]{1,0:T(8,128)(2,1)S(1)}, u32[]{:S(2)}, u32[]{:S(2)}) collective-permute-start(bf16[20,5120]{1,0:T(8,128)(2,1)S(1)} %collective-permute-done.14), channel_id=1, source_target_pairs={{1,0},{2,1},{3,2},{0,3},{5,4},{6,5},{7,6},{4,7},{9,8},{10,9},{11,1... | collective-permute-start | bytes 614408 | tf_op jit(solution)/shard_map/ppermute | solution.py:22
  20.2 8.9 %collective-permute-start.16 = (bf16[20,5120]{1,0:T(8,128)(2,1)S(1)}, bf16[20,5120]{1,0:T(8,128)(2,1)S(1)}, u32[]{:S(2)}, u32[]{:S(2)}) collective-permute-start(bf16[20,5120]{1,0:T(8,128)(2,1)S(1)} %collective-permute-done.14), channel_id=1, source_target_pairs={{3,0},{0,1},{1,2},{2,3},{7,4},{4,5},{5,6},{6,7},{11,8},{8,9},{9,10... | collective-permute-start | bytes 614408 | tf_op jit(solution)/shard_map/ppermute | solution.py:22
  20.2 8.9 %collective-permute-start.17 = (bf16[20,5120]{1,0:T(8,128)(2,1)S(1)}, bf16[20,5120]{1,0:T(8,128)(2,1)S(1)}, u32[]{:S(2)}, u32[]{:S(2)}) collective-permute-start(bf16[20,5120]{1,0:T(8,128)(2,1)S(1)} %collective-permute-done.14), channel_id=1, source_target_pairs={{2,0},{3,1},{0,2},{1,3},{6,4},{7,5},{4,6},{5,7},{10,8},{11,9},{8,1... | collective-permute-start | bytes 614408 | tf_op jit(solution)/shard_map/ppermute | solution.py:22
  30.2 10.4 %collective-permute-start = (bf16[20,5120]{1,0:T(8,128)(2,1)S(1)}, bf16[20,5120]{1,0:T(8,128)(2,1)S(1)}, u32[]{:S(2)}, u32[]{:S(2)}) collective-permute-start(bf16[20,5120]{1,0:T(8,128)(2,1)S(1)} %bitcast.40), channel_id=1, source_target_pairs={{0,0},{4,64},{64,4},{68,68},{1,1},{5,65},{65,5},{69,69},{2,2},{6,6... | collective-permute-start | bytes 614408 | tf_op jit(solution)/shard_map/ppermute | solution.py:27
  40.7 30.9 %copy-start.3 = (bf16[20,5120]{1,0:T(8,128)(2,1)}, bf16[20,5120]{1,0:T(8,128)(2,1)S(1)}, u32[]{:S(2)}) copy-start(bf16[20,5120]{1,0:T(8,128)(2,1)S(1)} %collective-permute-done) | copy-start | bytes 614404
  40.7 16.6 %collective-permute-start.1 = (bf16[20,5120]{1,0:T(8,128)(2,1)S(1)}, bf16[20,5120]{1,0:T(8,128)(2,1)S(1)}, u32[]{:S(2)}, u32[]{:S(2)}) collective-permute-start(bf16[20,5120]{1,0:T(8,128)(2,1)S(1)} %collective-permute-done), channel_id=1, source_target_pairs={{8,0},{16,8},{24,16},{32,24},{40,32},{48,40},{56,48},{0,56},{9,1},... | collective-permute-start | bytes 614408 | tf_op jit(solution)/shard_map/ppermute | solution.py:22
  46.3 14.5 %collective-permute-start.5 = (bf16[20,5120]{1,0:T(8,128)(2,1)S(1)}, bf16[20,5120]{1,0:T(8,128)(2,1)S(1)}, u32[]{:S(2)}, u32[]{:S(2)}) collective-permute-start(bf16[20,5120]{1,0:T(8,128)(2,1)S(1)} %collective-permute-done), channel_id=1, source_target_pairs={{56,0},{0,8},{8,16},{16,24},{24,32},{32,40},{40,48},{48,56},{57,1}... | collective-permute-start | bytes 614408 | tf_op jit(solution)/shard_map/ppermute | solution.py:22
  57.3 17.8 %copy-start.4 = (bf16[20,5120]{1,0:T(8,128)(2,1)}, bf16[20,5120]{1,0:T(8,128)(2,1)S(1)}, u32[]{:S(2)}) copy-start(bf16[20,5120]{1,0:T(8,128)(2,1)S(1)} %collective-permute-done.1) | copy-start | bytes 614404
  57.3 14.3 %collective-permute-start.2 = (bf16[20,5120]{1,0:T(8,128)(2,1)S(1)}, bf16[20,5120]{1,0:T(8,128)(2,1)S(1)}, u32[]{:S(2)}, u32[]{:S(2)}) collective-permute-start(bf16[20,5120]{1,0:T(8,128)(2,1)S(1)} %collective-permute-done.1), channel_id=1, source_target_pairs={{8,0},{16,8},{24,16},{32,24},{40,32},{48,40},{56,48},{0,56},{9,1},... | collective-permute-start | bytes 614408 | tf_op jit(solution)/shard_map/ppermute | solution.py:22
  60.8 17.8 %copy-start.5 = (bf16[20,5120]{1,0:T(8,128)(2,1)}, bf16[20,5120]{1,0:T(8,128)(2,1)S(1)}, u32[]{:S(2)}) copy-start(bf16[20,5120]{1,0:T(8,128)(2,1)S(1)} %collective-permute-done.5) | copy-start | bytes 614404
  60.8 18.4 %collective-permute-start.6 = (bf16[20,5120]{1,0:T(8,128)(2,1)S(1)}, bf16[20,5120]{1,0:T(8,128)(2,1)S(1)}, u32[]{:S(2)}, u32[]{:S(2)}) collective-permute-start(bf16[20,5120]{1,0:T(8,128)(2,1)S(1)} %collective-permute-done.5), channel_id=1, source_target_pairs={{56,0},{0,8},{8,16},{16,24},{24,32},{32,40},{40,48},{48,56},{57,1}... | collective-permute-start | bytes 614408 | tf_op jit(solution)/shard_map/ppermute | solution.py:22
  71.5 7.7 %copy-start.6 = (bf16[20,5120]{1,0:T(8,128)(2,1)}, bf16[20,5120]{1,0:T(8,128)(2,1)S(1)}, u32[]{:S(2)}) copy-start(bf16[20,5120]{1,0:T(8,128)(2,1)S(1)} %collective-permute-done.2) | copy-start | bytes 614404
  71.5 11.9 %collective-permute-start.3 = (bf16[20,5120]{1,0:T(8,128)(2,1)S(1)}, bf16[20,5120]{1,0:T(8,128)(2,1)S(1)}, u32[]{:S(2)}, u32[]{:S(2)}) collective-permute-start(bf16[20,5120]{1,0:T(8,128)(2,1)S(1)} %collective-permute-done.2), channel_id=1, source_target_pairs={{8,0},{16,8},{24,16},{32,24},{40,32},{48,40},{56,48},{0,56},{9,1},... | collective-permute-start | bytes 614408 | tf_op jit(solution)/shard_map/ppermute | solution.py:22
  75.1 20.2 %collective-permute-start.8 = (bf16[112,5120]{1,0:T(8,128)(2,1)}, bf16[112,5120]{1,0:T(8,128)(2,1)S(1)}, u32[]{:S(2)}, u32[]{:S(2)}) collective-permute-start(bf16[112,5120]{1,0:T(8,128)(2,1)} %param.16), channel_id=1, source_target_pairs={{0,0},{4,64},{64,4},{68,68},{1,1},{5,65},{65,5},{69,69},{2,2},{6,6... | collective-permute-start | bytes 3440648 | tf_op jit(solution)/shard_map/ppermute | solution.py:27
  79.2 16.0 %copy-start.7 = (bf16[20,5120]{1,0:T(8,128)(2,1)}, bf16[20,5120]{1,0:T(8,128)(2,1)S(1)}, u32[]{:S(2)}) copy-start(bf16[20,5120]{1,0:T(8,128)(2,1)S(1)} %collective-permute-done.6) | copy-start | bytes 614404
  79.2 16.1 %collective-permute-start.7 = (bf16[20,5120]{1,0:T(8,128)(2,1)S(1)}, bf16[20,5120]{1,0:T(8,128)(2,1)S(1)}, u32[]{:S(2)}, u32[]{:S(2)}) collective-permute-start(bf16[20,5120]{1,0:T(8,128)(2,1)S(1)} %collective-permute-done.6), channel_id=1, source_target_pairs={{56,0},{0,8},{8,16},{16,24},{24,32},{32,40},{40,48},{48,56},{57,1}... | collective-permute-start | bytes 614408 | tf_op jit(solution)/shard_map/ppermute | solution.py:22
  83.4 11.9 %copy-start.8 = (bf16[20,5120]{1,0:T(8,128)(2,1)}, bf16[20,5120]{1,0:T(8,128)(2,1)S(1)}, u32[]{:S(2)}) copy-start(bf16[20,5120]{1,0:T(8,128)(2,1)S(1)} %collective-permute-done.3) | copy-start | bytes 614404
  83.4 12.6 %collective-permute-start.4 = (bf16[20,5120]{1,0:T(8,128)(2,1)S(1)}, bf16[20,5120]{1,0:T(8,128)(2,1)}, u32[]{:S(2)}, u32[]{:S(2)}) collective-permute-start(bf16[20,5120]{1,0:T(8,128)(2,1)S(1)} %collective-permute-done.3), channel_id=1, source_target_pairs={{8,0},{16,8},{24,16},{32,24},{40,32},{48,40},{56,48},{0,56},{9,1},... | collective-permute-start | bytes 614408 | tf_op jit(solution)/shard_map/ppermute | solution.py:22
  88.1 32.3 %collective-permute-start.20 = (bf16[112,5120]{1,0:T(8,128)(2,1)}, bf16[112,5120]{1,0:T(8,128)(2,1)}, u32[]{:S(2)}, u32[]{:S(2)}) collective-permute-start(bf16[112,5120]{1,0:T(8,128)(2,1)} %fusion.8), channel_id=1, source_target_pairs={{0,0},{4,64},{64,4},{68,68},{1,1},{5,65},{65,5},{69,69},{2,2},{6,6... | collective-permute-start | bytes 3440648 | tf_op jit(solution)/shard_map/ppermute | solution.py:27
  92.4 28.1 %collective-permute-start.18 = (bf16[112,5120]{1,0:T(8,128)(2,1)}, bf16[112,5120]{1,0:T(8,128)(2,1)}, u32[]{:S(2)}, u32[]{:S(2)}) collective-permute-start(bf16[112,5120]{1,0:T(8,128)(2,1)} %param.15), channel_id=1, source_target_pairs={{0,0},{4,64},{64,4},{68,68},{1,1},{5,65},{65,5},{69,69},{2,2},{6,6... | collective-permute-start | bytes 3440648 | tf_op jit(solution)/shard_map/ppermute | solution.py:27
  95.2 26.6 %collective-permute-start.9 = (bf16[112,5120]{1,0:T(8,128)(2,1)S(1)}, bf16[112,5120]{1,0:T(8,128)(2,1)}, u32[]{:S(2)}, u32[]{:S(2)}) collective-permute-start(bf16[112,5120]{1,0:T(8,128)(2,1)S(1)} %collective-permute-done.8), channel_id=1, source_target_pairs={{64,0},{0,64},{65,1},{1,65},{66,2},{2,66},{67,3},{3,67},{68,4},{4,... | collective-permute-start | bytes 3440648 | tf_op jit(solution)/shard_map/ppermute | solution.py:22
  95.3 0.7 copy-start.9
  118.8 37.2 %collective-permute-start.10 = (bf16[160,5120]{1,0:T(8,128)(2,1)}, bf16[160,5120]{1,0:T(8,128)(2,1)}, u32[]{:S(2)}, u32[]{:S(2)}) collective-permute-start(bf16[160,5120]{1,0:T(8,128)(2,1)} %concatenate.21), channel_id=1, source_target_pairs={{1,0},{2,1},{3,2},{0,3},{5,4},{6,5},{7,6},{4,7},{9,8},{10,9},{11,1... | collective-permute-start | bytes 4915208 | tf_op jit(solution)/shard_map/ppermute | solution.py:22
  119.5 41.3 %collective-permute-start.11 = (bf16[160,5120]{1,0:T(8,128)(2,1)}, bf16[160,5120]{1,0:T(8,128)(2,1)}, u32[]{:S(2)}, u32[]{:S(2)}) collective-permute-start(bf16[160,5120]{1,0:T(8,128)(2,1)} %concatenate.21), channel_id=1, source_target_pairs={{3,0},{0,1},{1,2},{2,3},{7,4},{4,5},{5,6},{6,7},{11,8},{8,9},{9,10... | collective-permute-start | bytes 4915208 | tf_op jit(solution)/shard_map/ppermute | solution.py:22
  120.4 38.8 %copy-start.1 = (bf16[160,5120]{1,0:T(8,128)(2,1)S(1)}, bf16[160,5120]{1,0:T(8,128)(2,1)}, u32[]{:S(2)}) copy-start(bf16[160,5120]{1,0:T(8,128)(2,1)} %concatenate.21) | copy-start | bytes 4915204
  120.4 90.4 %collective-permute-start.25 = (f32[1,112,5120]{2,1,0:T(8,128)}, f32[1,112,5120]{2,1,0:T(8,128)}, u32[]{:S(2)}, u32[]{:S(2)}) collective-permute-start(f32[1,112,5120]{2,1,0:T(8,128)} %param.13), channel_id=1, source_target_pairs={{128,0},{0,128},{129,1},{1,129},{130,2},{2,130},{131,3},{3,131},{1... | collective-permute-start | bytes 6881288 | tf_op jit(solution)/shard_map/ppermute | solution.py:22
  120.5 65.8 %collective-permute-start.21 = (bf16[112,5120]{1,0:T(8,128)(2,1)}, bf16[112,5120]{1,0:T(8,128)(2,1)}, u32[]{:S(2)}, u32[]{:S(2)}) collective-permute-start(bf16[112,5120]{1,0:T(8,128)(2,1)} %collective-permute-done.20), channel_id=1, source_target_pairs={{64,0},{0,64},{65,1},{1,65},{66,2},{2,66},{67,3},{3,67},{68,4},{4,... | collective-permute-start | bytes 3440648 | tf_op jit(solution)/shard_map/ppermute | solution.py:22
  121.8 70.3 %collective-permute-start.19 = (bf16[112,5120]{1,0:T(8,128)(2,1)}, bf16[112,5120]{1,0:T(8,128)(2,1)}, u32[]{:S(2)}, u32[]{:S(2)}) collective-permute-start(bf16[112,5120]{1,0:T(8,128)(2,1)} %collective-permute-done.18), channel_id=1, source_target_pairs={{64,0},{0,64},{65,1},{1,65},{66,2},{2,66},{67,3},{3,67},{68,4},{4,... | collective-permute-start | bytes 3440648 | tf_op jit(solution)/shard_map/ppermute | solution.py:22
  157.2 18.5 %collective-permute-start.12 = (bf16[80,5120]{1,0:T(8,128)(2,1)S(1)}, bf16[80,5120]{1,0:T(8,128)(2,1)S(1)}, u32[]{:S(2)}, u32[]{:S(2)}) collective-permute-start(bf16[80,5120]{1,0:T(8,128)(2,1)S(1)} %slice.16), channel_id=1, source_target_pairs={{1,0},{2,1},{3,2},{0,3},{5,4},{6,5},{7,6},{4,7},{9,8},{10,9},{11,1... | collective-permute-start | bytes 2457608 | tf_op jit(solution)/shard_map/ppermute | solution.py:22
  161.9 19.4 %collective-permute-start.13 = (bf16[80,5120]{1,0:T(8,128)(2,1)S(1)}, bf16[80,5120]{1,0:T(8,128)(2,1)S(1)}, u32[]{:S(2)}, u32[]{:S(2)}) collective-permute-start(bf16[80,5120]{1,0:T(8,128)(2,1)S(1)} %slice.17), channel_id=1, source_target_pairs={{3,0},{0,1},{1,2},{2,3},{7,4},{4,5},{5,6},{6,7},{11,8},{8,9},{9,10... | collective-permute-start | bytes 2457608 | tf_op jit(solution)/shard_map/ppermute | solution.py:22
  208.2 7.0 %collective-permute-start.22 = (f32[112,5120]{1,0:T(8,128)}, f32[112,5120]{1,0:T(8,128)}, u32[]{:S(2)}, u32[]{:S(2)}) collective-permute-start(f32[112,5120]{1,0:T(8,128)} %slice.19), channel_id=1, source_target_pairs={{64,0},{0,64},{65,1},{1,65},{66,2},{2,66},{67,3},{3,67},{68,4},{4,... | collective-permute-start | bytes 6881288 | tf_op jit(solution)/shard_map/ppermute | solution.py:22
  210.8 4.4 %copy-start.2 = (f32[224,5120]{1,0:T(8,128)S(1)}, f32[224,5120]{1,0:T(8,128)}, u32[]{:S(2)}) copy-start(f32[224,5120]{1,0:T(8,128)} %convolution_multiply_fusion) | copy-start | bytes 13762564
  214.2 73.9 %collective-permute-start.26 = (f32[1,112,5120]{2,1,0:T(8,128)}, f32[1,112,5120]{2,1,0:T(8,128)}, u32[]{:S(2)}, u32[]{:S(2)}) collective-permute-start(f32[1,112,5120]{2,1,0:T(8,128)} %broadcast_select_fusion), channel_id=1, source_target_pairs={{64,0},{0,64},{65,1},{1,65},{66,2},{2,66},{67,3},{3,67},{68,4},{4,... | collective-permute-start | bytes 6881288 | tf_op jit(solution)/shard_map/ppermute | solution.py:22
  219.5 68.7 %collective-permute-start.24 = (f32[112,5120]{1,0:T(8,128)}, f32[112,5120]{1,0:T(8,128)}, u32[]{:S(2)}, u32[]{:S(2)}) collective-permute-start(f32[112,5120]{1,0:T(8,128)} %get-tuple-element.7), channel_id=1, source_target_pairs={{0,0},{4,64},{64,4},{68,68},{1,1},{5,65},{65,5},{69,69},{2,2},{6,6... | collective-permute-start | bytes 6881288 | tf_op jit(solution)/shard_map/ppermute | solution.py:27
  225.5 26.1 %collective-permute-start.27 = (f32[1]{0:T(128)}, f32[1]{0:T(128)}, u32[]{:S(2)}, u32[]{:S(2)}) collective-permute-start(f32[1]{0:T(128)} %param.14), channel_id=1, source_target_pairs={{128,0},{0,128},{129,1},{1,129},{130,2},{2,130},{131,3},{3,131},{1... | collective-permute-start | bytes 20 | tf_op jit(solution)/shard_map/ppermute | solution.py:22
  252.3 12.5 %collective-permute-start.28 = (f32[1]{0:T(128)}, f32[1]{0:T(128)}, u32[]{:S(2)}, u32[]{:S(2)}) collective-permute-start(f32[1]{0:T(128)} %select_n.58), channel_id=1, source_target_pairs={{64,0},{0,64},{65,1},{1,65},{66,2},{2,66},{67,3},{3,67},{68,4},{4,... | collective-permute-start | bytes 20 | tf_op jit(solution)/shard_map/ppermute | solution.py:22
  280.9 6.5 %collective-permute-start.23 = (f32[]{:T(128)}, f32[]{:T(128)}, u32[]{:S(2)}, u32[]{:S(2)}) collective-permute-start(f32[]{:T(128)} %psum.23), channel_id=1, source_target_pairs={{0,0},{4,64},{64,4},{68,68},{1,1},{5,65},{65,5},{69,69},{2,2},{6,6... | collective-permute-start | bytes 20 | tf_op jit(solution)/shard_map/ppermute | solution.py:27
Sparse Core Ops, SparseCore 0:
  30.3 90.9 all-gather.1

commit v2 on v1

v2 whole, which is shorter than its diff:
```python
import math

import jax
import jax.numpy as jnp
import numpy as np
from jax import lax
from jax.experimental import pallas as pl
from jax.experimental.pallas import tpu as pltpu
from jax.sharding import Mesh, PartitionSpec as P

D = 5120
FFW = 7168

eps = 1e-06

WIDTH_SCALE = D ** (-0.5)
MAX_NORM = 0.05 * math.sqrt(D * FFW)

SIZES = {"x_lo": 2, "core": 2, "z": 8, "x_hi": 2, "y": 4}
GOSSIP = ("x_lo", "core")
FSDP = ("z", "x_hi", "y")

ROWS = 112
HALF = 128
BLOCK = 512


def shifted(value, axis, steps):
    count = SIZES[axis]
    pairs = [((place + steps) % count, place) for place in range(count)]
    return lax.ppermute(value, axis, pairs)


def transposed(value, axis=None, steps=0):
    names = [name for name in SIZES if name in ("core", "x_hi", axis)]
    sizes = [SIZES[name] for name in names]
    pairs = []
    for place in np.ndindex(*sizes):
        here = dict(zip(names, place))
        there = dict(here, core=here["x_hi"], x_hi=here["core"])
        if axis is not None:
            there[axis] = (there[axis] + steps) % SIZES[axis]
        source = np.ravel_multi_index([there[name] for name in names], sizes)
        pairs.append((int(source), int(np.ravel_multi_index(place, sizes))))
    return lax.ppermute(value, tuple(names), pairs)


def after(ready, *values):
    zero = jnp.minimum(jnp.abs(ready[0, 0]), 0)
    return [value + zero.astype(value.dtype) for value in values]


def silu_slope(preact):
    sigmoid_val = jax.nn.sigmoid(preact)
    return sigmoid_val * (1.0 + preact * (1.0 - sigmoid_val))


def plan_rate(step):
    phase = (step[0] % 1000).astype(jnp.float32) / 1000.0
    return 0.4 + 1.8 * (1.0 + jnp.cos(math.pi * phase))


def deliver(stale, step):
    two_before = shifted(stale, "x_lo", 1)
    payload = jnp.where(lax.axis_index("core") == 1, two_before, stale)
    one_before = shifted(payload, "core", 1)
    return jnp.where(step[0] % 2 == 0, one_before, two_before)


def dot_t(rows, weights):
    return lax.dot_general(
        rows, weights, (((1,), (1,)), ((), ())), preferred_element_type=jnp.float32
    )


def both_cores(own):
    pad = jnp.zeros((HALF - ROWS, D), own.dtype)
    return jnp.concatenate([own, pad, shifted(own, "core", 1), pad], axis=0)


def stack_kernel(*refs):
    *blocks, out_ref = refs
    for at, block in enumerate(blocks):
        count = block.shape[0]
        out_ref[at * count : (at + 1) * count, :] = block[...]


def stacked(blocks):
    count = blocks[0].shape[0]
    wide = D // 4
    return pl.pallas_call(
        stack_kernel,
        grid=(4,),
        in_specs=[pl.BlockSpec((count, wide), lambda at: (0, at))] * len(blocks),
        out_specs=pl.BlockSpec((count * len(blocks), wide), lambda at: (0, at)),
        out_shape=jax.ShapeDtypeStruct((count * len(blocks), D), blocks[0].dtype),
        compiler_params=pltpu.CompilerParams(vmem_limit_bytes=32 * 2**20),
        name="stacked",
    )(*blocks)


def column_of(block):
    own, *ways = [transposed(block, "z", steps) for steps in (0, 1, 7)]
    up_way, down_way = [ways[0]], [ways[1]]
    for _ in range(3):
        up_way.append(shifted(up_way[-1], "z", 1))
    for _ in range(2):
        down_way.append(shifted(down_way[-1], "z", 7))
    return own, stacked([own] + up_way + down_way[::-1])


def hidden_of(column, down):
    following = shifted(column, "y", 1)
    before = shifted(column, "y", 3)
    half = column.shape[0] // 2
    far = [shifted(following[:half], "y", 1), shifted(before[half:], "y", 3)]
    hidden = jnp.concatenate(
        [dot_t(part, down) for part in (column, following, before, *far)], axis=0
    )
    width = hidden.shape[1]
    hidden = hidden.reshape(4, 8, -1, width).transpose(1, 0, 2, 3).reshape(-1, width)
    start = (8 - lax.axis_index("z")) % 8 * (hidden.shape[0] // 8)
    return lax.dynamic_slice_in_dim(
        jnp.concatenate([hidden, hidden], axis=0), start, hidden.shape[0], axis=0
    )


def other_kernel(x_ref, params_ref, up_ref, hidden_ref, own_ref, grad_ref, preact, up_proj, other):
    at = pl.program_id(0)
    blocks = D // BLOCK

    @pl.when(at == 0)
    def _():
        preact[...] = jnp.zeros_like(preact)
        up_proj[...] = jnp.zeros_like(up_proj)

    @pl.when(at < blocks)
    def _():
        rows = x_ref[...]
        preact[...] += dot_t(rows, params_ref[...])
        up_proj[...] += dot_t(rows, up_ref[...])

    @pl.when(at == blocks - 1)
    def _():
        slope = silu_slope(preact[...] * WIDTH_SCALE)
        turned = (hidden_ref[...] * up_proj[...] * slope).T.astype(jnp.bfloat16)
        own_ref[...] = turned[:HALF]
        other[...] = turned[HALF:]

    @pl.when(at >= blocks)
    def _():
        grad = jnp.dot(other[...], x_ref[...], preferred_element_type=jnp.float32)
        grad_ref[...] = grad[:ROWS] * WIDTH_SCALE


def other_half(rows_in, params, up, hidden):
    count = rows_in.shape[0]
    blocks = D // BLOCK
    weights = pl.BlockSpec((2 * HALF, BLOCK), lambda at: (0, jnp.minimum(at, blocks - 1)))
    return pl.pallas_call(
        other_kernel,
        grid=(2 * blocks,),
        in_specs=[
            pl.BlockSpec((count, BLOCK), lambda at: (0, lax.rem(at, blocks))),
            weights,
            weights,
            pl.BlockSpec((count, 2 * HALF), lambda at: (0, 0)),
        ],
        out_specs=[
            pl.BlockSpec((HALF, count), lambda at: (0, 0)),
            pl.BlockSpec((ROWS, BLOCK), lambda at: (0, jnp.maximum(at - blocks, 0))),
        ],
        out_shape=[
            jax.ShapeDtypeStruct((HALF, count), jnp.bfloat16),
            jax.ShapeDtypeStruct((ROWS, D), jnp.float32),
        ],
        scratch_shapes=[
            pltpu.VMEM((count, 2 * HALF), jnp.float32),
            pltpu.VMEM((count, 2 * HALF), jnp.float32),
            pltpu.VMEM((HALF, count), jnp.bfloat16),
        ],
        compiler_params=pltpu.CompilerParams(vmem_limit_bytes=32 * 2**20),
        cost_estimate=pl.CostEstimate(
            flops=2 * count * D * 640, bytes_accessed=4 * count * D + 2**23, transcendentals=0
        ),
        name="other_half",
    )(rows_in, params, up, hidden)


def own_kernel(x_ref, own_ref, grad_ref):
    grad = jnp.dot(own_ref[...], x_ref[...], preferred_element_type=jnp.float32)
    grad_ref[...] = grad[:ROWS] * WIDTH_SCALE


def own_half(rows_in, own):
    count = rows_in.shape[0]
    return pl.pallas_call(
        own_kernel,
        grid=(D // BLOCK,),
        in_specs=[
            pl.BlockSpec((count, BLOCK), lambda at: (0, at)),
            pl.BlockSpec((HALF, count), lambda at: (0, 0)),
        ],
        out_specs=pl.BlockSpec((ROWS, BLOCK), lambda at: (0, at)),
        out_shape=jax.ShapeDtypeStruct((ROWS, D), jnp.float32),
        compiler_params=pltpu.CompilerParams(vmem_limit_bytes=32 * 2**20),
        cost_estimate=pl.CostEstimate(
            flops=2 * count * D * HALF, bytes_accessed=2 * count * D + 2**21, transcendentals=0
        ),
        name="own_half",
    )(rows_in, own)


def shards(
    tokens, cotangent, gate_num, push_weight, stale_num, stale_weight, up_weight, down_weight, step
):
    rate = plan_rate(step)
    numerator = gate_num[0]

    near = [transposed(tokens[0], "y", steps) for steps in (0, 1, 3, 2)]
    own, column = column_of(cotangent[0])
    rows_in = lax.all_gather(stacked(near), "z", axis=0, tiled=True)

    params, up, down, stale = after(
        own,
        (numerator / push_weight[0]).astype(jnp.bfloat16),
        up_weight,
        down_weight,
        jnp.concatenate([stale_num[0], jnp.broadcast_to(stale_weight, (8, D))], axis=0),
    )
    params, up, down = (both_cores(transposed(value)) for value in (params, up, down))
    hidden = hidden_of(column, down)
    received = deliver(stale, step)
    rows_in, received = lax.optimization_barrier((rows_in, received))

    own, other_grad = other_half(rows_in, params, up, hidden)
    gate_grad = own_half(rows_in, own) + shifted(other_grad, "core", 1)
    norm_sq = jnp.sum(gate_grad * gate_grad)
    gate_grad = transposed(gate_grad)
    for axes in ("z", "y", "core"):
        norm_sq = lax.psum(norm_sq, axes)
    norm_sq = transposed(norm_sq)

    clip_factor = jnp.minimum(1.0, MAX_NORM / jnp.sqrt(norm_sq + eps))
    kept_half = 0.5 * (numerator - rate * clip_factor * gate_grad)
    kept_weight = 0.5 * push_weight
    new_num = kept_half + received[:ROWS]
    new_weight = kept_weight + received[ROWS, :1]
    return (new_num[None], new_weight, kept_half[None], kept_weight)


def solution(mesh):
    named = Mesh(np.asarray(mesh.devices).reshape(tuple(SIZES.values())), tuple(SIZES))
    groups = P(GOSSIP, FSDP, None)
    in_specs = (
        groups,
        groups,
        groups,
        P(GOSSIP),
        groups,
        P(GOSSIP),
        P(FSDP, None),
        P(FSDP, None),
        P(),
    )
    out_specs = (groups, P(GOSSIP), groups, P(GOSSIP))
    return jax.shard_map(shards, mesh=named, in_specs=in_specs, out_specs=out_specs, check_vma=False)
```

time: 307 us -> 284 us (0.925)
  waiting for transfers between devices: 114 us -> 87.3 us
  local copies, waits for them, and re-layouts: 34.1 us -> 12.2 us
  Pallas kernels: 0 us -> 16.2 us
  blocking collectives: 26.5 us -> 41.4 us
  matrix products: 29.2 us -> 17.3 us
  other arithmetic: 15.4 us -> 24.3 us
    ppermute x22 -> x15, waiting for transfers between devices: 103 us -> 17.9 us  [shifted(): return lax.ppermute(value, axis, pairs)]
    ppermute x7 -> x12, waiting for transfers between devices: 10.7 us -> 69.4 us  [transposed(): return lax.ppermute(value, tuple(names), pairs)]
    concatenate x2 -> x0, local copies, waits for them, and re-layouts: 24.1 us -> none  [the longest x1 22.8 us: hidden_of(): column = jnp.concatenate(up_way + down_way[:0:-1], axis=0)]
    pallas_call x0 -> x4, Pallas kernels: none -> 16.2 us  [the longest x1 10.7 us: other_half(): pl.pallas_call(other_kernel, grid=(2 * blocks,), in_specs=[pl.BlockSpec((...]
    psum x3, blocking collectives: 26.5 us -> 41.4 us  [shards(): norm_sq = lax.psum(norm_sq, axes)]
    dot_general x1 -> x0, matrix products: 12.8 us -> none  [shards(): lax.dot_general(pre_grad, rows_in, (((0,), (0,)), ((), ())), preferred_el...]
    ppermute x22 -> x15, starting transfers between devices: 29.6 us -> 16.9 us  [shifted(): return lax.ppermute(value, axis, pairs)]
    ppermute x7 -> x12, starting transfers between devices: 33.1 us -> 44.7 us  [transposed(): return lax.ppermute(value, tuple(names), pairs)]
  transfers between devices with their start and end apart: 30 -> 28, of which waited for: 13 -> 13; matrix products, arithmetic and copies ran while one was open for 24% -> 15% of each run, Pallas kernels for 0% -> 1%
where the time goes in v2:
time: 284 us; the launch traced here: 281 us
  waiting for transfers between devices  87.3 us (31%)
  starting transfers between devices  61.7 us (22%)
  blocking collectives  41.4 us (15%)
  other arithmetic  24.3 us (9%)
  between operations  20.5 us (7%)
  matrix products  17.3 us (6%)
  Pallas kernels  16.2 us (6%)
  local copies, waits for them, and re-layouts  12.2 us (4%)
    ppermute x12, waiting for transfers between devices, transposed(): return lax.ppermute(value, tuple(names), pairs)  69.4 us
    ppermute x12, starting transfers between devices, transposed(): return lax.ppermute(value, tuple(names), pairs)  44.7 us
    psum x3, blocking collectives, shards(): norm_sq = lax.psum(norm_sq, axes)  41.4 us
    ppermute x15, waiting for transfers between devices, shifted(): return lax.ppermute(value, axis, pairs)  17.9 us
    dot_general x5, matrix products, dot_t(): lax.dot_general(rows, weights, (((1,), (1,)), ((), ())), preferred_elemen...  17.3 us
    ppermute x15, starting transfers between devices, shifted(): return lax.ppermute(value, axis, pairs)  16.9 us
    pallas_call x1, Pallas kernels, other_half(): pl.pallas_call(other_kernel, grid=(2 * blocks,), in_specs=[pl.BlockSpec((...  10.7 us
    add x4, other arithmetic, after(): return [value + zero.astype(value.dtype) for value in values]  5.78 us
  transfers between devices with their start and end apart: 28, of which 13 were waited for; matrix products, arithmetic and copies ran while one was open for 15% of the time, Pallas kernels for 1%

profile of v2, /device:TPU:1, one launch (start us, length us, event | category | flops | bytes accessed | tf_op | source)
XLA Modules:
  0.0 281.0 jit_solution(10997605734143312082)
XLA Ops:
  7.2 6.2 %collective-permute-start = (bf16[20,5120]{1,0:T(8,128)(2,1)}, bf16[20,5120]{1,0:T(8,128)(2,1)S(1)}, u32[]{:S(2)}, u32[]{:S(2)}) collective-permute-start(bf16[20,5120]{1,0:T(8,128)(2,1)} %bitcast.41), channel_id=1, source_target_pairs={{0,0},{1,1},{2,2},{3,3},{64,4},{65,5},{66,6},{67,7},{4,64},{5,65},... | collective-permute-start | bytes 614408 | tf_op jit(solution)/shard_map/ppermute | solution.py:45
  13.4 2.5 collective-permute-start.1
  16.0 1.7 collective-permute-start.2
  17.6 2.6 collective-permute-start.3
  20.3 1.5 collective-permute-done.1.refs_1_
  21.8 4.3 %collective-permute-done.2.refs_2_ = bf16[20,5120]{1,0:T(8,128)(2,1)S(1)} collective-permute-done((bf16[20,5120]{1,0:T(8,128)(2,1)}, bf16[20,5120]{1,0:T(8,128)(2,1)S(1)}, u32[]{:S(2)}, u32[]{:S(2)}) %collective-permute-start.2) | collective-permute-done | bytes 204832 | tf_op jit(solution)/shard_map/ppermute | solution.py:45
  26.1 2.9 %collective-permute-done.3.refs_3_ = bf16[20,5120]{1,0:T(8,128)(2,1)S(1)} collective-permute-done((bf16[20,5120]{1,0:T(8,128)(2,1)}, bf16[20,5120]{1,0:T(8,128)(2,1)S(1)}, u32[]{:S(2)}, u32[]{:S(2)}) %collective-permute-start.3) | collective-permute-done | bytes 204832 | tf_op jit(solution)/shard_map/ppermute | solution.py:45
  29.0 1.6 stacked.2
  30.7 4.4 %collective-permute-start.4 = (bf16[20,5120]{1,0:T(8,128)(2,1)S(1)}, bf16[20,5120]{1,0:T(8,128)(2,1)S(1)}, u32[]{:S(2)}, u32[]{:S(2)}) collective-permute-start(bf16[20,5120]{1,0:T(8,128)(2,1)S(1)} %bitcast.45), channel_id=1, source_target_pairs={{0,0},{64,4},{8,8},{72,12},{16,16},{80,20},{24,24},{88,28},{32,32}... | collective-permute-start | bytes 614408 | tf_op jit(solution)/shard_map/ppermute | solution.py:45
  35.1 6.2 %collective-permute-start.11 = (bf16[20,5120]{1,0:T(8,128)(2,1)S(1)}, bf16[20,5120]{1,0:T(8,128)(2,1)S(1)}, u32[]{:S(2)}, u32[]{:S(2)}) collective-permute-start(bf16[20,5120]{1,0:T(8,128)(2,1)S(1)} %bitcast.46), channel_id=1, source_target_pairs={{8,0},{72,4},{16,8},{80,12},{24,16},{88,20},{32,24},{96,28},{40,32... | collective-permute-start | bytes 614408 | tf_op jit(solution)/shard_map/ppermute | solution.py:45
  42.5 0.5 slice.20
  43.7 6.5 %collective-permute-done.11.refs_1_ = bf16[20,5120]{1,0:T(8,128)(2,1)S(1)} collective-permute-done((bf16[20,5120]{1,0:T(8,128)(2,1)S(1)}, bf16[20,5120]{1,0:T(8,128)(2,1)S(1)}, u32[]{:S(2)}, u32[]{:S(2)}) %collective-permute-start.11) | collective-permute-done | bytes 204832 | tf_op jit(solution)/shard_map/ppermute | solution.py:45
  50.2 4.1 %collective-permute-start.12 = (bf16[20,5120]{1,0:T(8,128)(2,1)S(1)}, bf16[20,5120]{1,0:T(8,128)(2,1)S(1)}, u32[]{:S(2)}, u32[]{:S(2)}) collective-permute-start(bf16[20,5120]{1,0:T(8,128)(2,1)S(1)} %collective-permute-done.11.refs_1_), channel_id=1, source_target_pairs={{8,0},{16,8},{24,16},{32,24},{40,32},{48,40},{56,48},{0,56},{9,1},... | collective-permute-start | bytes 614408 | tf_op jit(solution)/shard_map/ppermute | solution.py:31
  54.2 1.1 broadcast_add_fusion
  55.3 4.6 %collective-permute-start.18 = (bf16[112,5120]{1,0:T(8,128)(2,1)}, bf16[112,5120]{1,0:T(8,128)(2,1)}, u32[]{:S(2)}, u32[]{:S(2)}) collective-permute-start(bf16[112,5120]{1,0:T(8,128)(2,1)} %broadcast_add_fusion), channel_id=1, source_target_pairs={{0,0},{64,4},{4,64},{68,68},{1,1},{65,5},{5,65},{69,69},{2,2},{66,... | collective-permute-start | bytes 3440648 | tf_op jit(solution)/shard_map/ppermute | solution.py:45
  60.0 0.1 collective-permute-start.16
  60.1 5.1 %collective-permute-done.12.refs_2_ = bf16[20,5120]{1,0:T(8,128)(2,1)S(1)} collective-permute-done((bf16[20,5120]{1,0:T(8,128)(2,1)S(1)}, bf16[20,5120]{1,0:T(8,128)(2,1)S(1)}, u32[]{:S(2)}, u32[]{:S(2)}) %collective-permute-start.12) | collective-permute-done | bytes 204832 | tf_op jit(solution)/shard_map/ppermute | solution.py:31
  65.2 3.5 %collective-permute-start.13 = (bf16[20,5120]{1,0:T(8,128)(2,1)S(1)}, bf16[20,5120]{1,0:T(8,128)(2,1)S(1)}, u32[]{:S(2)}, u32[]{:S(2)}) collective-permute-start(bf16[20,5120]{1,0:T(8,128)(2,1)S(1)} %collective-permute-done.12.refs_2_), channel_id=1, source_target_pairs={{8,0},{16,8},{24,16},{32,24},{40,32},{48,40},{56,48},{0,56},{9,1},... | collective-permute-start | bytes 614408 | tf_op jit(solution)/shard_map/ppermute | solution.py:31
  68.7 3.4 %pad_add_fusion = f32[120,5120]{1,0:T(8,128)} fusion(f32[112,5120]{1,0:T(8,128)} %bitcast.38, f32[]{:T(128)} %bitcast.32, f32[]{:T(128)S(6)} %convert_element_type.10), kind=kLoop, calls=%fused_computation.9 | loop fusion | flops 614400 | bytes 4751368 | tf_op jit(solution)/shard_map/add | solution.py:50
  72.1 1.1 collective-permute-done.16.refs_6_
  73.2 6.2 %collective-permute-done.13.refs_3_ = bf16[20,5120]{1,0:T(8,128)(2,1)S(1)} collective-permute-done((bf16[20,5120]{1,0:T(8,128)(2,1)S(1)}, bf16[20,5120]{1,0:T(8,128)(2,1)S(1)}, u32[]{:S(2)}, u32[]{:S(2)}) %collective-permute-start.13) | collective-permute-done | bytes 204832 | tf_op jit(solution)/shard_map/ppermute | solution.py:31
  79.4 3.5 %collective-permute-start.14 = (bf16[20,5120]{1,0:T(8,128)(2,1)S(1)}, bf16[20,5120]{1,0:T(8,128)(2,1)S(1)}, u32[]{:S(2)}, u32[]{:S(2)}) collective-permute-start(bf16[20,5120]{1,0:T(8,128)(2,1)S(1)} %collective-permute-done.13.refs_3_), channel_id=1, source_target_pairs={{8,0},{16,8},{24,16},{32,24},{40,32},{48,40},{56,48},{0,56},{9,1},... | collective-permute-start | bytes 614408 | tf_op jit(solution)/shard_map/ppermute | solution.py:31
  82.9 0.2 fusion.5
  83.2 3.5 %collective-permute-start.7 = (bf16[112,5120]{1,0:T(8,128)(2,1)S(1)}, bf16[112,5120]{1,0:T(8,128)(2,1)}, u32[]{:S(2)}, u32[]{:S(2)}) collective-permute-start(bf16[112,5120]{1,0:T(8,128)(2,1)S(1)} %fusion.5), channel_id=1, source_target_pairs={{0,0},{64,4},{4,64},{68,68},{1,1},{65,5},{5,65},{69,69},{2,2},{66,... | collective-permute-start | bytes 3440648 | tf_op jit(solution)/shard_map/ppermute | solution.py:45
  86.7 4.6 %collective-permute-done.14.refs_4_ = bf16[20,5120]{1,0:T(8,128)(2,1)S(1)} collective-permute-done((bf16[20,5120]{1,0:T(8,128)(2,1)S(1)}, bf16[20,5120]{1,0:T(8,128)(2,1)S(1)}, u32[]{:S(2)}, u32[]{:S(2)}) %collective-permute-start.14) | collective-permute-done | bytes 204832 | tf_op jit(solution)/shard_map/ppermute | solution.py:31
  91.3 0.6 stacked.3
  91.9 0.1 collective-permute-start.20
  92.0 1.5 collective-permute-start.21
  93.4 1.1 broadcast_add_fusion.1
  94.5 5.4 %collective-permute-start.9 = (bf16[112,5120]{1,0:T(8,128)(2,1)}, bf16[112,5120]{1,0:T(8,128)(2,1)S(1)}, u32[]{:S(2)}, u32[]{:S(2)}) collective-permute-start(bf16[112,5120]{1,0:T(8,128)(2,1)} %broadcast_add_fusion.1), channel_id=1, source_target_pairs={{0,0},{64,4},{4,64},{68,68},{1,1},{65,5},{5,65},{69,69},{2,2},{66,... | collective-permute-start | bytes 3440648 | tf_op jit(solution)/shard_map/ppermute | solution.py:45
  100.0 37.9 %collective-permute-done.7 = bf16[112,5120]{1,0:T(8,128)(2,1)} collective-permute-done((bf16[112,5120]{1,0:T(8,128)(2,1)S(1)}, bf16[112,5120]{1,0:T(8,128)(2,1)}, u32[]{:S(2)}, u32[]{:S(2)}) %collective-permute-start.7) | collective-permute-done | bytes 1146912 | tf_op jit(solution)/shard_map/ppermute | solution.py:45
  138.6 11.7 %collective-permute-done.9 = bf16[112,5120]{1,0:T(8,128)(2,1)S(1)} collective-permute-done((bf16[112,5120]{1,0:T(8,128)(2,1)}, bf16[112,5120]{1,0:T(8,128)(2,1)S(1)}, u32[]{:S(2)}, u32[]{:S(2)}) %collective-permute-start.9) | collective-permute-done | bytes 1146912 | tf_op jit(solution)/shard_map/ppermute | solution.py:45
  150.3 0.5 collective-permute-start.10
  150.8 1.2 slice.21
  152.0 2.4 collective-permute-start.22
  154.4 1.2 slice.22
  155.6 0.1 collective-permute-start.23
  155.7 3.4 %convolution_dynamic-update-slice_fusion.2 = f32[640,256]{1,0:T(8,128)} fusion(bf16[160,5120]{1,0:T(8,128)(2,1)S(1)} %stacked.3, bf16[16,5120]{1,0:T(8,128)(2,1)S(1)} %broadcast.10, bf16[112,5120]{1,0:T(8,128)(2,1)} %collective-permute-done.19, bf16[112,5120]{1,0:T(8,128)(2,1)} %collective-permute-done.18), kind=kOutput, calls=%fused_computation.22 | convolution fusion | flops 429916160 | bytes 4259840 | tf_op jit(solution)/shard_map/dot_general | solution.py:71
  159.2 3.5 %broadcast_select_fusion = f32[120,5120]{1,0:T(8,128)} fusion(f32[120,5120]{1,0:T(8,128)} %collective-permute-done.5, pred[]{:T(512)S(6)} %eq.11, f32[]{:T(128)S(6)} %convert_element_type.10, f32[112,5120]{1,0:T(8,128)S(1)} %bitcast.39, f32[]{:T(128)} %bitcast.33), kind=kLoop, calls=%fused_computation.18 | loop fusion | flops 1228800 | bytes 7208969 | tf_op jit(solution)/shard_map/jit(_where)/select_n | solution.py:65
  162.7 2.9 %pad_maximum_fusion.1 = (bf16[256,5120]{1,0:T(8,128)(2,1)S(1)}, bf16[256,5120]{1,0:T(8,128)(2,1)}) fusion(bf16[16,5120]{1,0:T(8,128)(2,1)S(1)} %broadcast.10, bf16[112,5120]{1,0:T(8,128)(2,1)S(1)} %collective-permute-done.10, bf16[112,5120]{1,0:T(8,128)(2,1)S(1)} %copy-done.6, bf16[112,5120]{1,0:T(8,128)(2,1)S(1)} %collective-permute-done.8, ...), kind=kLoop, calls=%fused_computation.1 | loop fusion | flops 18350080 | bytes 9994240 | tf_op jit(solution)/shard_map/concatenate | solution.py:78
  165.6 3.8 %convolution_dynamic-update-slice_fusion.1 = f32[640,256]{1,0:T(8,128)} fusion(f32[640,256]{1,0:T(8,128)} %convolution_dynamic-update-slice_fusion.2, bf16[160,5120]{1,0:T(8,128)(2,1)} %collective-permute-done.20, bf16[16,5120]{1,0:T(8,128)(2,1)S(1)} %broadcast.10, bf16[112,5120]{1,0:T(8,128)(2,1)} %collective-permute-done.19, ...), kind=kOutput, calls=%fused_computation.21 | convolution fusion | flops 429916160 | bytes 4259840 | tf_op jit(solution)/shard_map/dot_general | solution.py:71
  169.3 3.8 %convolution_dynamic-update-slice_fusion = f32[640,256]{1,0:T(8,128)} fusion(f32[640,256]{1,0:T(8,128)} %convolution_dynamic-update-slice_fusion.1, bf16[160,5120]{1,0:T(8,128)(2,1)} %collective-permute-done.21, bf16[16,5120]{1,0:T(8,128)(2,1)S(1)} %broadcast.10, bf16[112,5120]{1,0:T(8,128)(2,1)} %collective-permute-done.19, ...), kind=kOutput, calls=%fused_computation.20 | convolution fusion | flops 429916160 | bytes 4259840 | tf_op jit(solution)/shard_map/dot_general | solution.py:71
  173.1 3.2 %convolution_dynamic-update-slice_fusion.4 = f32[640,256]{1,0:T(8,128)} fusion(f32[640,256]{1,0:T(8,128)} %convolution_dynamic-update-slice_fusion, bf16[80,5120]{1,0:T(8,128)(2,1)S(1)} %collective-permute-done.22, bf16[16,5120]{1,0:T(8,128)(2,1)S(1)} %broadcast.10, bf16[112,5120]{1,0:T(8,128)(2,1)} %collective-permute-done.19, ...), kind=kOutput, calls=%fused_computation.25 | convolution fusion | flops 220200960 | bytes 3358720 | tf_op jit(solution)/shard_map/dot_general | solution.py:71
  176.3 3.2 %convolution_dynamic-update-slice_fusion.3 = f32[640,256]{1,0:T(8,128)} fusion(f32[640,256]{1,0:T(8,128)} %convolution_dynamic-update-slice_fusion.4, bf16[80,5120]{1,0:T(8,128)(2,1)S(1)} %collective-permute-done.23, bf16[16,5120]{1,0:T(8,128)(2,1)S(1)} %broadcast.10, bf16[112,5120]{1,0:T(8,128)(2,1)} %collective-permute-done.19, ...), kind=kOutput, calls=%fused_computation.24 | convolution fusion | flops 220200960 | bytes 3358720 | tf_op jit(solution)/shard_map/dot_general | solution.py:71
  179.5 1.2 reshape.18
  180.7 1.0 copy.14
  181.6 2.0 reshape.19
  183.7 1.3 fusion.7.hidden_ref
  184.9 3.4 %broadcast_select_fusion.1 = f32[120,5120]{1,0:T(8,128)} fusion(f32[120,5120]{1,0:T(8,128)} %collective-permute-done.6, f32[120,5120]{1,0:T(8,128)} %collective-permute-done.5, pred[]{:T(512)S(6)} %eq.10), kind=kLoop, calls=%fused_computation.19 | loop fusion | flops 614400 | bytes 7372801 | tf_op jit(solution)/shard_map/jit(_where)/select_n | solution.py:67
  188.4 2.9 %copy-done = bf16[640,5120]{1,0:T(8,128)(2,1)S(1)} copy-done((bf16[640,5120]{1,0:T(8,128)(2,1)S(1)}, bf16[640,5120]{1,0:T(8,128)(2,1)}, u32[]{:S(2)}) %copy-start) | copy-done | bytes 6553624
  191.2 1.7 copy-done.1
  193.0 10.7 %other_half.1 = (bf16[128,640]{1,0:T(8,128)(2,1)S(1)}, f32[112,5120]{1,0:T(8,128)S(1)}) custom-call(bf16[640,5120]{1,0:T(8,128)(2,1)S(1)} %copy-done, bf16[256,5120]{1,0:T(8,128)(2,1)S(1)} %copy-done.1, bf16[256,5120]{1,0:T(8,128)(2,1)S(1)} %get-tuple-element.16.up_ref, f32[640,256]{1,0:T(8,128)S(1)} %fusion.7.hidden_ref), custom_call_target="tpu_custom_call" | custom-call | flops 4194304000 | bytes 21495808 | tf_op jit(solution)/shard_map/other_half/pallas_call | solution.py:160
  203.7 1.3 collective-permute-start.24
  205.0 3.3 %own_half.1 = f32[112,5120]{1,0:T(8,128)S(1)} custom-call(bf16[640,5120]{1,0:T(8,128)(2,1)S(1)} %copy-done, bf16[128,640]{1,0:T(8,128)(2,1)S(1)} %get-tuple-element.9.own_ref), custom_call_target="tpu_custom_call" | custom-call | flops 838860800 | bytes 8650752 | tf_op jit(solution)/shard_map/own_half/pallas_call | solution.py:197
  208.3 0.7 collective-permute-done.24
  209.0 2.5 multiply_reduce_fusion
  211.6 5.7 %collective-permute-start.26 = (f32[112,5120]{1,0:T(8,128)}, f32[112,5120]{1,0:T(8,128)}, u32[]{:S(2)}, u32[]{:S(2)}) collective-permute-start(f32[112,5120]{1,0:T(8,128)} %get-tuple-element.13), channel_id=1, source_target_pairs={{0,0},{64,4},{4,64},{68,68},{1,1},{65,5},{5,65},{69,69},{2,2},{66,... | collective-permute-start | bytes 6881288 | tf_op jit(solution)/shard_map/ppermute | solution.py:45
  217.4 11.3 %psum.21 = f32[]{:T(128)} all-reduce(f32[]{:T(128)} %get-tuple-element.12), channel_id=1, replica_groups=mesh['x_lo'=2,'core'=2,'z'=8,'x_hi'=2,'y'=4] {'z'}, use_global_device_ids=true, to_apply=%region_1.2 | all-reduce | flops 1 | bytes 8 | tf_op jit(solution)/shard_map/psum | solution.py:241
  228.7 0.5 slice.19
  229.2 8.5 %psum.22 = f32[]{:T(128)} all-reduce(f32[]{:T(128)} %psum.21), channel_id=1, replica_groups=mesh['x_lo'=2,'core'=2,'z'=8,'x_hi'=2,'y'=4] {'y'}, use_global_device_ids=true, to_apply=%region_2.3 | all-reduce | flops 1 | bytes 8 | tf_op jit(solution)/shard_map/psum | solution.py:241
  238.3 21.6 %psum.23 = f32[]{:T(128)} all-reduce(f32[]{:T(128)} %psum.22), channel_id=1, replica_groups=mesh['x_lo'=2,'core'=2,'z'=8,'x_hi'=2,'y'=4] {'core'}, use_global_device_ids=true, to_apply=%region_3.4 | all-reduce | flops 1 | bytes 8 | tf_op jit(solution)/shard_map/psum | solution.py:241
  259.9 1.9 collective-permute-start.25
  261.8 4.5 %collective-permute-done.25 = f32[]{:T(128)} collective-permute-done((f32[]{:T(128)}, f32[]{:T(128)}, u32[]{:S(2)}, u32[]{:S(2)}) %collective-permute-start.25) | collective-permute-done | bytes 36 | tf_op jit(solution)/shard_map/ppermute | solution.py:45
  266.9 4.9 %fusion.6 = (f32[1,112,5120]{2,1,0:T(8,128)}, f32[1,112,5120]{2,1,0:T(8,128)}) fusion(f32[112,5120]{1,0:T(8,128)} %collective-permute-done.26, f32[]{:T(128)S(6)} %mul.26, f32[1,112,5120]{2,1,0:T(8,128)} %param.11, f32[120,5120]{1,0:T(8,128)S(1)} %copy-done.2), kind=kLoop, calls=%fused_computation.26 | loop fusion | flops 2293760 | bytes 11468804 | tf_op jit(solution)/shard_map/broadcast_in_dim | solution.py:249
  (43 shorter events, 0.2 us)
Async XLA Ops:
  7.2 23.5 %copy-start.9 = (bf16[1,20,5120]{2,1,0:T(8,128)(2,1)S(1)}, bf16[1,20,5120]{2,1,0:T(8,128)(2,1)}, u32[]{:S(2)}) copy-start(bf16[1,20,5120]{2,1,0:T(8,128)(2,1)} %param.10) | copy-start | bytes 614404
  7.2 47.1 %copy-start.7 = (bf16[112,5120]{1,0:T(8,128)(2,1)S(1)}, bf16[112,5120]{1,0:T(8,128)(2,1)}, u32[]{:S(2)}) copy-start(bf16[112,5120]{1,0:T(8,128)(2,1)} %param.16) | copy-start | bytes 3440644
  7.2 181.2 %all-gather.2.cloned.1.call-start = ((), (), s32[]{:S(2)}) async-start(), calls=%async_computation | async-start | bytes 7372800 | tf_op jit(solution)/shard_map/all_gather | solution.py:222
  7.2 13.1 %collective-permute-start = (bf16[20,5120]{1,0:T(8,128)(2,1)}, bf16[20,5120]{1,0:T(8,128)(2,1)S(1)}, u32[]{:S(2)}, u32[]{:S(2)}) collective-permute-start(bf16[20,5120]{1,0:T(8,128)(2,1)} %bitcast.41), channel_id=1, source_target_pairs={{0,0},{1,1},{2,2},{3,3},{64,4},{65,5},{66,6},{67,7},{4,64},{5,65},... | collective-permute-start | bytes 614408 | tf_op jit(solution)/shard_map/ppermute | solution.py:45
  13.4 8.4 %collective-permute-start.1 = (bf16[20,5120]{1,0:T(8,128)(2,1)}, bf16[20,5120]{1,0:T(8,128)(2,1)S(1)}, u32[]{:S(2)}, u32[]{:S(2)}) collective-permute-start(bf16[20,5120]{1,0:T(8,128)(2,1)} %bitcast.42), channel_id=1, source_target_pairs={{1,0},{2,1},{3,2},{0,3},{65,4},{66,5},{67,6},{64,7},{5,64},{6,65},... | collective-permute-start | bytes 614408 | tf_op jit(solution)/shard_map/ppermute | solution.py:45
  16.0 10.1 %collective-permute-start.2 = (bf16[20,5120]{1,0:T(8,128)(2,1)}, bf16[20,5120]{1,0:T(8,128)(2,1)S(1)}, u32[]{:S(2)}, u32[]{:S(2)}) collective-permute-start(bf16[20,5120]{1,0:T(8,128)(2,1)} %bitcast.43), channel_id=1, source_target_pairs={{3,0},{0,1},{1,2},{2,3},{67,4},{64,5},{65,6},{66,7},{7,64},{4,65},... | collective-permute-start | bytes 614408 | tf_op jit(solution)/shard_map/ppermute | solution.py:45
  17.6 11.4 %collective-permute-start.3 = (bf16[20,5120]{1,0:T(8,128)(2,1)}, bf16[20,5120]{1,0:T(8,128)(2,1)S(1)}, u32[]{:S(2)}, u32[]{:S(2)}) collective-permute-start(bf16[20,5120]{1,0:T(8,128)(2,1)} %bitcast.44), channel_id=1, source_target_pairs={{2,0},{3,1},{0,2},{1,3},{66,4},{67,5},{64,6},{65,7},{6,64},{7,65},... | collective-permute-start | bytes 614408 | tf_op jit(solution)/shard_map/ppermute | solution.py:45
  30.7 11.8 %collective-permute-start.4 = (bf16[20,5120]{1,0:T(8,128)(2,1)S(1)}, bf16[20,5120]{1,0:T(8,128)(2,1)S(1)}, u32[]{:S(2)}, u32[]{:S(2)}) collective-permute-start(bf16[20,5120]{1,0:T(8,128)(2,1)S(1)} %bitcast.45), channel_id=1, source_target_pairs={{0,0},{64,4},{8,8},{72,12},{16,16},{80,20},{24,24},{88,28},{32,32}... | collective-permute-start | bytes 614408 | tf_op jit(solution)/shard_map/ppermute | solution.py:45
  35.1 15.1 %collective-permute-start.11 = (bf16[20,5120]{1,0:T(8,128)(2,1)S(1)}, bf16[20,5120]{1,0:T(8,128)(2,1)S(1)}, u32[]{:S(2)}, u32[]{:S(2)}) collective-permute-start(bf16[20,5120]{1,0:T(8,128)(2,1)S(1)} %bitcast.46), channel_id=1, source_target_pairs={{8,0},{72,4},{16,8},{80,12},{24,16},{88,20},{32,24},{96,28},{40,32... | collective-permute-start | bytes 614408 | tf_op jit(solution)/shard_map/ppermute | solution.py:45
  41.2 18.7 %collective-permute-start.15 = (bf16[20,5120]{1,0:T(8,128)(2,1)S(1)}, bf16[20,5120]{1,0:T(8,128)(2,1)S(1)}, u32[]{:S(2)}, u32[]{:S(2)}) collective-permute-start(bf16[20,5120]{1,0:T(8,128)(2,1)S(1)} %bitcast.47), channel_id=1, source_target_pairs={{56,0},{120,4},{0,8},{64,12},{8,16},{72,20},{16,24},{80,28},{24,32... | collective-permute-start | bytes 614408 | tf_op jit(solution)/shard_map/ppermute | solution.py:45
  50.2 15.0 %collective-permute-start.12 = (bf16[20,5120]{1,0:T(8,128)(2,1)S(1)}, bf16[20,5120]{1,0:T(8,128)(2,1)S(1)}, u32[]{:S(2)}, u32[]{:S(2)}) collective-permute-start(bf16[20,5120]{1,0:T(8,128)(2,1)S(1)} %collective-permute-done.11.refs_1_), channel_id=1, source_target_pairs={{8,0},{16,8},{24,16},{32,24},{40,32},{48,40},{56,48},{0,56},{9,1},... | collective-permute-start | bytes 614408 | tf_op jit(solution)/shard_map/ppermute | solution.py:31
  55.3 27.6 %copy-start.3 = (f32[1,112,5120]{2,1,0:T(8,128)S(1)}, f32[1,112,5120]{2,1,0:T(8,128)}, u32[]{:S(2)}) copy-start(f32[1,112,5120]{2,1,0:T(8,128)} %param.11) | copy-start | bytes 6881284
  55.3 39.2 %collective-permute-start.18 = (bf16[112,5120]{1,0:T(8,128)(2,1)}, bf16[112,5120]{1,0:T(8,128)(2,1)}, u32[]{:S(2)}, u32[]{:S(2)}) collective-permute-start(bf16[112,5120]{1,0:T(8,128)(2,1)} %broadcast_add_fusion), channel_id=1, source_target_pairs={{0,0},{64,4},{4,64},{68,68},{1,1},{65,5},{5,65},{69,69},{2,2},{66,... | collective-permute-start | bytes 3440648 | tf_op jit(solution)/shard_map/ppermute | solution.py:45
  60.0 13.3 %collective-permute-start.16 = (bf16[20,5120]{1,0:T(8,128)(2,1)S(1)}, bf16[20,5120]{1,0:T(8,128)(2,1)S(1)}, u32[]{:S(2)}, u32[]{:S(2)}) collective-permute-start(bf16[20,5120]{1,0:T(8,128)(2,1)S(1)} %collective-permute-done.15.refs_7_), channel_id=1, source_target_pairs={{56,0},{0,8},{8,16},{16,24},{24,32},{32,40},{40,48},{48,56},{57,1}... | collective-permute-start | bytes 614408 | tf_op jit(solution)/shard_map/ppermute | solution.py:31
  65.2 14.2 %collective-permute-start.13 = (bf16[20,5120]{1,0:T(8,128)(2,1)S(1)}, bf16[20,5120]{1,0:T(8,128)(2,1)S(1)}, u32[]{:S(2)}, u32[]{:S(2)}) collective-permute-start(bf16[20,5120]{1,0:T(8,128)(2,1)S(1)} %collective-permute-done.12.refs_2_), channel_id=1, source_target_pairs={{8,0},{16,8},{24,16},{32,24},{40,32},{48,40},{56,48},{0,56},{9,1},... | collective-permute-start | bytes 614408 | tf_op jit(solution)/shard_map/ppermute | solution.py:31
  72.1 87.0 %collective-permute-start.5 = (f32[120,5120]{1,0:T(8,128)}, f32[120,5120]{1,0:T(8,128)}, u32[]{:S(2)}, u32[]{:S(2)}) collective-permute-start(f32[120,5120]{1,0:T(8,128)} %pad_add_fusion), channel_id=1, source_target_pairs={{128,0},{0,128},{129,1},{1,129},{130,2},{2,130},{131,3},{3,131},{1... | collective-permute-start | bytes 7372808 | tf_op jit(solution)/shard_map/ppermute | solution.py:31
  73.2 13.4 %collective-permute-start.17 = (bf16[20,5120]{1,0:T(8,128)(2,1)S(1)}, bf16[20,5120]{1,0:T(8,128)(2,1)S(1)}, u32[]{:S(2)}, u32[]{:S(2)}) collective-permute-start(bf16[20,5120]{1,0:T(8,128)(2,1)S(1)} %collective-permute-done.16.refs_6_), channel_id=1, source_target_pairs={{56,0},{0,8},{8,16},{16,24},{24,32},{32,40},{40,48},{48,56},{57,1}... | collective-permute-start | bytes 614408 | tf_op jit(solution)/shard_map/ppermute | solution.py:31
  79.4 11.9 %collective-permute-start.14 = (bf16[20,5120]{1,0:T(8,128)(2,1)S(1)}, bf16[20,5120]{1,0:T(8,128)(2,1)S(1)}, u32[]{:S(2)}, u32[]{:S(2)}) collective-permute-start(bf16[20,5120]{1,0:T(8,128)(2,1)S(1)} %collective-permute-done.13.refs_3_), channel_id=1, source_target_pairs={{8,0},{16,8},{24,16},{32,24},{40,32},{48,40},{56,48},{0,56},{9,1},... | collective-permute-start | bytes 614408 | tf_op jit(solution)/shard_map/ppermute | solution.py:31
  83.2 10.3 %copy-start.8 = (bf16[112,5120]{1,0:T(8,128)(2,1)S(1)}, bf16[112,5120]{1,0:T(8,128)(2,1)}, u32[]{:S(2)}) copy-start(bf16[112,5120]{1,0:T(8,128)(2,1)} %param.15) | copy-start | bytes 3440644
  83.2 54.7 %collective-permute-start.7 = (bf16[112,5120]{1,0:T(8,128)(2,1)S(1)}, bf16[112,5120]{1,0:T(8,128)(2,1)}, u32[]{:S(2)}, u32[]{:S(2)}) collective-permute-start(bf16[112,5120]{1,0:T(8,128)(2,1)S(1)} %fusion.5), channel_id=1, source_target_pairs={{0,0},{64,4},{4,64},{68,68},{1,1},{65,5},{5,65},{69,69},{2,2},{66,... | collective-permute-start | bytes 3440648 | tf_op jit(solution)/shard_map/ppermute | solution.py:45
  91.9 58.4 %collective-permute-start.20 = (bf16[160,5120]{1,0:T(8,128)(2,1)S(1)}, bf16[160,5120]{1,0:T(8,128)(2,1)}, u32[]{:S(2)}, u32[]{:S(2)}) collective-permute-start(bf16[160,5120]{1,0:T(8,128)(2,1)S(1)} %stacked.3), channel_id=1, source_target_pairs={{1,0},{2,1},{3,2},{0,3},{5,4},{6,5},{7,6},{4,7},{9,8},{10,9},{11,1... | collective-permute-start | bytes 4915208 | tf_op jit(solution)/shard_map/ppermute | solution.py:31
  92.0 60.0 %collective-permute-start.21 = (bf16[160,5120]{1,0:T(8,128)(2,1)S(1)}, bf16[160,5120]{1,0:T(8,128)(2,1)}, u32[]{:S(2)}, u32[]{:S(2)}) collective-permute-start(bf16[160,5120]{1,0:T(8,128)(2,1)S(1)} %stacked.3), channel_id=1, source_target_pairs={{3,0},{0,1},{1,2},{2,3},{7,4},{4,5},{5,6},{6,7},{11,8},{8,9},{9,10... | collective-permute-start | bytes 4915208 | tf_op jit(solution)/shard_map/ppermute | solution.py:31
  94.5 55.8 %collective-permute-start.9 = (bf16[112,5120]{1,0:T(8,128)(2,1)}, bf16[112,5120]{1,0:T(8,128)(2,1)S(1)}, u32[]{:S(2)}, u32[]{:S(2)}) collective-permute-start(bf16[112,5120]{1,0:T(8,128)(2,1)} %broadcast_add_fusion.1), channel_id=1, source_target_pairs={{0,0},{64,4},{4,64},{68,68},{1,1},{65,5},{5,65},{69,69},{2,2},{66,... | collective-permute-start | bytes 3440648 | tf_op jit(solution)/shard_map/ppermute | solution.py:45
  137.9 17.7 %collective-permute-start.19 = (bf16[112,5120]{1,0:T(8,128)(2,1)}, bf16[112,5120]{1,0:T(8,128)(2,1)}, u32[]{:S(2)}, u32[]{:S(2)}) collective-permute-start(bf16[112,5120]{1,0:T(8,128)(2,1)} %collective-permute-done.18), channel_id=1, source_target_pairs={{64,0},{0,64},{65,1},{1,65},{66,2},{2,66},{67,3},{3,67},{68,4},{4,... | collective-permute-start | bytes 3440648 | tf_op jit(solution)/shard_map/ppermute | solution.py:31
  150.3 8.9 %copy-start.5 = (bf16[112,5120]{1,0:T(8,128)(2,1)}, bf16[112,5120]{1,0:T(8,128)(2,1)S(1)}, u32[]{:S(2)}) copy-start(bf16[112,5120]{1,0:T(8,128)(2,1)S(1)} %collective-permute-done.9) | copy-start | bytes 3440644
  150.3 12.4 %collective-permute-start.8 = (bf16[112,5120]{1,0:T(8,128)(2,1)}, bf16[112,5120]{1,0:T(8,128)(2,1)S(1)}, u32[]{:S(2)}, u32[]{:S(2)}) collective-permute-start(bf16[112,5120]{1,0:T(8,128)(2,1)} %collective-permute-done.7), channel_id=1, source_target_pairs={{64,0},{0,64},{65,1},{1,65},{66,2},{2,66},{67,3},{3,67},{68,4},{4,... | collective-permute-start | bytes 3440648 | tf_op jit(solution)/shard_map/ppermute | solution.py:31
  150.3 12.4 %collective-permute-start.10 = (bf16[112,5120]{1,0:T(8,128)(2,1)S(1)}, bf16[112,5120]{1,0:T(8,128)(2,1)S(1)}, u32[]{:S(2)}, u32[]{:S(2)}) collective-permute-start(bf16[112,5120]{1,0:T(8,128)(2,1)S(1)} %collective-permute-done.9), channel_id=1, source_target_pairs={{64,0},{0,64},{65,1},{1,65},{66,2},{2,66},{67,3},{3,67},{68,4},{4,... | collective-permute-start | bytes 3440648 | tf_op jit(solution)/shard_map/ppermute | solution.py:31
  152.0 21.1 %collective-permute-start.22 = (bf16[80,5120]{1,0:T(8,128)(2,1)S(1)}, bf16[80,5120]{1,0:T(8,128)(2,1)S(1)}, u32[]{:S(2)}, u32[]{:S(2)}) collective-permute-start(bf16[80,5120]{1,0:T(8,128)(2,1)S(1)} %slice.21), channel_id=1, source_target_pairs={{1,0},{2,1},{3,2},{0,3},{5,4},{6,5},{7,6},{4,7},{9,8},{10,9},{11,1... | collective-permute-start | bytes 2457608 | tf_op jit(solution)/shard_map/ppermute | solution.py:31
  155.6 20.8 %collective-permute-start.23 = (bf16[80,5120]{1,0:T(8,128)(2,1)S(1)}, bf16[80,5120]{1,0:T(8,128)(2,1)S(1)}, u32[]{:S(2)}, u32[]{:S(2)}) collective-permute-start(bf16[80,5120]{1,0:T(8,128)(2,1)S(1)} %slice.22), channel_id=1, source_target_pairs={{3,0},{0,1},{1,2},{2,3},{7,4},{4,5},{5,6},{6,7},{11,8},{8,9},{9,10... | collective-permute-start | bytes 2457608 | tf_op jit(solution)/shard_map/ppermute | solution.py:31
  155.7 3.5 %copy-start.4 = (f32[1,112,5120]{2,1,0:T(8,128)S(1)}, f32[1,112,5120]{2,1,0:T(8,128)}, u32[]{:S(2)}) copy-start(f32[1,112,5120]{2,1,0:T(8,128)} %param.13) | copy-start | bytes 6881284
  159.2 3.6 %copy-start.6 = (bf16[112,5120]{1,0:T(8,128)(2,1)S(1)}, bf16[112,5120]{1,0:T(8,128)(2,1)}, u32[]{:S(2)}) copy-start(bf16[112,5120]{1,0:T(8,128)(2,1)} %copy-done.5) | copy-start | bytes 3440644
  162.7 22.2 %collective-permute-start.6 = (f32[120,5120]{1,0:T(8,128)}, f32[120,5120]{1,0:T(8,128)}, u32[]{:S(2)}, u32[]{:S(2)}) collective-permute-start(f32[120,5120]{1,0:T(8,128)} %broadcast_select_fusion), channel_id=1, source_target_pairs={{64,0},{0,64},{65,1},{1,65},{66,2},{2,66},{67,3},{3,67},{68,4},{4,... | collective-permute-start | bytes 7372808 | tf_op jit(solution)/shard_map/ppermute | solution.py:31
  188.4 2.9 %copy-start = (bf16[640,5120]{1,0:T(8,128)(2,1)S(1)}, bf16[640,5120]{1,0:T(8,128)(2,1)}, u32[]{:S(2)}) copy-start(bf16[640,5120]{1,0:T(8,128)(2,1)} %all-gather.2.cloned.1.call-done.x_ref) | copy-start | bytes 19660804
  191.2 1.7 copy-start.1
  203.7 5.3 %collective-permute-start.24 = (f32[112,5120]{1,0:T(8,128)S(1)}, f32[112,5120]{1,0:T(8,128)S(1)}, u32[]{:S(2)}, u32[]{:S(2)}) collective-permute-start(f32[112,5120]{1,0:T(8,128)S(1)} %get-tuple-element.10), channel_id=1, source_target_pairs={{64,0},{0,64},{65,1},{1,65},{66,2},{2,66},{67,3},{3,67},{68,4},{4,... | collective-permute-start | bytes 6881288 | tf_op jit(solution)/shard_map/ppermute | solution.py:31
  208.3 20.4 %copy-start.2 = (f32[120,5120]{1,0:T(8,128)S(1)}, f32[120,5120]{1,0:T(8,128)}, u32[]{:S(2)}) copy-start(f32[120,5120]{1,0:T(8,128)} %broadcast_select_fusion.1) | copy-start | bytes 7372804
  211.6 55.4 %collective-permute-start.26 = (f32[112,5120]{1,0:T(8,128)}, f32[112,5120]{1,0:T(8,128)}, u32[]{:S(2)}, u32[]{:S(2)}) collective-permute-start(f32[112,5120]{1,0:T(8,128)} %get-tuple-element.13), channel_id=1, source_target_pairs={{0,0},{64,4},{4,64},{68,68},{1,1},{65,5},{5,65},{69,69},{2,2},{66,... | collective-permute-start | bytes 6881288 | tf_op jit(solution)/shard_map/ppermute | solution.py:45
  259.9 6.4 %collective-permute-start.25 = (f32[]{:T(128)}, f32[]{:T(128)}, u32[]{:S(2)}, u32[]{:S(2)}) collective-permute-start(f32[]{:T(128)} %psum.23), channel_id=1, source_target_pairs={{0,0},{64,4},{4,64},{68,68},{1,1},{65,5},{5,65},{69,69},{2,2},{66,... | collective-permute-start | bytes 20 | tf_op jit(solution)/shard_map/ppermute | solution.py:45
Sparse Core Ops, SparseCore 0:
  30.8 90.1 all-gather.1

commit v3 on v2

v3 whole, which is shorter than its diff:
```python
import math

import jax
import jax.numpy as jnp
import numpy as np
from jax import lax
from jax.experimental import pallas as pl
from jax.experimental.pallas import tpu as pltpu
from jax.sharding import Mesh, PartitionSpec as P

D = 5120
FFW = 7168

eps = 1e-06

WIDTH_SCALE = D ** (-0.5)
MAX_NORM = 0.05 * math.sqrt(D * FFW)

SIZES = {"x_lo": 2, "core": 2, "z": 8, "x_hi": 2, "y": 4}
GOSSIP = ("x_lo", "core")
FSDP = ("z", "x_hi", "y")

ROWS = 112
HALF = 128
BLOCK = 1024


def shifted(value, axis, steps):
    count = SIZES[axis]
    pairs = [((place + steps) % count, place) for place in range(count)]
    return lax.ppermute(value, axis, pairs)


def transposed(value):
    pairs = [(2 * x_hi + core, 2 * core + x_hi) for core in range(2) for x_hi in range(2)]
    return lax.ppermute(value, ("core", "x_hi"), pairs)


def held(value, *ready):
    return pl.pallas_call(
        lambda *refs: None,
        in_specs=[pl.BlockSpec(memory_space=pl.ANY)] * (1 + len(ready)),
        out_specs=pl.BlockSpec(memory_space=pl.ANY),
        out_shape=jax.ShapeDtypeStruct(value.shape, value.dtype),
        input_output_aliases={0: 0},
        compiler_params=params_of(1),
        name="held",
    )(value, *ready)


def silu_slope(preact):
    sigmoid_val = jax.nn.sigmoid(preact)
    return sigmoid_val * (1.0 + preact * (1.0 - sigmoid_val))


def plan_rate(step):
    phase = (step[0] % 1000).astype(jnp.float32) / 1000.0
    return 0.4 + 1.8 * (1.0 + jnp.cos(math.pi * phase))


def deliver(stale, step, *ready):
    two_before = held(shifted(stale, "x_lo", 1), *ready)
    payload = jnp.where(lax.axis_index("core") == 1, two_before, stale)
    one_before = shifted(payload, "core", 1)
    return jnp.where(step[0] % 2 == 0, one_before, two_before)


def dot_t(rows, weights):
    return lax.dot_general(
        rows, weights, (((1,), (1,)), ((), ())), preferred_element_type=jnp.float32
    )


def params_of(vmem, **more):
    return pltpu.CompilerParams(vmem_limit_bytes=vmem * 2**20, **more)


def stack_kernel(*refs):
    *blocks, out_ref = refs
    for at, block in enumerate(blocks):
        count = block.shape[0]
        out_ref[at * count : (at + 1) * count, :] = block[...]


def stacked(blocks):
    count = blocks[0].shape[0]
    wide = D // 4
    return pl.pallas_call(
        stack_kernel,
        grid=(4,),
        in_specs=[pl.BlockSpec((count, wide), lambda at: (0, at))] * len(blocks),
        out_specs=pl.BlockSpec((count * len(blocks), wide), lambda at: (0, at)),
        out_shape=jax.ShapeDtypeStruct((count * len(blocks), D), blocks[0].dtype),
        compiler_params=params_of(32),
        name="stacked",
    )(*blocks)


def gathered_z(block):
    by = {0: block}
    for steps in (1, 7, 2, 6):
        by[steps] = shifted(block, "z", steps)
    by[3] = shifted(by[2], "z", 1)
    by[5] = shifted(by[6], "z", 7)
    by[4] = shifted(by[2], "z", 2)
    return stacked([by[steps] for steps in range(8)])


def gathered_y(column):
    following = shifted(column, "y", 1)
    before = shifted(column, "y", 3)
    half = column.shape[0] // 2
    far = [shifted(following[:half], "y", 1), shifted(before[half:], "y", 3)]
    return [column, following, before, *far]


def widen(wide, mine, theirs):
    wide[:ROWS, :] = mine[...]
    wide[HALF : HALF + ROWS, :] = theirs[...]


def clear(wide):
    pad = jnp.zeros((HALF - ROWS, wide.shape[1]), wide.dtype)
    wide[ROWS:HALF, :] = pad
    wide[HALF + ROWS :, :] = pad


def hidden_kernel(z_ref, *refs):
    *parts, mine, theirs, out_ref, total, wide, tile = refs
    at = pl.program_id(0)

    @pl.when(at == 0)
    def _():
        total[...] = jnp.zeros_like(total)
        clear(wide)

    widen(wide, mine, theirs)
    row = 0
    for part in parts:
        count = part.shape[0]
        total[row : row + count, :] += dot_t(part[...], wide[...])
        row += count

    @pl.when(at == pl.num_programs(0) - 1)
    def _():
        column, block = row // 4, row // 32
        for dz in range(8):
            for dy in range(4):
                start = dy * column + dz * block
                tile[dy * block : (dy + 1) * block, :] = total[start : start + block, :]
            place = pl.multiple_of(lax.rem(z_ref[0] + dz, 8) * (4 * block), 16)
            out_ref[pl.ds(place, 4 * block), :] = tile[...]


def hidden_of(parts, mine, theirs):
    count = sum(part.shape[0] for part in parts)
    z = jnp.reshape(lax.axis_index("z"), (1,)).astype(jnp.int32)
    weights = pl.BlockSpec((ROWS, BLOCK), lambda at: (2, at))
    return pl.pallas_call(
        hidden_kernel,
        grid=(D // BLOCK,),
        in_specs=[pl.BlockSpec(memory_space=pltpu.SMEM)]
        + [pl.BlockSpec((part.shape[0], BLOCK), lambda at: (0, at)) for part in parts]
        + [weights, weights],
        out_specs=pl.BlockSpec((count, 2 * HALF), lambda at: (0, 0)),
        out_shape=jax.ShapeDtypeStruct((count, 2 * HALF), jnp.float32),
        scratch_shapes=[
            pltpu.VMEM((count, 2 * HALF), jnp.float32),
            pltpu.VMEM((2 * HALF, BLOCK), jnp.bfloat16),
            pltpu.VMEM((count // 8, 2 * HALF), jnp.float32),
        ],
        compiler_params=params_of(40),
        cost_estimate=pl.CostEstimate(
            flops=2 * count * D * 2 * HALF, bytes_accessed=2 * count * D + 2**22, transcendentals=0
        ),
        name="hidden",
    )(z, *parts, mine, theirs)


def other_kernel(
    x_ref, my_params, their_params, my_up, their_up, hidden_ref, own_ref, grad_ref,
    preact, up_proj, other, wide_params, wide_up,
):
    at = pl.program_id(0)
    blocks = D // BLOCK

    @pl.when(at == 0)
    def _():
        preact[...] = jnp.zeros_like(preact)
        up_proj[...] = jnp.zeros_like(up_proj)
        clear(wide_params)
        clear(wide_up)

    @pl.when(at < blocks)
    def _():
        widen(wide_params, my_params, their_params)
        widen(wide_up, my_up, their_up)
        preact[...] += dot_t(x_ref[...], wide_params[...])
        up_proj[...] += dot_t(x_ref[...], wide_up[...])

    @pl.when(at == blocks - 1)
    def _():
        slope = silu_slope(preact[...] * WIDTH_SCALE)
        turned = (hidden_ref[...] * up_proj[...] * slope).T.astype(jnp.bfloat16)
        own_ref[...] = turned[:HALF]
        other[...] = turned[HALF:]

    @pl.when(at >= blocks)
    def _():
        grad = jnp.dot(other[...], x_ref[...], preferred_element_type=jnp.float32)
        grad_ref[...] = grad[:ROWS] * WIDTH_SCALE


def other_half(rows_in, mine, theirs, hidden):
    count = rows_in.shape[0]
    blocks = D // BLOCK

    def weights(which):
        return pl.BlockSpec((ROWS, BLOCK), lambda at: (which, jnp.minimum(at, blocks - 1)))

    return pl.pallas_call(
        other_kernel,
        grid=(2 * blocks,),
        in_specs=[
            pl.BlockSpec((count, BLOCK), lambda at: (0, lax.rem(at, blocks))),
            weights(0),
            weights(0),
            weights(1),
            weights(1),
            pl.BlockSpec((count, 2 * HALF), lambda at: (0, 0)),
        ],
        out_specs=[
            pl.BlockSpec((HALF, count), lambda at: (0, 0)),
            pl.BlockSpec((ROWS, BLOCK), lambda at: (0, jnp.maximum(at - blocks, 0))),
        ],
        out_shape=[
            jax.ShapeDtypeStruct((HALF, count), jnp.bfloat16),
            jax.ShapeDtypeStruct((ROWS, D), jnp.float32),
        ],
        scratch_shapes=[
            pltpu.VMEM((count, 2 * HALF), jnp.float32),
            pltpu.VMEM((count, 2 * HALF), jnp.float32),
            pltpu.VMEM((HALF, count), jnp.bfloat16),
            pltpu.VMEM((2 * HALF, BLOCK), jnp.bfloat16),
            pltpu.VMEM((2 * HALF, BLOCK), jnp.bfloat16),
        ],
        compiler_params=params_of(40),
        cost_estimate=pl.CostEstimate(
            flops=2 * count * D * 640, bytes_accessed=4 * count * D + 2**23, transcendentals=0
        ),
        name="other_half",
    )(rows_in, mine, theirs, mine, theirs, hidden)


def own_kernel(x_ref, own_ref, grad_ref):
    grad = jnp.dot(own_ref[...], x_ref[...], preferred_element_type=jnp.float32)
    grad_ref[...] = grad[:ROWS] * WIDTH_SCALE


def own_half(rows_in, own):
    count = rows_in.shape[0]
    return pl.pallas_call(
        own_kernel,
        grid=(D // BLOCK,),
        in_specs=[
            pl.BlockSpec((count, BLOCK), lambda at: (0, at)),
            pl.BlockSpec((HALF, count), lambda at: (0, 0)),
        ],
        out_specs=pl.BlockSpec((ROWS, BLOCK), lambda at: (0, at)),
        out_shape=jax.ShapeDtypeStruct((ROWS, D), jnp.float32),
        compiler_params=params_of(40),
        cost_estimate=pl.CostEstimate(
            flops=2 * count * D * HALF, bytes_accessed=2 * count * D + 2**21, transcendentals=0
        ),
        name="own_half",
    )(rows_in, own)


def crossed(value):
    pairs = [
        (2 * (1 - x_hi) + core, 2 * core + x_hi) for core in range(2) for x_hi in range(2)
    ]
    return lax.ppermute(value, ("core", "x_hi"), pairs)


def shards(
    tokens, cotangent, gate_num, push_weight, stale_num, stale_weight, up_weight, down_weight, step
):
    rate = plan_rate(step)
    numerator = gate_num[0]

    rows_in, rows_grad = transposed(tokens[0]), transposed(cotangent[0])
    rows_in = held(rows_in, rows_grad)
    near = [rows_in] + [shifted(rows_in, "y", steps) for steps in (1, 3, 2)]
    near = stacked(near)
    column = gathered_z(rows_grad)
    parts = gathered_y(held(column, near))

    params = (numerator / push_weight[0]).astype(jnp.bfloat16)
    weights = jnp.concatenate([params, up_weight, down_weight], axis=0)
    mine = held(transposed(held(weights, rows_grad)), *parts[1:3])
    theirs = shifted(mine, "core", 1)
    stale = jnp.concatenate([stale_num[0], jnp.broadcast_to(stale_weight, (8, D))], axis=0)
    received = deliver(held(stale, rows_in), step, *parts)
    rows_in = lax.all_gather(near, "z", axis=0, tiled=True)
    hidden = hidden_of(parts, mine, theirs)
    rows_in, received = lax.optimization_barrier((rows_in, received))

    own, other_grad = other_half(rows_in, mine, theirs, hidden)
    gate_grad = own_half(rows_in, own) + shifted(other_grad, "core", 1)
    norm_sq = jnp.sum(gate_grad * gate_grad)
    gate_grad = transposed(gate_grad)
    for axes in ("z", "y"):
        norm_sq = lax.psum(norm_sq, axes)
    norm_sq = transposed(norm_sq) + crossed(norm_sq)

    clip_factor = jnp.minimum(1.0, MAX_NORM / jnp.sqrt(norm_sq + eps))
    kept_half = 0.5 * (numerator - rate * clip_factor * gate_grad)
    kept_weight = 0.5 * push_weight
    new_num = kept_half + received[:ROWS]
    new_weight = kept_weight + received[ROWS, :1]
    return (new_num[None], new_weight, kept_half[None], kept_weight)


def solution(mesh):
    named = Mesh(np.asarray(mesh.devices).reshape(tuple(SIZES.values())), tuple(SIZES))
    groups = P(GOSSIP, FSDP, None)
    in_specs = (
        groups,
        groups,
        groups,
        P(GOSSIP),
        groups,
        P(GOSSIP),
        P(FSDP, None),
        P(FSDP, None),
        P(),
    )
    out_specs = (groups, P(GOSSIP), groups, P(GOSSIP))
    return jax.shard_map(shards, mesh=named, in_specs=in_specs, out_specs=out_specs, check_vma=False)
```

time: 284 us -> 243 us (0.86)
  blocking collectives: 41.4 us -> 19.5 us
  matrix products: 17.3 us -> 0 us
  other arithmetic: 24.3 us -> 16.5 us
  Pallas kernels: 16.2 us -> 23.4 us
    ppermute x15 -> x18, waiting for transfers between devices: 17.9 us -> 77 us  [shifted(): return lax.ppermute(value, axis, pairs)]
    ppermute x12 -> x6, waiting for transfers between devices: 69.4 us -> 10.9 us  [the longest x5 9.83 us: transposed(): return lax.ppermute(value, ('core', 'x_hi'), pairs)]
    psum x3 -> x2, blocking collectives: 41.4 us -> 19.5 us  [shards(): norm_sq = lax.psum(norm_sq, axes)]
    dot_general x5 -> x0, matrix products: 17.3 us -> none  [dot_t(): lax.dot_general(rows, weights, (((1,), (1,)), ((), ())), preferred_elemen...]
    ppermute x12 -> x6, starting transfers between devices: 44.7 us -> 37.3 us  [the longest x5 23.7 us: transposed(): return lax.ppermute(value, ('core', 'x_hi'), pairs)]
    pallas_call x0 -> x7, Pallas kernels: none -> 6.6 us  [the longest x1 6.59 us: hidden_of(): pl.pallas_call(hidden_kernel, grid=(D // BLOCK,), in_specs=[pl.BlockSpec(...]
    ppermute x15 -> x18, starting transfers between devices: 16.9 us -> 23.2 us  [shifted(): return lax.ppermute(value, axis, pairs)]
    add x4 -> x0, other arithmetic: 5.78 us -> none  [after(): return [value + zero.astype(value.dtype) for value in values]]
  transfers between devices with their start and end apart: 28 -> 25, of which waited for: 13 -> 17; matrix products, arithmetic and copies ran while one was open for 15% -> 6% of each run, Pallas kernels for 1% -> 4%
where the time goes in v3:
time: 243 us; the launch traced here: 240 us
  waiting for transfers between devices  88 us (36%)
  starting transfers between devices  60.5 us (25%)
  Pallas kernels  23.4 us (10%)
  between operations  20.5 us (8%)
  blocking collectives  19.5 us (8%)
  other arithmetic  16.5 us (7%)
  local copies, waits for them, and re-layouts  12.1 us (5%)
    ppermute x18, waiting for transfers between devices, shifted(): return lax.ppermute(value, axis, pairs)  77 us
    ppermute x5, starting transfers between devices, transposed(): return lax.ppermute(value, ('core', 'x_hi'), pairs)  23.7 us
    ppermute x18, starting transfers between devices, shifted(): return lax.ppermute(value, axis, pairs)  23.2 us
    psum x2, blocking collectives, shards(): norm_sq = lax.psum(norm_sq, axes)  19.5 us
    ppermute x1, starting transfers between devices, crossed(): return lax.ppermute(value, ('core', 'x_hi'), pairs)  13.5 us
    pallas_call x1, Pallas kernels, other_half(): pl.pallas_call(other_kernel, grid=(2 * blocks,), in_specs=[pl.BlockSpec((...  12.1 us
    ppermute x5, waiting for transfers between devices, transposed(): return lax.ppermute(value, ('core', 'x_hi'), pairs)  9.83 us
    unnamed x38, local copies, waits for them, and re-layouts  7.8 us
  transfers between devices with their start and end apart: 25, of which 17 were waited for; matrix products, arithmetic and copies ran while one was open for 6% of the time, Pallas kernels for 4%

profile of v3, /device:TPU:1, one launch (start us, length us, event | category | flops | bytes accessed | tf_op | source)
XLA Modules:
  0.0 240.4 jit_solution(5272089040063282504)
XLA Ops:
  7.2 0.0 all-gather.2.cloned.1.call-start
  7.2 6.2 %collective-permute-start.1 = (bf16[20,5120]{1,0:T(8,128)(2,1)}, bf16[20,5120]{1,0:T(8,128)(2,1)S(1)}, u32[]{:S(2)}, u32[]{:S(2)}) collective-permute-start(bf16[20,5120]{1,0:T(8,128)(2,1)} %bitcast.30), channel_id=1, source_target_pairs={{0,0},{64,4},{4,64},{68,68},{1,1},{65,5},{5,65},{69,69},{2,2},{66,... | collective-permute-start | bytes 614408 | tf_op jit(solution)/shard_map/ppermute | solution.py:36
  13.4 1.9 collective-permute-start
  15.3 2.1 collective-permute-done.1.refs_1_.refs_0_
  17.5 5.4 %collective-permute-done.refs_0_ = bf16[20,5120]{1,0:T(8,128)(2,1)S(1)} collective-permute-done((bf16[20,5120]{1,0:T(8,128)(2,1)}, bf16[20,5120]{1,0:T(8,128)(2,1)S(1)}, u32[]{:S(2)}, u32[]{:S(2)}) %collective-permute-start) | collective-permute-done | bytes 204832 | tf_op jit(solution)/shard_map/ppermute | solution.py:36
  22.9 2.4 %collective-permute-start.2 = (bf16[20,5120]{1,0:T(8,128)(2,1)S(1)}, bf16[20,5120]{1,0:T(8,128)(2,1)S(1)}, u32[]{:S(2)}, u32[]{:S(2)}) collective-permute-start(bf16[20,5120]{1,0:T(8,128)(2,1)S(1)} %held.6.refs_0_.refs_1_), channel_id=1, source_target_pairs={{1,0},{2,1},{3,2},{0,3},{5,4},{6,5},{7,6},{4,7},{9,8},{10,9},{11,1... | collective-permute-start | bytes 614408 | tf_op jit(solution)/shard_map/ppermute | solution.py:31
  25.4 1.6 collective-permute-start.4
  27.0 1.5 collective-permute-done.2.refs_1_
  28.5 5.9 %collective-permute-done.3.refs_2_ = bf16[20,5120]{1,0:T(8,128)(2,1)S(1)} collective-permute-done((bf16[20,5120]{1,0:T(8,128)(2,1)S(1)}, bf16[20,5120]{1,0:T(8,128)(2,1)S(1)}, u32[]{:S(2)}, u32[]{:S(2)}) %collective-permute-start.3) | collective-permute-done | bytes 204832 | tf_op jit(solution)/shard_map/ppermute | solution.py:31
  34.4 1.6 stacked.2.refs_1_
  36.1 6.3 %collective-permute-start.7 = (bf16[20,5120]{1,0:T(8,128)(2,1)S(1)}, bf16[20,5120]{1,0:T(8,128)(2,1)S(1)}, u32[]{:S(2)}, u32[]{:S(2)}) collective-permute-start(bf16[20,5120]{1,0:T(8,128)(2,1)S(1)} %collective-permute-done.1.refs_1_.refs_0_), channel_id=1, source_target_pairs={{16,0},{24,8},{32,16},{40,24},{48,32},{56,40},{0,48},{8,56},{17,1}... | collective-permute-start | bytes 614408 | tf_op jit(solution)/shard_map/ppermute | solution.py:31
  42.3 0.7 collective-permute-start.12
  43.1 2.4 collective-permute-start.6
  45.5 8.1 %collective-permute-done.7.refs_2_ = bf16[20,5120]{1,0:T(8,128)(2,1)S(1)} collective-permute-done((bf16[20,5120]{1,0:T(8,128)(2,1)S(1)}, bf16[20,5120]{1,0:T(8,128)(2,1)S(1)}, u32[]{:S(2)}, u32[]{:S(2)}) %collective-permute-start.7) | collective-permute-done | bytes 204832 | tf_op jit(solution)/shard_map/ppermute | solution.py:31
  53.6 0.8 collective-permute-start.8
  54.4 3.8 %collective-permute-start.9 = (bf16[20,5120]{1,0:T(8,128)(2,1)S(1)}, bf16[20,5120]{1,0:T(8,128)(2,1)S(1)}, u32[]{:S(2)}, u32[]{:S(2)}) collective-permute-start(bf16[20,5120]{1,0:T(8,128)(2,1)S(1)} %collective-permute-done.7.refs_2_), channel_id=1, source_target_pairs={{16,0},{24,8},{32,16},{40,24},{48,32},{56,40},{0,48},{8,56},{17,1}... | collective-permute-start | bytes 614408 | tf_op jit(solution)/shard_map/ppermute | solution.py:31
  58.3 1.5 collective-permute-start.11
  61.0 1.7 concatenate.6.refs_0_
  62.7 1.4 collective-permute-done.12.refs_7_
  64.1 0.4 collective-permute-start.5
  64.5 1.7 collective-permute-done.6.refs_1_
  66.1 8.2 %collective-permute-done.8.refs_3_ = bf16[20,5120]{1,0:T(8,128)(2,1)S(1)} collective-permute-done((bf16[20,5120]{1,0:T(8,128)(2,1)S(1)}, bf16[20,5120]{1,0:T(8,128)(2,1)S(1)}, u32[]{:S(2)}, u32[]{:S(2)}) %collective-permute-start.8) | collective-permute-done | bytes 204832 | tf_op jit(solution)/shard_map/ppermute | solution.py:31
  74.3 10.4 %collective-permute-done.9.refs_4_ = bf16[20,5120]{1,0:T(8,128)(2,1)S(1)} collective-permute-done((bf16[20,5120]{1,0:T(8,128)(2,1)S(1)}, bf16[20,5120]{1,0:T(8,128)(2,1)S(1)}, u32[]{:S(2)}, u32[]{:S(2)}) %collective-permute-start.9) | collective-permute-done | bytes 204832 | tf_op jit(solution)/shard_map/ppermute | solution.py:31
  84.7 0.6 stacked.3.refs_0_
  85.3 0.1 collective-permute-start.13
  85.4 1.5 collective-permute-start.14
  86.9 0.7 copy-done.15
  87.6 0.2 fusion
  87.7 0.1 copy-done.17
  87.9 0.3 copy-done.18
  88.2 1.9 pad_maximum_fusion.refs_0_
  90.1 2.4 collective-permute-start.18
  92.5 22.5 %collective-permute-done.13.refs_2_.refs_1_ = bf16[160,5120]{1,0:T(8,128)(2,1)S(1)} collective-permute-done((bf16[160,5120]{1,0:T(8,128)(2,1)S(1)}, bf16[160,5120]{1,0:T(8,128)(2,1)S(1)}, u32[]{:S(2)}, u32[]{:S(2)}) %collective-permute-start.13) | collective-permute-done | bytes 1638432 | tf_op jit(solution)/shard_map/ppermute | solution.py:31
  115.0 1.1 slice.16
  116.1 0.9 collective-permute-start.15
  117.0 1.1 slice.17
  118.1 0.4 copy-done.8
  118.5 0.5 collective-permute-start.16
  119.0 8.6 %collective-permute-done.15.refs_4_.refs_3_ = bf16[80,5120]{1,0:T(8,128)(2,1)} collective-permute-done((bf16[80,5120]{1,0:T(8,128)(2,1)}, bf16[80,5120]{1,0:T(8,128)(2,1)}, u32[]{:S(2)}, u32[]{:S(2)}) %collective-permute-start.15) | collective-permute-done | bytes 819232 | tf_op jit(solution)/shard_map/ppermute | solution.py:31
  127.6 3.6 %collective-permute-done.16.refs_5_.refs_4_ = bf16[80,5120]{1,0:T(8,128)(2,1)} collective-permute-done((bf16[80,5120]{1,0:T(8,128)(2,1)}, bf16[80,5120]{1,0:T(8,128)(2,1)}, u32[]{:S(2)}, u32[]{:S(2)}) %collective-permute-start.16) | collective-permute-done | bytes 819232 | tf_op jit(solution)/shard_map/ppermute | solution.py:31
  131.2 1.4 copy-done.2
  132.6 1.4 copy-done.5
  134.0 1.4 copy-done.9
  135.5 3.6 %broadcast_select_fusion = f32[120,5120]{1,0:T(8,128)} fusion(f32[120,5120]{1,0:T(8,128)} %held.9, f32[120,5120]{1,0:T(8,128)} %held.7, pred[]{:T(512)S(6)} %eq.10), kind=kLoop, calls=%fused_computation.7 | loop fusion | flops 614400 | bytes 7372801 | tf_op jit(solution)/shard_map/jit(_where)/select_n | solution.py:63
  139.0 2.2 collective-permute-done.18.refs_0_
  142.0 2.1 collective-permute-done.17
  144.1 3.4 %broadcast_select_fusion.1 = f32[120,5120]{1,0:T(8,128)} fusion(f32[120,5120]{1,0:T(8,128)} %collective-permute-done.17, f32[120,5120]{1,0:T(8,128)} %held.9, pred[]{:T(512)S(6)} %eq.9), kind=kLoop, calls=%fused_computation.8 | loop fusion | flops 614400 | bytes 7372801 | tf_op jit(solution)/shard_map/jit(_where)/select_n | solution.py:65
  147.5 1.3 collective-permute-done.19.refs_6_.their_params.their_up
  148.8 6.6 %hidden.1.hidden_ref = f32[640,256]{1,0:T(8,128)S(1)} custom-call(s32[1]{0:T(128)} %bitcast.7.z_ref, bf16[160,5120]{1,0:T(8,128)(2,1)S(1)} %copy-done.3, bf16[160,5120]{1,0:T(8,128)(2,1)S(1)} %copy-done.7, bf16[160,5120]{1,0:T(8,128)(2,1)S(1)} %copy-done.11, bf16[80,5120]{1,0:T(8,128)(2,1)} %collective-permute-done.15.refs_4_.refs_3_, ...), custom_call_target="tpu_custom_call" | custom-call | flops 1677721600 | bytes 10747904 | tf_op jit(solution)/shard_map/hidden/pallas_call | solution.py:159
  155.4 0.8 copy-done.12
  156.2 1.1 copy-done.13
  157.3 12.1 %other_half.1 = (bf16[128,640]{1,0:T(8,128)(2,1)S(1)}, f32[112,5120]{1,0:T(8,128)S(1)}) custom-call(bf16[640,5120]{1,0:T(8,128)(2,1)} %all-gather.2.cloned.1.call-done.x_ref, bf16[336,5120]{1,0:T(8,128)(2,1)S(1)} %held.11.refs_5_.my_params.my_up, bf16[336,5120]{1,0:T(8,128)(2,1)} %collective-permute-done.19.refs_6_.their_params.their_up, ...), custom_call_target="tpu_custom_call" | custom-call | flops 4194304000 | bytes 21495808 | tf_op jit(solution)/shard_map/other_half/pallas_call | solution.py:221
  169.4 0.2 collective-permute-start.20
  169.6 2.5 %own_half.1 = f32[112,5120]{1,0:T(8,128)S(1)} custom-call(bf16[640,5120]{1,0:T(8,128)(2,1)S(1)} %copy-done, bf16[128,640]{1,0:T(8,128)(2,1)S(1)} %get-tuple-element.9.own_ref), custom_call_target="tpu_custom_call" | custom-call | flops 838860800 | bytes 8650752 | tf_op jit(solution)/shard_map/own_half/pallas_call | solution.py:262
  172.1 1.8 collective-permute-done.20
  173.9 2.5 %multiply_reduce_fusion = (f32[]{:T(128)}, f32[112,5120]{1,0:T(8,128)}) fusion(f32[112,5120]{1,0:T(8,128)S(1)} %own_half.1, f32[112,5120]{1,0:T(8,128)S(1)} %collective-permute-done.20), kind=kLoop, calls=%fused_computation.6 | loop fusion | flops 1720319 | bytes 6881284 | tf_op jit(solution)/shard_map/reduce_sum | solution.py:311
  176.4 4.5 %collective-permute-start.23 = (f32[112,5120]{1,0:T(8,128)}, f32[112,5120]{1,0:T(8,128)}, u32[]{:S(2)}, u32[]{:S(2)}) collective-permute-start(f32[112,5120]{1,0:T(8,128)} %get-tuple-element.13), channel_id=1, source_target_pairs={{0,0},{64,4},{4,64},{68,68},{1,1},{65,5},{5,65},{69,69},{2,2},{66,... | collective-permute-start | bytes 6881288 | tf_op jit(solution)/shard_map/ppermute | solution.py:36
  181.1 0.5 slice.15
  181.6 12.2 %psum.14 = f32[]{:T(128)} all-reduce(f32[]{:T(128)} %get-tuple-element.12), channel_id=1, replica_groups=mesh['x_lo'=2,'core'=2,'z'=8,'x_hi'=2,'y'=4] {'z'}, use_global_device_ids=true, to_apply=%region_1.2 | all-reduce | flops 1 | bytes 8 | tf_op jit(solution)/shard_map/psum | solution.py:314
  194.4 7.2 %psum.15 = f32[]{:T(128)} all-reduce(f32[]{:T(128)} %psum.14), channel_id=1, replica_groups=mesh['x_lo'=2,'core'=2,'z'=8,'x_hi'=2,'y'=4] {'y'}, use_global_device_ids=true, to_apply=%region_2.3 | all-reduce | flops 1 | bytes 8 | tf_op jit(solution)/shard_map/psum | solution.py:314
  201.7 8.8 %collective-permute-start.21 = (f32[]{:T(128)}, f32[]{:T(128)}, u32[]{:S(2)}, u32[]{:S(2)}) collective-permute-start(f32[]{:T(128)} %psum.15), channel_id=1, source_target_pairs={{0,0},{64,4},{4,64},{68,68},{1,1},{65,5},{5,65},{69,69},{2,2},{66,... | collective-permute-start | bytes 20 | tf_op jit(solution)/shard_map/ppermute | solution.py:36
  210.5 13.5 %collective-permute-start.22 = (f32[]{:T(128)}, f32[]{:T(128)}, u32[]{:S(2)}, u32[]{:S(2)}) collective-permute-start(f32[]{:T(128)} %psum.15), channel_id=1, source_target_pairs={{64,0},{0,4},{68,64},{4,68},{65,1},{1,5},{69,65},{5,69},{66,2},{2,... | collective-permute-start | bytes 20 | tf_op jit(solution)/shard_map/ppermute | solution.py:283
  224.0 1.1 collective-permute-done.22
  226.4 4.9 %fusion.2 = (f32[1,112,5120]{2,1,0:T(8,128)}, f32[1,112,5120]{2,1,0:T(8,128)}) fusion(f32[112,5120]{1,0:T(8,128)} %collective-permute-done.23, f32[]{:T(128)S(6)} %mul.22, f32[1,112,5120]{2,1,0:T(8,128)} %param.11, f32[120,5120]{1,0:T(8,128)S(1)} %copy-done.14), kind=kLoop, calls=%fused_computation.9 | loop fusion | flops 2293760 | bytes 11468804 | tf_op jit(solution)/shard_map/broadcast_in_dim | solution.py:322
  (48 shorter events, 0.1 us)
Async XLA Ops:
  7.2 53.9 %copy-start.16 = (f32[1,112,5120]{2,1,0:T(8,128)S(1)}, f32[1,112,5120]{2,1,0:T(8,128)}, u32[]{:S(2)}) copy-start(f32[1,112,5120]{2,1,0:T(8,128)} %param.13) | copy-start | bytes 6881284
  7.2 149.0 %all-gather.2.cloned.1.call-start = ((), (), s32[]{:S(2)}) async-start(), calls=%async_computation | async-start | bytes 7372800 | tf_op jit(solution)/shard_map/all_gather | solution.py:305
  7.2 10.3 %collective-permute-start.1 = (bf16[20,5120]{1,0:T(8,128)(2,1)}, bf16[20,5120]{1,0:T(8,128)(2,1)S(1)}, u32[]{:S(2)}, u32[]{:S(2)}) collective-permute-start(bf16[20,5120]{1,0:T(8,128)(2,1)} %bitcast.30), channel_id=1, source_target_pairs={{0,0},{64,4},{4,64},{68,68},{1,1},{65,5},{5,65},{69,69},{2,2},{66,... | collective-permute-start | bytes 614408 | tf_op jit(solution)/shard_map/ppermute | solution.py:36
  13.4 9.5 %collective-permute-start = (bf16[20,5120]{1,0:T(8,128)(2,1)}, bf16[20,5120]{1,0:T(8,128)(2,1)S(1)}, u32[]{:S(2)}, u32[]{:S(2)}) collective-permute-start(bf16[20,5120]{1,0:T(8,128)(2,1)} %bitcast.31), channel_id=1, source_target_pairs={{0,0},{64,4},{4,64},{68,68},{1,1},{65,5},{5,65},{69,69},{2,2},{66,... | collective-permute-start | bytes 614408 | tf_op jit(solution)/shard_map/ppermute | solution.py:36
  22.9 5.6 %collective-permute-start.2 = (bf16[20,5120]{1,0:T(8,128)(2,1)S(1)}, bf16[20,5120]{1,0:T(8,128)(2,1)S(1)}, u32[]{:S(2)}, u32[]{:S(2)}) collective-permute-start(bf16[20,5120]{1,0:T(8,128)(2,1)S(1)} %held.6.refs_0_.refs_1_), channel_id=1, source_target_pairs={{1,0},{2,1},{3,2},{0,3},{5,4},{6,5},{7,6},{4,7},{9,8},{10,9},{11,1... | collective-permute-start | bytes 614408 | tf_op jit(solution)/shard_map/ppermute | solution.py:31
  25.4 9.0 %collective-permute-start.3 = (bf16[20,5120]{1,0:T(8,128)(2,1)S(1)}, bf16[20,5120]{1,0:T(8,128)(2,1)S(1)}, u32[]{:S(2)}, u32[]{:S(2)}) collective-permute-start(bf16[20,5120]{1,0:T(8,128)(2,1)S(1)} %held.6.refs_0_.refs_1_), channel_id=1, source_target_pairs={{3,0},{0,1},{1,2},{2,3},{7,4},{4,5},{5,6},{6,7},{11,8},{8,9},{9,10... | collective-permute-start | bytes 614408 | tf_op jit(solution)/shard_map/ppermute | solution.py:31
  25.4 9.0 %collective-permute-start.4 = (bf16[20,5120]{1,0:T(8,128)(2,1)S(1)}, bf16[20,5120]{1,0:T(8,128)(2,1)S(1)}, u32[]{:S(2)}, u32[]{:S(2)}) collective-permute-start(bf16[20,5120]{1,0:T(8,128)(2,1)S(1)} %held.6.refs_0_.refs_1_), channel_id=1, source_target_pairs={{2,0},{3,1},{0,2},{1,3},{6,4},{7,5},{4,6},{5,7},{10,8},{11,9},{8,1... | collective-permute-start | bytes 614408 | tf_op jit(solution)/shard_map/ppermute | solution.py:31
  36.1 17.5 %collective-permute-start.7 = (bf16[20,5120]{1,0:T(8,128)(2,1)S(1)}, bf16[20,5120]{1,0:T(8,128)(2,1)S(1)}, u32[]{:S(2)}, u32[]{:S(2)}) collective-permute-start(bf16[20,5120]{1,0:T(8,128)(2,1)S(1)} %collective-permute-done.1.refs_1_.refs_0_), channel_id=1, source_target_pairs={{16,0},{24,8},{32,16},{40,24},{48,32},{56,40},{0,48},{8,56},{17,1}... | collective-permute-start | bytes 614408 | tf_op jit(solution)/shard_map/ppermute | solution.py:31
  42.3 16.0 %collective-permute-start.10 = (bf16[20,5120]{1,0:T(8,128)(2,1)S(1)}, bf16[20,5120]{1,0:T(8,128)(2,1)S(1)}, u32[]{:S(2)}, u32[]{:S(2)}) collective-permute-start(bf16[20,5120]{1,0:T(8,128)(2,1)S(1)} %collective-permute-done.1.refs_1_.refs_0_), channel_id=1, source_target_pairs={{48,0},{56,8},{0,16},{8,24},{16,32},{24,40},{32,48},{40,56},{49,1}... | collective-permute-start | bytes 614408 | tf_op jit(solution)/shard_map/ppermute | solution.py:31
  42.3 21.8 %collective-permute-start.12 = (bf16[20,5120]{1,0:T(8,128)(2,1)S(1)}, bf16[20,5120]{1,0:T(8,128)(2,1)S(1)}, u32[]{:S(2)}, u32[]{:S(2)}) collective-permute-start(bf16[20,5120]{1,0:T(8,128)(2,1)S(1)} %collective-permute-done.1.refs_1_.refs_0_), channel_id=1, source_target_pairs={{56,0},{0,8},{8,16},{16,24},{24,32},{32,40},{40,48},{48,56},{57,1}... | collective-permute-start | bytes 614408 | tf_op jit(solution)/shard_map/ppermute | solution.py:31
  43.1 23.0 %collective-permute-start.6 = (bf16[20,5120]{1,0:T(8,128)(2,1)S(1)}, bf16[20,5120]{1,0:T(8,128)(2,1)S(1)}, u32[]{:S(2)}, u32[]{:S(2)}) collective-permute-start(bf16[20,5120]{1,0:T(8,128)(2,1)S(1)} %collective-permute-done.1.refs_1_.refs_0_), channel_id=1, source_target_pairs={{8,0},{16,8},{24,16},{32,24},{40,32},{48,40},{56,48},{0,56},{9,1},... | collective-permute-start | bytes 614408 | tf_op jit(solution)/shard_map/ppermute | solution.py:31
  53.6 20.7 %collective-permute-start.8 = (bf16[20,5120]{1,0:T(8,128)(2,1)S(1)}, bf16[20,5120]{1,0:T(8,128)(2,1)S(1)}, u32[]{:S(2)}, u32[]{:S(2)}) collective-permute-start(bf16[20,5120]{1,0:T(8,128)(2,1)S(1)} %collective-permute-done.7.refs_2_), channel_id=1, source_target_pairs={{8,0},{16,8},{24,16},{32,24},{40,32},{48,40},{56,48},{0,56},{9,1},... | collective-permute-start | bytes 614408 | tf_op jit(solution)/shard_map/ppermute | solution.py:31
  54.4 30.3 %collective-permute-start.9 = (bf16[20,5120]{1,0:T(8,128)(2,1)S(1)}, bf16[20,5120]{1,0:T(8,128)(2,1)S(1)}, u32[]{:S(2)}, u32[]{:S(2)}) collective-permute-start(bf16[20,5120]{1,0:T(8,128)(2,1)S(1)} %collective-permute-done.7.refs_2_), channel_id=1, source_target_pairs={{16,0},{24,8},{32,16},{40,24},{48,32},{56,40},{0,48},{8,56},{17,1}... | collective-permute-start | bytes 614408 | tf_op jit(solution)/shard_map/ppermute | solution.py:31
  58.3 26.4 %collective-permute-start.11 = (bf16[20,5120]{1,0:T(8,128)(2,1)S(1)}, bf16[20,5120]{1,0:T(8,128)(2,1)S(1)}, u32[]{:S(2)}, u32[]{:S(2)}) collective-permute-start(bf16[20,5120]{1,0:T(8,128)(2,1)S(1)} %collective-permute-done.10.refs_6_), channel_id=1, source_target_pairs={{56,0},{0,8},{8,16},{16,24},{24,32},{32,40},{40,48},{48,56},{57,1}... | collective-permute-start | bytes 614408 | tf_op jit(solution)/shard_map/ppermute | solution.py:31
  64.1 54.9 %collective-permute-start.5 = (f32[120,5120]{1,0:T(8,128)}, f32[120,5120]{1,0:T(8,128)}, u32[]{:S(2)}, u32[]{:S(2)}) collective-permute-start(f32[120,5120]{1,0:T(8,128)} %held.7), channel_id=1, source_target_pairs={{128,0},{0,128},{129,1},{1,129},{130,2},{2,130},{131,3},{3,131},{1... | collective-permute-start | bytes 7372808 | tf_op jit(solution)/shard_map/ppermute | solution.py:31
  85.3 2.3 copy-start.15
  85.3 4.8 %copy-start.1 = (bf16[160,5120]{1,0:T(8,128)(2,1)}, bf16[160,5120]{1,0:T(8,128)(2,1)S(1)}, u32[]{:S(2)}) copy-start(bf16[160,5120]{1,0:T(8,128)(2,1)S(1)} %held.8.refs_1_.refs_0_) | copy-start | bytes 4915204
  85.3 2.6 %copy-start.17 = (bf16[112,5120]{1,0:T(8,128)(2,1)S(1)}, bf16[112,5120]{1,0:T(8,128)(2,1)}, u32[]{:S(2)}) copy-start(bf16[112,5120]{1,0:T(8,128)(2,1)} %param.16) | copy-start | bytes 3440644
  85.3 2.9 %copy-start.18 = (bf16[112,5120]{1,0:T(8,128)(2,1)S(1)}, bf16[112,5120]{1,0:T(8,128)(2,1)}, u32[]{:S(2)}) copy-start(bf16[112,5120]{1,0:T(8,128)(2,1)} %param.15) | copy-start | bytes 3440644
  85.3 29.7 %collective-permute-start.13 = (bf16[160,5120]{1,0:T(8,128)(2,1)S(1)}, bf16[160,5120]{1,0:T(8,128)(2,1)S(1)}, u32[]{:S(2)}, u32[]{:S(2)}) collective-permute-start(bf16[160,5120]{1,0:T(8,128)(2,1)S(1)} %held.8.refs_1_.refs_0_), channel_id=1, source_target_pairs={{1,0},{2,1},{3,2},{0,3},{5,4},{6,5},{7,6},{4,7},{9,8},{10,9},{11,1... | collective-permute-start | bytes 4915208 | tf_op jit(solution)/shard_map/ppermute | solution.py:31
  85.4 31.6 %collective-permute-start.14 = (bf16[160,5120]{1,0:T(8,128)(2,1)S(1)}, bf16[160,5120]{1,0:T(8,128)(2,1)S(1)}, u32[]{:S(2)}, u32[]{:S(2)}) collective-permute-start(bf16[160,5120]{1,0:T(8,128)(2,1)S(1)} %held.8.refs_1_.refs_0_), channel_id=1, source_target_pairs={{3,0},{0,1},{1,2},{2,3},{7,4},{4,5},{5,6},{6,7},{11,8},{8,9},{9,10... | collective-permute-start | bytes 4915208 | tf_op jit(solution)/shard_map/ppermute | solution.py:31
  90.1 51.1 %collective-permute-start.18 = (bf16[336,5120]{1,0:T(8,128)(2,1)}, bf16[336,5120]{1,0:T(8,128)(2,1)S(1)}, u32[]{:S(2)}, u32[]{:S(2)}) collective-permute-start(bf16[336,5120]{1,0:T(8,128)(2,1)} %held.10), channel_id=1, source_target_pairs={{0,0},{64,4},{4,64},{68,68},{1,1},{65,5},{5,65},{69,69},{2,2},{66,... | collective-permute-start | bytes 10321928 | tf_op jit(solution)/shard_map/ppermute | solution.py:36
  115.0 2.0 copy-start.4
  116.1 11.5 %collective-permute-start.15 = (bf16[80,5120]{1,0:T(8,128)(2,1)}, bf16[80,5120]{1,0:T(8,128)(2,1)}, u32[]{:S(2)}, u32[]{:S(2)}) collective-permute-start(bf16[80,5120]{1,0:T(8,128)(2,1)} %slice.16), channel_id=1, source_target_pairs={{1,0},{2,1},{3,2},{0,3},{5,4},{6,5},{7,6},{4,7},{9,8},{10,9},{11,1... | collective-permute-start | bytes 2457608 | tf_op jit(solution)/shard_map/ppermute | solution.py:31
  117.0 1.4 copy-start.8
  118.5 12.7 %collective-permute-start.16 = (bf16[80,5120]{1,0:T(8,128)(2,1)}, bf16[80,5120]{1,0:T(8,128)(2,1)}, u32[]{:S(2)}, u32[]{:S(2)}) collective-permute-start(bf16[80,5120]{1,0:T(8,128)(2,1)} %slice.17), channel_id=1, source_target_pairs={{3,0},{0,1},{1,2},{2,3},{7,4},{4,5},{5,6},{6,7},{11,8},{8,9},{9,10... | collective-permute-start | bytes 2457608 | tf_op jit(solution)/shard_map/ppermute | solution.py:31
  131.2 1.4 copy-start.2
  132.6 1.4 copy-start.5
  134.0 1.4 copy-start.9
  135.5 5.8 %copy-start.6 = (bf16[160,5120]{1,0:T(8,128)(2,1)S(1)}, bf16[160,5120]{1,0:T(8,128)(2,1)}, u32[]{:S(2)}) copy-start(bf16[160,5120]{1,0:T(8,128)(2,1)} %copy-done.4) | copy-start | bytes 4915204
  135.5 5.8 %copy-start.10 = (bf16[160,5120]{1,0:T(8,128)(2,1)S(1)}, bf16[160,5120]{1,0:T(8,128)(2,1)}, u32[]{:S(2)}) copy-start(bf16[160,5120]{1,0:T(8,128)(2,1)} %copy-done.8) | copy-start | bytes 4915204
  139.0 5.0 %collective-permute-start.17 = (f32[120,5120]{1,0:T(8,128)}, f32[120,5120]{1,0:T(8,128)}, u32[]{:S(2)}, u32[]{:S(2)}) collective-permute-start(f32[120,5120]{1,0:T(8,128)} %broadcast_select_fusion), channel_id=1, source_target_pairs={{64,0},{0,64},{65,1},{1,65},{66,2},{2,66},{67,3},{3,67},{68,4},{4,... | collective-permute-start | bytes 7372808 | tf_op jit(solution)/shard_map/ppermute | solution.py:31
  141.3 7.5 %collective-permute-start.19 = (bf16[336,5120]{1,0:T(8,128)(2,1)S(1)}, bf16[336,5120]{1,0:T(8,128)(2,1)}, u32[]{:S(2)}, u32[]{:S(2)}) collective-permute-start(bf16[336,5120]{1,0:T(8,128)(2,1)S(1)} %held.11.refs_5_.my_params.my_up), channel_id=1, source_target_pairs={{64,0},{0,64},{65,1},{1,65},{66,2},{2,66},{67,3},{3,67},{68,4},{4,... | collective-permute-start | bytes 10321928 | tf_op jit(solution)/shard_map/ppermute | solution.py:31
  141.9 6.8 %copy-start.3 = (bf16[160,5120]{1,0:T(8,128)(2,1)S(1)}, bf16[160,5120]{1,0:T(8,128)(2,1)}, u32[]{:S(2)}) copy-start(bf16[160,5120]{1,0:T(8,128)(2,1)} %copy-done.1) | copy-start | bytes 4915204
  142.0 6.8 %copy-start.7 = (bf16[160,5120]{1,0:T(8,128)(2,1)S(1)}, bf16[160,5120]{1,0:T(8,128)(2,1)}, u32[]{:S(2)}) copy-start(bf16[160,5120]{1,0:T(8,128)(2,1)} %copy-done.4) | copy-start | bytes 4915204
  142.0 6.8 %copy-start.11 = (bf16[160,5120]{1,0:T(8,128)(2,1)S(1)}, bf16[160,5120]{1,0:T(8,128)(2,1)}, u32[]{:S(2)}) copy-start(bf16[160,5120]{1,0:T(8,128)(2,1)} %copy-done.8) | copy-start | bytes 4915204
  155.4 0.8 copy-start.12
  156.2 1.1 copy-start.13
  157.3 12.3 %copy-start = (bf16[640,5120]{1,0:T(8,128)(2,1)S(1)}, bf16[640,5120]{1,0:T(8,128)(2,1)}, u32[]{:S(2)}) copy-start(bf16[640,5120]{1,0:T(8,128)(2,1)} %all-gather.2.cloned.1.call-done.x_ref) | copy-start | bytes 19660804
  169.4 4.5 %collective-permute-start.20 = (f32[112,5120]{1,0:T(8,128)S(1)}, f32[112,5120]{1,0:T(8,128)S(1)}, u32[]{:S(2)}, u32[]{:S(2)}) collective-permute-start(f32[112,5120]{1,0:T(8,128)S(1)} %get-tuple-element.10), channel_id=1, source_target_pairs={{64,0},{0,64},{65,1},{1,65},{66,2},{2,66},{67,3},{3,67},{68,4},{4,... | collective-permute-start | bytes 6881288 | tf_op jit(solution)/shard_map/ppermute | solution.py:31
  172.1 9.0 %copy-start.14 = (f32[120,5120]{1,0:T(8,128)S(1)}, f32[120,5120]{1,0:T(8,128)}, u32[]{:S(2)}) copy-start(f32[120,5120]{1,0:T(8,128)} %broadcast_select_fusion.1) | copy-start | bytes 7372804
  176.4 49.9 %collective-permute-start.23 = (f32[112,5120]{1,0:T(8,128)}, f32[112,5120]{1,0:T(8,128)}, u32[]{:S(2)}, u32[]{:S(2)}) collective-permute-start(f32[112,5120]{1,0:T(8,128)} %get-tuple-element.13), channel_id=1, source_target_pairs={{0,0},{64,4},{4,64},{68,68},{1,1},{65,5},{5,65},{69,69},{2,2},{66,... | collective-permute-start | bytes 6881288 | tf_op jit(solution)/shard_map/ppermute | solution.py:36
  201.7 22.3 %collective-permute-start.21 = (f32[]{:T(128)}, f32[]{:T(128)}, u32[]{:S(2)}, u32[]{:S(2)}) collective-permute-start(f32[]{:T(128)} %psum.15), channel_id=1, source_target_pairs={{0,0},{64,4},{4,64},{68,68},{1,1},{65,5},{5,65},{69,69},{2,2},{66,... | collective-permute-start | bytes 20 | tf_op jit(solution)/shard_map/ppermute | solution.py:36
  210.5 14.6 %collective-permute-start.22 = (f32[]{:T(128)}, f32[]{:T(128)}, u32[]{:S(2)}, u32[]{:S(2)}) collective-permute-start(f32[]{:T(128)} %psum.15), channel_id=1, source_target_pairs={{64,0},{0,4},{68,64},{4,68},{65,1},{1,5},{69,65},{5,69},{66,2},{2,... | collective-permute-start | bytes 20 | tf_op jit(solution)/shard_map/ppermute | solution.py:283
Sparse Core Ops, SparseCore 0:
  36.2 91.8 all-gather.1

commit v4 on v3

v4 whole, which is shorter than its diff:
```python
import math

import jax
import jax.numpy as jnp
import numpy as np
from jax import lax
from jax.experimental import pallas as pl
from jax.experimental.pallas import tpu as pltpu
from jax.sharding import Mesh, PartitionSpec as P

D = 5120
FFW = 7168

eps = 1e-06

WIDTH_SCALE = D ** (-0.5)
MAX_NORM = 0.05 * math.sqrt(D * FFW)

SIZES = {"x_lo": 2, "core": 2, "z": 8, "x_hi": 2, "y": 4}
GOSSIP = ("x_lo", "core")
FSDP = ("z", "x_hi", "y")

ROWS = 112
HALF = 128
BLOCK = 1024


def shifted(value, axis, steps):
    count = SIZES[axis]
    pairs = [((place + steps) % count, place) for place in range(count)]
    return lax.ppermute(value, axis, pairs)


def transposed(value):
    pairs = [(2 * x_hi + core, 2 * core + x_hi) for core in range(2) for x_hi in range(2)]
    return lax.ppermute(value, ("core", "x_hi"), pairs)


def held(value, *ready):
    return pl.pallas_call(
        lambda *refs: None,
        in_specs=[pl.BlockSpec(memory_space=pl.ANY)] * (1 + len(ready)),
        out_specs=pl.BlockSpec(memory_space=pl.ANY),
        out_shape=jax.ShapeDtypeStruct(value.shape, value.dtype),
        input_output_aliases={0: 0},
        compiler_params=params_of(1),
        name="held",
    )(value, *ready)


def silu_slope(preact):
    sigmoid_val = jax.nn.sigmoid(preact)
    return sigmoid_val * (1.0 + preact * (1.0 - sigmoid_val))


def plan_rate(step):
    phase = (step[0] % 1000).astype(jnp.float32) / 1000.0
    return 0.4 + 1.8 * (1.0 + jnp.cos(math.pi * phase))


def dot_t(rows, weights):
    return lax.dot_general(
        rows, weights, (((1,), (1,)), ((), ())), preferred_element_type=jnp.float32
    )


def params_of(vmem, **more):
    return pltpu.CompilerParams(vmem_limit_bytes=vmem * 2**20, **more)


def stack_kernel(*refs):
    *blocks, out_ref = refs
    for at, block in enumerate(blocks):
        count = block.shape[0]
        out_ref[at * count : (at + 1) * count, :] = block[...]


def stacked(blocks):
    count = blocks[0].shape[0]
    wide = D // 4
    return pl.pallas_call(
        stack_kernel,
        grid=(4,),
        in_specs=[pl.BlockSpec((count, wide), lambda at: (0, at))] * len(blocks),
        out_specs=pl.BlockSpec((count * len(blocks), wide), lambda at: (0, at)),
        out_shape=jax.ShapeDtypeStruct((count * len(blocks), D), blocks[0].dtype),
        compiler_params=params_of(8),
        name="stacked",
    )(*blocks)


def widen(wide, mine, theirs):
    wide[:ROWS, :] = mine[...]
    wide[HALF : HALF + ROWS, :] = theirs[...]


def clear(wide):
    pad = jnp.zeros((HALF - ROWS, wide.shape[1]), wide.dtype)
    wide[ROWS:HALF, :] = pad
    wide[HALF + ROWS :, :] = pad


def hidden_kernel(*refs):
    *parts, mine, theirs, out_ref, total, wide = refs
    at = pl.program_id(0)

    @pl.when(at == 0)
    def _():
        total[...] = jnp.zeros_like(total)
        clear(wide)

    widen(wide, mine, theirs)
    row = 0
    for part in parts:
        count = part.shape[0]
        total[row : row + count, :] += dot_t(part[...], wide[...])
        row += count

    @pl.when(at == pl.num_programs(0) - 1)
    def _():
        column, block = row // 4, row // 32
        for dz in range(8):
            for dy in range(4):
                start, place = dy * column + dz * block, (4 * dz + dy) * block
                out_ref[place : place + block, :] = total[start : start + block, :]


def hidden_of(parts, mine, theirs):
    count = sum(part.shape[0] for part in parts)
    weights = pl.BlockSpec((ROWS, BLOCK), lambda at: (2, at))
    return pl.pallas_call(
        hidden_kernel,
        grid=(D // BLOCK,),
        in_specs=[pl.BlockSpec((part.shape[0], BLOCK), lambda at: (0, at)) for part in parts]
        + [weights, weights],
        out_specs=pl.BlockSpec((count, 2 * HALF), lambda at: (0, 0)),
        out_shape=jax.ShapeDtypeStruct((count, 2 * HALF), jnp.float32),
        scratch_shapes=[
            pltpu.VMEM((count, 2 * HALF), jnp.float32),
            pltpu.VMEM((2 * HALF, BLOCK), jnp.bfloat16),
        ],
        compiler_params=params_of(16),
        cost_estimate=pl.CostEstimate(
            flops=2 * count * D * 2 * HALF, bytes_accessed=2 * count * D + 2**22, transcendentals=0
        ),
        name="hidden",
    )(*parts, mine, theirs)


def grad_kernel(*refs):
    *parts, my_params, their_params, my_up, their_up, hidden_ref, own_ref, other_ref = refs[:-6]
    rows, preact, up_proj, turned, wide_params, wide_up = refs[-6:]
    at = pl.program_id(0)

    @pl.when(at == 0)
    def _():
        preact[...] = jnp.zeros_like(preact)
        up_proj[...] = jnp.zeros_like(up_proj)
        clear(wide_params)
        clear(wide_up)

    columns = pl.ds(pl.multiple_of(at * BLOCK, BLOCK), BLOCK)
    row = 0
    for part in parts:
        count = part.shape[0]
        rows[row : row + count, columns] = part[...]
        row += count
    widen(wide_params, my_params, their_params)
    widen(wide_up, my_up, their_up)
    preact[...] += dot_t(rows[:, columns], wide_params[...])
    up_proj[...] += dot_t(rows[:, columns], wide_up[...])

    @pl.when(at == pl.num_programs(0) - 1)
    def _():
        slope = silu_slope(preact[...] * WIDTH_SCALE)
        turned[...] = (hidden_ref[...] * up_proj[...] * slope).T.astype(jnp.bfloat16)

        @pl.loop(0, D // BLOCK)
        def _(block):
            columns = pl.ds(pl.multiple_of(block * BLOCK, BLOCK), BLOCK)
            grad = jnp.dot(turned[...], rows[:, columns], preferred_element_type=jnp.float32)
            own_ref[:, columns] = grad[:ROWS] * WIDTH_SCALE
            other_ref[:, columns] = grad[HALF : HALF + ROWS] * WIDTH_SCALE


def gate_grads(parts, mine, theirs, hidden):
    count = sum(part.shape[0] for part in parts)

    def weights(which):
        return pl.BlockSpec((ROWS, BLOCK), lambda at: (which, at))

    whole = pl.BlockSpec((ROWS, D), lambda at: (0, 0))
    return pl.pallas_call(
        grad_kernel,
        grid=(D // BLOCK,),
        in_specs=[pl.BlockSpec((part.shape[0], BLOCK), lambda at: (0, at)) for part in parts]
        + [weights(0), weights(0), weights(1), weights(1)]
        + [pl.BlockSpec((count, 2 * HALF), lambda at: (0, 0))],
        out_specs=[whole, whole],
        out_shape=[jax.ShapeDtypeStruct((ROWS, D), jnp.float32)] * 2,
        scratch_shapes=[
            pltpu.VMEM((count, D), jnp.bfloat16),
            pltpu.VMEM((count, 2 * HALF), jnp.float32),
            pltpu.VMEM((count, 2 * HALF), jnp.float32),
            pltpu.VMEM((2 * HALF, count), jnp.bfloat16),
            pltpu.VMEM((2 * HALF, BLOCK), jnp.bfloat16),
            pltpu.VMEM((2 * HALF, BLOCK), jnp.bfloat16),
        ],
        compiler_params=params_of(36),
        cost_estimate=pl.CostEstimate(
            flops=2 * count * D * 768, bytes_accessed=2 * count * D + 2**23, transcendentals=0
        ),
        name="gate_grads",
    )(*parts, mine, theirs, mine, theirs, hidden)


def crossed(value):
    pairs = [
        (2 * (1 - x_hi) + core, 2 * core + x_hi) for core in range(2) for x_hi in range(2)
    ]
    return lax.ppermute(value, ("core", "x_hi"), pairs)


def shards(
    tokens, cotangent, gate_num, push_weight, stale_num, stale_weight, up_weight, down_weight, step
):
    rate = plan_rate(step)
    numerator = gate_num[0]

    params = (numerator / push_weight[0]).astype(jnp.bfloat16)
    weights = jnp.concatenate([params, up_weight, down_weight], axis=0)
    rows_in, rows_grad = transposed(tokens[0]), transposed(cotangent[0])
    rows_in = held(rows_in, rows_grad, weights)
    near = [rows_in] + [shifted(rows_in, "y", steps) for steps in (1, 3, 2)]
    ring = {0: rows_grad, 1: shifted(rows_grad, "z", 1), 7: shifted(rows_grad, "z", 7)}
    mine = transposed(held(weights, rows_grad))
    ring[2], ring[6] = shifted(ring[1], "z", 1), shifted(ring[7], "z", 7)
    near[3] = held(near[3], ring[1], ring[7])
    blocks = {0: stacked(near)}
    for steps in (1, 7):
        blocks[steps] = shifted(blocks[0], "z", steps)
    ring[3], ring[5] = shifted(ring[2], "z", 1), shifted(ring[6], "z", 7)
    ring[4] = shifted(ring[2], "z", 2)
    column = stacked([ring[steps] for steps in range(8)])

    following, before = shifted(column, "y", 1), shifted(column, "y", 3)
    blocks[1], blocks[7] = held(blocks[1], column), held(blocks[7], column)
    blocks[2], blocks[6] = shifted(blocks[1], "z", 1), shifted(blocks[7], "z", 7)
    mine = held(mine, blocks[2], blocks[6])
    theirs = shifted(mine, "core", 1)
    stale = jnp.concatenate([stale_num[0], jnp.broadcast_to(stale_weight, (8, D))], axis=0)
    stale = held(stale, blocks[1])
    two_before = shifted(stale, "x_lo", 1)
    blocks[3], blocks[5] = shifted(blocks[2], "z", 1), shifted(blocks[6], "z", 7)
    following, before = held(following, blocks[2]), held(before, blocks[6])
    half = column.shape[0] // 2
    far = [shifted(following[:half], "y", 1), shifted(before[half:], "y", 3)]
    blocks[3], blocks[5] = held(blocks[3], following), held(blocks[5], before)
    cut = 48
    last = [shifted(blocks[3][:cut], "z", 1), shifted(blocks[5][cut:], "z", 7)]

    hidden = hidden_of([column, following, before, *far], mine, theirs)
    parts = [blocks[steps] for steps in (0, 1, 2, 3)] + last + [blocks[steps] for steps in (5, 6, 7)]
    own_grad, other_grad = gate_grads(parts, mine, theirs, hidden)
    two_before = held(two_before, own_grad)
    first = lax.axis_index("core") == 0
    one_before = jnp.where(first, shifted(two_before, "core", 1), shifted(stale, "core", 1))
    received = jnp.where(step[0] % 2 == 0, one_before, two_before)

    gate_grad = own_grad + shifted(other_grad, "core", 1)
    norm_sq = jnp.sum(gate_grad * gate_grad)
    gate_grad = transposed(gate_grad)
    for axes in ("z", "y"):
        norm_sq = lax.psum(norm_sq, axes)
    norm_sq = transposed(norm_sq) + crossed(norm_sq)

    clip_factor = jnp.minimum(1.0, MAX_NORM / jnp.sqrt(norm_sq + eps))
    kept_half = 0.5 * (numerator - rate * clip_factor * gate_grad)
    kept_weight = 0.5 * push_weight
    new_num = kept_half + received[:ROWS]
    new_weight = kept_weight + received[ROWS, :1]
    return (new_num[None], new_weight, kept_half[None], kept_weight)


def solution(mesh):
    named = Mesh(np.asarray(mesh.devices).reshape(tuple(SIZES.values())), tuple(SIZES))
    groups = P(GOSSIP, FSDP, None)
    in_specs = (
        groups,
        groups,
        groups,
        P(GOSSIP),
        groups,
        P(GOSSIP),
        P(FSDP, None),
        P(FSDP, None),
        P(),
    )
    out_specs = (groups, P(GOSSIP), groups, P(GOSSIP))
    return jax.shard_map(shards, mesh=named, in_specs=in_specs, out_specs=out_specs, check_vma=False)
```

time: 243 us -> 259 us (1.066)
  waiting for transfers between devices: 88 us -> 129 us
  between operations: 20.5 us -> 7.27 us
  starting transfers between devices: 60.5 us -> 71.3 us
  local copies, waits for them, and re-layouts: 12.1 us -> 2.4 us
  Pallas kernels: 23.4 us -> 15.4 us
  other arithmetic: 16.5 us -> 11.1 us
    ppermute x18 -> x27, waiting for transfers between devices: 77 us -> 122 us  [shifted(): return lax.ppermute(value, axis, pairs)]
    ppermute x18 -> x27, starting transfers between devices: 23.2 us -> 34.1 us  [shifted(): return lax.ppermute(value, axis, pairs)]
    unnamed x38 -> x8, local copies, waits for them, and re-layouts: 7.8 us -> 0.02 us
    pallas_call x2 -> x1, Pallas kernels: 14.6 us -> 8.86 us  [gate_grads(): pl.pallas_call(grad_kernel, grid=(D // BLOCK,), in_specs=[pl.BlockSpec((p...]
    ppermute x5, waiting for transfers between devices: 9.83 us -> 4.53 us  [transposed(): return lax.ppermute(value, ('core', 'x_hi'), pairs)]
    select_n x2 -> x1, other arithmetic: 6.96 us -> 2.21 us  [shards(): received = jnp.where(step[0] % 2 == 0, one_before, two_before)]
    ppermute x1, starting transfers between devices: 13.5 us -> 10.3 us  [crossed(): return lax.ppermute(value, ('core', 'x_hi'), pairs)]
    ppermute x5, starting transfers between devices: 23.7 us -> 26.9 us  [transposed(): return lax.ppermute(value, ('core', 'x_hi'), pairs)]
  transfers between devices with their start and end apart: 25 -> 33, of which waited for: 17 -> 16; matrix products, arithmetic and copies ran while one was open for 6% -> 4% of each run, Pallas kernels for 4% -> 6%
where the time goes in v4:
time: 259 us; the launch traced here: 257 us
  waiting for transfers between devices  129 us (50%)
  starting transfers between devices  71.3 us (28%)
  blocking collectives  20.6 us (8%)
  Pallas kernels  15.4 us (6%)
  other arithmetic  11.1 us (4%)
  between operations  7.27 us (3%)
    ppermute x27, waiting for transfers between devices, shifted(): return lax.ppermute(value, axis, pairs)  122 us
    ppermute x27, starting transfers between devices, shifted(): return lax.ppermute(value, axis, pairs)  34.1 us
    ppermute x5, starting transfers between devices, transposed(): return lax.ppermute(value, ('core', 'x_hi'), pairs)  26.9 us
    psum x2, blocking collectives, shards(): norm_sq = lax.psum(norm_sq, axes)  20.6 us
    ppermute x1, starting transfers between devices, crossed(): return lax.ppermute(value, ('core', 'x_hi'), pairs)  10.3 us
    pallas_call x1, Pallas kernels, gate_grads(): pl.pallas_call(grad_kernel, grid=(D // BLOCK,), in_specs=[pl.BlockSpec((p...  8.86 us
    pallas_call x1, Pallas kernels, hidden_of(): pl.pallas_call(hidden_kernel, grid=(D // BLOCK,), in_specs=[pl.BlockSpec(...  5.64 us
  transfers between devices with their start and end apart: 33, of which 16 were waited for; matrix products, arithmetic and copies ran while one was open for 4% of the time, Pallas kernels for 6%

profile of v4, /device:TPU:1, one launch (start us, length us, event | category | flops | bytes accessed | tf_op | source)
XLA Modules:
  0.0 257.0 jit_solution(11646432239302814651)
XLA Ops:
  0.7 6.2 %collective-permute-start.1 = (bf16[20,5120]{1,0:T(8,128)(2,1)}, bf16[20,5120]{1,0:T(8,128)(2,1)S(1)}, u32[]{:S(2)}, u32[]{:S(2)}) collective-permute-start(bf16[20,5120]{1,0:T(8,128)(2,1)} %bitcast.29), channel_id=1, source_target_pairs={{0,0},{64,4},{4,64},{68,68},{1,1},{65,5},{5,65},{69,69},{2,2},{66,... | collective-permute-start | bytes 614408 | tf_op jit(solution)/shard_map/ppermute | solution.py:36
  6.8 1.9 collective-permute-start
  9.4 1.8 fusion.1
  11.3 0.3 pad_maximum_fusion.refs_2_.refs_0_
  11.5 0.0 collective-permute-done.1.refs_1_.refs_0_
  11.5 4.5 %collective-permute-done.refs_0_ = bf16[20,5120]{1,0:T(8,128)(2,1)S(1)} collective-permute-done((bf16[20,5120]{1,0:T(8,128)(2,1)}, bf16[20,5120]{1,0:T(8,128)(2,1)S(1)}, u32[]{:S(2)}, u32[]{:S(2)}) %collective-permute-start) | collective-permute-done | bytes 204832 | tf_op jit(solution)/shard_map/ppermute | solution.py:36
  16.1 2.6 %collective-permute-start.22 = (bf16[336,5120]{1,0:T(8,128)(2,1)S(1)}, bf16[336,5120]{1,0:T(8,128)(2,1)S(1)}, u32[]{:S(2)}, u32[]{:S(2)}) collective-permute-start(bf16[336,5120]{1,0:T(8,128)(2,1)S(1)} %held.20), channel_id=1, source_target_pairs={{0,0},{64,4},{4,64},{68,68},{1,1},{65,5},{5,65},{69,69},{2,2},{66,... | collective-permute-start | bytes 10321928 | tf_op jit(solution)/shard_map/ppermute | solution.py:36
  18.7 5.7 %collective-permute-start.5 = (bf16[20,5120]{1,0:T(8,128)(2,1)S(1)}, bf16[20,5120]{1,0:T(8,128)(2,1)S(1)}, u32[]{:S(2)}, u32[]{:S(2)}) collective-permute-start(bf16[20,5120]{1,0:T(8,128)(2,1)S(1)} %collective-permute-done.1.refs_1_.refs_0_), channel_id=1, source_target_pairs={{8,0},{16,8},{24,16},{32,24},{40,32},{48,40},{56,48},{0,56},{9,1},... | collective-permute-start | bytes 614408 | tf_op jit(solution)/shard_map/ppermute | solution.py:31
  24.3 2.9 %collective-permute-start.4 = (bf16[20,5120]{1,0:T(8,128)(2,1)S(1)}, bf16[20,5120]{1,0:T(8,128)(2,1)S(1)}, u32[]{:S(2)}, u32[]{:S(2)}) collective-permute-start(bf16[20,5120]{1,0:T(8,128)(2,1)S(1)} %held.12.refs_0_), channel_id=1, source_target_pairs={{2,0},{3,1},{0,2},{1,3},{6,4},{7,5},{4,6},{5,7},{10,8},{11,9},{8,1... | collective-permute-start | bytes 614408 | tf_op jit(solution)/shard_map/ppermute | solution.py:31
  27.3 0.8 collective-permute-start.2
  28.0 0.7 collective-permute-start.3
  28.8 1.8 collective-permute-done.6.refs_2_.refs_7_
  30.6 0.3 collective-permute-done.4.refs_0_
  30.9 3.3 %collective-permute-done.2.refs_1_ = bf16[20,5120]{1,0:T(8,128)(2,1)S(1)} collective-permute-done((bf16[20,5120]{1,0:T(8,128)(2,1)S(1)}, bf16[20,5120]{1,0:T(8,128)(2,1)S(1)}, u32[]{:S(2)}, u32[]{:S(2)}) %collective-permute-start.2) | collective-permute-done | bytes 204832 | tf_op jit(solution)/shard_map/ppermute | solution.py:31
  34.2 0.1 collective-permute-done.3.refs_2_
  34.3 0.3 stacked.2.refs_0_
  34.6 3.0 %collective-permute-start.7 = (bf16[80,5120]{1,0:T(8,128)(2,1)S(1)}, bf16[80,5120]{1,0:T(8,128)(2,1)S(1)}, u32[]{:S(2)}, u32[]{:S(2)}) collective-permute-start(bf16[80,5120]{1,0:T(8,128)(2,1)S(1)} %stacked.2.refs_0_), channel_id=1, source_target_pairs={{8,0},{16,8},{24,16},{32,24},{40,32},{48,40},{56,48},{0,56},{9,1},... | collective-permute-start | bytes 2457608 | tf_op jit(solution)/shard_map/ppermute | solution.py:31
  37.7 0.0 collective-permute-start.17
  37.7 2.7 %collective-permute-start.8 = (bf16[20,5120]{1,0:T(8,128)(2,1)S(1)}, bf16[20,5120]{1,0:T(8,128)(2,1)S(1)}, u32[]{:S(2)}, u32[]{:S(2)}) collective-permute-start(bf16[20,5120]{1,0:T(8,128)(2,1)S(1)} %collective-permute-done.5.refs_1_), channel_id=1, source_target_pairs={{8,0},{16,8},{24,16},{32,24},{40,32},{48,40},{56,48},{0,56},{9,1},... | collective-permute-start | bytes 614408 | tf_op jit(solution)/shard_map/ppermute | solution.py:31
  40.4 20.6 %collective-permute-done.8.refs_2_ = bf16[20,5120]{1,0:T(8,128)(2,1)S(1)} collective-permute-done((bf16[20,5120]{1,0:T(8,128)(2,1)S(1)}, bf16[20,5120]{1,0:T(8,128)(2,1)S(1)}, u32[]{:S(2)}, u32[]{:S(2)}) %collective-permute-start.8) | collective-permute-done | bytes 204832 | tf_op jit(solution)/shard_map/ppermute | solution.py:31
  60.9 0.0 collective-permute-start.10
  60.9 0.0 collective-permute-done.11.refs_6_
  60.9 3.4 %collective-permute-start.9 = (bf16[20,5120]{1,0:T(8,128)(2,1)S(1)}, bf16[20,5120]{1,0:T(8,128)(2,1)S(1)}, u32[]{:S(2)}, u32[]{:S(2)}) collective-permute-start(bf16[20,5120]{1,0:T(8,128)(2,1)S(1)} %collective-permute-done.8.refs_2_), channel_id=1, source_target_pairs={{8,0},{16,8},{24,16},{32,24},{40,32},{48,40},{56,48},{0,56},{9,1},... | collective-permute-start | bytes 614408 | tf_op jit(solution)/shard_map/ppermute | solution.py:31
  64.3 5.8 %collective-permute-done.10.refs_4_ = bf16[20,5120]{1,0:T(8,128)(2,1)S(1)} collective-permute-done((bf16[20,5120]{1,0:T(8,128)(2,1)S(1)}, bf16[20,5120]{1,0:T(8,128)(2,1)S(1)}, u32[]{:S(2)}, u32[]{:S(2)}) %collective-permute-start.10) | collective-permute-done | bytes 204832 | tf_op jit(solution)/shard_map/ppermute | solution.py:31
  70.1 0.0 collective-permute-start.12
  70.1 5.3 %collective-permute-done.9.refs_3_ = bf16[20,5120]{1,0:T(8,128)(2,1)S(1)} collective-permute-done((bf16[20,5120]{1,0:T(8,128)(2,1)S(1)}, bf16[20,5120]{1,0:T(8,128)(2,1)S(1)}, u32[]{:S(2)}, u32[]{:S(2)}) %collective-permute-start.9) | collective-permute-done | bytes 204832 | tf_op jit(solution)/shard_map/ppermute | solution.py:31
  75.4 3.9 %collective-permute-done.12.refs_5_ = bf16[20,5120]{1,0:T(8,128)(2,1)S(1)} collective-permute-done((bf16[20,5120]{1,0:T(8,128)(2,1)S(1)}, bf16[20,5120]{1,0:T(8,128)(2,1)S(1)}, u32[]{:S(2)}, u32[]{:S(2)}) %collective-permute-start.12) | collective-permute-done | bytes 204832 | tf_op jit(solution)/shard_map/ppermute | solution.py:31
  79.3 0.6 stacked.3.refs_1_.refs_0_
  79.9 0.0 collective-permute-done.7.refs_0_
  79.9 0.7 collective-permute-start.13
  80.6 0.8 collective-permute-start.18
  81.4 9.7 %collective-permute-done.13.refs_1_.refs_2_ = bf16[80,5120]{1,0:T(8,128)(2,1)S(1)} collective-permute-done((bf16[80,5120]{1,0:T(8,128)(2,1)S(1)}, bf16[80,5120]{1,0:T(8,128)(2,1)S(1)}, u32[]{:S(2)}, u32[]{:S(2)}) %collective-permute-start.13) | collective-permute-done | bytes 819232 | tf_op jit(solution)/shard_map/ppermute | solution.py:31
  91.2 1.9 collective-permute-done.18.refs_1_.refs_2_.refs_7_
  93.0 0.0 collective-permute-start.23
  93.0 2.8 %collective-permute-start.15 = (bf16[160,5120]{1,0:T(8,128)(2,1)S(1)}, bf16[160,5120]{1,0:T(8,128)(2,1)S(1)}, u32[]{:S(2)}, u32[]{:S(2)}) collective-permute-start(bf16[160,5120]{1,0:T(8,128)(2,1)S(1)} %stacked.3.refs_1_.refs_0_), channel_id=1, source_target_pairs={{1,0},{2,1},{3,2},{0,3},{5,4},{6,5},{7,6},{4,7},{9,8},{10,9},{11,1... | collective-permute-start | bytes 4915208 | tf_op jit(solution)/shard_map/ppermute | solution.py:31
  95.8 0.3 collective-permute-start.14
  96.1 1.2 collective-permute-start.19
  97.3 33.3 %collective-permute-done.15.refs_0_ = bf16[160,5120]{1,0:T(8,128)(2,1)S(1)} collective-permute-done((bf16[160,5120]{1,0:T(8,128)(2,1)S(1)}, bf16[160,5120]{1,0:T(8,128)(2,1)S(1)}, u32[]{:S(2)}, u32[]{:S(2)}) %collective-permute-start.15) | collective-permute-done | bytes 1638432 | tf_op jit(solution)/shard_map/ppermute | solution.py:31
  130.6 0.1 slice.26
  130.6 0.0 copy-start.1
  130.7 3.5 %collective-permute-start.24 = (bf16[80,5120]{1,0:T(8,128)(2,1)S(1)}, bf16[80,5120]{1,0:T(8,128)(2,1)S(1)}, u32[]{:S(2)}, u32[]{:S(2)}) collective-permute-start(bf16[80,5120]{1,0:T(8,128)(2,1)S(1)} %slice.26), channel_id=1, source_target_pairs={{1,0},{2,1},{3,2},{0,3},{5,4},{6,5},{7,6},{4,7},{9,8},{10,9},{11,1... | collective-permute-start | bytes 2457608 | tf_op jit(solution)/shard_map/ppermute | solution.py:31
  134.2 0.1 slice.27
  134.2 0.1 collective-permute-start.25
  135.0 1.7 concatenate.7.refs_0_
  136.7 0.3 collective-permute-start.16
  137.1 13.3 %collective-permute-done.24.refs_3_ = bf16[80,5120]{1,0:T(8,128)(2,1)S(1)} collective-permute-done((bf16[80,5120]{1,0:T(8,128)(2,1)S(1)}, bf16[80,5120]{1,0:T(8,128)(2,1)S(1)}, u32[]{:S(2)}, u32[]{:S(2)}) %collective-permute-start.24) | collective-permute-done | bytes 819232 | tf_op jit(solution)/shard_map/ppermute | solution.py:31
  150.4 3.3 %collective-permute-done.25.refs_4_ = bf16[80,5120]{1,0:T(8,128)(2,1)S(1)} collective-permute-done((bf16[80,5120]{1,0:T(8,128)(2,1)S(1)}, bf16[80,5120]{1,0:T(8,128)(2,1)S(1)}, u32[]{:S(2)}, u32[]{:S(2)}) %collective-permute-start.25) | collective-permute-done | bytes 819232 | tf_op jit(solution)/shard_map/ppermute | solution.py:31
  153.7 5.6 %hidden.1.refs_13_ = f32[640,256]{1,0:T(8,128)S(1)} custom-call(bf16[160,5120]{1,0:T(8,128)(2,1)S(1)} %stacked.3.refs_1_.refs_0_, bf16[160,5120]{1,0:T(8,128)(2,1)S(1)} %held.15.refs_1_, bf16[160,5120]{1,0:T(8,128)(2,1)S(1)} %held.18.refs_1_.refs_2_, bf16[80,5120]{1,0:T(8,128)(2,1)S(1)} %collective-permute-done.24.refs_3_, ...), custom_call_target="tpu_custom_call" | custom-call | flops 1677721600 | bytes 10747904 | tf_op jit(solution)/shard_map/hidden/pallas_call | solution.py:131
  159.4 8.9 %gate_grads.1 = (f32[112,5120]{1,0:T(8,128)S(1)}, f32[112,5120]{1,0:T(8,128)S(1)}) custom-call(bf16[80,5120]{1,0:T(8,128)(2,1)S(1)} %stacked.2.refs_0_, bf16[80,5120]{1,0:T(8,128)(2,1)S(1)} %held.14.refs_1_, bf16[80,5120]{1,0:T(8,128)(2,1)S(1)} %collective-permute-done.13.refs_1_.refs_2_, bf16[80,5120]{1,0:T(8,128)(2,1)S(1)} %held.16.refs_3_, ...), custom_call_target="tpu_custom_call" | custom-call | flops 5033164800 | bytes 14942208 | tf_op jit(solution)/shard_map/gate_grads/pallas_call | solution.py:193
  168.2 2.6 collective-permute-start.26
  170.8 0.1 collective-permute-start.32
  170.9 19.3 %collective-permute-done.30.refs_0_ = f32[120,5120]{1,0:T(8,128)S(1)} collective-permute-done((f32[120,5120]{1,0:T(8,128)}, f32[120,5120]{1,0:T(8,128)S(1)}, u32[]{:S(2)}, u32[]{:S(2)}) %collective-permute-start.30) | collective-permute-done | bytes 2457632 | tf_op jit(solution)/shard_map/ppermute | solution.py:31
  190.2 2.5 collective-permute-start.31
  192.7 2.5 multiply_reduce_fusion
  195.2 8.6 %collective-permute-start.29 = (f32[112,5120]{1,0:T(8,128)}, f32[112,5120]{1,0:T(8,128)}, u32[]{:S(2)}, u32[]{:S(2)}) collective-permute-start(f32[112,5120]{1,0:T(8,128)} %get-tuple-element.9), channel_id=1, source_target_pairs={{0,0},{64,4},{4,64},{68,68},{1,1},{65,5},{5,65},{69,69},{2,2},{66,... | collective-permute-start | bytes 6881288 | tf_op jit(solution)/shard_map/ppermute | solution.py:36
  204.5 11.3 %psum.14 = f32[]{:T(128)} all-reduce(f32[]{:T(128)} %get-tuple-element.8), channel_id=1, replica_groups=mesh['x_lo'=2,'core'=2,'z'=8,'x_hi'=2,'y'=4] {'z'}, use_global_device_ids=true, to_apply=%region_1.2 | all-reduce | flops 1 | bytes 8 | tf_op jit(solution)/shard_map/psum | solution.py:274
  215.8 9.3 %psum.15 = f32[]{:T(128)} all-reduce(f32[]{:T(128)} %psum.14), channel_id=1, replica_groups=mesh['x_lo'=2,'core'=2,'z'=8,'x_hi'=2,'y'=4] {'y'}, use_global_device_ids=true, to_apply=%region_2.3 | all-reduce | flops 1 | bytes 8 | tf_op jit(solution)/shard_map/psum | solution.py:274
  225.1 7.6 %collective-permute-start.27 = (f32[]{:T(128)}, f32[]{:T(128)}, u32[]{:S(2)}, u32[]{:S(2)}) collective-permute-start(f32[]{:T(128)} %psum.15), channel_id=1, source_target_pairs={{0,0},{64,4},{4,64},{68,68},{1,1},{65,5},{5,65},{69,69},{2,2},{66,... | collective-permute-start | bytes 20 | tf_op jit(solution)/shard_map/ppermute | solution.py:36
  232.8 10.3 %collective-permute-start.28 = (f32[]{:T(128)}, f32[]{:T(128)}, u32[]{:S(2)}, u32[]{:S(2)}) collective-permute-start(f32[]{:T(128)} %psum.15), channel_id=1, source_target_pairs={{64,0},{0,4},{68,64},{4,68},{65,1},{1,5},{69,65},{5,69},{66,2},{2,... | collective-permute-start | bytes 20 | tf_op jit(solution)/shard_map/ppermute | solution.py:221
  243.1 2.6 %collective-permute-done.28 = f32[]{:T(128)} collective-permute-done((f32[]{:T(128)}, f32[]{:T(128)}, u32[]{:S(2)}, u32[]{:S(2)}) %collective-permute-start.28) | collective-permute-done | bytes 36 | tf_op jit(solution)/shard_map/ppermute | solution.py:221
  247.1 0.0 copy-start
  247.1 2.2 select_select_fusion
  249.3 0.5 slice.29
  250.5 4.2 %fusion.3 = (f32[1,112,5120]{2,1,0:T(8,128)}, f32[1,112,5120]{2,1,0:T(8,128)}) fusion(f32[112,5120]{1,0:T(8,128)} %collective-permute-done.29, f32[]{:T(128)S(6)} %mul.22, f32[1,112,5120]{2,1,0:T(8,128)S(1)} %copy-done, f32[120,5120]{1,0:T(8,128)S(1)} %select_select_fusion), kind=kLoop, calls=%fused_computation.9 | loop fusion | flops 2293760 | bytes 11468804 | tf_op jit(solution)/shard_map/broadcast_in_dim | solution.py:282
  (39 shorter events, 0.1 us)
Async XLA Ops:
  0.6 10.6 %copy-start.3 = (bf16[112,5120]{1,0:T(8,128)(2,1)S(1)}, bf16[112,5120]{1,0:T(8,128)(2,1)}, u32[]{:S(2)}) copy-start(bf16[112,5120]{1,0:T(8,128)(2,1)} %param.15) | copy-start | bytes 3440644
  0.6 10.6 %copy-start.2 = (bf16[112,5120]{1,0:T(8,128)(2,1)S(1)}, bf16[112,5120]{1,0:T(8,128)(2,1)}, u32[]{:S(2)}) copy-start(bf16[112,5120]{1,0:T(8,128)(2,1)} %param.16) | copy-start | bytes 3440644
  0.7 10.9 %collective-permute-start.1 = (bf16[20,5120]{1,0:T(8,128)(2,1)}, bf16[20,5120]{1,0:T(8,128)(2,1)S(1)}, u32[]{:S(2)}, u32[]{:S(2)}) collective-permute-start(bf16[20,5120]{1,0:T(8,128)(2,1)} %bitcast.29), channel_id=1, source_target_pairs={{0,0},{64,4},{4,64},{68,68},{1,1},{65,5},{5,65},{69,69},{2,2},{66,... | collective-permute-start | bytes 614408 | tf_op jit(solution)/shard_map/ppermute | solution.py:36
  6.8 9.2 %collective-permute-start = (bf16[20,5120]{1,0:T(8,128)(2,1)}, bf16[20,5120]{1,0:T(8,128)(2,1)S(1)}, u32[]{:S(2)}, u32[]{:S(2)}) collective-permute-start(bf16[20,5120]{1,0:T(8,128)(2,1)} %bitcast.30), channel_id=1, source_target_pairs={{0,0},{64,4},{4,64},{68,68},{1,1},{65,5},{5,65},{69,69},{2,2},{66,... | collective-permute-start | bytes 614408 | tf_op jit(solution)/shard_map/ppermute | solution.py:36
  16.1 77.0 %collective-permute-start.22 = (bf16[336,5120]{1,0:T(8,128)(2,1)S(1)}, bf16[336,5120]{1,0:T(8,128)(2,1)S(1)}, u32[]{:S(2)}, u32[]{:S(2)}) collective-permute-start(bf16[336,5120]{1,0:T(8,128)(2,1)S(1)} %held.20), channel_id=1, source_target_pairs={{0,0},{64,4},{4,64},{68,68},{1,1},{65,5},{5,65},{69,69},{2,2},{66,... | collective-permute-start | bytes 10321928 | tf_op jit(solution)/shard_map/ppermute | solution.py:36
  18.7 9.3 %collective-permute-start.5 = (bf16[20,5120]{1,0:T(8,128)(2,1)S(1)}, bf16[20,5120]{1,0:T(8,128)(2,1)S(1)}, u32[]{:S(2)}, u32[]{:S(2)}) collective-permute-start(bf16[20,5120]{1,0:T(8,128)(2,1)S(1)} %collective-permute-done.1.refs_1_.refs_0_), channel_id=1, source_target_pairs={{8,0},{16,8},{24,16},{32,24},{40,32},{48,40},{56,48},{0,56},{9,1},... | collective-permute-start | bytes 614408 | tf_op jit(solution)/shard_map/ppermute | solution.py:31
  24.3 6.3 %collective-permute-start.6 = (bf16[20,5120]{1,0:T(8,128)(2,1)S(1)}, bf16[20,5120]{1,0:T(8,128)(2,1)S(1)}, u32[]{:S(2)}, u32[]{:S(2)}) collective-permute-start(bf16[20,5120]{1,0:T(8,128)(2,1)S(1)} %collective-permute-done.1.refs_1_.refs_0_), channel_id=1, source_target_pairs={{56,0},{0,8},{8,16},{16,24},{24,32},{32,40},{40,48},{48,56},{57,1}... | collective-permute-start | bytes 614408 | tf_op jit(solution)/shard_map/ppermute | solution.py:31
  24.3 6.6 %collective-permute-start.4 = (bf16[20,5120]{1,0:T(8,128)(2,1)S(1)}, bf16[20,5120]{1,0:T(8,128)(2,1)S(1)}, u32[]{:S(2)}, u32[]{:S(2)}) collective-permute-start(bf16[20,5120]{1,0:T(8,128)(2,1)S(1)} %held.12.refs_0_), channel_id=1, source_target_pairs={{2,0},{3,1},{0,2},{1,3},{6,4},{7,5},{4,6},{5,7},{10,8},{11,9},{8,1... | collective-permute-start | bytes 614408 | tf_op jit(solution)/shard_map/ppermute | solution.py:31
  27.3 6.9 %collective-permute-start.2 = (bf16[20,5120]{1,0:T(8,128)(2,1)S(1)}, bf16[20,5120]{1,0:T(8,128)(2,1)S(1)}, u32[]{:S(2)}, u32[]{:S(2)}) collective-permute-start(bf16[20,5120]{1,0:T(8,128)(2,1)S(1)} %held.12.refs_0_), channel_id=1, source_target_pairs={{1,0},{2,1},{3,2},{0,3},{5,4},{6,5},{7,6},{4,7},{9,8},{10,9},{11,1... | collective-permute-start | bytes 614408 | tf_op jit(solution)/shard_map/ppermute | solution.py:31
  28.0 6.3 %collective-permute-start.3 = (bf16[20,5120]{1,0:T(8,128)(2,1)S(1)}, bf16[20,5120]{1,0:T(8,128)(2,1)S(1)}, u32[]{:S(2)}, u32[]{:S(2)}) collective-permute-start(bf16[20,5120]{1,0:T(8,128)(2,1)S(1)} %held.12.refs_0_), channel_id=1, source_target_pairs={{3,0},{0,1},{1,2},{2,3},{7,4},{4,5},{5,6},{6,7},{11,8},{8,9},{9,10... | collective-permute-start | bytes 614408 | tf_op jit(solution)/shard_map/ppermute | solution.py:31
  34.6 45.2 %collective-permute-start.7 = (bf16[80,5120]{1,0:T(8,128)(2,1)S(1)}, bf16[80,5120]{1,0:T(8,128)(2,1)S(1)}, u32[]{:S(2)}, u32[]{:S(2)}) collective-permute-start(bf16[80,5120]{1,0:T(8,128)(2,1)S(1)} %stacked.2.refs_0_), channel_id=1, source_target_pairs={{8,0},{16,8},{24,16},{32,24},{40,32},{48,40},{56,48},{0,56},{9,1},... | collective-permute-start | bytes 2457608 | tf_op jit(solution)/shard_map/ppermute | solution.py:31
  37.7 42.9 %collective-permute-start.17 = (bf16[80,5120]{1,0:T(8,128)(2,1)S(1)}, bf16[80,5120]{1,0:T(8,128)(2,1)S(1)}, u32[]{:S(2)}, u32[]{:S(2)}) collective-permute-start(bf16[80,5120]{1,0:T(8,128)(2,1)S(1)} %stacked.2.refs_0_), channel_id=1, source_target_pairs={{56,0},{0,8},{8,16},{16,24},{24,32},{32,40},{40,48},{48,56},{57,1}... | collective-permute-start | bytes 2457608 | tf_op jit(solution)/shard_map/ppermute | solution.py:31
  37.7 23.2 %collective-permute-start.8 = (bf16[20,5120]{1,0:T(8,128)(2,1)S(1)}, bf16[20,5120]{1,0:T(8,128)(2,1)S(1)}, u32[]{:S(2)}, u32[]{:S(2)}) collective-permute-start(bf16[20,5120]{1,0:T(8,128)(2,1)S(1)} %collective-permute-done.5.refs_1_), channel_id=1, source_target_pairs={{8,0},{16,8},{24,16},{32,24},{40,32},{48,40},{56,48},{0,56},{9,1},... | collective-permute-start | bytes 614408 | tf_op jit(solution)/shard_map/ppermute | solution.py:31
  40.4 20.6 %collective-permute-start.11 = (bf16[20,5120]{1,0:T(8,128)(2,1)S(1)}, bf16[20,5120]{1,0:T(8,128)(2,1)S(1)}, u32[]{:S(2)}, u32[]{:S(2)}) collective-permute-start(bf16[20,5120]{1,0:T(8,128)(2,1)S(1)} %collective-permute-done.6.refs_2_.refs_7_), channel_id=1, source_target_pairs={{56,0},{0,8},{8,16},{16,24},{24,32},{32,40},{40,48},{48,56},{57,1}... | collective-permute-start | bytes 614408 | tf_op jit(solution)/shard_map/ppermute | solution.py:31
  60.9 9.2 %collective-permute-start.10 = (bf16[20,5120]{1,0:T(8,128)(2,1)S(1)}, bf16[20,5120]{1,0:T(8,128)(2,1)S(1)}, u32[]{:S(2)}, u32[]{:S(2)}) collective-permute-start(bf16[20,5120]{1,0:T(8,128)(2,1)S(1)} %collective-permute-done.8.refs_2_), channel_id=1, source_target_pairs={{16,0},{24,8},{32,16},{40,24},{48,32},{56,40},{0,48},{8,56},{17,1}... | collective-permute-start | bytes 614408 | tf_op jit(solution)/shard_map/ppermute | solution.py:31
  60.9 14.5 %collective-permute-start.9 = (bf16[20,5120]{1,0:T(8,128)(2,1)S(1)}, bf16[20,5120]{1,0:T(8,128)(2,1)S(1)}, u32[]{:S(2)}, u32[]{:S(2)}) collective-permute-start(bf16[20,5120]{1,0:T(8,128)(2,1)S(1)} %collective-permute-done.8.refs_2_), channel_id=1, source_target_pairs={{8,0},{16,8},{24,16},{32,24},{40,32},{48,40},{56,48},{0,56},{9,1},... | collective-permute-start | bytes 614408 | tf_op jit(solution)/shard_map/ppermute | solution.py:31
  70.1 9.2 %collective-permute-start.12 = (bf16[20,5120]{1,0:T(8,128)(2,1)S(1)}, bf16[20,5120]{1,0:T(8,128)(2,1)S(1)}, u32[]{:S(2)}, u32[]{:S(2)}) collective-permute-start(bf16[20,5120]{1,0:T(8,128)(2,1)S(1)} %collective-permute-done.11.refs_6_), channel_id=1, source_target_pairs={{56,0},{0,8},{8,16},{16,24},{24,32},{32,40},{40,48},{48,56},{57,1}... | collective-permute-start | bytes 614408 | tf_op jit(solution)/shard_map/ppermute | solution.py:31
  79.9 11.3 %collective-permute-start.13 = (bf16[80,5120]{1,0:T(8,128)(2,1)S(1)}, bf16[80,5120]{1,0:T(8,128)(2,1)S(1)}, u32[]{:S(2)}, u32[]{:S(2)}) collective-permute-start(bf16[80,5120]{1,0:T(8,128)(2,1)S(1)} %held.14.refs_1_), channel_id=1, source_target_pairs={{8,0},{16,8},{24,16},{32,24},{40,32},{48,40},{56,48},{0,56},{9,1},... | collective-permute-start | bytes 2457608 | tf_op jit(solution)/shard_map/ppermute | solution.py:31
  80.6 12.4 %collective-permute-start.18 = (bf16[80,5120]{1,0:T(8,128)(2,1)S(1)}, bf16[80,5120]{1,0:T(8,128)(2,1)S(1)}, u32[]{:S(2)}, u32[]{:S(2)}) collective-permute-start(bf16[80,5120]{1,0:T(8,128)(2,1)S(1)} %held.17.refs_8_), channel_id=1, source_target_pairs={{56,0},{0,8},{8,16},{16,24},{24,32},{32,40},{40,48},{48,56},{57,1}... | collective-permute-start | bytes 2457608 | tf_op jit(solution)/shard_map/ppermute | solution.py:31
  93.0 60.7 %collective-permute-start.23 = (bf16[336,5120]{1,0:T(8,128)(2,1)S(1)}, bf16[336,5120]{1,0:T(8,128)(2,1)S(1)}, u32[]{:S(2)}, u32[]{:S(2)}) collective-permute-start(bf16[336,5120]{1,0:T(8,128)(2,1)S(1)} %held.21.refs_5_.refs_9_.refs_11_), channel_id=1, source_target_pairs={{64,0},{0,64},{65,1},{1,65},{66,2},{2,66},{67,3},{3,67},{68,4},{4,... | collective-permute-start | bytes 10321928 | tf_op jit(solution)/shard_map/ppermute | solution.py:31
  93.0 37.6 %collective-permute-start.15 = (bf16[160,5120]{1,0:T(8,128)(2,1)S(1)}, bf16[160,5120]{1,0:T(8,128)(2,1)S(1)}, u32[]{:S(2)}, u32[]{:S(2)}) collective-permute-start(bf16[160,5120]{1,0:T(8,128)(2,1)S(1)} %stacked.3.refs_1_.refs_0_), channel_id=1, source_target_pairs={{1,0},{2,1},{3,2},{0,3},{5,4},{6,5},{7,6},{4,7},{9,8},{10,9},{11,1... | collective-permute-start | bytes 4915208 | tf_op jit(solution)/shard_map/ppermute | solution.py:31
  95.8 38.3 %collective-permute-start.20 = (bf16[160,5120]{1,0:T(8,128)(2,1)S(1)}, bf16[160,5120]{1,0:T(8,128)(2,1)S(1)}, u32[]{:S(2)}, u32[]{:S(2)}) collective-permute-start(bf16[160,5120]{1,0:T(8,128)(2,1)S(1)} %stacked.3.refs_1_.refs_0_), channel_id=1, source_target_pairs={{3,0},{0,1},{1,2},{2,3},{7,4},{4,5},{5,6},{6,7},{11,8},{8,9},{9,10... | collective-permute-start | bytes 4915208 | tf_op jit(solution)/shard_map/ppermute | solution.py:31
  95.8 40.8 %collective-permute-start.14 = (bf16[80,5120]{1,0:T(8,128)(2,1)S(1)}, bf16[80,5120]{1,0:T(8,128)(2,1)S(1)}, u32[]{:S(2)}, u32[]{:S(2)}) collective-permute-start(bf16[80,5120]{1,0:T(8,128)(2,1)S(1)} %collective-permute-done.13.refs_1_.refs_2_), channel_id=1, source_target_pairs={{8,0},{16,8},{24,16},{32,24},{40,32},{48,40},{56,48},{0,56},{9,1},... | collective-permute-start | bytes 2457608 | tf_op jit(solution)/shard_map/ppermute | solution.py:31
  96.1 40.6 %collective-permute-start.19 = (bf16[80,5120]{1,0:T(8,128)(2,1)S(1)}, bf16[80,5120]{1,0:T(8,128)(2,1)S(1)}, u32[]{:S(2)}, u32[]{:S(2)}) collective-permute-start(bf16[80,5120]{1,0:T(8,128)(2,1)S(1)} %collective-permute-done.18.refs_1_.refs_2_.refs_7_), channel_id=1, source_target_pairs={{56,0},{0,8},{8,16},{16,24},{24,32},{32,40},{40,48},{48,56},{57,1}... | collective-permute-start | bytes 2457608 | tf_op jit(solution)/shard_map/ppermute | solution.py:31
  130.6 4.3 %copy-start.1 = (f32[1,112,5120]{2,1,0:T(8,128)S(1)}, f32[1,112,5120]{2,1,0:T(8,128)}, u32[]{:S(2)}) copy-start(f32[1,112,5120]{2,1,0:T(8,128)} %param.13) | copy-start | bytes 6881284
  130.7 19.8 %collective-permute-start.24 = (bf16[80,5120]{1,0:T(8,128)(2,1)S(1)}, bf16[80,5120]{1,0:T(8,128)(2,1)S(1)}, u32[]{:S(2)}, u32[]{:S(2)}) collective-permute-start(bf16[80,5120]{1,0:T(8,128)(2,1)S(1)} %slice.26), channel_id=1, source_target_pairs={{1,0},{2,1},{3,2},{0,3},{5,4},{6,5},{7,6},{4,7},{9,8},{10,9},{11,1... | collective-permute-start | bytes 2457608 | tf_op jit(solution)/shard_map/ppermute | solution.py:31
  134.2 19.5 %collective-permute-start.25 = (bf16[80,5120]{1,0:T(8,128)(2,1)S(1)}, bf16[80,5120]{1,0:T(8,128)(2,1)S(1)}, u32[]{:S(2)}, u32[]{:S(2)}) collective-permute-start(bf16[80,5120]{1,0:T(8,128)(2,1)S(1)} %slice.27), channel_id=1, source_target_pairs={{3,0},{0,1},{1,2},{2,3},{7,4},{4,5},{5,6},{6,7},{11,8},{8,9},{9,10... | collective-permute-start | bytes 2457608 | tf_op jit(solution)/shard_map/ppermute | solution.py:31
  136.7 53.5 %collective-permute-start.30 = (f32[120,5120]{1,0:T(8,128)}, f32[120,5120]{1,0:T(8,128)S(1)}, u32[]{:S(2)}, u32[]{:S(2)}) collective-permute-start(f32[120,5120]{1,0:T(8,128)} %held.22), channel_id=1, source_target_pairs={{128,0},{0,128},{129,1},{1,129},{130,2},{2,130},{131,3},{3,131},{1... | collective-permute-start | bytes 7372808 | tf_op jit(solution)/shard_map/ppermute | solution.py:31
  136.7 22.6 %collective-permute-start.16 = (bf16[48,5120]{1,0:T(8,128)(2,1)S(1)}, bf16[48,5120]{1,0:T(8,128)(2,1)S(1)}, u32[]{:S(2)}, u32[]{:S(2)}) collective-permute-start(bf16[48,5120]{1,0:T(8,128)(2,1)S(1)} %slice.24), channel_id=1, source_target_pairs={{8,0},{16,8},{24,16},{32,24},{40,32},{48,40},{56,48},{0,56},{9,1},... | collective-permute-start | bytes 1474568 | tf_op jit(solution)/shard_map/ppermute | solution.py:31
  150.4 8.9 %collective-permute-start.21 = (bf16[32,5120]{1,0:T(8,128)(2,1)S(1)}, bf16[32,5120]{1,0:T(8,128)(2,1)S(1)}, u32[]{:S(2)}, u32[]{:S(2)}) collective-permute-start(bf16[32,5120]{1,0:T(8,128)(2,1)S(1)} %slice.25), channel_id=1, source_target_pairs={{56,0},{0,8},{8,16},{16,24},{24,32},{32,40},{40,48},{48,56},{57,1}... | collective-permute-start | bytes 983048 | tf_op jit(solution)/shard_map/ppermute | solution.py:31
  168.2 24.4 %collective-permute-start.26 = (f32[112,5120]{1,0:T(8,128)S(1)}, f32[112,5120]{1,0:T(8,128)S(1)}, u32[]{:S(2)}, u32[]{:S(2)}) collective-permute-start(f32[112,5120]{1,0:T(8,128)S(1)} %get-tuple-element.7), channel_id=1, source_target_pairs={{64,0},{0,64},{65,1},{1,65},{66,2},{2,66},{67,3},{3,67},{68,4},{4,... | collective-permute-start | bytes 6881288 | tf_op jit(solution)/shard_map/ppermute | solution.py:31
  170.8 76.3 %collective-permute-start.32 = (f32[120,5120]{1,0:T(8,128)}, f32[120,5120]{1,0:T(8,128)}, u32[]{:S(2)}, u32[]{:S(2)}) collective-permute-start(f32[120,5120]{1,0:T(8,128)} %held.22), channel_id=1, source_target_pairs={{64,0},{0,64},{65,1},{1,65},{66,2},{2,66},{67,3},{3,67},{68,4},{4,... | collective-permute-start | bytes 7372808 | tf_op jit(solution)/shard_map/ppermute | solution.py:31
  190.2 56.9 %collective-permute-start.31 = (f32[120,5120]{1,0:T(8,128)S(1)}, f32[120,5120]{1,0:T(8,128)}, u32[]{:S(2)}, u32[]{:S(2)}) collective-permute-start(f32[120,5120]{1,0:T(8,128)S(1)} %held.23), channel_id=1, source_target_pairs={{64,0},{0,64},{65,1},{1,65},{66,2},{2,66},{67,3},{3,67},{68,4},{4,... | collective-permute-start | bytes 7372808 | tf_op jit(solution)/shard_map/ppermute | solution.py:31
  195.2 55.3 %collective-permute-start.29 = (f32[112,5120]{1,0:T(8,128)}, f32[112,5120]{1,0:T(8,128)}, u32[]{:S(2)}, u32[]{:S(2)}) collective-permute-start(f32[112,5120]{1,0:T(8,128)} %get-tuple-element.9), channel_id=1, source_target_pairs={{0,0},{64,4},{4,64},{68,68},{1,1},{65,5},{5,65},{69,69},{2,2},{66,... | collective-permute-start | bytes 6881288 | tf_op jit(solution)/shard_map/ppermute | solution.py:36
  225.1 18.0 %collective-permute-start.27 = (f32[]{:T(128)}, f32[]{:T(128)}, u32[]{:S(2)}, u32[]{:S(2)}) collective-permute-start(f32[]{:T(128)} %psum.15), channel_id=1, source_target_pairs={{0,0},{64,4},{4,64},{68,68},{1,1},{65,5},{5,65},{69,69},{2,2},{66,... | collective-permute-start | bytes 20 | tf_op jit(solution)/shard_map/ppermute | solution.py:36
  232.8 13.0 %collective-permute-start.28 = (f32[]{:T(128)}, f32[]{:T(128)}, u32[]{:S(2)}, u32[]{:S(2)}) collective-permute-start(f32[]{:T(128)} %psum.15), channel_id=1, source_target_pairs={{64,0},{0,4},{68,64},{4,68},{65,1},{1,5},{69,65},{5,69},{66,2},{2,... | collective-permute-start | bytes 20 | tf_op jit(solution)/shard_map/ppermute | solution.py:221
  247.1 3.4 %copy-start = (f32[1,112,5120]{2,1,0:T(8,128)S(1)}, f32[1,112,5120]{2,1,0:T(8,128)}, u32[]{:S(2)}) copy-start(f32[1,112,5120]{2,1,0:T(8,128)} %param.11) | copy-start | bytes 6881284

commit v5 on v4

--- a/solution.py
+++ b/solution.py
@@ -22,6 +22,7 @@
 
 ROWS = 112
 HALF = 128
+CUT = 64
 BLOCK = 1024
 
 
@@ -37,15 +38,18 @@
 
 
 def held(value, *ready):
-    return pl.pallas_call(
+    values = value if isinstance(value, tuple) else (value,)
+    anywhere = pl.BlockSpec(memory_space=pl.ANY)
+    out = pl.pallas_call(
         lambda *refs: None,
-        in_specs=[pl.BlockSpec(memory_space=pl.ANY)] * (1 + len(ready)),
-        out_specs=pl.BlockSpec(memory_space=pl.ANY),
-        out_shape=jax.ShapeDtypeStruct(value.shape, value.dtype),
-        input_output_aliases={0: 0},
+        in_specs=[anywhere] * (len(values) + len(ready)),
+        out_specs=[anywhere] * len(values),
+        out_shape=[jax.ShapeDtypeStruct(one.shape, one.dtype) for one in values],
+        input_output_aliases={at: at for at in range(len(values))},
         compiler_params=params_of(1),
         name="held",
-    )(value, *ready)
+    )(*values, *ready)
+    return tuple(out) if isinstance(value, tuple) else out[0]
 
 
 def silu_slope(preact):
@@ -214,6 +218,34 @@
     )(*parts, mine, theirs, mine, theirs, hidden)
 
 
+def updated_kernel(factor, which, numerator, grad, *refs):
+    *parts, kept_ref, new_ref = refs
+    kept = 0.5 * (numerator[...] - factor[0] * grad[...])
+    kept_ref[...] = kept
+    for at in range(3):
+
+        @pl.when(which[0] == at)
+        def _():
+            new_ref[:CUT, :] = kept[:CUT] + parts[2 * at][...]
+            new_ref[CUT:, :] = kept[CUT:] + parts[2 * at + 1][: ROWS - CUT, :]
+
+
+def updated(numerator, grad, factor, which, received):
+    own = pl.BlockSpec((ROWS, BLOCK), lambda at: (0, at))
+    scalar = pl.BlockSpec(memory_space=pltpu.SMEM)
+    more = [part for parts in received for part in parts]
+    return pl.pallas_call(
+        updated_kernel,
+        grid=(D // BLOCK,),
+        in_specs=[scalar, scalar, own, own]
+        + [pl.BlockSpec((part.shape[0], BLOCK), lambda at: (0, at)) for part in more],
+        out_specs=[own, own],
+        out_shape=[jax.ShapeDtypeStruct((ROWS, D), jnp.float32)] * 2,
+        compiler_params=params_of(16),
+        name="updated",
+    )(jnp.reshape(factor, (1,)), jnp.reshape(which, (1,)), numerator, grad, *more)
+
+
 def crossed(value):
     pairs = [
         (2 * (1 - x_hi) + core, 2 * core + x_hi) for core in range(2) for x_hi in range(2)
@@ -235,7 +267,7 @@
     ring = {0: rows_grad, 1: shifted(rows_grad, "z", 1), 7: shifted(rows_grad, "z", 7)}
     mine = transposed(held(weights, rows_grad))
     ring[2], ring[6] = shifted(ring[1], "z", 1), shifted(ring[7], "z", 7)
-    near[3] = held(near[3], ring[1], ring[7])
+    near[3] = held(near[3], ring[2], ring[6])
     blocks = {0: stacked(near)}
     for steps in (1, 7):
         blocks[steps] = shifted(blocks[0], "z", steps)
@@ -244,41 +276,45 @@
     column = stacked([ring[steps] for steps in range(8)])
 
     following, before = shifted(column, "y", 1), shifted(column, "y", 3)
-    blocks[1], blocks[7] = held(blocks[1], column), held(blocks[7], column)
+    blocks[1], blocks[7] = held((blocks[1], blocks[7]), column)
     blocks[2], blocks[6] = shifted(blocks[1], "z", 1), shifted(blocks[7], "z", 7)
-    mine = held(mine, blocks[2], blocks[6])
+    blocks[2], blocks[6] = held((blocks[2], blocks[6]))
+    blocks[3], blocks[5] = shifted(blocks[2], "z", 1), shifted(blocks[6], "z", 7)
+    following, before = held((following, before), blocks[2], blocks[6])
+    weight_rows = jnp.broadcast_to(stale_weight, (8, D))
+    stale = [stale_num[0, :CUT], jnp.concatenate([stale_num[0, CUT:], weight_rows], axis=0)]
+    stale[0] = held(stale[0], mine)
+    two_before = [shifted(stale[0], "x_lo", 1)]
+    stale[1] = held(stale[1], two_before[0])
+    two_before.append(shifted(stale[1], "x_lo", 1))
+    mine = held(mine, following, before)
     theirs = shifted(mine, "core", 1)
-    stale = jnp.concatenate([stale_num[0], jnp.broadcast_to(stale_weight, (8, D))], axis=0)
-    stale = held(stale, blocks[1])
-    two_before = shifted(stale, "x_lo", 1)
-    blocks[3], blocks[5] = shifted(blocks[2], "z", 1), shifted(blocks[6], "z", 7)
-    following, before = held(following, blocks[2]), held(before, blocks[6])
     half = column.shape[0] // 2
     far = [shifted(following[:half], "y", 1), shifted(before[half:], "y", 3)]
-    blocks[3], blocks[5] = held(blocks[3], following), held(blocks[5], before)
+    blocks[3], blocks[5] = held((blocks[3], blocks[5]), following, before)
     cut = 48
     last = [shifted(blocks[3][:cut], "z", 1), shifted(blocks[5][cut:], "z", 7)]
 
     hidden = hidden_of([column, following, before, *far], mine, theirs)
     parts = [blocks[steps] for steps in (0, 1, 2, 3)] + last + [blocks[steps] for steps in (5, 6, 7)]
+    first_hop = shifted(two_before[0], "core", 1)
+    stale_hop = [shifted(part, "core", 1) for part in stale]
+    hidden = held(hidden, first_hop, *stale_hop)
     own_grad, other_grad = gate_grads(parts, mine, theirs, hidden)
-    two_before = held(two_before, own_grad)
-    first = lax.axis_index("core") == 0
-    one_before = jnp.where(first, shifted(two_before, "core", 1), shifted(stale, "core", 1))
-    received = jnp.where(step[0] % 2 == 0, one_before, two_before)
-
     gate_grad = own_grad + shifted(other_grad, "core", 1)
     norm_sq = jnp.sum(gate_grad * gate_grad)
     gate_grad = transposed(gate_grad)
-    for axes in ("z", "y"):
-        norm_sq = lax.psum(norm_sq, axes)
+    norm_sq = lax.psum(norm_sq, "z")
+    two_before[1] = held(two_before[1], jnp.reshape(norm_sq, (1,)))
+    received = [two_before, [first_hop, shifted(two_before[1], "core", 1)], stale_hop]
+    norm_sq = lax.psum(norm_sq, "y")
     norm_sq = transposed(norm_sq) + crossed(norm_sq)
 
     clip_factor = jnp.minimum(1.0, MAX_NORM / jnp.sqrt(norm_sq + eps))
-    kept_half = 0.5 * (numerator - rate * clip_factor * gate_grad)
+    which = jnp.where(step[0] % 2 == 1, 0, 1 + lax.axis_index("core"))
+    kept_half, new_num = updated(numerator, gate_grad, rate * clip_factor, which, received)
     kept_weight = 0.5 * push_weight
-    new_num = kept_half + received[:ROWS]
-    new_weight = kept_weight + received[ROWS, :1]
+    new_weight = kept_weight + jnp.stack([parts[1][-1, :1] for parts in received])[which]
     return (new_num[None], new_weight, kept_half[None], kept_weight)
 
 

time: 259 us -> 248 us (0.958)
  waiting for transfers between devices: 129 us -> 110 us
  local copies, waits for them, and re-layouts: 2.4 us -> 10.4 us
  Pallas kernels: 15.4 us -> 22.2 us
  other arithmetic: 11.1 us -> 6.51 us
    ppermute x27 -> x30, starting transfers between devices: 34.1 us -> 53.9 us  [shifted(): return lax.ppermute(value, axis, pairs)]
    ppermute x27 -> x30, waiting for transfers between devices: 122 us -> 103 us  [shifted(): return lax.ppermute(value, axis, pairs)]
    ppermute x5, starting transfers between devices: 26.9 us -> 14.7 us  [transposed(): return lax.ppermute(value, ('core', 'x_hi'), pairs)]
    ppermute x1, starting transfers between devices: 10.3 us -> 1.73 us  [crossed(): return lax.ppermute(value, ('core', 'x_hi'), pairs)]
    pallas_call x12 -> x13, Pallas kernels: 0.01 us -> 6.81 us  [the longest x1 6.18 us: updated(): pl.pallas_call(updated_kernel, grid=(D // BLOCK,), in_specs=[scalar, scal...]
    unnamed x8 -> x20, local copies, waits for them, and re-layouts: 0.02 us -> 5.46 us
    broadcast_in_dim x1 -> x0, other arithmetic: 4.22 us -> none  [shards(): return (new_num[None], new_weight, kept_half[None], kept_weight)]
    ppermute x5, waiting for transfers between devices: 4.53 us -> 7.47 us  [transposed(): return lax.ppermute(value, ('core', 'x_hi'), pairs)]
  transfers between devices with their start and end apart: 33 -> 36, of which waited for: 16 -> 18; matrix products, arithmetic and copies ran while one was open for 4% -> 5% of each run, Pallas kernels for 6% -> 3%
where the time goes in v5:
time: 248 us; the launch traced here: 246 us
  waiting for transfers between devices  110 us (44%)
  starting transfers between devices  70.3 us (28%)
  Pallas kernels  22.2 us (9%)
  blocking collectives  19.4 us (8%)
  local copies, waits for them, and re-layouts  10.4 us (4%)
  between operations  7.36 us (3%)
  other arithmetic  6.51 us (3%)
    ppermute x30, waiting for transfers between devices, shifted(): return lax.ppermute(value, axis, pairs)  103 us
    ppermute x30, starting transfers between devices, shifted(): return lax.ppermute(value, axis, pairs)  53.9 us
    ppermute x5, starting transfers between devices, transposed(): return lax.ppermute(value, ('core', 'x_hi'), pairs)  14.7 us
    psum x1, blocking collectives, shards(): norm_sq = lax.psum(norm_sq, 'z')  12.8 us
    pallas_call x1, Pallas kernels, gate_grads(): pl.pallas_call(grad_kernel, grid=(D // BLOCK,), in_specs=[pl.BlockSpec((p...  8.85 us
    ppermute x5, waiting for transfers between devices, transposed(): return lax.ppermute(value, ('core', 'x_hi'), pairs)  7.47 us
    psum x1, blocking collectives, shards(): norm_sq = lax.psum(norm_sq, 'y')  6.61 us
    pallas_call x1, Pallas kernels, updated(): pl.pallas_call(updated_kernel, grid=(D // BLOCK,), in_specs=[scalar, scal...  6.18 us
  transfers between devices with their start and end apart: 36, of which 18 were waited for; matrix products, arithmetic and copies ran while one was open for 5% of the time, Pallas kernels for 3%

profile of v5, /device:TPU:1, one launch (start us, length us, event | category | flops | bytes accessed | tf_op | source)
XLA Modules:
  0.0 246.3 jit_solution(9912906602389663513)
XLA Ops:
  0.7 6.2 %collective-permute-start.1 = (bf16[20,5120]{1,0:T(8,128)(2,1)}, bf16[20,5120]{1,0:T(8,128)(2,1)S(1)}, u32[]{:S(2)}, u32[]{:S(2)}) collective-permute-start(bf16[20,5120]{1,0:T(8,128)(2,1)} %bitcast.29), channel_id=1, source_target_pairs={{0,0},{64,4},{4,64},{68,68},{1,1},{65,5},{5,65},{69,69},{2,2},{66,... | collective-permute-start | bytes 614408 | tf_op jit(solution)/shard_map/ppermute | solution.py:37
  6.8 1.9 collective-permute-start
  9.4 1.8 divide_convert_fusion
  11.5 4.5 %collective-permute-done.refs_0_ = bf16[20,5120]{1,0:T(8,128)(2,1)S(1)} collective-permute-done((bf16[20,5120]{1,0:T(8,128)(2,1)}, bf16[20,5120]{1,0:T(8,128)(2,1)S(1)}, u32[]{:S(2)}, u32[]{:S(2)}) %collective-permute-start) | collective-permute-done | bytes 204832 | tf_op jit(solution)/shard_map/ppermute | solution.py:37
  16.1 2.6 %collective-permute-start.22 = (bf16[336,5120]{1,0:T(8,128)(2,1)S(1)}, bf16[336,5120]{1,0:T(8,128)(2,1)S(1)}, u32[]{:S(2)}, u32[]{:S(2)}) collective-permute-start(bf16[336,5120]{1,0:T(8,128)(2,1)S(1)} %held.18), channel_id=1, source_target_pairs={{0,0},{64,4},{4,64},{68,68},{1,1},{65,5},{5,65},{69,69},{2,2},{66,... | collective-permute-start | bytes 10321928 | tf_op jit(solution)/shard_map/ppermute | solution.py:37
  18.7 5.7 %collective-permute-start.5 = (bf16[20,5120]{1,0:T(8,128)(2,1)S(1)}, bf16[20,5120]{1,0:T(8,128)(2,1)S(1)}, u32[]{:S(2)}, u32[]{:S(2)}) collective-permute-start(bf16[20,5120]{1,0:T(8,128)(2,1)S(1)} %collective-permute-done.1.refs_1_.refs_0_), channel_id=1, source_target_pairs={{8,0},{16,8},{24,16},{32,24},{40,32},{48,40},{56,48},{0,56},{9,1},... | collective-permute-start | bytes 614408 | tf_op jit(solution)/shard_map/ppermute | solution.py:32
  24.3 2.9 %collective-permute-start.4 = (bf16[20,5120]{1,0:T(8,128)(2,1)S(1)}, bf16[20,5120]{1,0:T(8,128)(2,1)S(1)}, u32[]{:S(2)}, u32[]{:S(2)}) collective-permute-start(bf16[20,5120]{1,0:T(8,128)(2,1)S(1)} %held.12.refs_0_), channel_id=1, source_target_pairs={{2,0},{3,1},{0,2},{1,3},{6,4},{7,5},{4,6},{5,7},{10,8},{11,9},{8,1... | collective-permute-start | bytes 614408 | tf_op jit(solution)/shard_map/ppermute | solution.py:32
  27.3 1.2 collective-permute-done.5.refs_1_
  28.5 3.1 %collective-permute-start.6 = (bf16[20,5120]{1,0:T(8,128)(2,1)S(1)}, bf16[20,5120]{1,0:T(8,128)(2,1)S(1)}, u32[]{:S(2)}, u32[]{:S(2)}) collective-permute-start(bf16[20,5120]{1,0:T(8,128)(2,1)S(1)} %collective-permute-done.5.refs_1_), channel_id=1, source_target_pairs={{8,0},{16,8},{24,16},{32,24},{40,32},{48,40},{56,48},{0,56},{9,1},... | collective-permute-start | bytes 614408 | tf_op jit(solution)/shard_map/ppermute | solution.py:32
  31.6 0.6 collective-permute-done.7.refs_7_
  32.2 2.7 %collective-permute-start.2 = (bf16[20,5120]{1,0:T(8,128)(2,1)S(1)}, bf16[20,5120]{1,0:T(8,128)(2,1)S(1)}, u32[]{:S(2)}, u32[]{:S(2)}) collective-permute-start(bf16[20,5120]{1,0:T(8,128)(2,1)S(1)} %held.12.refs_0_), channel_id=1, source_target_pairs={{1,0},{2,1},{3,2},{0,3},{5,4},{6,5},{7,6},{4,7},{9,8},{10,9},{11,1... | collective-permute-start | bytes 614408 | tf_op jit(solution)/shard_map/ppermute | solution.py:32
  34.9 1.9 collective-permute-done.6.refs_1_.refs_2_
  36.8 3.1 %collective-permute-start.11 = (bf16[20,5120]{1,0:T(8,128)(2,1)S(1)}, bf16[20,5120]{1,0:T(8,128)(2,1)S(1)}, u32[]{:S(2)}, u32[]{:S(2)}) collective-permute-start(bf16[20,5120]{1,0:T(8,128)(2,1)S(1)} %collective-permute-done.6.refs_1_.refs_2_), channel_id=1, source_target_pairs={{8,0},{16,8},{24,16},{32,24},{40,32},{48,40},{56,48},{0,56},{9,1},... | collective-permute-start | bytes 614408 | tf_op jit(solution)/shard_map/ppermute | solution.py:32
  40.0 1.5 collective-permute-done.3.refs_2_
  41.9 2.7 %collective-permute-start.9 = (bf16[80,5120]{1,0:T(8,128)(2,1)S(1)}, bf16[80,5120]{1,0:T(8,128)(2,1)S(1)}, u32[]{:S(2)}, u32[]{:S(2)}) collective-permute-start(bf16[80,5120]{1,0:T(8,128)(2,1)S(1)} %stacked.2.refs_0_), channel_id=1, source_target_pairs={{8,0},{16,8},{24,16},{32,24},{40,32},{48,40},{56,48},{0,56},{9,1},... | collective-permute-start | bytes 2457608 | tf_op jit(solution)/shard_map/ppermute | solution.py:32
  44.7 1.1 collective-permute-start.12
  45.8 1.5 collective-permute-start.13
  47.2 23.1 %collective-permute-done.12.refs_4_ = bf16[20,5120]{1,0:T(8,128)(2,1)S(1)} collective-permute-done((bf16[20,5120]{1,0:T(8,128)(2,1)S(1)}, bf16[20,5120]{1,0:T(8,128)(2,1)S(1)}, u32[]{:S(2)}, u32[]{:S(2)}) %collective-permute-start.12) | collective-permute-done | bytes 204832 | tf_op jit(solution)/shard_map/ppermute | solution.py:32
  70.4 0.6 stacked.3.refs_2_.refs_0_
  71.1 1.3 collective-permute-start.19
  72.5 0.9 collective-permute-start.14
  73.4 0.5 collective-permute-start.15
  74.0 13.4 %collective-permute-done.14.refs_0_ = bf16[80,5120]{1,0:T(8,128)(2,1)S(1)} collective-permute-done((bf16[80,5120]{1,0:T(8,128)(2,1)S(1)}, bf16[80,5120]{1,0:T(8,128)(2,1)S(1)}, u32[]{:S(2)}, u32[]{:S(2)}) %collective-permute-start.14) | collective-permute-done | bytes 819232 | tf_op jit(solution)/shard_map/ppermute | solution.py:32
  87.4 3.1 %collective-permute-done.15.refs_1_ = bf16[80,5120]{1,0:T(8,128)(2,1)S(1)} collective-permute-done((bf16[80,5120]{1,0:T(8,128)(2,1)S(1)}, bf16[80,5120]{1,0:T(8,128)(2,1)S(1)}, u32[]{:S(2)}, u32[]{:S(2)}) %collective-permute-start.15) | collective-permute-done | bytes 819232 | tf_op jit(solution)/shard_map/ppermute | solution.py:32
  90.5 11.6 %collective-permute-done.18.refs_0_ = bf16[160,5120]{1,0:T(8,128)(2,1)S(1)} collective-permute-done((bf16[160,5120]{1,0:T(8,128)(2,1)S(1)}, bf16[160,5120]{1,0:T(8,128)(2,1)S(1)}, u32[]{:S(2)}, u32[]{:S(2)}) %collective-permute-start.18) | collective-permute-done | bytes 1638432 | tf_op jit(solution)/shard_map/ppermute | solution.py:32
  102.1 2.6 %collective-permute-done.19.refs_1_ = bf16[160,5120]{1,0:T(8,128)(2,1)S(1)} collective-permute-done((bf16[160,5120]{1,0:T(8,128)(2,1)S(1)}, bf16[160,5120]{1,0:T(8,128)(2,1)S(1)}, u32[]{:S(2)}, u32[]{:S(2)}) %collective-permute-start.19) | collective-permute-done | bytes 1638432 | tf_op jit(solution)/shard_map/ppermute | solution.py:32
  105.1 0.6 collective-permute-start.16
  105.7 0.8 collective-permute-start.17
  106.8 17.4 %collective-permute-done.16.refs_0_ = bf16[80,5120]{1,0:T(8,128)(2,1)S(1)} collective-permute-done((bf16[80,5120]{1,0:T(8,128)(2,1)S(1)}, bf16[80,5120]{1,0:T(8,128)(2,1)S(1)}, u32[]{:S(2)}, u32[]{:S(2)}) %collective-permute-start.16) | collective-permute-done | bytes 819232 | tf_op jit(solution)/shard_map/ppermute | solution.py:32
  124.2 1.9 collective-permute-done.17.refs_1_
  126.1 1.5 collective-permute-start.28
  127.6 7.2 %collective-permute-done.26.refs_1_.refs_0_ = f32[64,5120]{1,0:T(8,128)S(1)} collective-permute-done((f32[64,5120]{1,0:T(8,128)S(1)}, f32[64,5120]{1,0:T(8,128)S(1)}, u32[]{:S(2)}, u32[]{:S(2)}) %collective-permute-start.26) | collective-permute-done | bytes 1310752 | tf_op jit(solution)/shard_map/ppermute | solution.py:32
  134.8 1.3 collective-permute-start.27
  136.7 1.1 concatenate.7.refs_0_
  137.9 5.6 %collective-permute-done.25.refs_4_ = bf16[80,5120]{1,0:T(8,128)(2,1)S(1)} collective-permute-done((bf16[80,5120]{1,0:T(8,128)(2,1)S(1)}, bf16[80,5120]{1,0:T(8,128)(2,1)S(1)}, u32[]{:S(2)}, u32[]{:S(2)}) %collective-permute-start.25) | collective-permute-done | bytes 819232 | tf_op jit(solution)/shard_map/ppermute | solution.py:32
  143.6 2.7 %collective-permute-start.20 = (bf16[48,5120]{1,0:T(8,128)(2,1)S(1)}, bf16[48,5120]{1,0:T(8,128)(2,1)S(1)}, u32[]{:S(2)}, u32[]{:S(2)}) collective-permute-start(bf16[48,5120]{1,0:T(8,128)(2,1)S(1)} %slice.27), channel_id=1, source_target_pairs={{8,0},{16,8},{24,16},{32,24},{40,32},{48,40},{56,48},{0,56},{9,1},... | collective-permute-start | bytes 1474568 | tf_op jit(solution)/shard_map/ppermute | solution.py:32
  146.3 2.1 collective-permute-start.21
  148.4 5.6 %hidden.1.refs_0_ = f32[640,256]{1,0:T(8,128)S(1)} custom-call(bf16[160,5120]{1,0:T(8,128)(2,1)S(1)} %stacked.3.refs_2_.refs_0_, bf16[160,5120]{1,0:T(8,128)(2,1)S(1)} %get-tuple-element.20.refs_2_.refs_1_, bf16[160,5120]{1,0:T(8,128)(2,1)S(1)} %get-tuple-element.21.refs_3_.refs_2_, bf16[80,5120]{1,0:T(8,128)(2,1)S(1)} %collective-permute-done.24.refs_3_, ...), custom_call_target="tpu_custom_call" | custom-call | flops 1677721600 | bytes 10747904 | tf_op jit(solution)/shard_map/hidden/pallas_call | solution.py:135
  154.1 1.0 copy-done.3
  155.1 0.5 copy-done.5
  155.6 2.5 %collective-permute-done.20.refs_4_ = bf16[48,5120]{1,0:T(8,128)(2,1)S(1)} collective-permute-done((bf16[48,5120]{1,0:T(8,128)(2,1)S(1)}, bf16[48,5120]{1,0:T(8,128)(2,1)S(1)}, u32[]{:S(2)}, u32[]{:S(2)}) %collective-permute-start.20) | collective-permute-done | bytes 491552 | tf_op jit(solution)/shard_map/ppermute | solution.py:32
  158.1 8.8 %gate_grads.1 = (f32[112,5120]{1,0:T(8,128)S(1)}, f32[112,5120]{1,0:T(8,128)S(1)}) custom-call(bf16[80,5120]{1,0:T(8,128)(2,1)S(1)} %stacked.2.refs_0_, bf16[80,5120]{1,0:T(8,128)(2,1)S(1)} %get-tuple-element.16.refs_1_, bf16[80,5120]{1,0:T(8,128)(2,1)S(1)} %get-tuple-element.18.refs_2_, bf16[80,5120]{1,0:T(8,128)(2,1)S(1)} %get-tuple-element.22.refs_3_, ...), custom_call_target="tpu_custom_call" | custom-call | flops 5033164800 | bytes 14942208 | tf_op jit(solution)/shard_map/gate_grads/pallas_call | solution.py:197
  166.9 2.5 collective-permute-start.30
  169.4 0.5 collective-permute-start.34
  169.9 3.6 %collective-permute-done.30 = f32[112,5120]{1,0:T(8,128)S(1)} collective-permute-done((f32[112,5120]{1,0:T(8,128)S(1)}, f32[112,5120]{1,0:T(8,128)S(1)}, u32[]{:S(2)}, u32[]{:S(2)}) %collective-permute-start.30) | collective-permute-done | bytes 2293792 | tf_op jit(solution)/shard_map/ppermute | solution.py:32
  173.5 2.5 %multiply_reduce_fusion = (f32[]{:T(128)}, f32[112,5120]{1,0:T(8,128)}) fusion(f32[112,5120]{1,0:T(8,128)S(1)} %get-tuple-element.24, f32[112,5120]{1,0:T(8,128)S(1)} %collective-permute-done.30), kind=kLoop, calls=%fused_computation.1 | loop fusion | flops 1720319 | bytes 6881284 | tf_op jit(solution)/shard_map/reduce_sum | solution.py:305
  176.0 2.0 collective-permute-start.33
  178.1 12.8 %psum.14 = f32[]{:T(128)} all-reduce(f32[]{:T(128)} %get-tuple-element.28), channel_id=1, replica_groups=mesh['x_lo'=2,'core'=2,'z'=8,'x_hi'=2,'y'=4] {'z'}, use_global_device_ids=true, to_apply=%region_1.2 | all-reduce | flops 1 | bytes 8 | tf_op jit(solution)/shard_map/psum | solution.py:307
  190.9 5.4 %collective-permute-done.34.refs_0_ = f32[56,5120]{1,0:T(8,128)} collective-permute-done((f32[56,5120]{1,0:T(8,128)}, f32[56,5120]{1,0:T(8,128)}, u32[]{:S(2)}, u32[]{:S(2)}) %collective-permute-start.34) | collective-permute-done | bytes 1146912 | tf_op jit(solution)/shard_map/ppermute | solution.py:32
  196.3 0.6 held.23.refs_1_
  196.9 15.6 %collective-permute-start.35 = (f32[56,5120]{1,0:T(8,128)}, f32[56,5120]{1,0:T(8,128)}, u32[]{:S(2)}, u32[]{:S(2)}) collective-permute-start(f32[56,5120]{1,0:T(8,128)} %held.23.refs_1_), channel_id=1, source_target_pairs={{64,0},{0,64},{65,1},{1,65},{66,2},{2,66},{67,3},{3,67},{68,4},{4,... | collective-permute-start | bytes 3440648 | tf_op jit(solution)/shard_map/ppermute | solution.py:32
  213.2 0.5 slice.38
  213.7 6.6 %psum.15 = f32[]{:T(128)} all-reduce(f32[]{:T(128)} %psum.14), channel_id=1, replica_groups=mesh['x_lo'=2,'core'=2,'z'=8,'x_hi'=2,'y'=4] {'y'}, use_global_device_ids=true, to_apply=%region_2.3 | all-reduce | flops 1 | bytes 8 | tf_op jit(solution)/shard_map/psum | solution.py:310
  220.3 1.3 slice.36
  221.5 1.9 collective-permute-start.31
  223.5 1.7 collective-permute-start.32
  225.2 2.9 %collective-permute-done.31 = f32[]{:T(128)} collective-permute-done((f32[]{:T(128)}, f32[]{:T(128)}, u32[]{:S(2)}, u32[]{:S(2)}) %collective-permute-start.31) | collective-permute-done | bytes 36 | tf_op jit(solution)/shard_map/ppermute | solution.py:37
  229.6 1.2 slice.37
  230.8 1.9 pad_maximum_fusion.1
  232.7 0.6 constant_dynamic-slice_fusion
  233.9 1.3 copy-done.2
  235.2 1.3 copy-done.4
  236.6 1.3 copy-done.6
  237.9 6.2 %updated.1 = (f32[112,5120]{1,0:T(8,128)}, f32[112,5120]{1,0:T(8,128)}) custom-call(f32[1]{0:T(128)} %bitcast.8.factor, s32[1]{0:T(128)} %bitcast.9.which, f32[112,5120]{1,0:T(8,128)S(1)} %bitcast.26, f32[112,5120]{1,0:T(8,128)} %collective-permute-done.33.grad, f32[64,5120]{1,0:T(8,128)S(1)} %copy-done.2, f32[56,5120]{1,0:T(8,128)} %held.23.refs_1_, ...), custom_call_target="tpu_custom_call" | custom-call | tf_op jit(solution)/shard_map/updated/pallas_call | solution.py:237
  (62 shorter events, 1.8 us)
Async XLA Ops:
  0.6 10.6 %copy-start.9 = (bf16[112,5120]{1,0:T(8,128)(2,1)S(1)}, bf16[112,5120]{1,0:T(8,128)(2,1)}, u32[]{:S(2)}) copy-start(bf16[112,5120]{1,0:T(8,128)(2,1)} %param.15) | copy-start | bytes 3440644
  0.6 10.6 %copy-start.8 = (bf16[112,5120]{1,0:T(8,128)(2,1)S(1)}, bf16[112,5120]{1,0:T(8,128)(2,1)}, u32[]{:S(2)}) copy-start(bf16[112,5120]{1,0:T(8,128)(2,1)} %param.16) | copy-start | bytes 3440644
  0.7 10.9 %collective-permute-start.1 = (bf16[20,5120]{1,0:T(8,128)(2,1)}, bf16[20,5120]{1,0:T(8,128)(2,1)S(1)}, u32[]{:S(2)}, u32[]{:S(2)}) collective-permute-start(bf16[20,5120]{1,0:T(8,128)(2,1)} %bitcast.29), channel_id=1, source_target_pairs={{0,0},{64,4},{4,64},{68,68},{1,1},{65,5},{5,65},{69,69},{2,2},{66,... | collective-permute-start | bytes 614408 | tf_op jit(solution)/shard_map/ppermute | solution.py:37
  6.8 9.2 %collective-permute-start = (bf16[20,5120]{1,0:T(8,128)(2,1)}, bf16[20,5120]{1,0:T(8,128)(2,1)S(1)}, u32[]{:S(2)}, u32[]{:S(2)}) collective-permute-start(bf16[20,5120]{1,0:T(8,128)(2,1)} %bitcast.30), channel_id=1, source_target_pairs={{0,0},{64,4},{4,64},{68,68},{1,1},{65,5},{5,65},{69,69},{2,2},{66,... | collective-permute-start | bytes 614408 | tf_op jit(solution)/shard_map/ppermute | solution.py:37
  16.1 88.7 %collective-permute-start.22 = (bf16[336,5120]{1,0:T(8,128)(2,1)S(1)}, bf16[336,5120]{1,0:T(8,128)(2,1)S(1)}, u32[]{:S(2)}, u32[]{:S(2)}) collective-permute-start(bf16[336,5120]{1,0:T(8,128)(2,1)S(1)} %held.18), channel_id=1, source_target_pairs={{0,0},{64,4},{4,64},{68,68},{1,1},{65,5},{5,65},{69,69},{2,2},{66,... | collective-permute-start | bytes 10321928 | tf_op jit(solution)/shard_map/ppermute | solution.py:37
  18.7 9.8 %collective-permute-start.5 = (bf16[20,5120]{1,0:T(8,128)(2,1)S(1)}, bf16[20,5120]{1,0:T(8,128)(2,1)S(1)}, u32[]{:S(2)}, u32[]{:S(2)}) collective-permute-start(bf16[20,5120]{1,0:T(8,128)(2,1)S(1)} %collective-permute-done.1.refs_1_.refs_0_), channel_id=1, source_target_pairs={{8,0},{16,8},{24,16},{32,24},{40,32},{48,40},{56,48},{0,56},{9,1},... | collective-permute-start | bytes 614408 | tf_op jit(solution)/shard_map/ppermute | solution.py:32
  24.3 7.8 %collective-permute-start.7 = (bf16[20,5120]{1,0:T(8,128)(2,1)S(1)}, bf16[20,5120]{1,0:T(8,128)(2,1)S(1)}, u32[]{:S(2)}, u32[]{:S(2)}) collective-permute-start(bf16[20,5120]{1,0:T(8,128)(2,1)S(1)} %collective-permute-done.1.refs_1_.refs_0_), channel_id=1, source_target_pairs={{56,0},{0,8},{8,16},{16,24},{24,32},{32,40},{40,48},{48,56},{57,1}... | collective-permute-start | bytes 614408 | tf_op jit(solution)/shard_map/ppermute | solution.py:32
  24.3 10.6 %collective-permute-start.4 = (bf16[20,5120]{1,0:T(8,128)(2,1)S(1)}, bf16[20,5120]{1,0:T(8,128)(2,1)S(1)}, u32[]{:S(2)}, u32[]{:S(2)}) collective-permute-start(bf16[20,5120]{1,0:T(8,128)(2,1)S(1)} %held.12.refs_0_), channel_id=1, source_target_pairs={{2,0},{3,1},{0,2},{1,3},{6,4},{7,5},{4,6},{5,7},{10,8},{11,9},{8,1... | collective-permute-start | bytes 614408 | tf_op jit(solution)/shard_map/ppermute | solution.py:32
  28.5 8.3 %collective-permute-start.6 = (bf16[20,5120]{1,0:T(8,128)(2,1)S(1)}, bf16[20,5120]{1,0:T(8,128)(2,1)S(1)}, u32[]{:S(2)}, u32[]{:S(2)}) collective-permute-start(bf16[20,5120]{1,0:T(8,128)(2,1)S(1)} %collective-permute-done.5.refs_1_), channel_id=1, source_target_pairs={{8,0},{16,8},{24,16},{32,24},{40,32},{48,40},{56,48},{0,56},{9,1},... | collective-permute-start | bytes 614408 | tf_op jit(solution)/shard_map/ppermute | solution.py:32
  32.2 7.8 %collective-permute-start.8 = (bf16[20,5120]{1,0:T(8,128)(2,1)S(1)}, bf16[20,5120]{1,0:T(8,128)(2,1)S(1)}, u32[]{:S(2)}, u32[]{:S(2)}) collective-permute-start(bf16[20,5120]{1,0:T(8,128)(2,1)S(1)} %collective-permute-done.7.refs_7_), channel_id=1, source_target_pairs={{56,0},{0,8},{8,16},{16,24},{24,32},{32,40},{40,48},{48,56},{57,1}... | collective-permute-start | bytes 614408 | tf_op jit(solution)/shard_map/ppermute | solution.py:32
  32.2 7.8 %collective-permute-start.2 = (bf16[20,5120]{1,0:T(8,128)(2,1)S(1)}, bf16[20,5120]{1,0:T(8,128)(2,1)S(1)}, u32[]{:S(2)}, u32[]{:S(2)}) collective-permute-start(bf16[20,5120]{1,0:T(8,128)(2,1)S(1)} %held.12.refs_0_), channel_id=1, source_target_pairs={{1,0},{2,1},{3,2},{0,3},{5,4},{6,5},{7,6},{4,7},{9,8},{10,9},{11,1... | collective-permute-start | bytes 614408 | tf_op jit(solution)/shard_map/ppermute | solution.py:32
  34.9 6.6 %collective-permute-start.3 = (bf16[20,5120]{1,0:T(8,128)(2,1)S(1)}, bf16[20,5120]{1,0:T(8,128)(2,1)S(1)}, u32[]{:S(2)}, u32[]{:S(2)}) collective-permute-start(bf16[20,5120]{1,0:T(8,128)(2,1)S(1)} %held.12.refs_0_), channel_id=1, source_target_pairs={{3,0},{0,1},{1,2},{2,3},{7,4},{4,5},{5,6},{6,7},{11,8},{8,9},{9,10... | collective-permute-start | bytes 614408 | tf_op jit(solution)/shard_map/ppermute | solution.py:32
  36.8 8.9 %collective-permute-start.11 = (bf16[20,5120]{1,0:T(8,128)(2,1)S(1)}, bf16[20,5120]{1,0:T(8,128)(2,1)S(1)}, u32[]{:S(2)}, u32[]{:S(2)}) collective-permute-start(bf16[20,5120]{1,0:T(8,128)(2,1)S(1)} %collective-permute-done.6.refs_1_.refs_2_), channel_id=1, source_target_pairs={{8,0},{16,8},{24,16},{32,24},{40,32},{48,40},{56,48},{0,56},{9,1},... | collective-permute-start | bytes 614408 | tf_op jit(solution)/shard_map/ppermute | solution.py:32
  41.8 30.7 %collective-permute-start.10 = (bf16[80,5120]{1,0:T(8,128)(2,1)S(1)}, bf16[80,5120]{1,0:T(8,128)(2,1)S(1)}, u32[]{:S(2)}, u32[]{:S(2)}) collective-permute-start(bf16[80,5120]{1,0:T(8,128)(2,1)S(1)} %stacked.2.refs_0_), channel_id=1, source_target_pairs={{56,0},{0,8},{8,16},{16,24},{24,32},{32,40},{40,48},{48,56},{57,1}... | collective-permute-start | bytes 2457608 | tf_op jit(solution)/shard_map/ppermute | solution.py:32
  41.9 30.6 %collective-permute-start.9 = (bf16[80,5120]{1,0:T(8,128)(2,1)S(1)}, bf16[80,5120]{1,0:T(8,128)(2,1)S(1)}, u32[]{:S(2)}, u32[]{:S(2)}) collective-permute-start(bf16[80,5120]{1,0:T(8,128)(2,1)S(1)} %stacked.2.refs_0_), channel_id=1, source_target_pairs={{8,0},{16,8},{24,16},{32,24},{40,32},{48,40},{56,48},{0,56},{9,1},... | collective-permute-start | bytes 2457608 | tf_op jit(solution)/shard_map/ppermute | solution.py:32
  44.7 25.7 %collective-permute-start.12 = (bf16[20,5120]{1,0:T(8,128)(2,1)S(1)}, bf16[20,5120]{1,0:T(8,128)(2,1)S(1)}, u32[]{:S(2)}, u32[]{:S(2)}) collective-permute-start(bf16[20,5120]{1,0:T(8,128)(2,1)S(1)} %collective-permute-done.6.refs_1_.refs_2_), channel_id=1, source_target_pairs={{16,0},{24,8},{32,16},{40,24},{48,32},{56,40},{0,48},{8,56},{17,1}... | collective-permute-start | bytes 614408 | tf_op jit(solution)/shard_map/ppermute | solution.py:32
  45.8 24.6 %collective-permute-start.13 = (bf16[20,5120]{1,0:T(8,128)(2,1)S(1)}, bf16[20,5120]{1,0:T(8,128)(2,1)S(1)}, u32[]{:S(2)}, u32[]{:S(2)}) collective-permute-start(bf16[20,5120]{1,0:T(8,128)(2,1)S(1)} %collective-permute-done.8.refs_2_.refs_6_), channel_id=1, source_target_pairs={{56,0},{0,8},{8,16},{16,24},{24,32},{32,40},{40,48},{48,56},{57,1}... | collective-permute-start | bytes 614408 | tf_op jit(solution)/shard_map/ppermute | solution.py:32
  70.9 3.0 %copy-start.7 = (f32[1,112,5120]{2,1,0:T(8,128)S(1)}, f32[1,112,5120]{2,1,0:T(8,128)}, u32[]{:S(2)}) copy-start(f32[1,112,5120]{2,1,0:T(8,128)} %param.13) | copy-start | bytes 6881284
  70.9 31.2 %collective-permute-start.18 = (bf16[160,5120]{1,0:T(8,128)(2,1)S(1)}, bf16[160,5120]{1,0:T(8,128)(2,1)S(1)}, u32[]{:S(2)}, u32[]{:S(2)}) collective-permute-start(bf16[160,5120]{1,0:T(8,128)(2,1)S(1)} %stacked.3.refs_2_.refs_0_), channel_id=1, source_target_pairs={{1,0},{2,1},{3,2},{0,3},{5,4},{6,5},{7,6},{4,7},{9,8},{10,9},{11,1... | collective-permute-start | bytes 4915208 | tf_op jit(solution)/shard_map/ppermute | solution.py:32
  71.1 33.6 %collective-permute-start.19 = (bf16[160,5120]{1,0:T(8,128)(2,1)S(1)}, bf16[160,5120]{1,0:T(8,128)(2,1)S(1)}, u32[]{:S(2)}, u32[]{:S(2)}) collective-permute-start(bf16[160,5120]{1,0:T(8,128)(2,1)S(1)} %stacked.3.refs_2_.refs_0_), channel_id=1, source_target_pairs={{3,0},{0,1},{1,2},{2,3},{7,4},{4,5},{5,6},{6,7},{11,8},{8,9},{9,10... | collective-permute-start | bytes 4915208 | tf_op jit(solution)/shard_map/ppermute | solution.py:32
  72.5 14.9 %collective-permute-start.14 = (bf16[80,5120]{1,0:T(8,128)(2,1)S(1)}, bf16[80,5120]{1,0:T(8,128)(2,1)S(1)}, u32[]{:S(2)}, u32[]{:S(2)}) collective-permute-start(bf16[80,5120]{1,0:T(8,128)(2,1)S(1)} %get-tuple-element.16.refs_1_), channel_id=1, source_target_pairs={{8,0},{16,8},{24,16},{32,24},{40,32},{48,40},{56,48},{0,56},{9,1},... | collective-permute-start | bytes 2457608 | tf_op jit(solution)/shard_map/ppermute | solution.py:32
  73.4 17.1 %collective-permute-start.15 = (bf16[80,5120]{1,0:T(8,128)(2,1)S(1)}, bf16[80,5120]{1,0:T(8,128)(2,1)S(1)}, u32[]{:S(2)}, u32[]{:S(2)}) collective-permute-start(bf16[80,5120]{1,0:T(8,128)(2,1)S(1)} %get-tuple-element.17.refs_8_), channel_id=1, source_target_pairs={{56,0},{0,8},{8,16},{16,24},{24,32},{32,40},{40,48},{48,56},{57,1}... | collective-permute-start | bytes 2457608 | tf_op jit(solution)/shard_map/ppermute | solution.py:32
  104.7 41.5 %collective-permute-start.23 = (bf16[336,5120]{1,0:T(8,128)(2,1)S(1)}, bf16[336,5120]{1,0:T(8,128)(2,1)S(1)}, u32[]{:S(2)}, u32[]{:S(2)}) collective-permute-start(bf16[336,5120]{1,0:T(8,128)(2,1)S(1)} %held.19.refs_5_.refs_9_.refs_11_), channel_id=1, source_target_pairs={{64,0},{0,64},{65,1},{1,65},{66,2},{2,66},{67,3},{3,67},{68,4},{4,... | collective-permute-start | bytes 10321928 | tf_op jit(solution)/shard_map/ppermute | solution.py:32
  104.7 30.0 %collective-permute-start.26 = (f32[64,5120]{1,0:T(8,128)S(1)}, f32[64,5120]{1,0:T(8,128)S(1)}, u32[]{:S(2)}, u32[]{:S(2)}) collective-permute-start(f32[64,5120]{1,0:T(8,128)S(1)} %held.20), channel_id=1, source_target_pairs={{128,0},{0,128},{129,1},{1,129},{130,2},{2,130},{131,3},{3,131},{1... | collective-permute-start | bytes 3932168 | tf_op jit(solution)/shard_map/ppermute | solution.py:32
  105.1 19.1 %collective-permute-start.16 = (bf16[80,5120]{1,0:T(8,128)(2,1)S(1)}, bf16[80,5120]{1,0:T(8,128)(2,1)S(1)}, u32[]{:S(2)}, u32[]{:S(2)}) collective-permute-start(bf16[80,5120]{1,0:T(8,128)(2,1)S(1)} %get-tuple-element.18.refs_2_), channel_id=1, source_target_pairs={{8,0},{16,8},{24,16},{32,24},{40,32},{48,40},{56,48},{0,56},{9,1},... | collective-permute-start | bytes 2457608 | tf_op jit(solution)/shard_map/ppermute | solution.py:32
  105.7 20.4 %collective-permute-start.17 = (bf16[80,5120]{1,0:T(8,128)(2,1)S(1)}, bf16[80,5120]{1,0:T(8,128)(2,1)S(1)}, u32[]{:S(2)}, u32[]{:S(2)}) collective-permute-start(bf16[80,5120]{1,0:T(8,128)(2,1)S(1)} %get-tuple-element.19.refs_3_.refs_7_), channel_id=1, source_target_pairs={{56,0},{0,8},{8,16},{16,24},{24,32},{32,40},{40,48},{48,56},{57,1}... | collective-permute-start | bytes 2457608 | tf_op jit(solution)/shard_map/ppermute | solution.py:32
  106.7 31.2 %collective-permute-start.24 = (bf16[80,5120]{1,0:T(8,128)(2,1)S(1)}, bf16[80,5120]{1,0:T(8,128)(2,1)S(1)}, u32[]{:S(2)}, u32[]{:S(2)}) collective-permute-start(bf16[80,5120]{1,0:T(8,128)(2,1)S(1)} %slice.29), channel_id=1, source_target_pairs={{1,0},{2,1},{3,2},{0,3},{5,4},{6,5},{7,6},{4,7},{9,8},{10,9},{11,1... | collective-permute-start | bytes 2457608 | tf_op jit(solution)/shard_map/ppermute | solution.py:32
  124.2 19.4 %collective-permute-start.25 = (bf16[80,5120]{1,0:T(8,128)(2,1)S(1)}, bf16[80,5120]{1,0:T(8,128)(2,1)S(1)}, u32[]{:S(2)}, u32[]{:S(2)}) collective-permute-start(bf16[80,5120]{1,0:T(8,128)(2,1)S(1)} %slice.30), channel_id=1, source_target_pairs={{3,0},{0,1},{1,2},{2,3},{7,4},{4,5},{5,6},{6,7},{11,8},{8,9},{9,10... | collective-permute-start | bytes 2457608 | tf_op jit(solution)/shard_map/ppermute | solution.py:32
  126.1 27.9 %collective-permute-start.28 = (f32[64,5120]{1,0:T(8,128)S(1)}, f32[64,5120]{1,0:T(8,128)S(1)}, u32[]{:S(2)}, u32[]{:S(2)}) collective-permute-start(f32[64,5120]{1,0:T(8,128)S(1)} %held.20), channel_id=1, source_target_pairs={{64,0},{0,64},{65,1},{1,65},{66,2},{2,66},{67,3},{3,67},{68,4},{4,... | collective-permute-start | bytes 3932168 | tf_op jit(solution)/shard_map/ppermute | solution.py:32
  134.8 3.1 %copy-start.1 = (f32[64,5120]{1,0:T(8,128)}, f32[64,5120]{1,0:T(8,128)S(1)}, u32[]{:S(2)}) copy-start(f32[64,5120]{1,0:T(8,128)S(1)} %collective-permute-done.26.refs_1_.refs_0_) | copy-start | bytes 3932164
  134.8 19.3 %collective-permute-start.27 = (f32[64,5120]{1,0:T(8,128)S(1)}, f32[64,5120]{1,0:T(8,128)S(1)}, u32[]{:S(2)}, u32[]{:S(2)}) collective-permute-start(f32[64,5120]{1,0:T(8,128)S(1)} %collective-permute-done.26.refs_1_.refs_0_), channel_id=1, source_target_pairs={{64,0},{0,64},{65,1},{1,65},{66,2},{2,66},{67,3},{3,67},{68,4},{4,... | collective-permute-start | bytes 3932168 | tf_op jit(solution)/shard_map/ppermute | solution.py:32
  137.9 16.2 %collective-permute-start.29 = (f32[56,5120]{1,0:T(8,128)}, f32[56,5120]{1,0:T(8,128)S(1)}, u32[]{:S(2)}, u32[]{:S(2)}) collective-permute-start(f32[56,5120]{1,0:T(8,128)} %held.21), channel_id=1, source_target_pairs={{64,0},{0,64},{65,1},{1,65},{66,2},{2,66},{67,3},{3,67},{68,4},{4,... | collective-permute-start | bytes 3440648 | tf_op jit(solution)/shard_map/ppermute | solution.py:32
  143.6 14.5 %collective-permute-start.20 = (bf16[48,5120]{1,0:T(8,128)(2,1)S(1)}, bf16[48,5120]{1,0:T(8,128)(2,1)S(1)}, u32[]{:S(2)}, u32[]{:S(2)}) collective-permute-start(bf16[48,5120]{1,0:T(8,128)(2,1)S(1)} %slice.27), channel_id=1, source_target_pairs={{8,0},{16,8},{24,16},{32,24},{40,32},{48,40},{56,48},{0,56},{9,1},... | collective-permute-start | bytes 1474568 | tf_op jit(solution)/shard_map/ppermute | solution.py:32
  146.3 9.3 %collective-permute-start.21 = (bf16[32,5120]{1,0:T(8,128)(2,1)S(1)}, bf16[32,5120]{1,0:T(8,128)(2,1)S(1)}, u32[]{:S(2)}, u32[]{:S(2)}) collective-permute-start(bf16[32,5120]{1,0:T(8,128)(2,1)S(1)} %slice.28), channel_id=1, source_target_pairs={{56,0},{0,8},{8,16},{16,24},{24,32},{32,40},{40,48},{48,56},{57,1}... | collective-permute-start | bytes 983048 | tf_op jit(solution)/shard_map/ppermute | solution.py:32
  154.0 1.1 copy-start.3
  154.1 1.5 copy-start.5
  166.9 6.5 %collective-permute-start.30 = (f32[112,5120]{1,0:T(8,128)S(1)}, f32[112,5120]{1,0:T(8,128)S(1)}, u32[]{:S(2)}, u32[]{:S(2)}) collective-permute-start(f32[112,5120]{1,0:T(8,128)S(1)} %get-tuple-element.25), channel_id=1, source_target_pairs={{64,0},{0,64},{65,1},{1,65},{66,2},{2,66},{67,3},{3,67},{68,4},{4,... | collective-permute-start | bytes 6881288 | tf_op jit(solution)/shard_map/ppermute | solution.py:32
  169.4 26.9 %collective-permute-start.34 = (f32[56,5120]{1,0:T(8,128)}, f32[56,5120]{1,0:T(8,128)}, u32[]{:S(2)}, u32[]{:S(2)}) collective-permute-start(f32[56,5120]{1,0:T(8,128)} %held.21), channel_id=1, source_target_pairs={{128,0},{0,128},{129,1},{1,129},{130,2},{2,130},{131,3},{3,131},{1... | collective-permute-start | bytes 3440648 | tf_op jit(solution)/shard_map/ppermute | solution.py:32
  176.0 57.9 %copy-start = (f32[1,112,5120]{2,1,0:T(8,128)S(1)}, f32[1,112,5120]{2,1,0:T(8,128)}, u32[]{:S(2)}) copy-start(f32[1,112,5120]{2,1,0:T(8,128)} %param.11) | copy-start | bytes 6881284
  176.0 57.9 %collective-permute-start.33 = (f32[112,5120]{1,0:T(8,128)}, f32[112,5120]{1,0:T(8,128)}, u32[]{:S(2)}, u32[]{:S(2)}) collective-permute-start(f32[112,5120]{1,0:T(8,128)} %get-tuple-element.29), channel_id=1, source_target_pairs={{0,0},{64,4},{4,64},{68,68},{1,1},{65,5},{5,65},{69,69},{2,2},{66,... | collective-permute-start | bytes 6881288 | tf_op jit(solution)/shard_map/ppermute | solution.py:37
  196.9 32.7 %collective-permute-start.35 = (f32[56,5120]{1,0:T(8,128)}, f32[56,5120]{1,0:T(8,128)}, u32[]{:S(2)}, u32[]{:S(2)}) collective-permute-start(f32[56,5120]{1,0:T(8,128)} %held.23.refs_1_), channel_id=1, source_target_pairs={{64,0},{0,64},{65,1},{1,65},{66,2},{2,66},{67,3},{3,67},{68,4},{4,... | collective-permute-start | bytes 3440648 | tf_op jit(solution)/shard_map/ppermute | solution.py:32
  221.5 6.6 %collective-permute-start.31 = (f32[]{:T(128)}, f32[]{:T(128)}, u32[]{:S(2)}, u32[]{:S(2)}) collective-permute-start(f32[]{:T(128)} %psum.15), channel_id=1, source_target_pairs={{0,0},{64,4},{4,64},{68,68},{1,1},{65,5},{5,65},{69,69},{2,2},{66,... | collective-permute-start | bytes 20 | tf_op jit(solution)/shard_map/ppermute | solution.py:37
  223.5 4.7 %collective-permute-start.32 = (f32[]{:T(128)}, f32[]{:T(128)}, u32[]{:S(2)}, u32[]{:S(2)}) collective-permute-start(f32[]{:T(128)} %psum.15), channel_id=1, source_target_pairs={{64,0},{0,4},{68,64},{4,68},{65,1},{1,5},{69,65},{5,69},{66,2},{2,... | collective-permute-start | bytes 20 | tf_op jit(solution)/shard_map/ppermute | solution.py:253
  233.9 1.3 copy-start.2
  235.2 1.3 copy-start.4
  236.6 1.3 copy-start.6

commit v6 on v4

--- a/solution.py
+++ b/solution.py
@@ -22,6 +22,7 @@
 
 ROWS = 112
 HALF = 128
+NO_COST = pl.CostEstimate(flops=1, bytes_accessed=1, transcendentals=0)
 BLOCK = 1024
 
 
@@ -37,15 +38,18 @@
 
 
 def held(value, *ready):
-    return pl.pallas_call(
+    values = value if isinstance(value, tuple) else (value,)
+    anywhere = pl.BlockSpec(memory_space=pl.ANY)
+    out = pl.pallas_call(
         lambda *refs: None,
-        in_specs=[pl.BlockSpec(memory_space=pl.ANY)] * (1 + len(ready)),
-        out_specs=pl.BlockSpec(memory_space=pl.ANY),
-        out_shape=jax.ShapeDtypeStruct(value.shape, value.dtype),
-        input_output_aliases={0: 0},
+        in_specs=[anywhere] * (len(values) + len(ready)),
+        out_specs=[anywhere] * len(values),
+        out_shape=[jax.ShapeDtypeStruct(one.shape, one.dtype) for one in values],
+        input_output_aliases={at: at for at in range(len(values))},
         compiler_params=params_of(1),
         name="held",
-    )(value, *ready)
+    )(*values, *ready)
+    return tuple(out) if isinstance(value, tuple) else out[0]
 
 
 def silu_slope(preact):
@@ -100,8 +104,8 @@
     wide[HALF + ROWS :, :] = pad
 
 
-def hidden_kernel(*refs):
-    *parts, mine, theirs, out_ref, total, wide = refs
+def hidden_kernel(z_ref, *refs):
+    *parts, mine, theirs, out_ref, total, wide, tile = refs
     at = pl.program_id(0)
 
     @pl.when(at == 0)
@@ -121,61 +125,72 @@
         column, block = row // 4, row // 32
         for dz in range(8):
             for dy in range(4):
-                start, place = dy * column + dz * block, (4 * dz + dy) * block
-                out_ref[place : place + block, :] = total[start : start + block, :]
+                start = dy * column + dz * block
+                tile[dy * block : (dy + 1) * block, :] = total[start : start + block, :]
+            place = pl.multiple_of(lax.rem(z_ref[0] + dz, 8) * (4 * block), 16)
+            out_ref[pl.ds(place, 4 * block), :] = tile[...]
 
 
 def hidden_of(parts, mine, theirs):
     count = sum(part.shape[0] for part in parts)
+    z = jnp.reshape(lax.axis_index("z"), (1,)).astype(jnp.int32)
     weights = pl.BlockSpec((ROWS, BLOCK), lambda at: (2, at))
     return pl.pallas_call(
         hidden_kernel,
         grid=(D // BLOCK,),
-        in_specs=[pl.BlockSpec((part.shape[0], BLOCK), lambda at: (0, at)) for part in parts]
+        in_specs=[pl.BlockSpec(memory_space=pltpu.SMEM)]
+        + [pl.BlockSpec((part.shape[0], BLOCK), lambda at: (0, at)) for part in parts]
         + [weights, weights],
         out_specs=pl.BlockSpec((count, 2 * HALF), lambda at: (0, 0)),
         out_shape=jax.ShapeDtypeStruct((count, 2 * HALF), jnp.float32),
         scratch_shapes=[
             pltpu.VMEM((count, 2 * HALF), jnp.float32),
             pltpu.VMEM((2 * HALF, BLOCK), jnp.bfloat16),
+            pltpu.VMEM((count // 8, 2 * HALF), jnp.float32),
         ],
         compiler_params=params_of(16),
-        cost_estimate=pl.CostEstimate(
-            flops=2 * count * D * 2 * HALF, bytes_accessed=2 * count * D + 2**22, transcendentals=0
-        ),
+        cost_estimate=NO_COST,
         name="hidden",
-    )(*parts, mine, theirs)
-
-
-def grad_kernel(*refs):
-    *parts, my_params, their_params, my_up, their_up, hidden_ref, own_ref, other_ref = refs[:-6]
-    rows, preact, up_proj, turned, wide_params, wide_up = refs[-6:]
+    )(z, *parts, mine, theirs)
+
+
+def grad_kernel(
+    x_ref, my_params, their_params, my_up, their_up, hidden_ref, own_ref, other_ref,
+    rows, preact, up_proj, turned, wide_params, wide_up, sems,
+):
     at = pl.program_id(0)
+    blocks = D // BLOCK
+
+    def copy(block):
+        columns = pl.ds(block * BLOCK, BLOCK)
+        return pltpu.make_async_copy(x_ref.at[:, columns], rows.at[:, columns], sems.at[block])
 
     @pl.when(at == 0)
     def _():
+        for block in range(blocks):
+            copy(block).start()
         preact[...] = jnp.zeros_like(preact)
         up_proj[...] = jnp.zeros_like(up_proj)
         clear(wide_params)
         clear(wide_up)
 
-    columns = pl.ds(pl.multiple_of(at * BLOCK, BLOCK), BLOCK)
-    row = 0
-    for part in parts:
-        count = part.shape[0]
-        rows[row : row + count, columns] = part[...]
-        row += count
     widen(wide_params, my_params, their_params)
     widen(wide_up, my_up, their_up)
-    preact[...] += dot_t(rows[:, columns], wide_params[...])
-    up_proj[...] += dot_t(rows[:, columns], wide_up[...])
-
-    @pl.when(at == pl.num_programs(0) - 1)
+    for block in range(blocks):
+
+        @pl.when(at == block)
+        def _():
+            copy(block).wait()
+            part = rows[:, block * BLOCK : (block + 1) * BLOCK]
+            preact[...] += dot_t(part, wide_params[...])
+            up_proj[...] += dot_t(part, wide_up[...])
+
+    @pl.when(at == blocks - 1)
     def _():
         slope = silu_slope(preact[...] * WIDTH_SCALE)
         turned[...] = (hidden_ref[...] * up_proj[...] * slope).T.astype(jnp.bfloat16)
 
-        @pl.loop(0, D // BLOCK)
+        @pl.loop(0, blocks)
         def _(block):
             columns = pl.ds(pl.multiple_of(block * BLOCK, BLOCK), BLOCK)
             grad = jnp.dot(turned[...], rows[:, columns], preferred_element_type=jnp.float32)
@@ -183,8 +198,9 @@
             other_ref[:, columns] = grad[HALF : HALF + ROWS] * WIDTH_SCALE
 
 
-def gate_grads(parts, mine, theirs, hidden):
-    count = sum(part.shape[0] for part in parts)
+def gate_grads(rows_in, mine, theirs, hidden):
+    count = rows_in.shape[0]
+    blocks = D // BLOCK
 
     def weights(which):
         return pl.BlockSpec((ROWS, BLOCK), lambda at: (which, at))
@@ -192,8 +208,8 @@
     whole = pl.BlockSpec((ROWS, D), lambda at: (0, 0))
     return pl.pallas_call(
         grad_kernel,
-        grid=(D // BLOCK,),
-        in_specs=[pl.BlockSpec((part.shape[0], BLOCK), lambda at: (0, at)) for part in parts]
+        grid=(blocks,),
+        in_specs=[pl.BlockSpec(memory_space=pl.ANY)]
         + [weights(0), weights(0), weights(1), weights(1)]
         + [pl.BlockSpec((count, 2 * HALF), lambda at: (0, 0))],
         out_specs=[whole, whole],
@@ -205,13 +221,71 @@
             pltpu.VMEM((2 * HALF, count), jnp.bfloat16),
             pltpu.VMEM((2 * HALF, BLOCK), jnp.bfloat16),
             pltpu.VMEM((2 * HALF, BLOCK), jnp.bfloat16),
+            pltpu.SemaphoreType.DMA((blocks,)),
         ],
         compiler_params=params_of(36),
-        cost_estimate=pl.CostEstimate(
-            flops=2 * count * D * 768, bytes_accessed=2 * count * D + 2**23, transcendentals=0
-        ),
+        cost_estimate=NO_COST,
         name="gate_grads",
-    )(*parts, mine, theirs, mine, theirs, hidden)
+    )(rows_in, mine, theirs, mine, theirs, hidden)
+
+
+def updated_kernel(factor, which, kept_weight, numerator, grad, *refs):
+    *received, kept_ref, new_ref, weight_ref, part, sems = refs
+    at = pl.program_id(0)
+    blocks = D // BLOCK
+
+    def copy(source, block):
+        columns = pl.ds(block * BLOCK, BLOCK)
+        return pltpu.make_async_copy(source.at[:, columns], part.at[:, columns], sems.at[block])
+
+    @pl.when(at == 0)
+    def _():
+        for place, source in enumerate(received):
+
+            @pl.when(which[0] == place)
+            def _():
+                for block in range(blocks):
+                    copy(source, block).start()
+
+    kept = 0.5 * (numerator[...] - factor[0] * grad[...])
+    kept_ref[...] = kept
+    for block in range(blocks):
+
+        @pl.when(at == block)
+        def _():
+            copy(received[0], block).wait()
+            new_ref[...] = kept + part[:ROWS, block * BLOCK : (block + 1) * BLOCK]
+
+    @pl.when(at == 0)
+    def _():
+        weight_ref[0] = kept_weight[0] + jnp.max(part[ROWS:, :128])
+
+
+def updated(numerator, grad, kept_weight, factor, which, received):
+    own = pl.BlockSpec((ROWS, BLOCK), lambda at: (0, at))
+    scalar = pl.BlockSpec(memory_space=pltpu.SMEM)
+    anywhere = pl.BlockSpec(memory_space=pl.ANY)
+    blocks = D // BLOCK
+    return pl.pallas_call(
+        updated_kernel,
+        grid=(blocks,),
+        in_specs=[scalar, scalar, scalar, own, own] + [anywhere] * len(received),
+        out_specs=[own, own, scalar],
+        out_shape=[
+            jax.ShapeDtypeStruct((ROWS, D), jnp.float32),
+            jax.ShapeDtypeStruct((ROWS, D), jnp.float32),
+            jax.ShapeDtypeStruct((1,), jnp.float32),
+        ],
+        scratch_shapes=[
+            pltpu.VMEM(received[0].shape, jnp.float32),
+            pltpu.SemaphoreType.DMA((blocks,)),
+        ],
+        compiler_params=params_of(16),
+        name="updated",
+    )(
+        jnp.reshape(factor, (1,)), jnp.reshape(which, (1,)), kept_weight,
+        numerator, grad, *received,
+    )
 
 
 def crossed(value):
@@ -233,40 +307,30 @@
     rows_in = held(rows_in, rows_grad, weights)
     near = [rows_in] + [shifted(rows_in, "y", steps) for steps in (1, 3, 2)]
     ring = {0: rows_grad, 1: shifted(rows_grad, "z", 1), 7: shifted(rows_grad, "z", 7)}
+    near[3] = held(near[3], ring[1], ring[7])
+    near = stacked(near)
+    rows_in = lax.all_gather(near, "z", axis=0, tiled=True)
     mine = transposed(held(weights, rows_grad))
     ring[2], ring[6] = shifted(ring[1], "z", 1), shifted(ring[7], "z", 7)
-    near[3] = held(near[3], ring[1], ring[7])
-    blocks = {0: stacked(near)}
-    for steps in (1, 7):
-        blocks[steps] = shifted(blocks[0], "z", steps)
     ring[3], ring[5] = shifted(ring[2], "z", 1), shifted(ring[6], "z", 7)
     ring[4] = shifted(ring[2], "z", 2)
     column = stacked([ring[steps] for steps in range(8)])
-
+    column = held(column, near)
     following, before = shifted(column, "y", 1), shifted(column, "y", 3)
-    blocks[1], blocks[7] = held(blocks[1], column), held(blocks[7], column)
-    blocks[2], blocks[6] = shifted(blocks[1], "z", 1), shifted(blocks[7], "z", 7)
-    mine = held(mine, blocks[2], blocks[6])
+    mine = held(mine, column)
     theirs = shifted(mine, "core", 1)
     stale = jnp.concatenate([stale_num[0], jnp.broadcast_to(stale_weight, (8, D))], axis=0)
-    stale = held(stale, blocks[1])
+    stale = held(stale, mine)
     two_before = shifted(stale, "x_lo", 1)
-    blocks[3], blocks[5] = shifted(blocks[2], "z", 1), shifted(blocks[6], "z", 7)
-    following, before = held(following, blocks[2]), held(before, blocks[6])
+    following, before = held((following, before), theirs)
     half = column.shape[0] // 2
     far = [shifted(following[:half], "y", 1), shifted(before[half:], "y", 3)]
-    blocks[3], blocks[5] = held(blocks[3], following), held(blocks[5], before)
-    cut = 48
-    last = [shifted(blocks[3][:cut], "z", 1), shifted(blocks[5][cut:], "z", 7)]
-
     hidden = hidden_of([column, following, before, *far], mine, theirs)
-    parts = [blocks[steps] for steps in (0, 1, 2, 3)] + last + [blocks[steps] for steps in (5, 6, 7)]
-    own_grad, other_grad = gate_grads(parts, mine, theirs, hidden)
-    two_before = held(two_before, own_grad)
-    first = lax.axis_index("core") == 0
-    one_before = jnp.where(first, shifted(two_before, "core", 1), shifted(stale, "core", 1))
-    received = jnp.where(step[0] % 2 == 0, one_before, two_before)
-
+
+    two_before = held(two_before, hidden)
+    received = (two_before, shifted(two_before, "core", 1), shifted(stale, "core", 1))
+    hidden = held(hidden, *received[1:])
+    own_grad, other_grad = gate_grads(rows_in, mine, theirs, hidden)
     gate_grad = own_grad + shifted(other_grad, "core", 1)
     norm_sq = jnp.sum(gate_grad * gate_grad)
     gate_grad = transposed(gate_grad)
@@ -275,10 +339,11 @@
     norm_sq = transposed(norm_sq) + crossed(norm_sq)
 
     clip_factor = jnp.minimum(1.0, MAX_NORM / jnp.sqrt(norm_sq + eps))
-    kept_half = 0.5 * (numerator - rate * clip_factor * gate_grad)
     kept_weight = 0.5 * push_weight
-    new_num = kept_half + received[:ROWS]
-    new_weight = kept_weight + received[ROWS, :1]
+    which = jnp.where(step[0] % 2 == 1, 0, 1 + lax.axis_index("core"))
+    kept_half, new_num, new_weight = updated(
+        numerator, gate_grad, kept_weight, rate * clip_factor, which, received
+    )
     return (new_num[None], new_weight, kept_half[None], kept_weight)
 
 

time: 259 us -> 269 us (1.039)
  local copies, waits for them, and re-layouts: 2.4 us -> 30.3 us
  waiting for transfers between devices: 129 us -> 107 us
  between operations: 7.27 us -> 18.7 us
  Pallas kernels: 15.4 us -> 23 us
  starting transfers between devices: 71.3 us -> 64.2 us
  other arithmetic: 11.1 us -> 4.62 us
    unnamed x8 -> x60, local copies, waits for them, and re-layouts: 0.02 us -> 26.6 us
    ppermute x27 -> x19, waiting for transfers between devices: 122 us -> 106 us  [shifted(): return lax.ppermute(value, axis, pairs)]
    ppermute x27 -> x19, starting transfers between devices: 34.1 us -> 25.2 us  [shifted(): return lax.ppermute(value, axis, pairs)]
    pallas_call x13 -> x11, Pallas kernels: 8.87 us -> 15.7 us  [the longest x1 9.29 us: gate_grads(): pl.pallas_call(grad_kernel, grid=(blocks,), in_specs=[pl.BlockSpec(memory...]
    ppermute x5, waiting for transfers between devices: 4.53 us -> 0.01 us  [transposed(): return lax.ppermute(value, ('core', 'x_hi'), pairs)]
    broadcast_in_dim x1 -> x0, other arithmetic: 4.22 us -> none  [shards(): return (new_num[None], new_weight, kept_half[None], kept_weight)]
    ppermute x1, starting transfers between devices: 10.3 us -> 13.7 us  [crossed(): return lax.ppermute(value, ('core', 'x_hi'), pairs)]
  transfers between devices with their start and end apart: 33 -> 26, of which waited for: 16 -> 14; matrix products, arithmetic and copies ran while one was open for 4% -> 2% of each run, Pallas kernels for 6% -> 3%
where the time goes in v6:
time: 269 us; the launch traced here: 266 us
  waiting for transfers between devices  107 us (40%)
  starting transfers between devices  64.2 us (24%)
  local copies, waits for them, and re-layouts  30.3 us (11%)
  Pallas kernels  23 us (9%)
  between operations  18.7 us (7%)
  blocking collectives  18.2 us (7%)
  other arithmetic  4.62 us (2%)
    ppermute x19, waiting for transfers between devices, shifted(): return lax.ppermute(value, axis, pairs)  106 us
    unnamed x60, local copies, waits for them, and re-layouts  26.6 us
    ppermute x5, starting transfers between devices, transposed(): return lax.ppermute(value, ('core', 'x_hi'), pairs)  25.3 us
    ppermute x19, starting transfers between devices, shifted(): return lax.ppermute(value, axis, pairs)  25.2 us
    psum x2, blocking collectives, shards(): norm_sq = lax.psum(norm_sq, axes)  18.2 us
    ppermute x1, starting transfers between devices, crossed(): return lax.ppermute(value, ('core', 'x_hi'), pairs)  13.7 us
    pallas_call x1, Pallas kernels, gate_grads(): pl.pallas_call(grad_kernel, grid=(blocks,), in_specs=[pl.BlockSpec(memory...  9.29 us
    pallas_call x1, Pallas kernels, hidden_of(): pl.pallas_call(hidden_kernel, grid=(D // BLOCK,), in_specs=[pl.BlockSpec(...  6.42 us
  transfers between devices with their start and end apart: 26, of which 14 were waited for; matrix products, arithmetic and copies ran while one was open for 2% of the time, Pallas kernels for 3%

profile of v6, /device:TPU:1, one launch (start us, length us, event | category | flops | bytes accessed | tf_op | source)
XLA Modules:
  0.0 265.9 jit_solution(613564773326181781)
XLA Ops:
  7.2 6.2 %collective-permute-start.1 = (bf16[20,5120]{1,0:T(8,128)(2,1)}, bf16[20,5120]{1,0:T(8,128)(2,1)S(1)}, u32[]{:S(2)}, u32[]{:S(2)}) collective-permute-start(bf16[20,5120]{1,0:T(8,128)(2,1)} %bitcast.23), channel_id=1, source_target_pairs={{0,0},{64,4},{4,64},{68,68},{1,1},{65,5},{5,65},{69,69},{2,2},{66,... | collective-permute-start | bytes 614408 | tf_op jit(solution)/shard_map/ppermute | solution.py:37
  13.4 1.9 collective-permute-start
  16.0 1.8 divide_convert_fusion
  17.8 0.3 pad_maximum_fusion.refs_2_.refs_0_
  18.1 5.7 %collective-permute-start.5 = (bf16[20,5120]{1,0:T(8,128)(2,1)S(1)}, bf16[20,5120]{1,0:T(8,128)(2,1)S(1)}, u32[]{:S(2)}, u32[]{:S(2)}) collective-permute-start(bf16[20,5120]{1,0:T(8,128)(2,1)S(1)} %collective-permute-done.1.refs_1_.refs_0_), channel_id=1, source_target_pairs={{8,0},{16,8},{24,16},{32,24},{40,32},{48,40},{56,48},{0,56},{9,1},... | collective-permute-start | bytes 614408 | tf_op jit(solution)/shard_map/ppermute | solution.py:32
  23.8 2.9 %collective-permute-start.4 = (bf16[20,5120]{1,0:T(8,128)(2,1)S(1)}, bf16[20,5120]{1,0:T(8,128)(2,1)S(1)}, u32[]{:S(2)}, u32[]{:S(2)}) collective-permute-start(bf16[20,5120]{1,0:T(8,128)(2,1)S(1)} %held.9.refs_0_), channel_id=1, source_target_pairs={{2,0},{3,1},{0,2},{1,3},{6,4},{7,5},{4,6},{5,7},{10,8},{11,9},{8,1... | collective-permute-start | bytes 614408 | tf_op jit(solution)/shard_map/ppermute | solution.py:32
  26.7 0.8 collective-permute-start.2
  27.5 0.7 collective-permute-start.3
  28.2 2.3 collective-permute-done.6.refs_2_.refs_7_
  30.4 2.6 collective-permute-done.4.refs_0_
  33.1 3.0 %collective-permute-done.2.refs_1_ = bf16[20,5120]{1,0:T(8,128)(2,1)S(1)} collective-permute-done((bf16[20,5120]{1,0:T(8,128)(2,1)S(1)}, bf16[20,5120]{1,0:T(8,128)(2,1)S(1)}, u32[]{:S(2)}, u32[]{:S(2)}) %collective-permute-start.2) | collective-permute-done | bytes 204832 | tf_op jit(solution)/shard_map/ppermute | solution.py:32
  36.4 0.3 stacked.2.refs_1_
  36.7 0.9 copy-done.17
  37.6 0.9 copy-done.21
  38.6 1.8 copy-done.3
  40.4 4.6 %collective-permute-start.7 = (bf16[336,5120]{1,0:T(8,128)(2,1)}, bf16[336,5120]{1,0:T(8,128)(2,1)S(1)}, u32[]{:S(2)}, u32[]{:S(2)}) collective-permute-start(bf16[336,5120]{1,0:T(8,128)(2,1)} %copy-done.3), channel_id=1, source_target_pairs={{0,0},{64,4},{4,64},{68,68},{1,1},{65,5},{5,65},{69,69},{2,2},{66,... | collective-permute-start | bytes 10321928 | tf_op jit(solution)/shard_map/ppermute | solution.py:37
  45.1 3.0 %collective-permute-start.8 = (bf16[20,5120]{1,0:T(8,128)(2,1)S(1)}, bf16[20,5120]{1,0:T(8,128)(2,1)S(1)}, u32[]{:S(2)}, u32[]{:S(2)}) collective-permute-start(bf16[20,5120]{1,0:T(8,128)(2,1)S(1)} %copy-done.24), channel_id=1, source_target_pairs={{8,0},{16,8},{24,16},{32,24},{40,32},{48,40},{56,48},{0,56},{9,1},... | collective-permute-start | bytes 614408 | tf_op jit(solution)/shard_map/ppermute | solution.py:32
  48.1 10.6 %collective-permute-done.8.refs_2_ = bf16[20,5120]{1,0:T(8,128)(2,1)S(1)} collective-permute-done((bf16[20,5120]{1,0:T(8,128)(2,1)S(1)}, bf16[20,5120]{1,0:T(8,128)(2,1)S(1)}, u32[]{:S(2)}, u32[]{:S(2)}) %collective-permute-start.8) | collective-permute-done | bytes 204832 | tf_op jit(solution)/shard_map/ppermute | solution.py:32
  58.8 3.5 %collective-permute-start.9 = (bf16[20,5120]{1,0:T(8,128)(2,1)S(1)}, bf16[20,5120]{1,0:T(8,128)(2,1)S(1)}, u32[]{:S(2)}, u32[]{:S(2)}) collective-permute-start(bf16[20,5120]{1,0:T(8,128)(2,1)S(1)} %collective-permute-done.8.refs_2_), channel_id=1, source_target_pairs={{8,0},{16,8},{24,16},{32,24},{40,32},{48,40},{56,48},{0,56},{9,1},... | collective-permute-start | bytes 614408 | tf_op jit(solution)/shard_map/ppermute | solution.py:32
  62.3 1.2 collective-permute-start.12
  63.5 12.7 %collective-permute-done.10.refs_4_ = bf16[20,5120]{1,0:T(8,128)(2,1)S(1)} collective-permute-done((bf16[20,5120]{1,0:T(8,128)(2,1)S(1)}, bf16[20,5120]{1,0:T(8,128)(2,1)S(1)}, u32[]{:S(2)}, u32[]{:S(2)}) %collective-permute-start.10) | collective-permute-done | bytes 204832 | tf_op jit(solution)/shard_map/ppermute | solution.py:32
  76.1 13.6 %collective-permute-done.9.refs_3_ = bf16[20,5120]{1,0:T(8,128)(2,1)S(1)} collective-permute-done((bf16[20,5120]{1,0:T(8,128)(2,1)S(1)}, bf16[20,5120]{1,0:T(8,128)(2,1)S(1)}, u32[]{:S(2)}, u32[]{:S(2)}) %collective-permute-start.9) | collective-permute-done | bytes 204832 | tf_op jit(solution)/shard_map/ppermute | solution.py:32
  89.7 0.6 stacked.3.refs_0_
  90.5 0.3 collective-permute-start.14
  90.8 0.7 copy-done.4
  91.5 0.5 collective-permute-start.15
  92.7 1.7 concatenate.7.refs_0_
  94.4 1.4 collective-permute-start.18
  95.8 31.9 %collective-permute-done.14.refs_0_ = bf16[160,5120]{1,0:T(8,128)(2,1)S(1)} collective-permute-done((bf16[160,5120]{1,0:T(8,128)(2,1)S(1)}, bf16[160,5120]{1,0:T(8,128)(2,1)S(1)}, u32[]{:S(2)}, u32[]{:S(2)}) %collective-permute-start.14) | collective-permute-done | bytes 1638432 | tf_op jit(solution)/shard_map/ppermute | solution.py:32
  127.6 2.5 collective-permute-done.15.refs_1_
  130.2 1.8 copy-done
  132.0 1.0 slice.6
  133.0 1.2 copy-done.8
  134.2 0.9 slice.7
  135.1 1.5 collective-permute-start.17
  136.6 1.3 collective-permute-start.20
  137.9 15.6 %collective-permute-done.16.refs_3_ = bf16[80,5120]{1,0:T(8,128)(2,1)} collective-permute-done((bf16[80,5120]{1,0:T(8,128)(2,1)}, bf16[80,5120]{1,0:T(8,128)(2,1)}, u32[]{:S(2)}, u32[]{:S(2)}) %collective-permute-start.16) | collective-permute-done | bytes 819232 | tf_op jit(solution)/shard_map/ppermute | solution.py:32
  153.5 2.2 collective-permute-done.17.refs_4_
  155.7 2.0 copy-done.1
  157.6 1.4 copy-done.5
  159.1 1.4 copy-done.9
  160.5 1.4 copy-done.11
  161.9 6.4 %hidden.1.refs_1_.refs_0_ = f32[640,256]{1,0:T(8,128)S(1)} custom-call(s32[1]{0:T(128)} %bitcast.5.z_ref, bf16[160,5120]{1,0:T(8,128)(2,1)S(1)} %copy-done.5, bf16[160,5120]{1,0:T(8,128)(2,1)S(1)} %copy-done.9, bf16[160,5120]{1,0:T(8,128)(2,1)S(1)} %copy-done.11, bf16[80,5120]{1,0:T(8,128)(2,1)} %collective-permute-done.16.refs_3_, ...), custom_call_target="tpu_custom_call" | custom-call | flops 1 | bytes 1 | tf_op jit(solution)/shard_map/hidden/pallas_call | solution.py:138
  168.4 1.8 collective-permute-start.19
  170.1 4.5 %collective-permute-done.19.refs_1_ = f32[120,5120]{1,0:T(8,128)S(1)} collective-permute-done((f32[120,5120]{1,0:T(8,128)}, f32[120,5120]{1,0:T(8,128)S(1)}, u32[]{:S(2)}, u32[]{:S(2)}) %collective-permute-start.19) | collective-permute-done | bytes 2457632 | tf_op jit(solution)/shard_map/ppermute | solution.py:32
  174.7 0.8 copy-done.6
  175.5 1.4 copy-done.12
  176.9 1.4 copy-done.14
  178.4 2.0 copy-done.2
  180.3 1.1 copy-done.7
  181.4 2.9 %copy-done.19 = bf16[640,5120]{1,0:T(8,128)(2,1)S(1)} copy-done((bf16[640,5120]{1,0:T(8,128)(2,1)S(1)}, bf16[640,5120]{1,0:T(8,128)(2,1)}, u32[]{:S(2)}) %copy-start.19) | copy-done | bytes 6553624
  184.3 9.3 %gate_grads.1 = (f32[112,5120]{1,0:T(8,128)S(1)}, f32[112,5120]{1,0:T(8,128)S(1)}) custom-call(bf16[640,5120]{1,0:T(8,128)(2,1)S(1)} %copy-done.19, bf16[336,5120]{1,0:T(8,128)(2,1)S(1)} %held.13.refs_5_.refs_1_.my_params.my_up, bf16[336,5120]{1,0:T(8,128)(2,1)S(1)} %copy-done.2, bf16[336,5120]{1,0:T(8,128)(2,1)S(1)} %held.13.refs_5_.refs_1_.my_params.my_up, ...), custom_call_target="tpu_custom_call" | custom-call | flops 1 | bytes 1 | tf_op jit(solution)/shard_map/gate_grads/pallas_call | solution.py:209
  193.6 0.5 collective-permute-start.21
  194.0 4.1 %collective-permute-done.21 = f32[112,5120]{1,0:T(8,128)S(1)} collective-permute-done((f32[112,5120]{1,0:T(8,128)S(1)}, f32[112,5120]{1,0:T(8,128)S(1)}, u32[]{:S(2)}, u32[]{:S(2)}) %collective-permute-start.21) | collective-permute-done | bytes 2293792 | tf_op jit(solution)/shard_map/ppermute | solution.py:32
  198.1 2.5 multiply_reduce_fusion
  200.6 1.9 collective-permute-start.24
  203.3 11.3 %psum.14 = f32[]{:T(128)} all-reduce(f32[]{:T(128)} %get-tuple-element.18), channel_id=1, replica_groups=mesh['x_lo'=2,'core'=2,'z'=8,'x_hi'=2,'y'=4] {'z'}, use_global_device_ids=true, to_apply=%region_1.2 | all-reduce | flops 1 | bytes 8 | tf_op jit(solution)/shard_map/psum | solution.py:338
  214.6 6.9 %psum.15 = f32[]{:T(128)} all-reduce(f32[]{:T(128)} %psum.14), channel_id=1, replica_groups=mesh['x_lo'=2,'core'=2,'z'=8,'x_hi'=2,'y'=4] {'y'}, use_global_device_ids=true, to_apply=%region_2.3 | all-reduce | flops 1 | bytes 8 | tf_op jit(solution)/shard_map/psum | solution.py:338
  221.5 10.6 %collective-permute-start.22 = (f32[]{:T(128)}, f32[]{:T(128)}, u32[]{:S(2)}, u32[]{:S(2)}) collective-permute-start(f32[]{:T(128)} %psum.15), channel_id=1, source_target_pairs={{0,0},{64,4},{4,64},{68,68},{1,1},{65,5},{5,65},{69,69},{2,2},{66,... | collective-permute-start | bytes 20 | tf_op jit(solution)/shard_map/ppermute | solution.py:37
  232.1 13.7 %collective-permute-start.23 = (f32[]{:T(128)}, f32[]{:T(128)}, u32[]{:S(2)}, u32[]{:S(2)}) collective-permute-start(f32[]{:T(128)} %psum.15), channel_id=1, source_target_pairs={{64,0},{0,4},{68,64},{4,68},{65,1},{1,5},{69,65},{5,69},{66,2},{2,... | collective-permute-start | bytes 20 | tf_op jit(solution)/shard_map/ppermute | solution.py:295
  245.9 1.1 collective-permute-done.23
  248.1 1.7 copy-done.15
  249.8 1.6 copy-done.16
  251.5 6.4 %updated.1 = (f32[112,5120]{1,0:T(8,128)}, f32[112,5120]{1,0:T(8,128)}, f32[1]{0:T(128)}) custom-call(f32[1]{0:T(128)} %bitcast.8.factor, s32[1]{0:T(128)} %bitcast.9.which, f32[1]{0:T(128)} %mul.11.kept_weight, f32[112,5120]{1,0:T(8,128)S(1)} %bitcast.19, f32[112,5120]{1,0:T(8,128)} %collective-permute-done.24.grad, f32[120,5120]{1,0:T(8,128)} %held.16.refs_0_, ...), custom_call_target="tpu_custom_call" | custom-call | tf_op jit(solution)/shard_map/updated/pallas_call | solution.py:269
  (71 shorter events, 0.6 us)
Async XLA Ops:
  7.2 171.2 %all-gather.2.cloned.1.call-start = ((), (), s32[]{:S(2)}) async-start(), calls=%async_computation | async-start | bytes 7372800 | tf_op jit(solution)/shard_map/all_gather | solution.py:312
  7.2 10.6 %copy-start.28 = (bf16[112,5120]{1,0:T(8,128)(2,1)S(1)}, bf16[112,5120]{1,0:T(8,128)(2,1)}, u32[]{:S(2)}) copy-start(bf16[112,5120]{1,0:T(8,128)(2,1)} %param.16) | copy-start | bytes 3440644
  7.2 10.6 %copy-start.29 = (bf16[112,5120]{1,0:T(8,128)(2,1)S(1)}, bf16[112,5120]{1,0:T(8,128)(2,1)}, u32[]{:S(2)}) copy-start(bf16[112,5120]{1,0:T(8,128)(2,1)} %param.15) | copy-start | bytes 3440644
  7.2 10.9 %collective-permute-start.1 = (bf16[20,5120]{1,0:T(8,128)(2,1)}, bf16[20,5120]{1,0:T(8,128)(2,1)S(1)}, u32[]{:S(2)}, u32[]{:S(2)}) collective-permute-start(bf16[20,5120]{1,0:T(8,128)(2,1)} %bitcast.23), channel_id=1, source_target_pairs={{0,0},{64,4},{4,64},{68,68},{1,1},{65,5},{5,65},{69,69},{2,2},{66,... | collective-permute-start | bytes 614408 | tf_op jit(solution)/shard_map/ppermute | solution.py:37
  13.4 10.4 %collective-permute-start = (bf16[20,5120]{1,0:T(8,128)(2,1)}, bf16[20,5120]{1,0:T(8,128)(2,1)S(1)}, u32[]{:S(2)}, u32[]{:S(2)}) collective-permute-start(bf16[20,5120]{1,0:T(8,128)(2,1)} %bitcast.24), channel_id=1, source_target_pairs={{0,0},{64,4},{4,64},{68,68},{1,1},{65,5},{5,65},{69,69},{2,2},{66,... | collective-permute-start | bytes 614408 | tf_op jit(solution)/shard_map/ppermute | solution.py:37
  18.1 14.9 %copy-start.20 = (bf16[20,5120]{1,0:T(8,128)(2,1)}, bf16[20,5120]{1,0:T(8,128)(2,1)S(1)}, u32[]{:S(2)}) copy-start(bf16[20,5120]{1,0:T(8,128)(2,1)S(1)} %collective-permute-done.1.refs_1_.refs_0_) | copy-start | bytes 614404
  18.1 10.0 %collective-permute-start.5 = (bf16[20,5120]{1,0:T(8,128)(2,1)S(1)}, bf16[20,5120]{1,0:T(8,128)(2,1)S(1)}, u32[]{:S(2)}, u32[]{:S(2)}) collective-permute-start(bf16[20,5120]{1,0:T(8,128)(2,1)S(1)} %collective-permute-done.1.refs_1_.refs_0_), channel_id=1, source_target_pairs={{8,0},{16,8},{24,16},{32,24},{40,32},{48,40},{56,48},{0,56},{9,1},... | collective-permute-start | bytes 614408 | tf_op jit(solution)/shard_map/ppermute | solution.py:32
  23.8 6.7 %collective-permute-start.6 = (bf16[20,5120]{1,0:T(8,128)(2,1)S(1)}, bf16[20,5120]{1,0:T(8,128)(2,1)S(1)}, u32[]{:S(2)}, u32[]{:S(2)}) collective-permute-start(bf16[20,5120]{1,0:T(8,128)(2,1)S(1)} %collective-permute-done.1.refs_1_.refs_0_), channel_id=1, source_target_pairs={{56,0},{0,8},{8,16},{16,24},{24,32},{32,40},{40,48},{48,56},{57,1}... | collective-permute-start | bytes 614408 | tf_op jit(solution)/shard_map/ppermute | solution.py:32
  23.8 9.2 %collective-permute-start.4 = (bf16[20,5120]{1,0:T(8,128)(2,1)S(1)}, bf16[20,5120]{1,0:T(8,128)(2,1)S(1)}, u32[]{:S(2)}, u32[]{:S(2)}) collective-permute-start(bf16[20,5120]{1,0:T(8,128)(2,1)S(1)} %held.9.refs_0_), channel_id=1, source_target_pairs={{2,0},{3,1},{0,2},{1,3},{6,4},{7,5},{4,6},{5,7},{10,8},{11,9},{8,1... | collective-permute-start | bytes 614408 | tf_op jit(solution)/shard_map/ppermute | solution.py:32
  26.7 9.4 %collective-permute-start.2 = (bf16[20,5120]{1,0:T(8,128)(2,1)S(1)}, bf16[20,5120]{1,0:T(8,128)(2,1)S(1)}, u32[]{:S(2)}, u32[]{:S(2)}) collective-permute-start(bf16[20,5120]{1,0:T(8,128)(2,1)S(1)} %held.9.refs_0_), channel_id=1, source_target_pairs={{1,0},{2,1},{3,2},{0,3},{5,4},{6,5},{7,6},{4,7},{9,8},{10,9},{11,1... | collective-permute-start | bytes 614408 | tf_op jit(solution)/shard_map/ppermute | solution.py:32
  27.5 8.9 %collective-permute-start.3 = (bf16[20,5120]{1,0:T(8,128)(2,1)S(1)}, bf16[20,5120]{1,0:T(8,128)(2,1)S(1)}, u32[]{:S(2)}, u32[]{:S(2)}) collective-permute-start(bf16[20,5120]{1,0:T(8,128)(2,1)S(1)} %held.9.refs_0_), channel_id=1, source_target_pairs={{3,0},{0,1},{1,2},{2,3},{7,4},{4,5},{5,6},{6,7},{11,8},{8,9},{9,10... | collective-permute-start | bytes 614408 | tf_op jit(solution)/shard_map/ppermute | solution.py:32
  28.2 7.9 %copy-start.23 = (bf16[20,5120]{1,0:T(8,128)(2,1)}, bf16[20,5120]{1,0:T(8,128)(2,1)S(1)}, u32[]{:S(2)}) copy-start(bf16[20,5120]{1,0:T(8,128)(2,1)S(1)} %collective-permute-done.5.refs_1_) | copy-start | bytes 614404
  30.4 5.6 %copy-start.25 = (bf16[20,5120]{1,0:T(8,128)(2,1)}, bf16[20,5120]{1,0:T(8,128)(2,1)S(1)}, u32[]{:S(2)}) copy-start(bf16[20,5120]{1,0:T(8,128)(2,1)S(1)} %collective-permute-done.6.refs_2_.refs_7_) | copy-start | bytes 614404
  36.7 0.9 copy-start.17
  37.6 0.9 copy-start.21
  38.6 6.5 %copy-start.24 = (bf16[20,5120]{1,0:T(8,128)(2,1)S(1)}, bf16[20,5120]{1,0:T(8,128)(2,1)}, u32[]{:S(2)}) copy-start(bf16[20,5120]{1,0:T(8,128)(2,1)} %copy-done.23) | copy-start | bytes 614404
  38.6 9.5 %copy-start.26 = (bf16[20,5120]{1,0:T(8,128)(2,1)S(1)}, bf16[20,5120]{1,0:T(8,128)(2,1)}, u32[]{:S(2)}) copy-start(bf16[20,5120]{1,0:T(8,128)(2,1)} %copy-done.25) | copy-start | bytes 614404
  38.6 51.2 %copy-start.22 = (bf16[20,5120]{1,0:T(8,128)(2,1)S(1)}, bf16[20,5120]{1,0:T(8,128)(2,1)}, u32[]{:S(2)}) copy-start(bf16[20,5120]{1,0:T(8,128)(2,1)} %copy-done.20) | copy-start | bytes 614404
  38.6 1.8 copy-start.3
  40.4 49.9 %copy-start.18 = (bf16[80,5120]{1,0:T(8,128)(2,1)S(1)}, bf16[80,5120]{1,0:T(8,128)(2,1)}, u32[]{:S(2)}) copy-start(bf16[80,5120]{1,0:T(8,128)(2,1)} %copy-done.17) | copy-start | bytes 2457604
  40.4 49.9 %collective-permute-start.7 = (bf16[336,5120]{1,0:T(8,128)(2,1)}, bf16[336,5120]{1,0:T(8,128)(2,1)S(1)}, u32[]{:S(2)}, u32[]{:S(2)}) collective-permute-start(bf16[336,5120]{1,0:T(8,128)(2,1)} %copy-done.3), channel_id=1, source_target_pairs={{0,0},{64,4},{4,64},{68,68},{1,1},{65,5},{5,65},{69,69},{2,2},{66,... | collective-permute-start | bytes 10321928 | tf_op jit(solution)/shard_map/ppermute | solution.py:37
  45.1 13.7 %collective-permute-start.8 = (bf16[20,5120]{1,0:T(8,128)(2,1)S(1)}, bf16[20,5120]{1,0:T(8,128)(2,1)S(1)}, u32[]{:S(2)}, u32[]{:S(2)}) collective-permute-start(bf16[20,5120]{1,0:T(8,128)(2,1)S(1)} %copy-done.24), channel_id=1, source_target_pairs={{8,0},{16,8},{24,16},{32,24},{40,32},{48,40},{56,48},{0,56},{9,1},... | collective-permute-start | bytes 614408 | tf_op jit(solution)/shard_map/ppermute | solution.py:32
  48.1 14.2 %collective-permute-start.11 = (bf16[20,5120]{1,0:T(8,128)(2,1)S(1)}, bf16[20,5120]{1,0:T(8,128)(2,1)S(1)}, u32[]{:S(2)}, u32[]{:S(2)}) collective-permute-start(bf16[20,5120]{1,0:T(8,128)(2,1)S(1)} %copy-done.26), channel_id=1, source_target_pairs={{56,0},{0,8},{8,16},{16,24},{24,32},{32,40},{40,48},{48,56},{57,1}... | collective-permute-start | bytes 614408 | tf_op jit(solution)/shard_map/ppermute | solution.py:32
  58.8 17.4 %collective-permute-start.10 = (bf16[20,5120]{1,0:T(8,128)(2,1)S(1)}, bf16[20,5120]{1,0:T(8,128)(2,1)S(1)}, u32[]{:S(2)}, u32[]{:S(2)}) collective-permute-start(bf16[20,5120]{1,0:T(8,128)(2,1)S(1)} %collective-permute-done.8.refs_2_), channel_id=1, source_target_pairs={{16,0},{24,8},{32,16},{40,24},{48,32},{56,40},{0,48},{8,56},{17,1}... | collective-permute-start | bytes 614408 | tf_op jit(solution)/shard_map/ppermute | solution.py:32
  58.8 31.0 %collective-permute-start.9 = (bf16[20,5120]{1,0:T(8,128)(2,1)S(1)}, bf16[20,5120]{1,0:T(8,128)(2,1)S(1)}, u32[]{:S(2)}, u32[]{:S(2)}) collective-permute-start(bf16[20,5120]{1,0:T(8,128)(2,1)S(1)} %collective-permute-done.8.refs_2_), channel_id=1, source_target_pairs={{8,0},{16,8},{24,16},{32,24},{40,32},{48,40},{56,48},{0,56},{9,1},... | collective-permute-start | bytes 614408 | tf_op jit(solution)/shard_map/ppermute | solution.py:32
  62.3 27.5 %collective-permute-start.12 = (bf16[20,5120]{1,0:T(8,128)(2,1)S(1)}, bf16[20,5120]{1,0:T(8,128)(2,1)S(1)}, u32[]{:S(2)}, u32[]{:S(2)}) collective-permute-start(bf16[20,5120]{1,0:T(8,128)(2,1)S(1)} %collective-permute-done.11.refs_6_), channel_id=1, source_target_pairs={{56,0},{0,8},{8,16},{16,24},{24,32},{32,40},{40,48},{48,56},{57,1}... | collective-permute-start | bytes 614408 | tf_op jit(solution)/shard_map/ppermute | solution.py:32
  90.3 1.2 copy-start.4
  90.4 2.3 copy-start.27
  90.4 39.8 %collective-permute-start.13 = (bf16[336,5120]{1,0:T(8,128)(2,1)S(1)}, bf16[336,5120]{1,0:T(8,128)(2,1)S(1)}, u32[]{:S(2)}, u32[]{:S(2)}) collective-permute-start(bf16[336,5120]{1,0:T(8,128)(2,1)S(1)} %held.13.refs_5_.refs_1_.my_params.my_up), channel_id=1, source_target_pairs={{64,0},{0,64},{65,1},{1,65},{66,2},{2,66},{67,3},{3,67},{68,4},{4,... | collective-permute-start | bytes 10321928 | tf_op jit(solution)/shard_map/ppermute | solution.py:32
  90.5 37.1 %collective-permute-start.14 = (bf16[160,5120]{1,0:T(8,128)(2,1)S(1)}, bf16[160,5120]{1,0:T(8,128)(2,1)S(1)}, u32[]{:S(2)}, u32[]{:S(2)}) collective-permute-start(bf16[160,5120]{1,0:T(8,128)(2,1)S(1)} %held.12.refs_1_.refs_0_), channel_id=1, source_target_pairs={{1,0},{2,1},{3,2},{0,3},{5,4},{6,5},{7,6},{4,7},{9,8},{10,9},{11,1... | collective-permute-start | bytes 4915208 | tf_op jit(solution)/shard_map/ppermute | solution.py:32
  91.5 38.6 %collective-permute-start.15 = (bf16[160,5120]{1,0:T(8,128)(2,1)S(1)}, bf16[160,5120]{1,0:T(8,128)(2,1)S(1)}, u32[]{:S(2)}, u32[]{:S(2)}) collective-permute-start(bf16[160,5120]{1,0:T(8,128)(2,1)S(1)} %held.12.refs_1_.refs_0_), channel_id=1, source_target_pairs={{3,0},{0,1},{1,2},{2,3},{7,4},{4,5},{5,6},{6,7},{11,8},{8,9},{9,10... | collective-permute-start | bytes 4915208 | tf_op jit(solution)/shard_map/ppermute | solution.py:32
  94.4 74.0 %collective-permute-start.18 = (f32[120,5120]{1,0:T(8,128)}, f32[120,5120]{1,0:T(8,128)}, u32[]{:S(2)}, u32[]{:S(2)}) collective-permute-start(f32[120,5120]{1,0:T(8,128)} %held.15), channel_id=1, source_target_pairs={{128,0},{0,128},{129,1},{1,129},{130,2},{2,130},{131,3},{3,131},{1... | collective-permute-start | bytes 7372808 | tf_op jit(solution)/shard_map/ppermute | solution.py:32
  130.2 1.8 copy-start
  132.0 2.2 copy-start.10
  133.0 1.2 copy-start.8
  134.2 19.3 %collective-permute-start.16 = (bf16[80,5120]{1,0:T(8,128)(2,1)}, bf16[80,5120]{1,0:T(8,128)(2,1)}, u32[]{:S(2)}, u32[]{:S(2)}) collective-permute-start(bf16[80,5120]{1,0:T(8,128)(2,1)} %slice.6), channel_id=1, source_target_pairs={{1,0},{2,1},{3,2},{0,3},{5,4},{6,5},{7,6},{4,7},{9,8},{10,9},{11,1... | collective-permute-start | bytes 2457608 | tf_op jit(solution)/shard_map/ppermute | solution.py:32
  135.1 20.5 %collective-permute-start.17 = (bf16[80,5120]{1,0:T(8,128)(2,1)}, bf16[80,5120]{1,0:T(8,128)(2,1)}, u32[]{:S(2)}, u32[]{:S(2)}) collective-permute-start(bf16[80,5120]{1,0:T(8,128)(2,1)} %slice.7), channel_id=1, source_target_pairs={{3,0},{0,1},{1,2},{2,3},{7,4},{4,5},{5,6},{6,7},{11,8},{8,9},{9,10... | collective-permute-start | bytes 2457608 | tf_op jit(solution)/shard_map/ppermute | solution.py:32
  136.6 33.5 %collective-permute-start.20 = (f32[120,5120]{1,0:T(8,128)}, f32[120,5120]{1,0:T(8,128)S(1)}, u32[]{:S(2)}, u32[]{:S(2)}) collective-permute-start(f32[120,5120]{1,0:T(8,128)} %held.15), channel_id=1, source_target_pairs={{64,0},{0,64},{65,1},{1,65},{66,2},{2,66},{67,3},{3,67},{68,4},{4,... | collective-permute-start | bytes 7372808 | tf_op jit(solution)/shard_map/ppermute | solution.py:32
  155.7 2.0 copy-start.1
  157.6 1.4 copy-start.5
  159.1 1.4 copy-start.9
  160.5 1.4 copy-start.11
  168.4 6.3 %collective-permute-start.19 = (f32[120,5120]{1,0:T(8,128)}, f32[120,5120]{1,0:T(8,128)S(1)}, u32[]{:S(2)}, u32[]{:S(2)}) collective-permute-start(f32[120,5120]{1,0:T(8,128)} %held.16.refs_0_), channel_id=1, source_target_pairs={{64,0},{0,64},{65,1},{1,65},{66,2},{2,66},{67,3},{3,67},{68,4},{4,... | collective-permute-start | bytes 7372808 | tf_op jit(solution)/shard_map/ppermute | solution.py:32
  174.7 0.8 copy-start.6
  175.5 1.4 copy-start.12
  176.9 1.4 copy-start.14
  178.3 2.0 copy-start.2
  180.3 1.1 copy-start.7
  181.4 2.9 %copy-start.19 = (bf16[640,5120]{1,0:T(8,128)(2,1)S(1)}, bf16[640,5120]{1,0:T(8,128)(2,1)}, u32[]{:S(2)}) copy-start(bf16[640,5120]{1,0:T(8,128)(2,1)} %all-gather.2.cloned.1.call-done.x_ref) | copy-start | bytes 19660804
  193.6 4.5 %collective-permute-start.21 = (f32[112,5120]{1,0:T(8,128)S(1)}, f32[112,5120]{1,0:T(8,128)S(1)}, u32[]{:S(2)}, u32[]{:S(2)}) collective-permute-start(f32[112,5120]{1,0:T(8,128)S(1)} %get-tuple-element.14), channel_id=1, source_target_pairs={{64,0},{0,64},{65,1},{1,65},{66,2},{2,66},{67,3},{3,67},{68,4},{4,... | collective-permute-start | bytes 6881288 | tf_op jit(solution)/shard_map/ppermute | solution.py:32
  198.1 50.0 %copy-start.13 = (f32[120,5120]{1,0:T(8,128)S(1)}, f32[120,5120]{1,0:T(8,128)}, u32[]{:S(2)}) copy-start(f32[120,5120]{1,0:T(8,128)} %copy-done.12) | copy-start | bytes 7372804
  200.6 47.5 %collective-permute-start.24 = (f32[112,5120]{1,0:T(8,128)}, f32[112,5120]{1,0:T(8,128)}, u32[]{:S(2)}, u32[]{:S(2)}) collective-permute-start(f32[112,5120]{1,0:T(8,128)} %get-tuple-element.19), channel_id=1, source_target_pairs={{0,0},{64,4},{4,64},{68,68},{1,1},{65,5},{5,65},{69,69},{2,2},{66,... | collective-permute-start | bytes 6881288 | tf_op jit(solution)/shard_map/ppermute | solution.py:37
  221.5 24.4 %collective-permute-start.22 = (f32[]{:T(128)}, f32[]{:T(128)}, u32[]{:S(2)}, u32[]{:S(2)}) collective-permute-start(f32[]{:T(128)} %psum.15), channel_id=1, source_target_pairs={{0,0},{64,4},{4,64},{68,68},{1,1},{65,5},{5,65},{69,69},{2,2},{66,... | collective-permute-start | bytes 20 | tf_op jit(solution)/shard_map/ppermute | solution.py:37
  232.1 14.8 %collective-permute-start.23 = (f32[]{:T(128)}, f32[]{:T(128)}, u32[]{:S(2)}, u32[]{:S(2)}) collective-permute-start(f32[]{:T(128)} %psum.15), channel_id=1, source_target_pairs={{64,0},{0,4},{68,64},{4,68},{65,1},{1,5},{69,65},{5,69},{66,2},{2,... | collective-permute-start | bytes 20 | tf_op jit(solution)/shard_map/ppermute | solution.py:295
  248.1 1.7 copy-start.15
  249.8 1.6 copy-start.16
Sparse Core Ops, SparseCore 0:
  37.7 91.2 all-gather.1

commit v7 on v5

--- a/solution.py
+++ b/solution.py
@@ -23,6 +23,7 @@
 ROWS = 112
 HALF = 128
 CUT = 64
+NO_COST = pl.CostEstimate(flops=1, bytes_accessed=1, transcendentals=0)
 BLOCK = 1024
 
 
@@ -144,9 +145,7 @@
             pltpu.VMEM((2 * HALF, BLOCK), jnp.bfloat16),
         ],
         compiler_params=params_of(16),
-        cost_estimate=pl.CostEstimate(
-            flops=2 * count * D * 2 * HALF, bytes_accessed=2 * count * D + 2**22, transcendentals=0
-        ),
+        cost_estimate=NO_COST,
         name="hidden",
     )(*parts, mine, theirs)
 
@@ -211,39 +210,80 @@
             pltpu.VMEM((2 * HALF, BLOCK), jnp.bfloat16),
         ],
         compiler_params=params_of(36),
-        cost_estimate=pl.CostEstimate(
-            flops=2 * count * D * 768, bytes_accessed=2 * count * D + 2**23, transcendentals=0
-        ),
+        cost_estimate=NO_COST,
         name="gate_grads",
     )(*parts, mine, theirs, mine, theirs, hidden)
 
 
-def updated_kernel(factor, which, numerator, grad, *refs):
-    *parts, kept_ref, new_ref = refs
+def updated_kernel(factor, which, kept_weight, numerator, grad, *refs):
+    two_top, two_rest, one_top, one_rest, other = refs[:5]
+    kept_ref, new_ref, weight_ref, part, sems = refs[5:]
+    received = (
+        (two_top, two_rest),
+        (one_top, one_rest),
+        (other.at[:CUT, :], other.at[CUT:, :]),
+    )
+    at = pl.program_id(0)
+    blocks = D // BLOCK
+
+    def copies(sources, block):
+        columns = pl.ds(block * BLOCK, BLOCK)
+        targets = (part.at[:CUT, columns], part.at[CUT:, columns])
+        return [
+            pltpu.make_async_copy(source.at[:, columns], target, sems.at[half, block])
+            for half, (source, target) in enumerate(zip(sources, targets))
+        ]
+
+    @pl.when(at == 0)
+    def _():
+        for place, sources in enumerate(received):
+
+            @pl.when(which[0] == place)
+            def _():
+                for block in range(blocks):
+                    for copy in copies(sources, block):
+                        copy.start()
+
     kept = 0.5 * (numerator[...] - factor[0] * grad[...])
     kept_ref[...] = kept
-    for at in range(3):
-
-        @pl.when(which[0] == at)
+    for block in range(blocks):
+
+        @pl.when(at == block)
         def _():
-            new_ref[:CUT, :] = kept[:CUT] + parts[2 * at][...]
-            new_ref[CUT:, :] = kept[CUT:] + parts[2 * at + 1][: ROWS - CUT, :]
-
-
-def updated(numerator, grad, factor, which, received):
+            for copy in copies(received[0], block):
+                copy.wait()
+            new_ref[...] = kept + part[:ROWS, block * BLOCK : (block + 1) * BLOCK]
+
+    @pl.when(at == 0)
+    def _():
+        weight_ref[0] = kept_weight[0] + jnp.max(part[ROWS:, :128])
+
+
+def updated(numerator, grad, kept_weight, factor, which, two_before, one_before, other):
     own = pl.BlockSpec((ROWS, BLOCK), lambda at: (0, at))
     scalar = pl.BlockSpec(memory_space=pltpu.SMEM)
-    more = [part for parts in received for part in parts]
+    anywhere = pl.BlockSpec(memory_space=pl.ANY)
+    blocks = D // BLOCK
     return pl.pallas_call(
         updated_kernel,
-        grid=(D // BLOCK,),
-        in_specs=[scalar, scalar, own, own]
-        + [pl.BlockSpec((part.shape[0], BLOCK), lambda at: (0, at)) for part in more],
-        out_specs=[own, own],
-        out_shape=[jax.ShapeDtypeStruct((ROWS, D), jnp.float32)] * 2,
+        grid=(blocks,),
+        in_specs=[scalar, scalar, scalar, own, own] + [anywhere] * 5,
+        out_specs=[own, own, scalar],
+        out_shape=[
+            jax.ShapeDtypeStruct((ROWS, D), jnp.float32),
+            jax.ShapeDtypeStruct((ROWS, D), jnp.float32),
+            jax.ShapeDtypeStruct((1,), jnp.float32),
+        ],
+        scratch_shapes=[
+            pltpu.VMEM(other.shape, jnp.float32),
+            pltpu.SemaphoreType.DMA((2, blocks)),
+        ],
         compiler_params=params_of(16),
         name="updated",
-    )(jnp.reshape(factor, (1,)), jnp.reshape(which, (1,)), numerator, grad, *more)
+    )(
+        jnp.reshape(factor, (1,)), jnp.reshape(which, (1,)), kept_weight,
+        numerator, grad, *two_before, *one_before, other,
+    )
 
 
 def crossed(value):
@@ -267,54 +307,53 @@
     ring = {0: rows_grad, 1: shifted(rows_grad, "z", 1), 7: shifted(rows_grad, "z", 7)}
     mine = transposed(held(weights, rows_grad))
     ring[2], ring[6] = shifted(ring[1], "z", 1), shifted(ring[7], "z", 7)
-    near[3] = held(near[3], ring[2], ring[6])
+    ring[2], ring[6] = held((ring[2], ring[6]), *near[1:])
+    ring[3], ring[5] = shifted(ring[2], "z", 1), shifted(ring[6], "z", 7)
+    ring[4] = shifted(ring[2], "z", 2)
+    near[3] = held(near[3], ring[3], ring[4], ring[5])
     blocks = {0: stacked(near)}
     for steps in (1, 7):
         blocks[steps] = shifted(blocks[0], "z", steps)
-    ring[3], ring[5] = shifted(ring[2], "z", 1), shifted(ring[6], "z", 7)
-    ring[4] = shifted(ring[2], "z", 2)
     column = stacked([ring[steps] for steps in range(8)])
 
     following, before = shifted(column, "y", 1), shifted(column, "y", 3)
     blocks[1], blocks[7] = held((blocks[1], blocks[7]), column)
     blocks[2], blocks[6] = shifted(blocks[1], "z", 1), shifted(blocks[7], "z", 7)
-    blocks[2], blocks[6] = held((blocks[2], blocks[6]))
+    mine = held(mine, blocks[1], blocks[7])
+    theirs = shifted(mine, "core", 1)
+    stale = jnp.concatenate([stale_num[0], jnp.broadcast_to(stale_weight, (8, D))], axis=0)
+    blocks[2], blocks[6] = held((blocks[2], blocks[6]), theirs)
+    two_before = [shifted(held(stale[:CUT], theirs), "x_lo", 1)]
+    two_before.append(shifted(held(stale[CUT:], two_before[0]), "x_lo", 1))
     blocks[3], blocks[5] = shifted(blocks[2], "z", 1), shifted(blocks[6], "z", 7)
     following, before = held((following, before), blocks[2], blocks[6])
-    weight_rows = jnp.broadcast_to(stale_weight, (8, D))
-    stale = [stale_num[0, :CUT], jnp.concatenate([stale_num[0, CUT:], weight_rows], axis=0)]
-    stale[0] = held(stale[0], mine)
-    two_before = [shifted(stale[0], "x_lo", 1)]
-    stale[1] = held(stale[1], two_before[0])
-    two_before.append(shifted(stale[1], "x_lo", 1))
-    mine = held(mine, following, before)
-    theirs = shifted(mine, "core", 1)
     half = column.shape[0] // 2
     far = [shifted(following[:half], "y", 1), shifted(before[half:], "y", 3)]
-    blocks[3], blocks[5] = held((blocks[3], blocks[5]), following, before)
+    blocks[3], blocks[5] = held((blocks[3], blocks[5]), following, before, two_before[0])
     cut = 48
     last = [shifted(blocks[3][:cut], "z", 1), shifted(blocks[5][cut:], "z", 7)]
 
     hidden = hidden_of([column, following, before, *far], mine, theirs)
     parts = [blocks[steps] for steps in (0, 1, 2, 3)] + last + [blocks[steps] for steps in (5, 6, 7)]
-    first_hop = shifted(two_before[0], "core", 1)
-    stale_hop = [shifted(part, "core", 1) for part in stale]
-    hidden = held(hidden, first_hop, *stale_hop)
+    hidden = held(hidden, two_before[1])
     own_grad, other_grad = gate_grads(parts, mine, theirs, hidden)
+    two_before = held(tuple(two_before), own_grad)
+    one_before = [shifted(part, "core", 1) for part in two_before]
+    stale_hop = shifted(held(stale, own_grad), "core", 1)
     gate_grad = own_grad + shifted(other_grad, "core", 1)
     norm_sq = jnp.sum(gate_grad * gate_grad)
     gate_grad = transposed(gate_grad)
-    norm_sq = lax.psum(norm_sq, "z")
-    two_before[1] = held(two_before[1], jnp.reshape(norm_sq, (1,)))
-    received = [two_before, [first_hop, shifted(two_before[1], "core", 1)], stale_hop]
-    norm_sq = lax.psum(norm_sq, "y")
+    for axes in ("z", "y"):
+        norm_sq = lax.psum(norm_sq, axes)
+    norm_sq = held(jnp.reshape(norm_sq, (1,)), *one_before, stale_hop)[0]
     norm_sq = transposed(norm_sq) + crossed(norm_sq)
 
     clip_factor = jnp.minimum(1.0, MAX_NORM / jnp.sqrt(norm_sq + eps))
+    kept_weight = 0.5 * push_weight
     which = jnp.where(step[0] % 2 == 1, 0, 1 + lax.axis_index("core"))
-    kept_half, new_num = updated(numerator, gate_grad, rate * clip_factor, which, received)
-    kept_weight = 0.5 * push_weight
-    new_weight = kept_weight + jnp.stack([parts[1][-1, :1] for parts in received])[which]
+    kept_half, new_num, new_weight = updated(
+        numerator, gate_grad, kept_weight, rate * clip_factor, which, two_before, one_before, stale_hop
+    )
     return (new_num[None], new_weight, kept_half[None], kept_weight)
 
 

time: 248 us -> 224 us (0.903)
  waiting for transfers between devices: 110 us -> 92.6 us
  local copies, waits for them, and re-layouts: 10.4 us -> 3.69 us
  starting transfers between devices: 70.3 us -> 75.6 us
    ppermute x30 -> x29, waiting for transfers between devices: 103 us -> 84.1 us  [shifted(): return lax.ppermute(value, axis, pairs)]
    ppermute x5, starting transfers between devices: 14.7 us -> 30.8 us  [transposed(): return lax.ppermute(value, ('core', 'x_hi'), pairs)]
    ppermute x30 -> x29, starting transfers between devices: 53.9 us -> 44.7 us  [shifted(): return lax.ppermute(value, axis, pairs)]
    unnamed x20 -> x10, local copies, waits for them, and re-layouts: 5.46 us -> 1.66 us
    slice x3 -> x2, local copies, waits for them, and re-layouts: 2.93 us -> 0.16 us  [the longest x1 0.09 us: shards(): two_before = [shifted(held(stale[:CUT], theirs), 'x_lo', 1)]]
    ppermute x1, waiting for transfers between devices: 0.01 us -> 2.62 us  [crossed(): return lax.ppermute(value, ('core', 'x_hi'), pairs)]
  transfers between devices with their start and end apart: 36 -> 35, of which waited for: 18 -> 20; matrix products, arithmetic and copies ran while one was open for 5% -> 3% of each run, Pallas kernels for 3% -> 3%
where the time goes in v7:
time: 224 us; the launch traced here: 222 us
  waiting for transfers between devices  92.6 us (41%)
  starting transfers between devices  75.6 us (34%)
  Pallas kernels  22.3 us (10%)
  blocking collectives  18 us (8%)
  between operations  5.42 us (2%)
  other arithmetic  4.71 us (2%)
  local copies, waits for them, and re-layouts  3.69 us (2%)
    ppermute x29, waiting for transfers between devices, shifted(): return lax.ppermute(value, axis, pairs)  84.1 us
    ppermute x29, starting transfers between devices, shifted(): return lax.ppermute(value, axis, pairs)  44.7 us
    ppermute x5, starting transfers between devices, transposed(): return lax.ppermute(value, ('core', 'x_hi'), pairs)  30.8 us
    psum x2, blocking collectives, shards(): norm_sq = lax.psum(norm_sq, axes)  18 us
    pallas_call x1, Pallas kernels, gate_grads(): pl.pallas_call(grad_kernel, grid=(D // BLOCK,), in_specs=[pl.BlockSpec((p...  8.87 us
    ppermute x5, waiting for transfers between devices, transposed(): return lax.ppermute(value, ('core', 'x_hi'), pairs)  5.87 us
    pallas_call x1, Pallas kernels, updated(): pl.pallas_call(updated_kernel, grid=(blocks,), in_specs=[scalar, scalar,...  5.76 us
    pallas_call x1, Pallas kernels, hidden_of(): pl.pallas_call(hidden_kernel, grid=(D // BLOCK,), in_specs=[pl.BlockSpec(...  5.64 us
  transfers between devices with their start and end apart: 35, of which 20 were waited for; matrix products, arithmetic and copies ran while one was open for 3% of the time, Pallas kernels for 3%

profile of v7, /device:TPU:1, one launch (start us, length us, event | category | flops | bytes accessed | tf_op | source)
XLA Modules:
  0.0 222.4 jit_solution(11123552078863198734)
XLA Ops:
  0.7 6.2 %collective-permute-start.1 = (bf16[20,5120]{1,0:T(8,128)(2,1)}, bf16[20,5120]{1,0:T(8,128)(2,1)S(1)}, u32[]{:S(2)}, u32[]{:S(2)}) collective-permute-start(bf16[20,5120]{1,0:T(8,128)(2,1)} %bitcast.28), channel_id=1, source_target_pairs={{0,0},{64,4},{4,64},{68,68},{1,1},{65,5},{5,65},{69,69},{2,2},{66,... | collective-permute-start | bytes 614408 | tf_op jit(solution)/shard_map/ppermute | solution.py:38
  6.8 1.9 collective-permute-start
  9.4 1.8 divide_convert_fusion
  11.3 0.3 pad_maximum_fusion.refs_2_.refs_0_
  11.5 4.5 %collective-permute-done.refs_0_ = bf16[20,5120]{1,0:T(8,128)(2,1)S(1)} collective-permute-done((bf16[20,5120]{1,0:T(8,128)(2,1)}, bf16[20,5120]{1,0:T(8,128)(2,1)S(1)}, u32[]{:S(2)}, u32[]{:S(2)}) %collective-permute-start) | collective-permute-done | bytes 204832 | tf_op jit(solution)/shard_map/ppermute | solution.py:38
  16.1 2.6 %collective-permute-start.16 = (bf16[336,5120]{1,0:T(8,128)(2,1)S(1)}, bf16[336,5120]{1,0:T(8,128)(2,1)S(1)}, u32[]{:S(2)}, u32[]{:S(2)}) collective-permute-start(bf16[336,5120]{1,0:T(8,128)(2,1)S(1)} %held.19), channel_id=1, source_target_pairs={{0,0},{64,4},{4,64},{68,68},{1,1},{65,5},{5,65},{69,69},{2,2},{66,... | collective-permute-start | bytes 10321928 | tf_op jit(solution)/shard_map/ppermute | solution.py:38
  18.7 2.8 %collective-permute-start.2 = (bf16[20,5120]{1,0:T(8,128)(2,1)S(1)}, bf16[20,5120]{1,0:T(8,128)(2,1)S(1)}, u32[]{:S(2)}, u32[]{:S(2)}) collective-permute-start(bf16[20,5120]{1,0:T(8,128)(2,1)S(1)} %held.15.refs_0_), channel_id=1, source_target_pairs={{1,0},{2,1},{3,2},{0,3},{5,4},{6,5},{7,6},{4,7},{9,8},{10,9},{11,1... | collective-permute-start | bytes 614408 | tf_op jit(solution)/shard_map/ppermute | solution.py:33
  21.5 5.6 %collective-permute-start.5 = (bf16[20,5120]{1,0:T(8,128)(2,1)S(1)}, bf16[20,5120]{1,0:T(8,128)(2,1)S(1)}, u32[]{:S(2)}, u32[]{:S(2)}) collective-permute-start(bf16[20,5120]{1,0:T(8,128)(2,1)S(1)} %collective-permute-done.1.refs_1_.refs_0_), channel_id=1, source_target_pairs={{8,0},{16,8},{24,16},{32,24},{40,32},{48,40},{56,48},{0,56},{9,1},... | collective-permute-start | bytes 614408 | tf_op jit(solution)/shard_map/ppermute | solution.py:33
  27.1 0.2 collective-permute-done.2.refs_2_.refs_1_
  27.3 1.7 collective-permute-start.4
  29.0 2.5 %collective-permute-done.5.refs_1_ = bf16[20,5120]{1,0:T(8,128)(2,1)S(1)} collective-permute-done((bf16[20,5120]{1,0:T(8,128)(2,1)S(1)}, bf16[20,5120]{1,0:T(8,128)(2,1)S(1)}, u32[]{:S(2)}, u32[]{:S(2)}) %collective-permute-start.5) | collective-permute-done | bytes 204832 | tf_op jit(solution)/shard_map/ppermute | solution.py:33
  31.5 3.1 %collective-permute-start.6 = (bf16[20,5120]{1,0:T(8,128)(2,1)S(1)}, bf16[20,5120]{1,0:T(8,128)(2,1)S(1)}, u32[]{:S(2)}, u32[]{:S(2)}) collective-permute-start(bf16[20,5120]{1,0:T(8,128)(2,1)S(1)} %collective-permute-done.5.refs_1_), channel_id=1, source_target_pairs={{8,0},{16,8},{24,16},{32,24},{40,32},{48,40},{56,48},{0,56},{9,1},... | collective-permute-start | bytes 614408 | tf_op jit(solution)/shard_map/ppermute | solution.py:33
  34.6 0.3 collective-permute-done.7.refs_7_
  34.9 1.1 collective-permute-done.3.refs_3_.refs_2_
  36.0 7.0 %collective-permute-done.6.refs_0_ = bf16[20,5120]{1,0:T(8,128)(2,1)S(1)} collective-permute-done((bf16[20,5120]{1,0:T(8,128)(2,1)S(1)}, bf16[20,5120]{1,0:T(8,128)(2,1)S(1)}, u32[]{:S(2)}, u32[]{:S(2)}) %collective-permute-start.6) | collective-permute-done | bytes 204832 | tf_op jit(solution)/shard_map/ppermute | solution.py:33
  42.9 1.0 collective-permute-done.8.refs_1_
  43.9 2.2 collective-permute-start.9
  46.1 1.1 collective-permute-start.11
  47.2 6.1 %collective-permute-done.10.refs_2_.refs_4_ = bf16[20,5120]{1,0:T(8,128)(2,1)S(1)} collective-permute-done((bf16[20,5120]{1,0:T(8,128)(2,1)S(1)}, bf16[20,5120]{1,0:T(8,128)(2,1)S(1)}, u32[]{:S(2)}, u32[]{:S(2)}) %collective-permute-start.10) | collective-permute-done | bytes 204832 | tf_op jit(solution)/shard_map/ppermute | solution.py:33
  53.3 6.5 %collective-permute-done.9.refs_1_.refs_3_ = bf16[20,5120]{1,0:T(8,128)(2,1)S(1)} collective-permute-done((bf16[20,5120]{1,0:T(8,128)(2,1)S(1)}, bf16[20,5120]{1,0:T(8,128)(2,1)S(1)}, u32[]{:S(2)}, u32[]{:S(2)}) %collective-permute-start.9) | collective-permute-done | bytes 204832 | tf_op jit(solution)/shard_map/ppermute | solution.py:33
  59.8 0.3 stacked.2.refs_0_
  60.2 0.1 collective-permute-start.12
  60.2 1.5 collective-permute-start.13
  61.7 0.6 stacked.3.refs_2_.refs_0_
  62.3 10.9 %collective-permute-done.12.refs_0_ = bf16[80,5120]{1,0:T(8,128)(2,1)S(1)} collective-permute-done((bf16[80,5120]{1,0:T(8,128)(2,1)S(1)}, bf16[80,5120]{1,0:T(8,128)(2,1)S(1)}, u32[]{:S(2)}, u32[]{:S(2)}) %collective-permute-start.12) | collective-permute-done | bytes 819232 | tf_op jit(solution)/shard_map/ppermute | solution.py:33
  73.2 0.1 collective-permute-start.17
  73.3 1.9 collective-permute-start.20
  75.2 0.7 collective-permute-start.14
  75.9 0.8 collective-permute-start.15
  76.7 0.1 slice_bitcast_fusion.refs_0_
  76.8 2.6 %collective-permute-done.17.refs_2_.refs_1_.refs_6_.refs_10_.refs_12_ = bf16[336,5120]{1,0:T(8,128)(2,1)S(1)} collective-permute-done((bf16[336,5120]{1,0:T(8,128)(2,1)S(1)}, bf16[336,5120]{1,0:T(8,128)(2,1)S(1)}, u32[]{:S(2)}, u32[]{:S(2)}) %collective-permute-start.17) | collective-permute-done | bytes 3440672 | tf_op jit(solution)/shard_map/ppermute | solution.py:33
  79.4 3.1 %collective-permute-start.22 = (f32[64,5120]{1,0:T(8,128)S(1)}, f32[64,5120]{1,0:T(8,128)S(1)}, u32[]{:S(2)}, u32[]{:S(2)}) collective-permute-start(f32[64,5120]{1,0:T(8,128)S(1)} %held.23), channel_id=1, source_target_pairs={{128,0},{0,128},{129,1},{1,129},{130,2},{2,130},{131,3},{3,131},{1... | collective-permute-start | bytes 3932168 | tf_op jit(solution)/shard_map/ppermute | solution.py:33
  83.1 11.2 %collective-permute-done.14.refs_0_ = bf16[80,5120]{1,0:T(8,128)(2,1)S(1)} collective-permute-done((bf16[80,5120]{1,0:T(8,128)(2,1)S(1)}, bf16[80,5120]{1,0:T(8,128)(2,1)S(1)}, u32[]{:S(2)}, u32[]{:S(2)}) %collective-permute-start.14) | collective-permute-done | bytes 819232 | tf_op jit(solution)/shard_map/ppermute | solution.py:33
  94.3 1.3 collective-permute-done.15.refs_1_
  95.6 0.3 collective-permute-start.18
  95.9 1.2 collective-permute-start.19
  97.1 0.1 pad_slice_fusion.refs_0_
  97.1 14.4 %collective-permute-done.22.refs_4_.refs_1_.refs_0_ = f32[64,5120]{1,0:T(8,128)S(1)} collective-permute-done((f32[64,5120]{1,0:T(8,128)S(1)}, f32[64,5120]{1,0:T(8,128)S(1)}, u32[]{:S(2)}, u32[]{:S(2)}) %collective-permute-start.22) | collective-permute-done | bytes 1310752 | tf_op jit(solution)/shard_map/ppermute | solution.py:33
  111.5 1.2 collective-permute-start.27
  112.7 0.3 collective-permute-done.21.refs_1_
  113.1 0.1 slice.25
  113.1 0.4 collective-permute-start.25
  113.6 1.2 collective-permute-start.26
  114.9 0.2 collective-permute-start.23
  115.1 1.4 collective-permute-start.24
  116.5 14.9 %collective-permute-done.25.refs_3_ = bf16[80,5120]{1,0:T(8,128)(2,1)S(1)} collective-permute-done((bf16[80,5120]{1,0:T(8,128)(2,1)S(1)}, bf16[80,5120]{1,0:T(8,128)(2,1)S(1)}, u32[]{:S(2)}, u32[]{:S(2)}) %collective-permute-start.25) | collective-permute-done | bytes 819232 | tf_op jit(solution)/shard_map/ppermute | solution.py:33
  131.4 1.7 collective-permute-done.26.refs_4_
  133.1 5.6 %hidden.1.refs_0_ = f32[640,256]{1,0:T(8,128)S(1)} custom-call(bf16[160,5120]{1,0:T(8,128)(2,1)S(1)} %stacked.3.refs_2_.refs_0_, bf16[160,5120]{1,0:T(8,128)(2,1)S(1)} %get-tuple-element.27.refs_2_.refs_1_, bf16[160,5120]{1,0:T(8,128)(2,1)S(1)} %get-tuple-element.28.refs_3_.refs_2_, bf16[80,5120]{1,0:T(8,128)(2,1)S(1)} %collective-permute-done.25.refs_3_, ...), custom_call_target="tpu_custom_call" | custom-call | flops 1 | bytes 1 | tf_op jit(solution)/shard_map/hidden/pallas_call | solution.py:136
  138.8 8.9 %gate_grads.1 = (f32[112,5120]{1,0:T(8,128)S(1)}, f32[112,5120]{1,0:T(8,128)S(1)}) custom-call(bf16[80,5120]{1,0:T(8,128)(2,1)S(1)} %stacked.2.refs_0_, bf16[80,5120]{1,0:T(8,128)(2,1)S(1)} %get-tuple-element.23.refs_1_, bf16[80,5120]{1,0:T(8,128)(2,1)S(1)} %get-tuple-element.25.refs_2_, bf16[80,5120]{1,0:T(8,128)(2,1)S(1)} %get-tuple-element.29.refs_3_, ...), custom_call_target="tpu_custom_call" | custom-call | flops 1 | bytes 1 | tf_op jit(solution)/shard_map/gate_grads/pallas_call | solution.py:196
  147.7 2.6 %collective-permute-start.28 = (f32[112,5120]{1,0:T(8,128)S(1)}, f32[112,5120]{1,0:T(8,128)S(1)}, u32[]{:S(2)}, u32[]{:S(2)}) collective-permute-start(f32[112,5120]{1,0:T(8,128)S(1)} %get-tuple-element.32), channel_id=1, source_target_pairs={{64,0},{0,64},{65,1},{1,65},{66,2},{2,66},{67,3},{3,67},{68,4},{4,... | collective-permute-start | bytes 6881288 | tf_op jit(solution)/shard_map/ppermute | solution.py:33
  150.2 1.7 concatenate.7.refs_0_
  152.0 2.3 %collective-permute-done.28 = f32[112,5120]{1,0:T(8,128)S(1)} collective-permute-done((f32[112,5120]{1,0:T(8,128)S(1)}, f32[112,5120]{1,0:T(8,128)S(1)}, u32[]{:S(2)}, u32[]{:S(2)}) %collective-permute-start.28) | collective-permute-done | bytes 2293792 | tf_op jit(solution)/shard_map/ppermute | solution.py:33
  154.3 2.6 %multiply_reduce_fusion = (f32[]{:T(128)}, f32[112,5120]{1,0:T(8,128)}) fusion(f32[112,5120]{1,0:T(8,128)S(1)} %get-tuple-element.31.refs_2_.refs_1_, f32[112,5120]{1,0:T(8,128)S(1)} %collective-permute-done.28), kind=kLoop, calls=%fused_computation.1 | loop fusion | flops 1720319 | bytes 6881284 | tf_op jit(solution)/shard_map/reduce_sum | solution.py:344
  156.9 7.6 %collective-permute-start.34 = (f32[112,5120]{1,0:T(8,128)}, f32[112,5120]{1,0:T(8,128)}, u32[]{:S(2)}, u32[]{:S(2)}) collective-permute-start(f32[112,5120]{1,0:T(8,128)} %get-tuple-element.39), channel_id=1, source_target_pairs={{0,0},{64,4},{4,64},{68,68},{1,1},{65,5},{5,65},{69,69},{2,2},{66,... | collective-permute-start | bytes 6881288 | tf_op jit(solution)/shard_map/ppermute | solution.py:38
  164.5 11.4 %collective-permute-start.29 = (f32[64,5120]{1,0:T(8,128)S(1)}, f32[64,5120]{1,0:T(8,128)}, u32[]{:S(2)}, u32[]{:S(2)}) collective-permute-start(f32[64,5120]{1,0:T(8,128)S(1)} %get-tuple-element.33.refs_0_), channel_id=1, source_target_pairs={{64,0},{0,64},{65,1},{1,65},{66,2},{2,66},{67,3},{3,67},{68,4},{4,... | collective-permute-start | bytes 3932168 | tf_op jit(solution)/shard_map/ppermute | solution.py:33
  176.7 11.4 %psum.14 = f32[]{:T(128)} all-reduce(f32[]{:T(128)} %get-tuple-element.38), channel_id=1, replica_groups=mesh['x_lo'=2,'core'=2,'z'=8,'x_hi'=2,'y'=4] {'z'}, use_global_device_ids=true, to_apply=%region_1.2 | all-reduce | flops 1 | bytes 8 | tf_op jit(solution)/shard_map/psum | solution.py:347
  188.2 6.6 %psum.15.refs_0_ = f32[1]{0:T(128)} all-reduce(f32[1]{0:T(128)} %bitcast.8), channel_id=1, replica_groups=mesh['x_lo'=2,'core'=2,'z'=8,'x_hi'=2,'y'=4] {'y'}, use_global_device_ids=true, to_apply=%region_2.3 | all-reduce | flops 1 | bytes 8 | tf_op jit(solution)/shard_map/psum | solution.py:347
  194.8 1.2 held.29
  196.0 12.5 %collective-permute-start.32 = (f32[]{:T(128)}, f32[]{:T(128)}, u32[]{:S(2)}, u32[]{:S(2)}) collective-permute-start(f32[]{:T(128)} %bitcast.9), channel_id=1, source_target_pairs={{0,0},{64,4},{4,64},{68,68},{1,1},{65,5},{5,65},{69,69},{2,2},{66,... | collective-permute-start | bytes 20 | tf_op jit(solution)/shard_map/ppermute | solution.py:38
  208.5 0.1 collective-permute-start.33
  208.6 1.3 collective-permute-done.32
  209.9 2.6 %collective-permute-done.33 = f32[]{:T(128)} collective-permute-done((f32[]{:T(128)}, f32[]{:T(128)}, u32[]{:S(2)}, u32[]{:S(2)}) %collective-permute-start.33) | collective-permute-done | bytes 36 | tf_op jit(solution)/shard_map/ppermute | solution.py:293
  213.8 1.6 copy-done
  215.5 5.8 %updated.1 = (f32[112,5120]{1,0:T(8,128)}, f32[112,5120]{1,0:T(8,128)}, f32[1]{0:T(128)}) custom-call(f32[1]{0:T(128)} %bitcast.10.factor, s32[1]{0:T(128)} %bitcast.11.which, f32[1]{0:T(128)} %mul.11.kept_weight, f32[112,5120]{1,0:T(8,128)S(1)} %bitcast.23, f32[112,5120]{1,0:T(8,128)} %collective-permute-done.34.grad, ...), custom_call_target="tpu_custom_call" | custom-call | tf_op jit(solution)/shard_map/updated/pallas_call | solution.py:267
  (48 shorter events, 0.2 us)
Async XLA Ops:
  0.6 10.6 %copy-start.4 = (bf16[112,5120]{1,0:T(8,128)(2,1)S(1)}, bf16[112,5120]{1,0:T(8,128)(2,1)}, u32[]{:S(2)}) copy-start(bf16[112,5120]{1,0:T(8,128)(2,1)} %param.15) | copy-start | bytes 3440644
  0.6 10.6 %copy-start.3 = (bf16[112,5120]{1,0:T(8,128)(2,1)S(1)}, bf16[112,5120]{1,0:T(8,128)(2,1)}, u32[]{:S(2)}) copy-start(bf16[112,5120]{1,0:T(8,128)(2,1)} %param.16) | copy-start | bytes 3440644
  0.7 10.9 %collective-permute-start.1 = (bf16[20,5120]{1,0:T(8,128)(2,1)}, bf16[20,5120]{1,0:T(8,128)(2,1)S(1)}, u32[]{:S(2)}, u32[]{:S(2)}) collective-permute-start(bf16[20,5120]{1,0:T(8,128)(2,1)} %bitcast.28), channel_id=1, source_target_pairs={{0,0},{64,4},{4,64},{68,68},{1,1},{65,5},{5,65},{69,69},{2,2},{66,... | collective-permute-start | bytes 614408 | tf_op jit(solution)/shard_map/ppermute | solution.py:38
  6.8 9.2 %collective-permute-start = (bf16[20,5120]{1,0:T(8,128)(2,1)}, bf16[20,5120]{1,0:T(8,128)(2,1)S(1)}, u32[]{:S(2)}, u32[]{:S(2)}) collective-permute-start(bf16[20,5120]{1,0:T(8,128)(2,1)} %bitcast.29), channel_id=1, source_target_pairs={{0,0},{64,4},{4,64},{68,68},{1,1},{65,5},{5,65},{69,69},{2,2},{66,... | collective-permute-start | bytes 614408 | tf_op jit(solution)/shard_map/ppermute | solution.py:38
  16.1 57.1 %collective-permute-start.16 = (bf16[336,5120]{1,0:T(8,128)(2,1)S(1)}, bf16[336,5120]{1,0:T(8,128)(2,1)S(1)}, u32[]{:S(2)}, u32[]{:S(2)}) collective-permute-start(bf16[336,5120]{1,0:T(8,128)(2,1)S(1)} %held.19), channel_id=1, source_target_pairs={{0,0},{64,4},{4,64},{68,68},{1,1},{65,5},{5,65},{69,69},{2,2},{66,... | collective-permute-start | bytes 10321928 | tf_op jit(solution)/shard_map/ppermute | solution.py:38
  18.7 8.6 %collective-permute-start.2 = (bf16[20,5120]{1,0:T(8,128)(2,1)S(1)}, bf16[20,5120]{1,0:T(8,128)(2,1)S(1)}, u32[]{:S(2)}, u32[]{:S(2)}) collective-permute-start(bf16[20,5120]{1,0:T(8,128)(2,1)S(1)} %held.15.refs_0_), channel_id=1, source_target_pairs={{1,0},{2,1},{3,2},{0,3},{5,4},{6,5},{7,6},{4,7},{9,8},{10,9},{11,1... | collective-permute-start | bytes 614408 | tf_op jit(solution)/shard_map/ppermute | solution.py:33
  21.5 10.0 %collective-permute-start.5 = (bf16[20,5120]{1,0:T(8,128)(2,1)S(1)}, bf16[20,5120]{1,0:T(8,128)(2,1)S(1)}, u32[]{:S(2)}, u32[]{:S(2)}) collective-permute-start(bf16[20,5120]{1,0:T(8,128)(2,1)S(1)} %collective-permute-done.1.refs_1_.refs_0_), channel_id=1, source_target_pairs={{8,0},{16,8},{24,16},{32,24},{40,32},{48,40},{56,48},{0,56},{9,1},... | collective-permute-start | bytes 614408 | tf_op jit(solution)/shard_map/ppermute | solution.py:33
  27.1 7.8 %collective-permute-start.7 = (bf16[20,5120]{1,0:T(8,128)(2,1)S(1)}, bf16[20,5120]{1,0:T(8,128)(2,1)S(1)}, u32[]{:S(2)}, u32[]{:S(2)}) collective-permute-start(bf16[20,5120]{1,0:T(8,128)(2,1)S(1)} %collective-permute-done.1.refs_1_.refs_0_), channel_id=1, source_target_pairs={{56,0},{0,8},{8,16},{16,24},{24,32},{32,40},{40,48},{48,56},{57,1}... | collective-permute-start | bytes 614408 | tf_op jit(solution)/shard_map/ppermute | solution.py:33
  27.1 8.9 %collective-permute-start.3 = (bf16[20,5120]{1,0:T(8,128)(2,1)S(1)}, bf16[20,5120]{1,0:T(8,128)(2,1)S(1)}, u32[]{:S(2)}, u32[]{:S(2)}) collective-permute-start(bf16[20,5120]{1,0:T(8,128)(2,1)S(1)} %held.15.refs_0_), channel_id=1, source_target_pairs={{3,0},{0,1},{1,2},{2,3},{7,4},{4,5},{5,6},{6,7},{11,8},{8,9},{9,10... | collective-permute-start | bytes 614408 | tf_op jit(solution)/shard_map/ppermute | solution.py:33
  27.3 8.7 %collective-permute-start.4 = (bf16[20,5120]{1,0:T(8,128)(2,1)S(1)}, bf16[20,5120]{1,0:T(8,128)(2,1)S(1)}, u32[]{:S(2)}, u32[]{:S(2)}) collective-permute-start(bf16[20,5120]{1,0:T(8,128)(2,1)S(1)} %held.15.refs_0_), channel_id=1, source_target_pairs={{2,0},{3,1},{0,2},{1,3},{6,4},{7,5},{4,6},{5,7},{10,8},{11,9},{8,1... | collective-permute-start | bytes 614408 | tf_op jit(solution)/shard_map/ppermute | solution.py:33
  31.5 11.4 %collective-permute-start.6 = (bf16[20,5120]{1,0:T(8,128)(2,1)S(1)}, bf16[20,5120]{1,0:T(8,128)(2,1)S(1)}, u32[]{:S(2)}, u32[]{:S(2)}) collective-permute-start(bf16[20,5120]{1,0:T(8,128)(2,1)S(1)} %collective-permute-done.5.refs_1_), channel_id=1, source_target_pairs={{8,0},{16,8},{24,16},{32,24},{40,32},{48,40},{56,48},{0,56},{9,1},... | collective-permute-start | bytes 614408 | tf_op jit(solution)/shard_map/ppermute | solution.py:33
  34.9 9.0 %collective-permute-start.8 = (bf16[20,5120]{1,0:T(8,128)(2,1)S(1)}, bf16[20,5120]{1,0:T(8,128)(2,1)S(1)}, u32[]{:S(2)}, u32[]{:S(2)}) collective-permute-start(bf16[20,5120]{1,0:T(8,128)(2,1)S(1)} %collective-permute-done.7.refs_7_), channel_id=1, source_target_pairs={{56,0},{0,8},{8,16},{16,24},{24,32},{32,40},{40,48},{48,56},{57,1}... | collective-permute-start | bytes 614408 | tf_op jit(solution)/shard_map/ppermute | solution.py:33
  43.9 9.4 %collective-permute-start.10 = (bf16[20,5120]{1,0:T(8,128)(2,1)S(1)}, bf16[20,5120]{1,0:T(8,128)(2,1)S(1)}, u32[]{:S(2)}, u32[]{:S(2)}) collective-permute-start(bf16[20,5120]{1,0:T(8,128)(2,1)S(1)} %get-tuple-element.21.refs_2_), channel_id=1, source_target_pairs={{16,0},{24,8},{32,16},{40,24},{48,32},{56,40},{0,48},{8,56},{17,1}... | collective-permute-start | bytes 614408 | tf_op jit(solution)/shard_map/ppermute | solution.py:33
  43.9 15.9 %collective-permute-start.9 = (bf16[20,5120]{1,0:T(8,128)(2,1)S(1)}, bf16[20,5120]{1,0:T(8,128)(2,1)S(1)}, u32[]{:S(2)}, u32[]{:S(2)}) collective-permute-start(bf16[20,5120]{1,0:T(8,128)(2,1)S(1)} %get-tuple-element.21.refs_2_), channel_id=1, source_target_pairs={{8,0},{16,8},{24,16},{32,24},{40,32},{48,40},{56,48},{0,56},{9,1},... | collective-permute-start | bytes 614408 | tf_op jit(solution)/shard_map/ppermute | solution.py:33
  46.1 13.7 %collective-permute-start.11 = (bf16[20,5120]{1,0:T(8,128)(2,1)S(1)}, bf16[20,5120]{1,0:T(8,128)(2,1)S(1)}, u32[]{:S(2)}, u32[]{:S(2)}) collective-permute-start(bf16[20,5120]{1,0:T(8,128)(2,1)S(1)} %get-tuple-element.22.refs_6_), channel_id=1, source_target_pairs={{56,0},{0,8},{8,16},{16,24},{24,32},{32,40},{40,48},{48,56},{57,1}... | collective-permute-start | bytes 614408 | tf_op jit(solution)/shard_map/ppermute | solution.py:33
  60.2 13.0 %collective-permute-start.12 = (bf16[80,5120]{1,0:T(8,128)(2,1)S(1)}, bf16[80,5120]{1,0:T(8,128)(2,1)S(1)}, u32[]{:S(2)}, u32[]{:S(2)}) collective-permute-start(bf16[80,5120]{1,0:T(8,128)(2,1)S(1)} %stacked.2.refs_0_), channel_id=1, source_target_pairs={{8,0},{16,8},{24,16},{32,24},{40,32},{48,40},{56,48},{0,56},{9,1},... | collective-permute-start | bytes 2457608 | tf_op jit(solution)/shard_map/ppermute | solution.py:33
  60.2 12.9 %collective-permute-start.13 = (bf16[80,5120]{1,0:T(8,128)(2,1)S(1)}, bf16[80,5120]{1,0:T(8,128)(2,1)S(1)}, u32[]{:S(2)}, u32[]{:S(2)}) collective-permute-start(bf16[80,5120]{1,0:T(8,128)(2,1)S(1)} %stacked.2.refs_0_), channel_id=1, source_target_pairs={{56,0},{0,8},{8,16},{16,24},{24,32},{32,40},{40,48},{48,56},{57,1}... | collective-permute-start | bytes 2457608 | tf_op jit(solution)/shard_map/ppermute | solution.py:33
  73.2 3.5 %copy-start.1 = (f32[1,112,5120]{2,1,0:T(8,128)S(1)}, f32[1,112,5120]{2,1,0:T(8,128)}, u32[]{:S(2)}) copy-start(f32[1,112,5120]{2,1,0:T(8,128)} %param.13) | copy-start | bytes 6881284
  73.2 6.2 %collective-permute-start.17 = (bf16[336,5120]{1,0:T(8,128)(2,1)S(1)}, bf16[336,5120]{1,0:T(8,128)(2,1)S(1)}, u32[]{:S(2)}, u32[]{:S(2)}) collective-permute-start(bf16[336,5120]{1,0:T(8,128)(2,1)S(1)} %held.20.refs_5_.refs_9_.refs_11_), channel_id=1, source_target_pairs={{64,0},{0,64},{65,1},{1,65},{66,2},{2,66},{67,3},{3,67},{68,4},{4,... | collective-permute-start | bytes 10321928 | tf_op jit(solution)/shard_map/ppermute | solution.py:33
  73.3 39.4 %collective-permute-start.20 = (bf16[160,5120]{1,0:T(8,128)(2,1)S(1)}, bf16[160,5120]{1,0:T(8,128)(2,1)S(1)}, u32[]{:S(2)}, u32[]{:S(2)}) collective-permute-start(bf16[160,5120]{1,0:T(8,128)(2,1)S(1)} %stacked.3.refs_2_.refs_0_), channel_id=1, source_target_pairs={{1,0},{2,1},{3,2},{0,3},{5,4},{6,5},{7,6},{4,7},{9,8},{10,9},{11,1... | collective-permute-start | bytes 4915208 | tf_op jit(solution)/shard_map/ppermute | solution.py:33
  75.2 37.8 %collective-permute-start.21 = (bf16[160,5120]{1,0:T(8,128)(2,1)S(1)}, bf16[160,5120]{1,0:T(8,128)(2,1)S(1)}, u32[]{:S(2)}, u32[]{:S(2)}) collective-permute-start(bf16[160,5120]{1,0:T(8,128)(2,1)S(1)} %stacked.3.refs_2_.refs_0_), channel_id=1, source_target_pairs={{3,0},{0,1},{1,2},{2,3},{7,4},{4,5},{5,6},{6,7},{11,8},{8,9},{9,10... | collective-permute-start | bytes 4915208 | tf_op jit(solution)/shard_map/ppermute | solution.py:33
  75.2 19.1 %collective-permute-start.14 = (bf16[80,5120]{1,0:T(8,128)(2,1)S(1)}, bf16[80,5120]{1,0:T(8,128)(2,1)S(1)}, u32[]{:S(2)}, u32[]{:S(2)}) collective-permute-start(bf16[80,5120]{1,0:T(8,128)(2,1)S(1)} %get-tuple-element.23.refs_1_), channel_id=1, source_target_pairs={{8,0},{16,8},{24,16},{32,24},{40,32},{48,40},{56,48},{0,56},{9,1},... | collective-permute-start | bytes 2457608 | tf_op jit(solution)/shard_map/ppermute | solution.py:33
  75.9 19.7 %collective-permute-start.15 = (bf16[80,5120]{1,0:T(8,128)(2,1)S(1)}, bf16[80,5120]{1,0:T(8,128)(2,1)S(1)}, u32[]{:S(2)}, u32[]{:S(2)}) collective-permute-start(bf16[80,5120]{1,0:T(8,128)(2,1)S(1)} %get-tuple-element.24.refs_2_.refs_8_), channel_id=1, source_target_pairs={{56,0},{0,8},{8,16},{16,24},{24,32},{32,40},{40,48},{48,56},{57,1}... | collective-permute-start | bytes 2457608 | tf_op jit(solution)/shard_map/ppermute | solution.py:33
  79.4 32.1 %collective-permute-start.22 = (f32[64,5120]{1,0:T(8,128)S(1)}, f32[64,5120]{1,0:T(8,128)S(1)}, u32[]{:S(2)}, u32[]{:S(2)}) collective-permute-start(f32[64,5120]{1,0:T(8,128)S(1)} %held.23), channel_id=1, source_target_pairs={{128,0},{0,128},{129,1},{1,129},{130,2},{2,130},{131,3},{3,131},{1... | collective-permute-start | bytes 3932168 | tf_op jit(solution)/shard_map/ppermute | solution.py:33
  95.6 19.2 %collective-permute-start.18 = (bf16[80,5120]{1,0:T(8,128)(2,1)S(1)}, bf16[80,5120]{1,0:T(8,128)(2,1)S(1)}, u32[]{:S(2)}, u32[]{:S(2)}) collective-permute-start(bf16[80,5120]{1,0:T(8,128)(2,1)S(1)} %get-tuple-element.25.refs_2_), channel_id=1, source_target_pairs={{8,0},{16,8},{24,16},{32,24},{40,32},{48,40},{56,48},{0,56},{9,1},... | collective-permute-start | bytes 2457608 | tf_op jit(solution)/shard_map/ppermute | solution.py:33
  95.9 18.9 %collective-permute-start.19 = (bf16[80,5120]{1,0:T(8,128)(2,1)S(1)}, bf16[80,5120]{1,0:T(8,128)(2,1)S(1)}, u32[]{:S(2)}, u32[]{:S(2)}) collective-permute-start(bf16[80,5120]{1,0:T(8,128)(2,1)S(1)} %get-tuple-element.26.refs_3_.refs_7_), channel_id=1, source_target_pairs={{56,0},{0,8},{8,16},{16,24},{24,32},{32,40},{40,48},{48,56},{57,1}... | collective-permute-start | bytes 2457608 | tf_op jit(solution)/shard_map/ppermute | solution.py:33
  111.5 27.2 %collective-permute-start.27 = (f32[56,5120]{1,0:T(8,128)S(1)}, f32[56,5120]{1,0:T(8,128)S(1)}, u32[]{:S(2)}, u32[]{:S(2)}) collective-permute-start(f32[56,5120]{1,0:T(8,128)S(1)} %held.25), channel_id=1, source_target_pairs={{128,0},{0,128},{129,1},{1,129},{130,2},{2,130},{131,3},{3,131},{1... | collective-permute-start | bytes 3440648 | tf_op jit(solution)/shard_map/ppermute | solution.py:33
  113.1 18.2 %collective-permute-start.25 = (bf16[80,5120]{1,0:T(8,128)(2,1)S(1)}, bf16[80,5120]{1,0:T(8,128)(2,1)S(1)}, u32[]{:S(2)}, u32[]{:S(2)}) collective-permute-start(bf16[80,5120]{1,0:T(8,128)(2,1)S(1)} %slice.25), channel_id=1, source_target_pairs={{1,0},{2,1},{3,2},{0,3},{5,4},{6,5},{7,6},{4,7},{9,8},{10,9},{11,1... | collective-permute-start | bytes 2457608 | tf_op jit(solution)/shard_map/ppermute | solution.py:33
  113.6 19.5 %collective-permute-start.26 = (bf16[80,5120]{1,0:T(8,128)(2,1)S(1)}, bf16[80,5120]{1,0:T(8,128)(2,1)S(1)}, u32[]{:S(2)}, u32[]{:S(2)}) collective-permute-start(bf16[80,5120]{1,0:T(8,128)(2,1)S(1)} %slice.26), channel_id=1, source_target_pairs={{3,0},{0,1},{1,2},{2,3},{7,4},{4,5},{5,6},{6,7},{11,8},{8,9},{9,10... | collective-permute-start | bytes 2457608 | tf_op jit(solution)/shard_map/ppermute | solution.py:33
  114.9 23.9 %collective-permute-start.23 = (bf16[48,5120]{1,0:T(8,128)(2,1)S(1)}, bf16[48,5120]{1,0:T(8,128)(2,1)S(1)}, u32[]{:S(2)}, u32[]{:S(2)}) collective-permute-start(bf16[48,5120]{1,0:T(8,128)(2,1)S(1)} %slice.23), channel_id=1, source_target_pairs={{8,0},{16,8},{24,16},{32,24},{40,32},{48,40},{56,48},{0,56},{9,1},... | collective-permute-start | bytes 1474568 | tf_op jit(solution)/shard_map/ppermute | solution.py:33
  115.1 23.7 %collective-permute-start.24 = (bf16[32,5120]{1,0:T(8,128)(2,1)S(1)}, bf16[32,5120]{1,0:T(8,128)(2,1)S(1)}, u32[]{:S(2)}, u32[]{:S(2)}) collective-permute-start(bf16[32,5120]{1,0:T(8,128)(2,1)S(1)} %slice.24), channel_id=1, source_target_pairs={{56,0},{0,8},{8,16},{16,24},{24,32},{32,40},{40,48},{48,56},{57,1}... | collective-permute-start | bytes 983048 | tf_op jit(solution)/shard_map/ppermute | solution.py:33
  138.8 11.5 %copy-start.2 = (f32[1,112,5120]{2,1,0:T(8,128)S(1)}, f32[1,112,5120]{2,1,0:T(8,128)}, u32[]{:S(2)}) copy-start(f32[1,112,5120]{2,1,0:T(8,128)} %param.13) | copy-start | bytes 6881284
  147.7 6.6 %collective-permute-start.28 = (f32[112,5120]{1,0:T(8,128)S(1)}, f32[112,5120]{1,0:T(8,128)S(1)}, u32[]{:S(2)}, u32[]{:S(2)}) collective-permute-start(f32[112,5120]{1,0:T(8,128)S(1)} %get-tuple-element.32), channel_id=1, source_target_pairs={{64,0},{0,64},{65,1},{1,65},{66,2},{2,66},{67,3},{3,67},{68,4},{4,... | collective-permute-start | bytes 6881288 | tf_op jit(solution)/shard_map/ppermute | solution.py:33
  151.9 42.9 %collective-permute-start.31 = (f32[120,5120]{1,0:T(8,128)}, f32[120,5120]{1,0:T(8,128)}, u32[]{:S(2)}, u32[]{:S(2)}) collective-permute-start(f32[120,5120]{1,0:T(8,128)} %held.28), channel_id=1, source_target_pairs={{64,0},{0,64},{65,1},{1,65},{66,2},{2,66},{67,3},{3,67},{68,4},{4,... | collective-permute-start | bytes 7372808 | tf_op jit(solution)/shard_map/ppermute | solution.py:33
  156.9 56.9 %collective-permute-start.34 = (f32[112,5120]{1,0:T(8,128)}, f32[112,5120]{1,0:T(8,128)}, u32[]{:S(2)}, u32[]{:S(2)}) collective-permute-start(f32[112,5120]{1,0:T(8,128)} %get-tuple-element.39), channel_id=1, source_target_pairs={{0,0},{64,4},{4,64},{68,68},{1,1},{65,5},{5,65},{69,69},{2,2},{66,... | collective-permute-start | bytes 6881288 | tf_op jit(solution)/shard_map/ppermute | solution.py:38
  164.5 30.3 %collective-permute-start.29 = (f32[64,5120]{1,0:T(8,128)S(1)}, f32[64,5120]{1,0:T(8,128)}, u32[]{:S(2)}, u32[]{:S(2)}) collective-permute-start(f32[64,5120]{1,0:T(8,128)S(1)} %get-tuple-element.33.refs_0_), channel_id=1, source_target_pairs={{64,0},{0,64},{65,1},{1,65},{66,2},{2,66},{67,3},{3,67},{68,4},{4,... | collective-permute-start | bytes 3932168 | tf_op jit(solution)/shard_map/ppermute | solution.py:33
  176.0 18.8 %collective-permute-start.30 = (f32[56,5120]{1,0:T(8,128)S(1)}, f32[56,5120]{1,0:T(8,128)}, u32[]{:S(2)}, u32[]{:S(2)}) collective-permute-start(f32[56,5120]{1,0:T(8,128)S(1)} %get-tuple-element.34.refs_1_), channel_id=1, source_target_pairs={{64,0},{0,64},{65,1},{1,65},{66,2},{2,66},{67,3},{3,67},{68,4},{4,... | collective-permute-start | bytes 3440648 | tf_op jit(solution)/shard_map/ppermute | solution.py:33
  196.0 14.0 %collective-permute-start.32 = (f32[]{:T(128)}, f32[]{:T(128)}, u32[]{:S(2)}, u32[]{:S(2)}) collective-permute-start(f32[]{:T(128)} %bitcast.9), channel_id=1, source_target_pairs={{0,0},{64,4},{4,64},{68,68},{1,1},{65,5},{5,65},{69,69},{2,2},{66,... | collective-permute-start | bytes 20 | tf_op jit(solution)/shard_map/ppermute | solution.py:38
  208.5 4.1 %collective-permute-start.33 = (f32[]{:T(128)}, f32[]{:T(128)}, u32[]{:S(2)}, u32[]{:S(2)}) collective-permute-start(f32[]{:T(128)} %bitcast.9), channel_id=1, source_target_pairs={{64,0},{0,4},{68,64},{4,68},{65,1},{1,5},{69,65},{5,69},{66,2},{2,... | collective-permute-start | bytes 20 | tf_op jit(solution)/shard_map/ppermute | solution.py:293
  213.8 1.6 copy-start

commit v8 on v7

--- a/solution.py
+++ b/solution.py
@@ -24,6 +24,7 @@
 HALF = 128
 CUT = 64
 NO_COST = pl.CostEstimate(flops=1, bytes_accessed=1, transcendentals=0)
+MUCH_COST = pl.CostEstimate(flops=3 * 10**10, bytes_accessed=1, transcendentals=0)
 BLOCK = 1024
 
 
@@ -33,8 +34,13 @@
     return lax.ppermute(value, axis, pairs)
 
 
-def transposed(value):
-    pairs = [(2 * x_hi + core, 2 * core + x_hi) for core in range(2) for x_hi in range(2)]
+def transposed(value, stay=True):
+    pairs = [
+        (2 * x_hi + core, 2 * core + x_hi)
+        for core in range(2)
+        for x_hi in range(2)
+        if stay or core != x_hi
+    ]
     return lax.ppermute(value, ("core", "x_hi"), pairs)
 
 
@@ -145,7 +151,7 @@
             pltpu.VMEM((2 * HALF, BLOCK), jnp.bfloat16),
         ],
         compiler_params=params_of(16),
-        cost_estimate=NO_COST,
+        cost_estimate=MUCH_COST,
         name="hidden",
     )(*parts, mine, theirs)
 
@@ -215,59 +221,72 @@
     )(*parts, mine, theirs, mine, theirs, hidden)
 
 
-def updated_kernel(factor, which, kept_weight, numerator, grad, *refs):
-    two_top, two_rest, one_top, one_rest, other = refs[:5]
-    kept_ref, new_ref, weight_ref, part, sems = refs[5:]
+def updated_kernel(factor, kept_weight, which, numerator, *refs):
+    two_top, two_rest, one_top, one_rest, hop, stayed, returned = refs[:7]
+    kept_ref, new_ref, weight_ref, part, grad, sems, grad_sems = refs[7:]
     received = (
         (two_top, two_rest),
         (one_top, one_rest),
-        (other.at[:CUT, :], other.at[CUT:, :]),
+        (hop.at[:CUT, :], hop.at[CUT:, :]),
     )
     at = pl.program_id(0)
     blocks = D // BLOCK
 
-    def copies(sources, block):
+    def copies(sources, source, block):
         columns = pl.ds(block * BLOCK, BLOCK)
         targets = (part.at[:CUT, columns], part.at[CUT:, columns])
-        return [
-            pltpu.make_async_copy(source.at[:, columns], target, sems.at[half, block])
-            for half, (source, target) in enumerate(zip(sources, targets))
+        parts = [
+            pltpu.make_async_copy(one.at[:, columns], target, sems.at[half, block])
+            for half, (one, target) in enumerate(zip(sources, targets))
         ]
+        whole = pltpu.make_async_copy(
+            source.at[:, columns], grad.at[:, columns], grad_sems.at[block]
+        )
+        return parts, whole
 
     @pl.when(at == 0)
     def _():
-        for place, sources in enumerate(received):
-
-            @pl.when(which[0] == place)
-            def _():
-                for block in range(blocks):
-                    for copy in copies(sources, block):
+        for block in range(blocks):
+            for place, sources in enumerate(received):
+
+                @pl.when(which[0] == place)
+                def _():
+                    for copy in copies(sources, stayed, block)[0]:
                         copy.start()
 
-    kept = 0.5 * (numerator[...] - factor[0] * grad[...])
-    kept_ref[...] = kept
+            for place, source in enumerate((stayed, returned)):
+
+                @pl.when(which[1] == place)
+                def _():
+                    copies(received[0], source, block)[1].start()
+
     for block in range(blocks):
 
         @pl.when(at == block)
         def _():
-            for copy in copies(received[0], block):
+            parts, whole = copies(received[0], stayed, block)
+            for copy in (*parts, whole):
                 copy.wait()
-            new_ref[...] = kept + part[:ROWS, block * BLOCK : (block + 1) * BLOCK]
+            columns = slice(block * BLOCK, (block + 1) * BLOCK)
+            kept = 0.5 * (numerator[...] - factor[0] * grad[:, columns])
+            kept_ref[...] = kept
+            new_ref[...] = kept + part[:ROWS, columns]
 
     @pl.when(at == 0)
     def _():
         weight_ref[0] = kept_weight[0] + jnp.max(part[ROWS:, :128])
 
 
-def updated(numerator, grad, kept_weight, factor, which, two_before, one_before, other):
+def updated(numerator, factor, kept_weight, which, received, grads):
     own = pl.BlockSpec((ROWS, BLOCK), lambda at: (0, at))
     scalar = pl.BlockSpec(memory_space=pltpu.SMEM)
     anywhere = pl.BlockSpec(memory_space=pl.ANY)
+    more = [part for parts in received for part in parts] + grads
     blocks = D // BLOCK
     return pl.pallas_call(
         updated_kernel,
         grid=(blocks,),
-        in_specs=[scalar, scalar, scalar, own, own] + [anywhere] * 5,
+        in_specs=[scalar, scalar, scalar, own] + [anywhere] * len(more),
         out_specs=[own, own, scalar],
         out_shape=[
             jax.ShapeDtypeStruct((ROWS, D), jnp.float32),
@@ -275,22 +294,14 @@
             jax.ShapeDtypeStruct((1,), jnp.float32),
         ],
         scratch_shapes=[
-            pltpu.VMEM(other.shape, jnp.float32),
+            pltpu.VMEM((ROWS + 8, D), jnp.float32),
+            pltpu.VMEM((ROWS, D), jnp.float32),
             pltpu.SemaphoreType.DMA((2, blocks)),
+            pltpu.SemaphoreType.DMA((blocks,)),
         ],
         compiler_params=params_of(16),
         name="updated",
-    )(
-        jnp.reshape(factor, (1,)), jnp.reshape(which, (1,)), kept_weight,
-        numerator, grad, *two_before, *one_before, other,
-    )
-
-
-def crossed(value):
-    pairs = [
-        (2 * (1 - x_hi) + core, 2 * core + x_hi) for core in range(2) for x_hi in range(2)
-    ]
-    return lax.ppermute(value, ("core", "x_hi"), pairs)
+    )(factor, kept_weight, which, numerator, *more)
 
 
 def shards(
@@ -312,47 +323,57 @@
     ring[4] = shifted(ring[2], "z", 2)
     near[3] = held(near[3], ring[3], ring[4], ring[5])
     blocks = {0: stacked(near)}
-    for steps in (1, 7):
-        blocks[steps] = shifted(blocks[0], "z", steps)
-    column = stacked([ring[steps] for steps in range(8)])
-
-    following, before = shifted(column, "y", 1), shifted(column, "y", 3)
-    blocks[1], blocks[7] = held((blocks[1], blocks[7]), column)
+    columns = [stacked([ring[steps] for steps in some]) for some in (range(4), range(4, 8))]
+
+    blocks[1], blocks[7] = shifted(blocks[0], "z", 1), shifted(blocks[0], "z", 7)
+    following, before = [shifted(columns[0], "y", 1)], [shifted(columns[0], "y", 3)]
+    blocks[1], blocks[7] = held((blocks[1], blocks[7]), columns[1], following[0], before[0])
+
     blocks[2], blocks[6] = shifted(blocks[1], "z", 1), shifted(blocks[7], "z", 7)
+    columns[1] = held(columns[1], blocks[1], blocks[7])
+    following.append(shifted(columns[1], "y", 1))
+    before.append(shifted(columns[1], "y", 3))
     mine = held(mine, blocks[1], blocks[7])
     theirs = shifted(mine, "core", 1)
+    blocks[2], blocks[6] = held((blocks[2], blocks[6]), theirs, following[1], before[1])
+
+    blocks[3], blocks[5] = shifted(blocks[2], "z", 1), shifted(blocks[6], "z", 7)
+    following[0] = held(following[0], blocks[2])
+    far = [shifted(following[0], "y", 1), shifted(before[1], "y", 3)]
     stale = jnp.concatenate([stale_num[0], jnp.broadcast_to(stale_weight, (8, D))], axis=0)
-    blocks[2], blocks[6] = held((blocks[2], blocks[6]), theirs)
     two_before = [shifted(held(stale[:CUT], theirs), "x_lo", 1)]
-    two_before.append(shifted(held(stale[CUT:], two_before[0]), "x_lo", 1))
-    blocks[3], blocks[5] = shifted(blocks[2], "z", 1), shifted(blocks[6], "z", 7)
-    following, before = held((following, before), blocks[2], blocks[6])
-    half = column.shape[0] // 2
-    far = [shifted(following[:half], "y", 1), shifted(before[half:], "y", 3)]
-    blocks[3], blocks[5] = held((blocks[3], blocks[5]), following, before, two_before[0])
+    blocks[3], blocks[5] = held((blocks[3], blocks[5]), two_before[0], *far)
+
     cut = 48
     last = [shifted(blocks[3][:cut], "z", 1), shifted(blocks[5][cut:], "z", 7)]
-
-    hidden = hidden_of([column, following, before, *far], mine, theirs)
+    two_before.append(shifted(held(stale[CUT:], two_before[0]), "x_lo", 1))
+    hidden = hidden_of([*columns, *following, *before, *far], mine, theirs)
+    hidden = held(hidden, two_before[1])
     parts = [blocks[steps] for steps in (0, 1, 2, 3)] + last + [blocks[steps] for steps in (5, 6, 7)]
-    hidden = held(hidden, two_before[1])
+
     own_grad, other_grad = gate_grads(parts, mine, theirs, hidden)
     two_before = held(tuple(two_before), own_grad)
     one_before = [shifted(part, "core", 1) for part in two_before]
     stale_hop = shifted(held(stale, own_grad), "core", 1)
     gate_grad = own_grad + shifted(other_grad, "core", 1)
     norm_sq = jnp.sum(gate_grad * gate_grad)
-    gate_grad = transposed(gate_grad)
+    returned = transposed(gate_grad, stay=False)
     for axes in ("z", "y"):
         norm_sq = lax.psum(norm_sq, axes)
-    norm_sq = held(jnp.reshape(norm_sq, (1,)), *one_before, stale_hop)[0]
-    norm_sq = transposed(norm_sq) + crossed(norm_sq)
+    x_hi, core = lax.axis_index("x_hi"), lax.axis_index("core")
+    norms = lax.psum(jnp.where(jnp.arange(2) == x_hi, norm_sq, 0.0), ("core", "x_hi"))
+    norm_sq = jnp.where(core == 0, norms[0], norms[1])
 
     clip_factor = jnp.minimum(1.0, MAX_NORM / jnp.sqrt(norm_sq + eps))
     kept_weight = 0.5 * push_weight
-    which = jnp.where(step[0] % 2 == 1, 0, 1 + lax.axis_index("core"))
+    which = jnp.where(step[0] % 2 == 1, 0, 1 + core)
     kept_half, new_num, new_weight = updated(
-        numerator, gate_grad, kept_weight, rate * clip_factor, which, two_before, one_before, stale_hop
+        numerator,
+        jnp.reshape(rate * clip_factor, (1,)),
+        kept_weight,
+        jnp.stack([which, jnp.where(core == x_hi, 0, 1)]),
+        [two_before, one_before, [stale_hop]],
+        [gate_grad, returned],
     )
     return (new_num[None], new_weight, kept_half[None], kept_weight)
 

time: 224 us -> 210 us (0.938)
  starting transfers between devices: 75.6 us -> 52.5 us
  blocking collectives: 18 us -> 33.9 us
  waiting for transfers between devices: 92.6 us -> 84.9 us
    psum x0 -> x1, blocking collectives: none -> 13.5 us  [shards(): lax.psum(jnp.where(jnp.arange(2) == x_hi, norm_sq, 0.0), ('core', 'x_hi'))]
    ppermute x5 -> x4, starting transfers between devices: 30.8 us -> 17.5 us  [transposed(): return lax.ppermute(value, ('core', 'x_hi'), pairs)]
    ppermute x29 -> x31, starting transfers between devices: 44.7 us -> 35 us  [shifted(): return lax.ppermute(value, axis, pairs)]
    ppermute x29 -> x31, waiting for transfers between devices: 84.1 us -> 80.4 us  [shifted(): return lax.ppermute(value, axis, pairs)]
    ppermute x1 -> x0, waiting for transfers between devices: 2.62 us -> none  [crossed(): return lax.ppermute(value, ('core', 'x_hi'), pairs)]
    psum x2, blocking collectives: 18 us -> 20.3 us  [shards(): norm_sq = lax.psum(norm_sq, axes)]
    ppermute x5 -> x4, waiting for transfers between devices: 5.87 us -> 4.52 us  [transposed(): return lax.ppermute(value, ('core', 'x_hi'), pairs)]
  transfers between devices with their start and end apart: 35 -> 35, of which waited for: 20 -> 22; matrix products, arithmetic and copies ran while one was open for 3% -> 4% of each run, Pallas kernels for 3% -> 4%
where the time goes in v8:
time: 210 us; the launch traced here: 209 us
  waiting for transfers between devices  84.9 us (40%)
  starting transfers between devices  52.5 us (25%)
  blocking collectives  33.9 us (16%)
  Pallas kernels  22.9 us (11%)
  between operations  5.49 us (3%)
  other arithmetic  5.37 us (3%)
  local copies, waits for them, and re-layouts  4.17 us (2%)
    ppermute x31, waiting for transfers between devices, shifted(): return lax.ppermute(value, axis, pairs)  80.4 us
    ppermute x31, starting transfers between devices, shifted(): return lax.ppermute(value, axis, pairs)  35 us
    psum x2, blocking collectives, shards(): norm_sq = lax.psum(norm_sq, axes)  20.3 us
    ppermute x4, starting transfers between devices, transposed(): return lax.ppermute(value, ('core', 'x_hi'), pairs)  17.5 us
    psum x1, blocking collectives, shards(): lax.psum(jnp.where(jnp.arange(2) == x_hi, norm_sq, 0.0), ('core', 'x_hi'))  13.5 us
    pallas_call x1, Pallas kernels, gate_grads(): pl.pallas_call(grad_kernel, grid=(D // BLOCK,), in_specs=[pl.BlockSpec((p...  8.86 us
    pallas_call x1, Pallas kernels, hidden_of(): pl.pallas_call(hidden_kernel, grid=(D // BLOCK,), in_specs=[pl.BlockSpec(...  7.83 us
    pallas_call x1, Pallas kernels, updated(): pl.pallas_call(updated_kernel, grid=(blocks,), in_specs=[scalar, scalar,...  5.22 us
  transfers between devices with their start and end apart: 35, of which 22 were waited for; matrix products, arithmetic and copies ran while one was open for 4% of the time, Pallas kernels for 4%

profile of v8, /device:TPU:1, one launch (start us, length us, event | category | flops | bytes accessed | tf_op | source)
XLA Modules:
  0.0 209.2 jit_solution(12436700213576938968)
XLA Ops:
  0.7 6.2 %collective-permute-start.1 = (bf16[20,5120]{1,0:T(8,128)(2,1)}, bf16[20,5120]{1,0:T(8,128)(2,1)S(1)}, u32[]{:S(2)}, u32[]{:S(2)}) collective-permute-start(bf16[20,5120]{1,0:T(8,128)(2,1)} %bitcast.29), channel_id=1, source_target_pairs={{0,0},{64,4},{4,64},{68,68},{1,1},{65,5},{5,65},{69,69},{2,2},{66,... | collective-permute-start | bytes 614408 | tf_op jit(solution)/shard_map/ppermute | solution.py:44
  6.8 1.9 collective-permute-start
  9.4 1.8 divide_convert_fusion
  11.3 0.3 pad_maximum_fusion.refs_2_.refs_0_
  11.5 4.5 %collective-permute-done.refs_0_ = bf16[20,5120]{1,0:T(8,128)(2,1)S(1)} collective-permute-done((bf16[20,5120]{1,0:T(8,128)(2,1)}, bf16[20,5120]{1,0:T(8,128)(2,1)S(1)}, u32[]{:S(2)}, u32[]{:S(2)}) %collective-permute-start) | collective-permute-done | bytes 204832 | tf_op jit(solution)/shard_map/ppermute | solution.py:44
  16.1 2.6 %collective-permute-start.18 = (bf16[336,5120]{1,0:T(8,128)(2,1)S(1)}, bf16[336,5120]{1,0:T(8,128)(2,1)S(1)}, u32[]{:S(2)}, u32[]{:S(2)}) collective-permute-start(bf16[336,5120]{1,0:T(8,128)(2,1)S(1)} %held.19), channel_id=1, source_target_pairs={{0,0},{64,4},{4,64},{68,68},{1,1},{65,5},{5,65},{69,69},{2,2},{66,... | collective-permute-start | bytes 10321928 | tf_op jit(solution)/shard_map/ppermute | solution.py:44
  18.7 2.8 %collective-permute-start.2 = (bf16[20,5120]{1,0:T(8,128)(2,1)S(1)}, bf16[20,5120]{1,0:T(8,128)(2,1)S(1)}, u32[]{:S(2)}, u32[]{:S(2)}) collective-permute-start(bf16[20,5120]{1,0:T(8,128)(2,1)S(1)} %held.15.refs_0_), channel_id=1, source_target_pairs={{1,0},{2,1},{3,2},{0,3},{5,4},{6,5},{7,6},{4,7},{9,8},{10,9},{11,1... | collective-permute-start | bytes 614408 | tf_op jit(solution)/shard_map/ppermute | solution.py:34
  21.5 5.6 %collective-permute-start.5 = (bf16[20,5120]{1,0:T(8,128)(2,1)S(1)}, bf16[20,5120]{1,0:T(8,128)(2,1)S(1)}, u32[]{:S(2)}, u32[]{:S(2)}) collective-permute-start(bf16[20,5120]{1,0:T(8,128)(2,1)S(1)} %collective-permute-done.1.refs_1_.refs_0_), channel_id=1, source_target_pairs={{8,0},{16,8},{24,16},{32,24},{40,32},{48,40},{56,48},{0,56},{9,1},... | collective-permute-start | bytes 614408 | tf_op jit(solution)/shard_map/ppermute | solution.py:34
  27.1 0.2 collective-permute-done.2.refs_2_.refs_1_
  27.3 1.7 collective-permute-start.4
  29.0 2.5 %collective-permute-done.5.refs_1_ = bf16[20,5120]{1,0:T(8,128)(2,1)S(1)} collective-permute-done((bf16[20,5120]{1,0:T(8,128)(2,1)S(1)}, bf16[20,5120]{1,0:T(8,128)(2,1)S(1)}, u32[]{:S(2)}, u32[]{:S(2)}) %collective-permute-start.5) | collective-permute-done | bytes 204832 | tf_op jit(solution)/shard_map/ppermute | solution.py:34
  31.5 3.1 %collective-permute-start.6 = (bf16[20,5120]{1,0:T(8,128)(2,1)S(1)}, bf16[20,5120]{1,0:T(8,128)(2,1)S(1)}, u32[]{:S(2)}, u32[]{:S(2)}) collective-permute-start(bf16[20,5120]{1,0:T(8,128)(2,1)S(1)} %collective-permute-done.5.refs_1_), channel_id=1, source_target_pairs={{8,0},{16,8},{24,16},{32,24},{40,32},{48,40},{56,48},{0,56},{9,1},... | collective-permute-start | bytes 614408 | tf_op jit(solution)/shard_map/ppermute | solution.py:34
  34.6 0.3 collective-permute-done.7.refs_3_
  34.9 1.1 collective-permute-done.3.refs_3_.refs_2_
  36.0 7.0 %collective-permute-done.6.refs_0_ = bf16[20,5120]{1,0:T(8,128)(2,1)S(1)} collective-permute-done((bf16[20,5120]{1,0:T(8,128)(2,1)S(1)}, bf16[20,5120]{1,0:T(8,128)(2,1)S(1)}, u32[]{:S(2)}, u32[]{:S(2)}) %collective-permute-start.6) | collective-permute-done | bytes 204832 | tf_op jit(solution)/shard_map/ppermute | solution.py:34
  42.9 1.0 collective-permute-done.8.refs_1_
  43.9 2.2 %collective-permute-start.9 = (bf16[20,5120]{1,0:T(8,128)(2,1)S(1)}, bf16[20,5120]{1,0:T(8,128)(2,1)S(1)}, u32[]{:S(2)}, u32[]{:S(2)}) collective-permute-start(bf16[20,5120]{1,0:T(8,128)(2,1)S(1)} %get-tuple-element.19.refs_2_), channel_id=1, source_target_pairs={{8,0},{16,8},{24,16},{32,24},{40,32},{48,40},{56,48},{0,56},{9,1},... | collective-permute-start | bytes 614408 | tf_op jit(solution)/shard_map/ppermute | solution.py:34
  46.1 1.1 collective-permute-start.11
  47.2 6.1 %collective-permute-done.10.refs_2_.refs_0_ = bf16[20,5120]{1,0:T(8,128)(2,1)S(1)} collective-permute-done((bf16[20,5120]{1,0:T(8,128)(2,1)S(1)}, bf16[20,5120]{1,0:T(8,128)(2,1)S(1)}, u32[]{:S(2)}, u32[]{:S(2)}) %collective-permute-start.10) | collective-permute-done | bytes 204832 | tf_op jit(solution)/shard_map/ppermute | solution.py:34
  53.3 6.5 %collective-permute-done.9.refs_1_.refs_3_ = bf16[20,5120]{1,0:T(8,128)(2,1)S(1)} collective-permute-done((bf16[20,5120]{1,0:T(8,128)(2,1)S(1)}, bf16[20,5120]{1,0:T(8,128)(2,1)S(1)}, u32[]{:S(2)}, u32[]{:S(2)}) %collective-permute-start.9) | collective-permute-done | bytes 204832 | tf_op jit(solution)/shard_map/ppermute | solution.py:34
  59.8 0.3 stacked.3.refs_0_
  60.2 0.1 collective-permute-start.12
  60.2 1.5 collective-permute-start.13
  61.7 0.3 stacked.5.refs_0_
  62.1 1.8 collective-permute-start.15
  63.9 0.3 stacked.4.refs_2_.refs_0_
  64.2 8.9 %collective-permute-done.12.refs_0_ = bf16[80,5120]{1,0:T(8,128)(2,1)S(1)} collective-permute-done((bf16[80,5120]{1,0:T(8,128)(2,1)S(1)}, bf16[80,5120]{1,0:T(8,128)(2,1)S(1)}, u32[]{:S(2)}, u32[]{:S(2)}) %collective-permute-start.12) | collective-permute-done | bytes 819232 | tf_op jit(solution)/shard_map/ppermute | solution.py:34
  73.2 0.4 collective-permute-done.14.refs_3_.refs_0_
  73.5 2.2 %collective-permute-done.15.refs_4_ = bf16[80,5120]{1,0:T(8,128)(2,1)S(1)} collective-permute-done((bf16[80,5120]{1,0:T(8,128)(2,1)S(1)}, bf16[80,5120]{1,0:T(8,128)(2,1)S(1)}, u32[]{:S(2)}, u32[]{:S(2)}) %collective-permute-start.15) | collective-permute-done | bytes 819232 | tf_op jit(solution)/shard_map/ppermute | solution.py:34
  75.8 0.3 collective-permute-start.19
  76.1 1.5 collective-permute-start.21
  77.6 2.9 %collective-permute-start.16 = (bf16[80,5120]{1,0:T(8,128)(2,1)S(1)}, bf16[80,5120]{1,0:T(8,128)(2,1)S(1)}, u32[]{:S(2)}, u32[]{:S(2)}) collective-permute-start(bf16[80,5120]{1,0:T(8,128)(2,1)S(1)} %get-tuple-element.21.refs_1_), channel_id=1, source_target_pairs={{8,0},{16,8},{24,16},{32,24},{40,32},{48,40},{56,48},{0,56},{9,1},... | collective-permute-start | bytes 2457608 | tf_op jit(solution)/shard_map/ppermute | solution.py:34
  80.5 0.1 slice_bitcast_fusion.refs_0_
  80.6 1.5 collective-permute-done.19.refs_2_.refs_1_.refs_9_.refs_10_.refs_12_
  82.1 1.9 collective-permute-start.24
  84.0 12.8 %collective-permute-done.21.refs_4_.refs_5_ = bf16[80,5120]{1,0:T(8,128)(2,1)S(1)} collective-permute-done((bf16[80,5120]{1,0:T(8,128)(2,1)S(1)}, bf16[80,5120]{1,0:T(8,128)(2,1)S(1)}, u32[]{:S(2)}, u32[]{:S(2)}) %collective-permute-start.21) | collective-permute-done | bytes 819232 | tf_op jit(solution)/shard_map/ppermute | solution.py:34
  96.8 0.3 collective-permute-done.16.refs_0_
  97.1 3.1 %collective-permute-done.17.refs_1_ = bf16[80,5120]{1,0:T(8,128)(2,1)S(1)} collective-permute-done((bf16[80,5120]{1,0:T(8,128)(2,1)S(1)}, bf16[80,5120]{1,0:T(8,128)(2,1)S(1)}, u32[]{:S(2)}, u32[]{:S(2)}) %collective-permute-start.17) | collective-permute-done | bytes 819232 | tf_op jit(solution)/shard_map/ppermute | solution.py:34
  100.2 0.3 collective-permute-start.22
  100.5 2.1 %collective-permute-start.25 = (bf16[80,5120]{1,0:T(8,128)(2,1)S(1)}, bf16[80,5120]{1,0:T(8,128)(2,1)S(1)}, u32[]{:S(2)}, u32[]{:S(2)}) collective-permute-start(bf16[80,5120]{1,0:T(8,128)(2,1)S(1)} %held.24.refs_2_), channel_id=1, source_target_pairs={{1,0},{2,1},{3,2},{0,3},{5,4},{6,5},{7,6},{4,7},{9,8},{10,9},{11,1... | collective-permute-start | bytes 2457608 | tf_op jit(solution)/shard_map/ppermute | solution.py:34
  102.6 0.7 collective-permute-start.23
  104.1 8.9 %collective-permute-done.24.refs_2_.refs_1_.refs_0_ = f32[64,5120]{1,0:T(8,128)S(1)} collective-permute-done((f32[64,5120]{1,0:T(8,128)S(1)}, f32[64,5120]{1,0:T(8,128)S(1)}, u32[]{:S(2)}, u32[]{:S(2)}) %collective-permute-start.24) | collective-permute-done | bytes 1310752 | tf_op jit(solution)/shard_map/ppermute | solution.py:34
  113.0 1.2 collective-permute-start.29
  114.2 2.2 %collective-permute-done.26.refs_4_.refs_7_ = bf16[80,5120]{1,0:T(8,128)(2,1)S(1)} collective-permute-done((bf16[80,5120]{1,0:T(8,128)(2,1)S(1)}, bf16[80,5120]{1,0:T(8,128)(2,1)S(1)}, u32[]{:S(2)}, u32[]{:S(2)}) %collective-permute-start.26) | collective-permute-done | bytes 819232 | tf_op jit(solution)/shard_map/ppermute | solution.py:34
  116.4 2.0 collective-permute-done.25.refs_3_.refs_6_
  118.4 3.1 %collective-permute-done.23.refs_1_ = bf16[80,5120]{1,0:T(8,128)(2,1)S(1)} collective-permute-done((bf16[80,5120]{1,0:T(8,128)(2,1)S(1)}, bf16[80,5120]{1,0:T(8,128)(2,1)S(1)}, u32[]{:S(2)}, u32[]{:S(2)}) %collective-permute-start.23) | collective-permute-done | bytes 819232 | tf_op jit(solution)/shard_map/ppermute | solution.py:34
  121.7 1.5 collective-permute-start.28
  123.2 7.8 %hidden.1.refs_0_ = f32[640,256]{1,0:T(8,128)S(1)} custom-call(bf16[80,5120]{1,0:T(8,128)(2,1)S(1)} %stacked.5.refs_0_, bf16[80,5120]{1,0:T(8,128)(2,1)S(1)} %held.21.refs_1_, bf16[80,5120]{1,0:T(8,128)(2,1)S(1)} %held.24.refs_2_, bf16[80,5120]{1,0:T(8,128)(2,1)S(1)} %collective-permute-done.20.refs_3_, ...), custom_call_target="tpu_custom_call" | custom-call | flops 30000001024 | bytes 1 | tf_op jit(solution)/shard_map/hidden/pallas_call | solution.py:142
  131.1 8.0 %collective-permute-done.29.refs_1_ = f32[56,5120]{1,0:T(8,128)S(1)} collective-permute-done((f32[56,5120]{1,0:T(8,128)S(1)}, f32[56,5120]{1,0:T(8,128)S(1)}, u32[]{:S(2)}, u32[]{:S(2)}) %collective-permute-start.29) | collective-permute-done | bytes 1146912 | tf_op jit(solution)/shard_map/ppermute | solution.py:34
  139.1 8.9 %gate_grads.1 = (f32[112,5120]{1,0:T(8,128)S(1)}, f32[112,5120]{1,0:T(8,128)S(1)}) custom-call(bf16[80,5120]{1,0:T(8,128)(2,1)S(1)} %stacked.3.refs_0_, bf16[80,5120]{1,0:T(8,128)(2,1)S(1)} %get-tuple-element.21.refs_1_, bf16[80,5120]{1,0:T(8,128)(2,1)S(1)} %get-tuple-element.23.refs_1_.refs_2_, bf16[80,5120]{1,0:T(8,128)(2,1)S(1)} %get-tuple-element.25.refs_3_, ...), custom_call_target="tpu_custom_call" | custom-call | flops 1 | bytes 1 | tf_op jit(solution)/shard_map/gate_grads/pallas_call | solution.py:202
  148.0 1.9 collective-permute-start.30
  149.9 1.7 concatenate.7.refs_0_
  151.6 2.3 %collective-permute-done.30 = f32[112,5120]{1,0:T(8,128)S(1)} collective-permute-done((f32[112,5120]{1,0:T(8,128)S(1)}, f32[112,5120]{1,0:T(8,128)S(1)}, u32[]{:S(2)}, u32[]{:S(2)}) %collective-permute-start.30) | collective-permute-done | bytes 2293792 | tf_op jit(solution)/shard_map/ppermute | solution.py:34
  153.9 2.5 %multiply_reduce_fusion = (f32[]{:T(128)}, f32[112,5120]{1,0:T(8,128)}) fusion(f32[112,5120]{1,0:T(8,128)S(1)} %get-tuple-element.27.refs_2_.refs_1_, f32[112,5120]{1,0:T(8,128)S(1)} %collective-permute-done.30), kind=kLoop, calls=%fused_computation.1 | loop fusion | flops 1720319 | bytes 6881284 | tf_op jit(solution)/shard_map/reduce_sum | solution.py:359
  156.5 6.8 %collective-permute-start.34 = (f32[112,5120]{1,0:T(8,128)}, f32[112,5120]{1,0:T(8,128)}, u32[]{:S(2)}, u32[]{:S(2)}) collective-permute-start(f32[112,5120]{1,0:T(8,128)} %get-tuple-element.35.refs_5_), channel_id=1, source_target_pairs={{64,4},{4,64},{65,5},{5,65},{66,6},{6,66},{67,7},{7,67},{72,12},{1... | collective-permute-start | bytes 6881288 | tf_op jit(solution)/shard_map/ppermute | solution.py:44
  163.3 0.1 collective-permute-start.31
  163.4 0.5 collective-permute-start.32
  164.7 13.4 %psum.21 = f32[]{:T(128)} all-reduce(f32[]{:T(128)} %get-tuple-element.34), channel_id=1, replica_groups=mesh['x_lo'=2,'core'=2,'z'=8,'x_hi'=2,'y'=4] {'z'}, use_global_device_ids=true, to_apply=%region_1.2 | all-reduce | flops 1 | bytes 8 | tf_op jit(solution)/shard_map/psum | solution.py:362
  178.1 6.9 %psum.22 = f32[]{:T(128)} all-reduce(f32[]{:T(128)} %psum.21), channel_id=1, replica_groups=mesh['x_lo'=2,'core'=2,'z'=8,'x_hi'=2,'y'=4] {'y'}, use_global_device_ids=true, to_apply=%region_2.3 | all-reduce | flops 1 | bytes 8 | tf_op jit(solution)/shard_map/psum | solution.py:362
  185.0 0.6 compare_select_fusion
  185.7 13.5 %psum.23 = f32[2]{0:T(128)S(1)} all-reduce(f32[2]{0:T(128)S(1)} %compare_select_fusion), channel_id=1, replica_groups=mesh['x_lo'=2,'core'=2,'z'=8,'x_hi'=2,'y'=4] {'core','x_hi'}, use_global_device_ids=true, to_apply=%region_3.4 | all-reduce | flops 2 | bytes 16 | tf_op jit(solution)/shard_map/psum | solution.py:364
  199.2 0.6 fusion
  201.2 1.6 copy-done
  202.9 5.2 %updated.1 = (f32[112,5120]{1,0:T(8,128)}, f32[112,5120]{1,0:T(8,128)}, f32[1]{0:T(128)}) custom-call(f32[1]{0:T(128)} %bitcast.10.factor, f32[1]{0:T(128)} %mul.11.kept_weight, s32[2]{0:T(128)S(1)} %pad_add_fusion.which, f32[112,5120]{1,0:T(8,128)S(1)} %bitcast.24, f32[64,5120]{1,0:T(8,128)S(1)} %get-tuple-element.29.refs_0_, ...), custom_call_target="tpu_custom_call" | custom-call | tf_op jit(solution)/shard_map/updated/pallas_call | solution.py:286
  (51 shorter events, 0.6 us)
Async XLA Ops:
  0.6 10.6 %copy-start.4 = (bf16[112,5120]{1,0:T(8,128)(2,1)S(1)}, bf16[112,5120]{1,0:T(8,128)(2,1)}, u32[]{:S(2)}) copy-start(bf16[112,5120]{1,0:T(8,128)(2,1)} %param.15) | copy-start | bytes 3440644
  0.6 10.6 %copy-start.3 = (bf16[112,5120]{1,0:T(8,128)(2,1)S(1)}, bf16[112,5120]{1,0:T(8,128)(2,1)}, u32[]{:S(2)}) copy-start(bf16[112,5120]{1,0:T(8,128)(2,1)} %param.16) | copy-start | bytes 3440644
  0.7 10.9 %collective-permute-start.1 = (bf16[20,5120]{1,0:T(8,128)(2,1)}, bf16[20,5120]{1,0:T(8,128)(2,1)S(1)}, u32[]{:S(2)}, u32[]{:S(2)}) collective-permute-start(bf16[20,5120]{1,0:T(8,128)(2,1)} %bitcast.29), channel_id=1, source_target_pairs={{0,0},{64,4},{4,64},{68,68},{1,1},{65,5},{5,65},{69,69},{2,2},{66,... | collective-permute-start | bytes 614408 | tf_op jit(solution)/shard_map/ppermute | solution.py:44
  6.8 9.2 %collective-permute-start = (bf16[20,5120]{1,0:T(8,128)(2,1)}, bf16[20,5120]{1,0:T(8,128)(2,1)S(1)}, u32[]{:S(2)}, u32[]{:S(2)}) collective-permute-start(bf16[20,5120]{1,0:T(8,128)(2,1)} %bitcast.30), channel_id=1, source_target_pairs={{0,0},{64,4},{4,64},{68,68},{1,1},{65,5},{5,65},{69,69},{2,2},{66,... | collective-permute-start | bytes 614408 | tf_op jit(solution)/shard_map/ppermute | solution.py:44
  16.1 59.7 %collective-permute-start.18 = (bf16[336,5120]{1,0:T(8,128)(2,1)S(1)}, bf16[336,5120]{1,0:T(8,128)(2,1)S(1)}, u32[]{:S(2)}, u32[]{:S(2)}) collective-permute-start(bf16[336,5120]{1,0:T(8,128)(2,1)S(1)} %held.19), channel_id=1, source_target_pairs={{0,0},{64,4},{4,64},{68,68},{1,1},{65,5},{5,65},{69,69},{2,2},{66,... | collective-permute-start | bytes 10321928 | tf_op jit(solution)/shard_map/ppermute | solution.py:44
  18.7 8.6 %collective-permute-start.2 = (bf16[20,5120]{1,0:T(8,128)(2,1)S(1)}, bf16[20,5120]{1,0:T(8,128)(2,1)S(1)}, u32[]{:S(2)}, u32[]{:S(2)}) collective-permute-start(bf16[20,5120]{1,0:T(8,128)(2,1)S(1)} %held.15.refs_0_), channel_id=1, source_target_pairs={{1,0},{2,1},{3,2},{0,3},{5,4},{6,5},{7,6},{4,7},{9,8},{10,9},{11,1... | collective-permute-start | bytes 614408 | tf_op jit(solution)/shard_map/ppermute | solution.py:34
  21.5 10.0 %collective-permute-start.5 = (bf16[20,5120]{1,0:T(8,128)(2,1)S(1)}, bf16[20,5120]{1,0:T(8,128)(2,1)S(1)}, u32[]{:S(2)}, u32[]{:S(2)}) collective-permute-start(bf16[20,5120]{1,0:T(8,128)(2,1)S(1)} %collective-permute-done.1.refs_1_.refs_0_), channel_id=1, source_target_pairs={{8,0},{16,8},{24,16},{32,24},{40,32},{48,40},{56,48},{0,56},{9,1},... | collective-permute-start | bytes 614408 | tf_op jit(solution)/shard_map/ppermute | solution.py:34
  27.1 7.8 %collective-permute-start.7 = (bf16[20,5120]{1,0:T(8,128)(2,1)S(1)}, bf16[20,5120]{1,0:T(8,128)(2,1)S(1)}, u32[]{:S(2)}, u32[]{:S(2)}) collective-permute-start(bf16[20,5120]{1,0:T(8,128)(2,1)S(1)} %collective-permute-done.1.refs_1_.refs_0_), channel_id=1, source_target_pairs={{56,0},{0,8},{8,16},{16,24},{24,32},{32,40},{40,48},{48,56},{57,1}... | collective-permute-start | bytes 614408 | tf_op jit(solution)/shard_map/ppermute | solution.py:34
  27.1 8.9 %collective-permute-start.3 = (bf16[20,5120]{1,0:T(8,128)(2,1)S(1)}, bf16[20,5120]{1,0:T(8,128)(2,1)S(1)}, u32[]{:S(2)}, u32[]{:S(2)}) collective-permute-start(bf16[20,5120]{1,0:T(8,128)(2,1)S(1)} %held.15.refs_0_), channel_id=1, source_target_pairs={{3,0},{0,1},{1,2},{2,3},{7,4},{4,5},{5,6},{6,7},{11,8},{8,9},{9,10... | collective-permute-start | bytes 614408 | tf_op jit(solution)/shard_map/ppermute | solution.py:34
  27.3 8.7 %collective-permute-start.4 = (bf16[20,5120]{1,0:T(8,128)(2,1)S(1)}, bf16[20,5120]{1,0:T(8,128)(2,1)S(1)}, u32[]{:S(2)}, u32[]{:S(2)}) collective-permute-start(bf16[20,5120]{1,0:T(8,128)(2,1)S(1)} %held.15.refs_0_), channel_id=1, source_target_pairs={{2,0},{3,1},{0,2},{1,3},{6,4},{7,5},{4,6},{5,7},{10,8},{11,9},{8,1... | collective-permute-start | bytes 614408 | tf_op jit(solution)/shard_map/ppermute | solution.py:34
  31.5 11.4 %collective-permute-start.6 = (bf16[20,5120]{1,0:T(8,128)(2,1)S(1)}, bf16[20,5120]{1,0:T(8,128)(2,1)S(1)}, u32[]{:S(2)}, u32[]{:S(2)}) collective-permute-start(bf16[20,5120]{1,0:T(8,128)(2,1)S(1)} %collective-permute-done.5.refs_1_), channel_id=1, source_target_pairs={{8,0},{16,8},{24,16},{32,24},{40,32},{48,40},{56,48},{0,56},{9,1},... | collective-permute-start | bytes 614408 | tf_op jit(solution)/shard_map/ppermute | solution.py:34
  34.9 9.0 %collective-permute-start.8 = (bf16[20,5120]{1,0:T(8,128)(2,1)S(1)}, bf16[20,5120]{1,0:T(8,128)(2,1)S(1)}, u32[]{:S(2)}, u32[]{:S(2)}) collective-permute-start(bf16[20,5120]{1,0:T(8,128)(2,1)S(1)} %collective-permute-done.7.refs_3_), channel_id=1, source_target_pairs={{56,0},{0,8},{8,16},{16,24},{24,32},{32,40},{40,48},{48,56},{57,1}... | collective-permute-start | bytes 614408 | tf_op jit(solution)/shard_map/ppermute | solution.py:34
  43.9 9.4 %collective-permute-start.10 = (bf16[20,5120]{1,0:T(8,128)(2,1)S(1)}, bf16[20,5120]{1,0:T(8,128)(2,1)S(1)}, u32[]{:S(2)}, u32[]{:S(2)}) collective-permute-start(bf16[20,5120]{1,0:T(8,128)(2,1)S(1)} %get-tuple-element.19.refs_2_), channel_id=1, source_target_pairs={{16,0},{24,8},{32,16},{40,24},{48,32},{56,40},{0,48},{8,56},{17,1}... | collective-permute-start | bytes 614408 | tf_op jit(solution)/shard_map/ppermute | solution.py:34
  43.9 15.9 %collective-permute-start.9 = (bf16[20,5120]{1,0:T(8,128)(2,1)S(1)}, bf16[20,5120]{1,0:T(8,128)(2,1)S(1)}, u32[]{:S(2)}, u32[]{:S(2)}) collective-permute-start(bf16[20,5120]{1,0:T(8,128)(2,1)S(1)} %get-tuple-element.19.refs_2_), channel_id=1, source_target_pairs={{8,0},{16,8},{24,16},{32,24},{40,32},{48,40},{56,48},{0,56},{9,1},... | collective-permute-start | bytes 614408 | tf_op jit(solution)/shard_map/ppermute | solution.py:34
  46.1 13.7 %collective-permute-start.11 = (bf16[20,5120]{1,0:T(8,128)(2,1)S(1)}, bf16[20,5120]{1,0:T(8,128)(2,1)S(1)}, u32[]{:S(2)}, u32[]{:S(2)}) collective-permute-start(bf16[20,5120]{1,0:T(8,128)(2,1)S(1)} %get-tuple-element.20.refs_2_), channel_id=1, source_target_pairs={{56,0},{0,8},{8,16},{16,24},{24,32},{32,40},{40,48},{48,56},{57,1}... | collective-permute-start | bytes 614408 | tf_op jit(solution)/shard_map/ppermute | solution.py:34
  60.2 13.0 %collective-permute-start.12 = (bf16[80,5120]{1,0:T(8,128)(2,1)S(1)}, bf16[80,5120]{1,0:T(8,128)(2,1)S(1)}, u32[]{:S(2)}, u32[]{:S(2)}) collective-permute-start(bf16[80,5120]{1,0:T(8,128)(2,1)S(1)} %stacked.3.refs_0_), channel_id=1, source_target_pairs={{8,0},{16,8},{24,16},{32,24},{40,32},{48,40},{56,48},{0,56},{9,1},... | collective-permute-start | bytes 2457608 | tf_op jit(solution)/shard_map/ppermute | solution.py:34
  60.2 12.9 %collective-permute-start.13 = (bf16[80,5120]{1,0:T(8,128)(2,1)S(1)}, bf16[80,5120]{1,0:T(8,128)(2,1)S(1)}, u32[]{:S(2)}, u32[]{:S(2)}) collective-permute-start(bf16[80,5120]{1,0:T(8,128)(2,1)S(1)} %stacked.3.refs_0_), channel_id=1, source_target_pairs={{56,0},{0,8},{8,16},{16,24},{24,32},{32,40},{40,48},{48,56},{57,1}... | collective-permute-start | bytes 2457608 | tf_op jit(solution)/shard_map/ppermute | solution.py:34
  62.0 11.5 %collective-permute-start.14 = (bf16[80,5120]{1,0:T(8,128)(2,1)S(1)}, bf16[80,5120]{1,0:T(8,128)(2,1)S(1)}, u32[]{:S(2)}, u32[]{:S(2)}) collective-permute-start(bf16[80,5120]{1,0:T(8,128)(2,1)S(1)} %stacked.5.refs_0_), channel_id=1, source_target_pairs={{1,0},{2,1},{3,2},{0,3},{5,4},{6,5},{7,6},{4,7},{9,8},{10,9},{11,1... | collective-permute-start | bytes 2457608 | tf_op jit(solution)/shard_map/ppermute | solution.py:34
  62.1 13.6 %collective-permute-start.15 = (bf16[80,5120]{1,0:T(8,128)(2,1)S(1)}, bf16[80,5120]{1,0:T(8,128)(2,1)S(1)}, u32[]{:S(2)}, u32[]{:S(2)}) collective-permute-start(bf16[80,5120]{1,0:T(8,128)(2,1)S(1)} %stacked.5.refs_0_), channel_id=1, source_target_pairs={{3,0},{0,1},{1,2},{2,3},{7,4},{4,5},{5,6},{6,7},{11,8},{8,9},{9,10... | collective-permute-start | bytes 2457608 | tf_op jit(solution)/shard_map/ppermute | solution.py:34
  75.8 4.8 %copy-start.1 = (f32[1,112,5120]{2,1,0:T(8,128)S(1)}, f32[1,112,5120]{2,1,0:T(8,128)}, u32[]{:S(2)}) copy-start(f32[1,112,5120]{2,1,0:T(8,128)} %param.13) | copy-start | bytes 6881284
  75.8 6.3 %collective-permute-start.19 = (bf16[336,5120]{1,0:T(8,128)(2,1)S(1)}, bf16[336,5120]{1,0:T(8,128)(2,1)S(1)}, u32[]{:S(2)}, u32[]{:S(2)}) collective-permute-start(bf16[336,5120]{1,0:T(8,128)(2,1)S(1)} %held.20.refs_8_.refs_9_.refs_11_), channel_id=1, source_target_pairs={{64,0},{0,64},{65,1},{1,65},{66,2},{2,66},{67,3},{3,67},{68,4},{4,... | collective-permute-start | bytes 10321928 | tf_op jit(solution)/shard_map/ppermute | solution.py:34
  76.0 20.7 %collective-permute-start.20 = (bf16[80,5120]{1,0:T(8,128)(2,1)S(1)}, bf16[80,5120]{1,0:T(8,128)(2,1)S(1)}, u32[]{:S(2)}, u32[]{:S(2)}) collective-permute-start(bf16[80,5120]{1,0:T(8,128)(2,1)S(1)} %held.21.refs_1_), channel_id=1, source_target_pairs={{1,0},{2,1},{3,2},{0,3},{5,4},{6,5},{7,6},{4,7},{9,8},{10,9},{11,1... | collective-permute-start | bytes 2457608 | tf_op jit(solution)/shard_map/ppermute | solution.py:34
  76.1 20.7 %collective-permute-start.21 = (bf16[80,5120]{1,0:T(8,128)(2,1)S(1)}, bf16[80,5120]{1,0:T(8,128)(2,1)S(1)}, u32[]{:S(2)}, u32[]{:S(2)}) collective-permute-start(bf16[80,5120]{1,0:T(8,128)(2,1)S(1)} %held.21.refs_1_), channel_id=1, source_target_pairs={{3,0},{0,1},{1,2},{2,3},{7,4},{4,5},{5,6},{6,7},{11,8},{8,9},{9,10... | collective-permute-start | bytes 2457608 | tf_op jit(solution)/shard_map/ppermute | solution.py:34
  77.6 19.5 %collective-permute-start.16 = (bf16[80,5120]{1,0:T(8,128)(2,1)S(1)}, bf16[80,5120]{1,0:T(8,128)(2,1)S(1)}, u32[]{:S(2)}, u32[]{:S(2)}) collective-permute-start(bf16[80,5120]{1,0:T(8,128)(2,1)S(1)} %get-tuple-element.21.refs_1_), channel_id=1, source_target_pairs={{8,0},{16,8},{24,16},{32,24},{40,32},{48,40},{56,48},{0,56},{9,1},... | collective-permute-start | bytes 2457608 | tf_op jit(solution)/shard_map/ppermute | solution.py:34
  80.5 19.7 %collective-permute-start.17 = (bf16[80,5120]{1,0:T(8,128)(2,1)S(1)}, bf16[80,5120]{1,0:T(8,128)(2,1)S(1)}, u32[]{:S(2)}, u32[]{:S(2)}) collective-permute-start(bf16[80,5120]{1,0:T(8,128)(2,1)S(1)} %get-tuple-element.22.refs_2_.refs_8_), channel_id=1, source_target_pairs={{56,0},{0,8},{8,16},{16,24},{24,32},{32,40},{40,48},{48,56},{57,1}... | collective-permute-start | bytes 2457608 | tf_op jit(solution)/shard_map/ppermute | solution.py:34
  82.1 30.9 %collective-permute-start.24 = (f32[64,5120]{1,0:T(8,128)S(1)}, f32[64,5120]{1,0:T(8,128)S(1)}, u32[]{:S(2)}, u32[]{:S(2)}) collective-permute-start(f32[64,5120]{1,0:T(8,128)S(1)} %held.23), channel_id=1, source_target_pairs={{128,0},{0,128},{129,1},{1,129},{130,2},{2,130},{131,3},{3,131},{1... | collective-permute-start | bytes 3932168 | tf_op jit(solution)/shard_map/ppermute | solution.py:34
  96.8 19.7 %collective-permute-start.26 = (bf16[80,5120]{1,0:T(8,128)(2,1)S(1)}, bf16[80,5120]{1,0:T(8,128)(2,1)S(1)}, u32[]{:S(2)}, u32[]{:S(2)}) collective-permute-start(bf16[80,5120]{1,0:T(8,128)(2,1)S(1)} %collective-permute-done.21.refs_4_.refs_5_), channel_id=1, source_target_pairs={{3,0},{0,1},{1,2},{2,3},{7,4},{4,5},{5,6},{6,7},{11,8},{8,9},{9,10... | collective-permute-start | bytes 2457608 | tf_op jit(solution)/shard_map/ppermute | solution.py:34
  100.2 18.2 %collective-permute-start.22 = (bf16[80,5120]{1,0:T(8,128)(2,1)S(1)}, bf16[80,5120]{1,0:T(8,128)(2,1)S(1)}, u32[]{:S(2)}, u32[]{:S(2)}) collective-permute-start(bf16[80,5120]{1,0:T(8,128)(2,1)S(1)} %get-tuple-element.23.refs_1_.refs_2_), channel_id=1, source_target_pairs={{8,0},{16,8},{24,16},{32,24},{40,32},{48,40},{56,48},{0,56},{9,1},... | collective-permute-start | bytes 2457608 | tf_op jit(solution)/shard_map/ppermute | solution.py:34
  100.5 17.9 %collective-permute-start.25 = (bf16[80,5120]{1,0:T(8,128)(2,1)S(1)}, bf16[80,5120]{1,0:T(8,128)(2,1)S(1)}, u32[]{:S(2)}, u32[]{:S(2)}) collective-permute-start(bf16[80,5120]{1,0:T(8,128)(2,1)S(1)} %held.24.refs_2_), channel_id=1, source_target_pairs={{1,0},{2,1},{3,2},{0,3},{5,4},{6,5},{7,6},{4,7},{9,8},{10,9},{11,1... | collective-permute-start | bytes 2457608 | tf_op jit(solution)/shard_map/ppermute | solution.py:34
  102.6 18.9 %collective-permute-start.23 = (bf16[80,5120]{1,0:T(8,128)(2,1)S(1)}, bf16[80,5120]{1,0:T(8,128)(2,1)S(1)}, u32[]{:S(2)}, u32[]{:S(2)}) collective-permute-start(bf16[80,5120]{1,0:T(8,128)(2,1)S(1)} %get-tuple-element.24.refs_7_), channel_id=1, source_target_pairs={{56,0},{0,8},{8,16},{16,24},{24,32},{32,40},{40,48},{48,56},{57,1}... | collective-permute-start | bytes 2457608 | tf_op jit(solution)/shard_map/ppermute | solution.py:34
  113.0 26.1 %collective-permute-start.29 = (f32[56,5120]{1,0:T(8,128)S(1)}, f32[56,5120]{1,0:T(8,128)S(1)}, u32[]{:S(2)}, u32[]{:S(2)}) collective-permute-start(f32[56,5120]{1,0:T(8,128)S(1)} %held.26), channel_id=1, source_target_pairs={{128,0},{0,128},{129,1},{1,129},{130,2},{2,130},{131,3},{3,131},{1... | collective-permute-start | bytes 3440648 | tf_op jit(solution)/shard_map/ppermute | solution.py:34
  121.6 17.5 %collective-permute-start.27 = (bf16[48,5120]{1,0:T(8,128)(2,1)S(1)}, bf16[48,5120]{1,0:T(8,128)(2,1)S(1)}, u32[]{:S(2)}, u32[]{:S(2)}) collective-permute-start(bf16[48,5120]{1,0:T(8,128)(2,1)S(1)} %slice.23), channel_id=1, source_target_pairs={{8,0},{16,8},{24,16},{32,24},{40,32},{48,40},{56,48},{0,56},{9,1},... | collective-permute-start | bytes 1474568 | tf_op jit(solution)/shard_map/ppermute | solution.py:34
  121.7 17.4 %collective-permute-start.28 = (bf16[32,5120]{1,0:T(8,128)(2,1)S(1)}, bf16[32,5120]{1,0:T(8,128)(2,1)S(1)}, u32[]{:S(2)}, u32[]{:S(2)}) collective-permute-start(bf16[32,5120]{1,0:T(8,128)(2,1)S(1)} %slice.24), channel_id=1, source_target_pairs={{56,0},{0,8},{8,16},{16,24},{24,32},{32,40},{40,48},{48,56},{57,1}... | collective-permute-start | bytes 983048 | tf_op jit(solution)/shard_map/ppermute | solution.py:34
  139.1 10.8 %copy-start.2 = (f32[1,112,5120]{2,1,0:T(8,128)S(1)}, f32[1,112,5120]{2,1,0:T(8,128)}, u32[]{:S(2)}) copy-start(f32[1,112,5120]{2,1,0:T(8,128)} %param.13) | copy-start | bytes 6881284
  148.0 6.0 %collective-permute-start.30 = (f32[112,5120]{1,0:T(8,128)S(1)}, f32[112,5120]{1,0:T(8,128)S(1)}, u32[]{:S(2)}, u32[]{:S(2)}) collective-permute-start(f32[112,5120]{1,0:T(8,128)S(1)} %get-tuple-element.28), channel_id=1, source_target_pairs={{64,0},{0,64},{65,1},{1,65},{66,2},{2,66},{67,3},{3,67},{68,4},{4,... | collective-permute-start | bytes 6881288 | tf_op jit(solution)/shard_map/ppermute | solution.py:34
  151.6 49.6 %collective-permute-start.33 = (f32[120,5120]{1,0:T(8,128)}, f32[120,5120]{1,0:T(8,128)}, u32[]{:S(2)}, u32[]{:S(2)}) collective-permute-start(f32[120,5120]{1,0:T(8,128)} %held.29), channel_id=1, source_target_pairs={{64,0},{0,64},{65,1},{1,65},{66,2},{2,66},{67,3},{3,67},{68,4},{4,... | collective-permute-start | bytes 7372808 | tf_op jit(solution)/shard_map/ppermute | solution.py:34
  156.5 44.7 %collective-permute-start.34 = (f32[112,5120]{1,0:T(8,128)}, f32[112,5120]{1,0:T(8,128)}, u32[]{:S(2)}, u32[]{:S(2)}) collective-permute-start(f32[112,5120]{1,0:T(8,128)} %get-tuple-element.35.refs_5_), channel_id=1, source_target_pairs={{64,4},{4,64},{65,5},{5,65},{66,6},{6,66},{67,7},{7,67},{72,12},{1... | collective-permute-start | bytes 6881288 | tf_op jit(solution)/shard_map/ppermute | solution.py:44
  163.3 37.9 %collective-permute-start.31 = (f32[64,5120]{1,0:T(8,128)S(1)}, f32[64,5120]{1,0:T(8,128)}, u32[]{:S(2)}, u32[]{:S(2)}) collective-permute-start(f32[64,5120]{1,0:T(8,128)S(1)} %get-tuple-element.29.refs_0_), channel_id=1, source_target_pairs={{64,0},{0,64},{65,1},{1,65},{66,2},{2,66},{67,3},{3,67},{68,4},{4,... | collective-permute-start | bytes 3932168 | tf_op jit(solution)/shard_map/ppermute | solution.py:34
  163.4 37.8 %collective-permute-start.32 = (f32[56,5120]{1,0:T(8,128)S(1)}, f32[56,5120]{1,0:T(8,128)}, u32[]{:S(2)}, u32[]{:S(2)}) collective-permute-start(f32[56,5120]{1,0:T(8,128)S(1)} %get-tuple-element.30.refs_1_), channel_id=1, source_target_pairs={{64,0},{0,64},{65,1},{1,65},{66,2},{2,66},{67,3},{3,67},{68,4},{4,... | collective-permute-start | bytes 3440648 | tf_op jit(solution)/shard_map/ppermute | solution.py:34
  201.2 1.6 copy-start

commit v9 on v8

--- a/solution.py
+++ b/solution.py
@@ -24,7 +24,6 @@
 HALF = 128
 CUT = 64
 NO_COST = pl.CostEstimate(flops=1, bytes_accessed=1, transcendentals=0)
-MUCH_COST = pl.CostEstimate(flops=3 * 10**10, bytes_accessed=1, transcendentals=0)
 BLOCK = 1024
 
 
@@ -129,11 +128,7 @@
 
     @pl.when(at == pl.num_programs(0) - 1)
     def _():
-        column, block = row // 4, row // 32
-        for dz in range(8):
-            for dy in range(4):
-                start, place = dy * column + dz * block, (4 * dz + dy) * block
-                out_ref[place : place + block, :] = total[start : start + block, :]
+        out_ref[...] = total[...]
 
 
 def hidden_of(parts, mine, theirs):
@@ -151,14 +146,14 @@
             pltpu.VMEM((2 * HALF, BLOCK), jnp.bfloat16),
         ],
         compiler_params=params_of(16),
-        cost_estimate=MUCH_COST,
+        cost_estimate=NO_COST,
         name="hidden",
     )(*parts, mine, theirs)
 
 
 def grad_kernel(*refs):
-    *parts, my_params, their_params, my_up, their_up, hidden_ref, own_ref, other_ref = refs[:-6]
-    rows, preact, up_proj, turned, wide_params, wide_up = refs[-6:]
+    *parts, my_params, their_params, my_up, their_up, most_ref, far_ref = refs[:-9]
+    own_ref, other_ref, rows, preact, up_proj, hidden, turned, wide_params, wide_up = refs[-9:]
     at = pl.program_id(0)
 
     @pl.when(at == 0)
@@ -167,6 +162,14 @@
         up_proj[...] = jnp.zeros_like(up_proj)
         clear(wide_params)
         clear(wide_up)
+        column, block = hidden.shape[0] // 4, hidden.shape[0] // 32
+        for dz in range(8):
+            for dy in range(4):
+                place, start = (4 * dz + dy) * block, dz * block
+                if dy < 3:
+                    start += dy * column
+                source = most_ref if dy < 3 else far_ref
+                hidden[place : place + block, :] = source[start : start + block, :]
 
     columns = pl.ds(pl.multiple_of(at * BLOCK, BLOCK), BLOCK)
     row = 0
@@ -182,7 +185,7 @@
     @pl.when(at == pl.num_programs(0) - 1)
     def _():
         slope = silu_slope(preact[...] * WIDTH_SCALE)
-        turned[...] = (hidden_ref[...] * up_proj[...] * slope).T.astype(jnp.bfloat16)
+        turned[...] = (hidden[...] * up_proj[...] * slope).T.astype(jnp.bfloat16)
 
         @pl.loop(0, D // BLOCK)
         def _(block):
@@ -192,7 +195,7 @@
             other_ref[:, columns] = grad[HALF : HALF + ROWS] * WIDTH_SCALE
 
 
-def gate_grads(parts, mine, theirs, hidden):
+def gate_grads(parts, mine, theirs, hidden_most, hidden_far):
     count = sum(part.shape[0] for part in parts)
 
     def weights(which):
@@ -204,11 +207,12 @@
         grid=(D // BLOCK,),
         in_specs=[pl.BlockSpec((part.shape[0], BLOCK), lambda at: (0, at)) for part in parts]
         + [weights(0), weights(0), weights(1), weights(1)]
-        + [pl.BlockSpec((count, 2 * HALF), lambda at: (0, 0))],
+        + [pl.BlockSpec(one.shape, lambda at: (0, 0)) for one in (hidden_most, hidden_far)],
         out_specs=[whole, whole],
         out_shape=[jax.ShapeDtypeStruct((ROWS, D), jnp.float32)] * 2,
         scratch_shapes=[
             pltpu.VMEM((count, D), jnp.bfloat16),
+            pltpu.VMEM((count, 2 * HALF), jnp.float32),
             pltpu.VMEM((count, 2 * HALF), jnp.float32),
             pltpu.VMEM((count, 2 * HALF), jnp.float32),
             pltpu.VMEM((2 * HALF, count), jnp.bfloat16),
@@ -218,7 +222,7 @@
         compiler_params=params_of(36),
         cost_estimate=NO_COST,
         name="gate_grads",
-    )(*parts, mine, theirs, mine, theirs, hidden)
+    )(*parts, mine, theirs, mine, theirs, hidden_most, hidden_far)
 
 
 def updated_kernel(factor, kept_weight, which, numerator, *refs):
@@ -299,7 +303,7 @@
             pltpu.SemaphoreType.DMA((2, blocks)),
             pltpu.SemaphoreType.DMA((blocks,)),
         ],
-        compiler_params=params_of(16),
+        compiler_params=params_of(56),
         name="updated",
     )(factor, kept_weight, which, numerator, *more)
 
@@ -316,7 +320,7 @@
     rows_in = held(rows_in, rows_grad, weights)
     near = [rows_in] + [shifted(rows_in, "y", steps) for steps in (1, 3, 2)]
     ring = {0: rows_grad, 1: shifted(rows_grad, "z", 1), 7: shifted(rows_grad, "z", 7)}
-    mine = transposed(held(weights, rows_grad))
+    mine = transposed(held(weights, ring[1], ring[7]))
     ring[2], ring[6] = shifted(ring[1], "z", 1), shifted(ring[7], "z", 7)
     ring[2], ring[6] = held((ring[2], ring[6]), *near[1:])
     ring[3], ring[5] = shifted(ring[2], "z", 1), shifted(ring[6], "z", 7)
@@ -327,31 +331,33 @@
 
     blocks[1], blocks[7] = shifted(blocks[0], "z", 1), shifted(blocks[0], "z", 7)
     following, before = [shifted(columns[0], "y", 1)], [shifted(columns[0], "y", 3)]
-    blocks[1], blocks[7] = held((blocks[1], blocks[7]), columns[1], following[0], before[0])
+    ready = (columns[1], following[0], before[0], mine)
+    blocks[1], blocks[7] = held((blocks[1], blocks[7]), *ready)
 
     blocks[2], blocks[6] = shifted(blocks[1], "z", 1), shifted(blocks[7], "z", 7)
     columns[1] = held(columns[1], blocks[1], blocks[7])
     following.append(shifted(columns[1], "y", 1))
     before.append(shifted(columns[1], "y", 3))
-    mine = held(mine, blocks[1], blocks[7])
-    theirs = shifted(mine, "core", 1)
-    blocks[2], blocks[6] = held((blocks[2], blocks[6]), theirs, following[1], before[1])
+    stale = jnp.concatenate([stale_num[0], jnp.broadcast_to(stale_weight, (8, D))], axis=0)
+    two_before = [shifted(held(stale[:CUT], mine), "x_lo", 1)]
+    ready = (two_before[0], following[1], before[1])
+    blocks[2], blocks[6] = held((blocks[2], blocks[6]), *ready)
 
     blocks[3], blocks[5] = shifted(blocks[2], "z", 1), shifted(blocks[6], "z", 7)
     following[0] = held(following[0], blocks[2])
     far = [shifted(following[0], "y", 1), shifted(before[1], "y", 3)]
-    stale = jnp.concatenate([stale_num[0], jnp.broadcast_to(stale_weight, (8, D))], axis=0)
-    two_before = [shifted(held(stale[:CUT], theirs), "x_lo", 1)]
-    blocks[3], blocks[5] = held((blocks[3], blocks[5]), two_before[0], *far)
+    mine = held(mine, blocks[2], blocks[6])
+    theirs = shifted(mine, "core", 1)
+    two_before.append(shifted(held(stale[CUT:], two_before[0]), "x_lo", 1))
+    hidden_most = hidden_of([*columns, *following, *before], mine, theirs)
+    blocks[3], blocks[5] = held((blocks[3], blocks[5]), hidden_most, *far)
 
     cut = 48
     last = [shifted(blocks[3][:cut], "z", 1), shifted(blocks[5][cut:], "z", 7)]
-    two_before.append(shifted(held(stale[CUT:], two_before[0]), "x_lo", 1))
-    hidden = hidden_of([*columns, *following, *before, *far], mine, theirs)
-    hidden = held(hidden, two_before[1])
+    hidden_far = held(hidden_of(far, mine, theirs), two_before[1])
     parts = [blocks[steps] for steps in (0, 1, 2, 3)] + last + [blocks[steps] for steps in (5, 6, 7)]
 
-    own_grad, other_grad = gate_grads(parts, mine, theirs, hidden)
+    own_grad, other_grad = gate_grads(parts, mine, theirs, hidden_most, hidden_far)
     two_before = held(tuple(two_before), own_grad)
     one_before = [shifted(part, "core", 1) for part in two_before]
     stale_hop = shifted(held(stale, own_grad), "core", 1)

time: 210 us -> 218 us (1.038)
  starting transfers between devices: 52.5 us -> 60.1 us
  waiting for transfers between devices: 84.9 us -> 79.8 us
  blocking collectives: 33.9 us -> 37.4 us
  Pallas kernels: 22.9 us -> 25.9 us
    ppermute x31, waiting for transfers between devices: 80.4 us -> 56 us  [shifted(): return lax.ppermute(value, axis, pairs)]
    ppermute x4, waiting for transfers between devices: 4.52 us -> 23.9 us  [transposed(): return lax.ppermute(value, ('core', 'x_hi'), pairs)]
    ppermute x4, starting transfers between devices: 17.5 us -> 23.8 us  [transposed(): return lax.ppermute(value, ('core', 'x_hi'), pairs)]
    psum x2, blocking collectives: 20.3 us -> 23.9 us  [shards(): norm_sq = lax.psum(norm_sq, axes)]
    pallas_call x1 -> x2, Pallas kernels: 7.83 us -> 8.71 us  [hidden_of(): pl.pallas_call(hidden_kernel, grid=(D // BLOCK,), in_specs=[pl.BlockSpec(...]
  transfers between devices with their start and end apart: 35 -> 35, of which waited for: 22 -> 19; matrix products, arithmetic and copies ran while one was open for 4% -> 4% of each run, Pallas kernels for 4% -> 4%
where the time goes in v9:
time: 218 us; the launch traced here: 217 us
  waiting for transfers between devices  79.8 us (37%)
  starting transfers between devices  60.1 us (28%)
  blocking collectives  37.4 us (17%)
  Pallas kernels  25.9 us (12%)
  other arithmetic  5.88 us (3%)
  between operations  5.56 us (3%)
  local copies, waits for them, and re-layouts  2.53 us (1%)
    ppermute x31, waiting for transfers between devices, shifted(): return lax.ppermute(value, axis, pairs)  56 us
    ppermute x31, starting transfers between devices, shifted(): return lax.ppermute(value, axis, pairs)  36.3 us
    psum x2, blocking collectives, shards(): norm_sq = lax.psum(norm_sq, axes)  23.9 us
    ppermute x4, waiting for transfers between devices, transposed(): return lax.ppermute(value, ('core', 'x_hi'), pairs)  23.9 us
    ppermute x4, starting transfers between devices, transposed(): return lax.ppermute(value, ('core', 'x_hi'), pairs)  23.8 us
    psum x1, blocking collectives, shards(): lax.psum(jnp.where(jnp.arange(2) == x_hi, norm_sq, 0.0), ('core', 'x_hi'))  13.6 us
    pallas_call x1, Pallas kernels, gate_grads(): pl.pallas_call(grad_kernel, grid=(D // BLOCK,), in_specs=[pl.BlockSpec((p...  9.01 us
    pallas_call x2, Pallas kernels, hidden_of(): pl.pallas_call(hidden_kernel, grid=(D // BLOCK,), in_specs=[pl.BlockSpec(...  8.71 us
  transfers between devices with their start and end apart: 35, of which 19 were waited for; matrix products, arithmetic and copies ran while one was open for 4% of the time, Pallas kernels for 4%

profile of v9, /device:TPU:1, one launch (start us, length us, event | category | flops | bytes accessed | tf_op | source)
XLA Modules:
  0.0 217.3 jit_solution(13191446086989432686)
XLA Ops:
  0.7 6.2 %collective-permute-start = (bf16[20,5120]{1,0:T(8,128)(2,1)}, bf16[20,5120]{1,0:T(8,128)(2,1)S(1)}, u32[]{:S(2)}, u32[]{:S(2)}) collective-permute-start(bf16[20,5120]{1,0:T(8,128)(2,1)} %bitcast.30), channel_id=1, source_target_pairs={{0,0},{64,4},{4,64},{68,68},{1,1},{65,5},{5,65},{69,69},{2,2},{66,... | collective-permute-start | bytes 614408 | tf_op jit(solution)/shard_map/ppermute | solution.py:43
  6.8 1.9 collective-permute-start.1
  9.4 1.8 divide_convert_fusion
  11.2 4.8 %collective-permute-done.1.refs_1_.refs_0_ = bf16[20,5120]{1,0:T(8,128)(2,1)S(1)} collective-permute-done((bf16[20,5120]{1,0:T(8,128)(2,1)}, bf16[20,5120]{1,0:T(8,128)(2,1)S(1)}, u32[]{:S(2)}, u32[]{:S(2)}) %collective-permute-start.1) | collective-permute-done | bytes 204832 | tf_op jit(solution)/shard_map/ppermute | solution.py:43
  16.1 5.6 %collective-permute-start.5 = (bf16[20,5120]{1,0:T(8,128)(2,1)S(1)}, bf16[20,5120]{1,0:T(8,128)(2,1)S(1)}, u32[]{:S(2)}, u32[]{:S(2)}) collective-permute-start(bf16[20,5120]{1,0:T(8,128)(2,1)S(1)} %collective-permute-done.1.refs_1_.refs_0_), channel_id=1, source_target_pairs={{8,0},{16,8},{24,16},{32,24},{40,32},{48,40},{56,48},{0,56},{9,1},... | collective-permute-start | bytes 614408 | tf_op jit(solution)/shard_map/ppermute | solution.py:33
  21.7 0.3 pad_maximum_fusion.refs_2_.refs_0_
  22.0 2.8 %collective-permute-done.5.refs_1_ = bf16[20,5120]{1,0:T(8,128)(2,1)S(1)} collective-permute-done((bf16[20,5120]{1,0:T(8,128)(2,1)S(1)}, bf16[20,5120]{1,0:T(8,128)(2,1)S(1)}, u32[]{:S(2)}, u32[]{:S(2)}) %collective-permute-start.5) | collective-permute-done | bytes 204832 | tf_op jit(solution)/shard_map/ppermute | solution.py:33
  24.8 3.1 %collective-permute-done.7.refs_3_.refs_2_ = bf16[20,5120]{1,0:T(8,128)(2,1)S(1)} collective-permute-done((bf16[20,5120]{1,0:T(8,128)(2,1)S(1)}, bf16[20,5120]{1,0:T(8,128)(2,1)S(1)}, u32[]{:S(2)}, u32[]{:S(2)}) %collective-permute-start.7) | collective-permute-done | bytes 204832 | tf_op jit(solution)/shard_map/ppermute | solution.py:33
  27.9 4.0 %collective-permute-start.16 = (bf16[336,5120]{1,0:T(8,128)(2,1)S(1)}, bf16[336,5120]{1,0:T(8,128)(2,1)S(1)}, u32[]{:S(2)}, u32[]{:S(2)}) collective-permute-start(bf16[336,5120]{1,0:T(8,128)(2,1)S(1)} %held.18), channel_id=1, source_target_pairs={{0,0},{64,4},{4,64},{68,68},{1,1},{65,5},{5,65},{69,69},{2,2},{66,... | collective-permute-start | bytes 10321928 | tf_op jit(solution)/shard_map/ppermute | solution.py:43
  32.0 2.8 %collective-permute-start.2 = (bf16[20,5120]{1,0:T(8,128)(2,1)S(1)}, bf16[20,5120]{1,0:T(8,128)(2,1)S(1)}, u32[]{:S(2)}, u32[]{:S(2)}) collective-permute-start(bf16[20,5120]{1,0:T(8,128)(2,1)S(1)} %held.15.refs_0_), channel_id=1, source_target_pairs={{1,0},{2,1},{3,2},{0,3},{5,4},{6,5},{7,6},{4,7},{9,8},{10,9},{11,1... | collective-permute-start | bytes 614408 | tf_op jit(solution)/shard_map/ppermute | solution.py:33
  34.8 1.6 collective-permute-start.4
  36.4 1.5 collective-permute-done.2.refs_2_.refs_1_
  37.9 6.0 %collective-permute-done.3.refs_3_.refs_2_ = bf16[20,5120]{1,0:T(8,128)(2,1)S(1)} collective-permute-done((bf16[20,5120]{1,0:T(8,128)(2,1)S(1)}, bf16[20,5120]{1,0:T(8,128)(2,1)S(1)}, u32[]{:S(2)}, u32[]{:S(2)}) %collective-permute-start.3) | collective-permute-done | bytes 204832 | tf_op jit(solution)/shard_map/ppermute | solution.py:33
  44.0 0.0 collective-permute-done.6.refs_0_
  44.0 2.2 collective-permute-done.8.refs_1_
  46.2 1.5 collective-permute-start.11
  47.6 7.6 %collective-permute-done.9.refs_1_.refs_3_ = bf16[20,5120]{1,0:T(8,128)(2,1)S(1)} collective-permute-done((bf16[20,5120]{1,0:T(8,128)(2,1)S(1)}, bf16[20,5120]{1,0:T(8,128)(2,1)S(1)}, u32[]{:S(2)}, u32[]{:S(2)}) %collective-permute-start.9) | collective-permute-done | bytes 204832 | tf_op jit(solution)/shard_map/ppermute | solution.py:33
  55.2 0.7 collective-permute-done.10.refs_2_.refs_0_
  55.9 0.3 stacked.3.refs_0_
  56.3 7.0 %collective-permute-start.12 = (bf16[80,5120]{1,0:T(8,128)(2,1)S(1)}, bf16[80,5120]{1,0:T(8,128)(2,1)S(1)}, u32[]{:S(2)}, u32[]{:S(2)}) collective-permute-start(bf16[80,5120]{1,0:T(8,128)(2,1)S(1)} %stacked.3.refs_0_), channel_id=1, source_target_pairs={{8,0},{16,8},{24,16},{32,24},{40,32},{48,40},{56,48},{0,56},{9,1},... | collective-permute-start | bytes 2457608 | tf_op jit(solution)/shard_map/ppermute | solution.py:33
  63.3 0.3 stacked.5.refs_0_
  63.6 2.3 %collective-permute-start.14 = (bf16[80,5120]{1,0:T(8,128)(2,1)S(1)}, bf16[80,5120]{1,0:T(8,128)(2,1)S(1)}, u32[]{:S(2)}, u32[]{:S(2)}) collective-permute-start(bf16[80,5120]{1,0:T(8,128)(2,1)S(1)} %stacked.5.refs_0_), channel_id=1, source_target_pairs={{1,0},{2,1},{3,2},{0,3},{5,4},{6,5},{7,6},{4,7},{9,8},{10,9},{11,1... | collective-permute-start | bytes 2457608 | tf_op jit(solution)/shard_map/ppermute | solution.py:33
  65.9 0.1 slice_bitcast_fusion.refs_0_
  66.0 19.0 %collective-permute-done.16.refs_5_.refs_1_.refs_0_ = bf16[336,5120]{1,0:T(8,128)(2,1)S(1)} collective-permute-done((bf16[336,5120]{1,0:T(8,128)(2,1)S(1)}, bf16[336,5120]{1,0:T(8,128)(2,1)S(1)}, u32[]{:S(2)}, u32[]{:S(2)}) %collective-permute-start.16) | collective-permute-done | bytes 3440672 | tf_op jit(solution)/shard_map/ppermute | solution.py:43
  85.0 0.8 collective-permute-start.19
  85.8 0.3 stacked.4.refs_2_.refs_0_
  86.2 0.1 collective-permute-start.17
  86.3 1.5 collective-permute-start.18
  87.7 3.0 %collective-permute-start.20 = (bf16[80,5120]{1,0:T(8,128)(2,1)S(1)}, bf16[80,5120]{1,0:T(8,128)(2,1)S(1)}, u32[]{:S(2)}, u32[]{:S(2)}) collective-permute-start(bf16[80,5120]{1,0:T(8,128)(2,1)S(1)} %held.21.refs_1_), channel_id=1, source_target_pairs={{1,0},{2,1},{3,2},{0,3},{5,4},{6,5},{7,6},{4,7},{9,8},{10,9},{11,1... | collective-permute-start | bytes 2457608 | tf_op jit(solution)/shard_map/ppermute | solution.py:33
  90.8 6.7 %collective-permute-done.17.refs_0_ = bf16[80,5120]{1,0:T(8,128)(2,1)S(1)} collective-permute-done((bf16[80,5120]{1,0:T(8,128)(2,1)S(1)}, bf16[80,5120]{1,0:T(8,128)(2,1)S(1)}, u32[]{:S(2)}, u32[]{:S(2)}) %collective-permute-start.17) | collective-permute-done | bytes 819232 | tf_op jit(solution)/shard_map/ppermute | solution.py:33
  97.5 1.3 collective-permute-done.18.refs_1_
  98.8 1.3 collective-permute-done.20.refs_3_
  100.0 3.1 %collective-permute-done.21.refs_4_.refs_5_ = bf16[80,5120]{1,0:T(8,128)(2,1)S(1)} collective-permute-done((bf16[80,5120]{1,0:T(8,128)(2,1)S(1)}, bf16[80,5120]{1,0:T(8,128)(2,1)S(1)}, u32[]{:S(2)}, u32[]{:S(2)}) %collective-permute-start.21) | collective-permute-done | bytes 819232 | tf_op jit(solution)/shard_map/ppermute | solution.py:33
  103.8 0.1 collective-permute-start.26
  103.9 1.4 collective-permute-start.22
  105.3 0.2 collective-permute-start.23
  105.5 2.6 %collective-permute-start.25 = (bf16[80,5120]{1,0:T(8,128)(2,1)S(1)}, bf16[80,5120]{1,0:T(8,128)(2,1)S(1)}, u32[]{:S(2)}, u32[]{:S(2)}) collective-permute-start(bf16[80,5120]{1,0:T(8,128)(2,1)S(1)} %held.23.refs_2_), channel_id=1, source_target_pairs={{1,0},{2,1},{3,2},{0,3},{5,4},{6,5},{7,6},{4,7},{9,8},{10,9},{11,1... | collective-permute-start | bytes 2457608 | tf_op jit(solution)/shard_map/ppermute | solution.py:33
  108.0 0.1 pad_slice_fusion.refs_0_
  108.1 1.1 collective-permute-done.24.refs_7_.refs_3_.refs_10_.refs_12_
  109.2 0.9 collective-permute-start.29
  110.1 6.1 %hidden.2.refs_2_.refs_13_ = f32[480,256]{1,0:T(8,128)S(1)} custom-call(bf16[80,5120]{1,0:T(8,128)(2,1)S(1)} %stacked.5.refs_0_, bf16[80,5120]{1,0:T(8,128)(2,1)S(1)} %held.21.refs_1_, bf16[80,5120]{1,0:T(8,128)(2,1)S(1)} %held.23.refs_2_, bf16[80,5120]{1,0:T(8,128)(2,1)S(1)} %collective-permute-done.20.refs_3_, ...), custom_call_target="tpu_custom_call" | custom-call | flops 1 | bytes 1 | tf_op jit(solution)/shard_map/hidden/pallas_call | solution.py:137
  116.2 8.2 %collective-permute-done.26.refs_4_.refs_1_ = bf16[80,5120]{1,0:T(8,128)(2,1)S(1)} collective-permute-done((bf16[80,5120]{1,0:T(8,128)(2,1)S(1)}, bf16[80,5120]{1,0:T(8,128)(2,1)S(1)}, u32[]{:S(2)}, u32[]{:S(2)}) %collective-permute-start.26) | collective-permute-done | bytes 819232 | tf_op jit(solution)/shard_map/ppermute | solution.py:33
  124.4 1.1 collective-permute-done.23.refs_1_
  125.5 1.3 collective-permute-start.27
  126.9 0.3 collective-permute-start.28
  127.2 2.6 %hidden.3.refs_0_ = f32[160,256]{1,0:T(8,128)S(1)} custom-call(bf16[80,5120]{1,0:T(8,128)(2,1)S(1)} %collective-permute-done.25.refs_3_.refs_0_, bf16[80,5120]{1,0:T(8,128)(2,1)S(1)} %collective-permute-done.26.refs_4_.refs_1_, bf16[336,5120]{1,0:T(8,128)(2,1)S(1)} %held.24.refs_6_.refs_2_.refs_9_.refs_11_, ...), custom_call_target="tpu_custom_call" | custom-call | flops 1 | bytes 1 | tf_op jit(solution)/shard_map/hidden/pallas_call | solution.py:137
  129.8 5.7 %collective-permute-done.29.refs_1_ = f32[56,5120]{1,0:T(8,128)S(1)} collective-permute-done((f32[56,5120]{1,0:T(8,128)S(1)}, f32[56,5120]{1,0:T(8,128)S(1)}, u32[]{:S(2)}, u32[]{:S(2)}) %collective-permute-start.29) | collective-permute-done | bytes 1146912 | tf_op jit(solution)/shard_map/ppermute | solution.py:33
  135.5 1.2 collective-permute-done.27.refs_4_
  136.6 9.0 %gate_grads.1 = (f32[112,5120]{1,0:T(8,128)S(1)}, f32[112,5120]{1,0:T(8,128)S(1)}) custom-call(bf16[80,5120]{1,0:T(8,128)(2,1)S(1)} %stacked.3.refs_0_, bf16[80,5120]{1,0:T(8,128)(2,1)S(1)} %get-tuple-element.21.refs_1_, bf16[80,5120]{1,0:T(8,128)(2,1)S(1)} %get-tuple-element.23.refs_1_.refs_2_, bf16[80,5120]{1,0:T(8,128)(2,1)S(1)} %get-tuple-element.25.refs_3_, ...), custom_call_target="tpu_custom_call" | custom-call | flops 1 | bytes 1 | tf_op jit(solution)/shard_map/gate_grads/pallas_call | solution.py:205
  145.7 2.9 %collective-permute-start.30 = (f32[112,5120]{1,0:T(8,128)S(1)}, f32[112,5120]{1,0:T(8,128)S(1)}, u32[]{:S(2)}, u32[]{:S(2)}) collective-permute-start(f32[112,5120]{1,0:T(8,128)S(1)} %get-tuple-element.28), channel_id=1, source_target_pairs={{64,0},{0,64},{65,1},{1,65},{66,2},{2,66},{67,3},{3,67},{68,4},{4,... | collective-permute-start | bytes 6881288 | tf_op jit(solution)/shard_map/ppermute | solution.py:33
  148.6 1.7 concatenate.7.refs_0_
  150.3 0.0 collective-permute-start.33
  150.3 2.3 %collective-permute-done.30 = f32[112,5120]{1,0:T(8,128)S(1)} collective-permute-done((f32[112,5120]{1,0:T(8,128)S(1)}, f32[112,5120]{1,0:T(8,128)S(1)}, u32[]{:S(2)}, u32[]{:S(2)}) %collective-permute-start.30) | collective-permute-done | bytes 2293792 | tf_op jit(solution)/shard_map/ppermute | solution.py:33
  152.6 2.5 %multiply_reduce_fusion = (f32[]{:T(128)}, f32[112,5120]{1,0:T(8,128)}) fusion(f32[112,5120]{1,0:T(8,128)S(1)} %get-tuple-element.27.refs_2_.refs_1_, f32[112,5120]{1,0:T(8,128)S(1)} %collective-permute-done.30), kind=kLoop, calls=%fused_computation.1 | loop fusion | flops 1720319 | bytes 6881284 | tf_op jit(solution)/shard_map/reduce_sum | solution.py:365
  155.2 11.7 %collective-permute-start.34 = (f32[112,5120]{1,0:T(8,128)}, f32[112,5120]{1,0:T(8,128)}, u32[]{:S(2)}, u32[]{:S(2)}) collective-permute-start(f32[112,5120]{1,0:T(8,128)} %get-tuple-element.35.refs_5_), channel_id=1, source_target_pairs={{64,4},{4,64},{65,5},{5,65},{66,6},{6,66},{67,7},{7,67},{72,12},{1... | collective-permute-start | bytes 6881288 | tf_op jit(solution)/shard_map/ppermute | solution.py:43
  166.9 0.1 collective-permute-start.31
  167.0 0.5 collective-permute-start.32
  168.3 0.6 pad_add_fusion.which
  168.9 13.9 %psum.21 = f32[]{:T(128)} all-reduce(f32[]{:T(128)} %get-tuple-element.34), channel_id=1, replica_groups=mesh['x_lo'=2,'core'=2,'z'=8,'x_hi'=2,'y'=4] {'z'}, use_global_device_ids=true, to_apply=%region_1.2 | all-reduce | flops 1 | bytes 8 | tf_op jit(solution)/shard_map/psum | solution.py:368
  182.7 10.0 %psum.22 = f32[]{:T(128)} all-reduce(f32[]{:T(128)} %psum.21), channel_id=1, replica_groups=mesh['x_lo'=2,'core'=2,'z'=8,'x_hi'=2,'y'=4] {'y'}, use_global_device_ids=true, to_apply=%region_2.3 | all-reduce | flops 1 | bytes 8 | tf_op jit(solution)/shard_map/psum | solution.py:368
  192.8 0.6 compare_select_fusion
  193.4 13.6 %psum.23 = f32[2]{0:T(128)S(1)} all-reduce(f32[2]{0:T(128)S(1)} %compare_select_fusion), channel_id=1, replica_groups=mesh['x_lo'=2,'core'=2,'z'=8,'x_hi'=2,'y'=4] {'core','x_hi'}, use_global_device_ids=true, to_apply=%region_3.4 | all-reduce | flops 2 | bytes 16 | tf_op jit(solution)/shard_map/psum | solution.py:370
  207.0 0.6 fusion
  209.0 7.2 %updated.1 = (f32[112,5120]{1,0:T(8,128)}, f32[112,5120]{1,0:T(8,128)}, f32[1]{0:T(128)}) custom-call(f32[1]{0:T(128)} %bitcast.10.factor, f32[1]{0:T(128)} %mul.11.kept_weight, s32[2]{0:T(128)} %pad_add_fusion.which, f32[112,5120]{1,0:T(8,128)} %bitcast.26, f32[64,5120]{1,0:T(8,128)} %copy-done, f32[56,5120]{1,0:T(8,128)} %copy-done.1, ...), custom_call_target="tpu_custom_call" | custom-call | tf_op jit(solution)/shard_map/updated/pallas_call | solution.py:290
  (52 shorter events, 0.2 us)
Async XLA Ops:
  0.6 21.0 %copy-start.3 = (bf16[112,5120]{1,0:T(8,128)(2,1)S(1)}, bf16[112,5120]{1,0:T(8,128)(2,1)}, u32[]{:S(2)}) copy-start(bf16[112,5120]{1,0:T(8,128)(2,1)} %param.16) | copy-start | bytes 3440644
  0.6 21.0 %copy-start.4 = (bf16[112,5120]{1,0:T(8,128)(2,1)S(1)}, bf16[112,5120]{1,0:T(8,128)(2,1)}, u32[]{:S(2)}) copy-start(bf16[112,5120]{1,0:T(8,128)(2,1)} %param.15) | copy-start | bytes 3440644
  0.7 21.3 %collective-permute-start = (bf16[20,5120]{1,0:T(8,128)(2,1)}, bf16[20,5120]{1,0:T(8,128)(2,1)S(1)}, u32[]{:S(2)}, u32[]{:S(2)}) collective-permute-start(bf16[20,5120]{1,0:T(8,128)(2,1)} %bitcast.30), channel_id=1, source_target_pairs={{0,0},{64,4},{4,64},{68,68},{1,1},{65,5},{5,65},{69,69},{2,2},{66,... | collective-permute-start | bytes 614408 | tf_op jit(solution)/shard_map/ppermute | solution.py:43
  6.8 9.2 %collective-permute-start.1 = (bf16[20,5120]{1,0:T(8,128)(2,1)}, bf16[20,5120]{1,0:T(8,128)(2,1)S(1)}, u32[]{:S(2)}, u32[]{:S(2)}) collective-permute-start(bf16[20,5120]{1,0:T(8,128)(2,1)} %bitcast.29), channel_id=1, source_target_pairs={{0,0},{64,4},{4,64},{68,68},{1,1},{65,5},{5,65},{69,69},{2,2},{66,... | collective-permute-start | bytes 614408 | tf_op jit(solution)/shard_map/ppermute | solution.py:43
  16.1 8.7 %collective-permute-start.5 = (bf16[20,5120]{1,0:T(8,128)(2,1)S(1)}, bf16[20,5120]{1,0:T(8,128)(2,1)S(1)}, u32[]{:S(2)}, u32[]{:S(2)}) collective-permute-start(bf16[20,5120]{1,0:T(8,128)(2,1)S(1)} %collective-permute-done.1.refs_1_.refs_0_), channel_id=1, source_target_pairs={{8,0},{16,8},{24,16},{32,24},{40,32},{48,40},{56,48},{0,56},{9,1},... | collective-permute-start | bytes 614408 | tf_op jit(solution)/shard_map/ppermute | solution.py:33
  21.6 6.3 %collective-permute-start.7 = (bf16[20,5120]{1,0:T(8,128)(2,1)S(1)}, bf16[20,5120]{1,0:T(8,128)(2,1)S(1)}, u32[]{:S(2)}, u32[]{:S(2)}) collective-permute-start(bf16[20,5120]{1,0:T(8,128)(2,1)S(1)} %collective-permute-done.1.refs_1_.refs_0_), channel_id=1, source_target_pairs={{56,0},{0,8},{8,16},{16,24},{24,32},{32,40},{40,48},{48,56},{57,1}... | collective-permute-start | bytes 614408 | tf_op jit(solution)/shard_map/ppermute | solution.py:33
  27.9 57.1 %collective-permute-start.16 = (bf16[336,5120]{1,0:T(8,128)(2,1)S(1)}, bf16[336,5120]{1,0:T(8,128)(2,1)S(1)}, u32[]{:S(2)}, u32[]{:S(2)}) collective-permute-start(bf16[336,5120]{1,0:T(8,128)(2,1)S(1)} %held.18), channel_id=1, source_target_pairs={{0,0},{64,4},{4,64},{68,68},{1,1},{65,5},{5,65},{69,69},{2,2},{66,... | collective-permute-start | bytes 10321928 | tf_op jit(solution)/shard_map/ppermute | solution.py:43
  32.0 6.0 %collective-permute-start.2 = (bf16[20,5120]{1,0:T(8,128)(2,1)S(1)}, bf16[20,5120]{1,0:T(8,128)(2,1)S(1)}, u32[]{:S(2)}, u32[]{:S(2)}) collective-permute-start(bf16[20,5120]{1,0:T(8,128)(2,1)S(1)} %held.15.refs_0_), channel_id=1, source_target_pairs={{1,0},{2,1},{3,2},{0,3},{5,4},{6,5},{7,6},{4,7},{9,8},{10,9},{11,1... | collective-permute-start | bytes 614408 | tf_op jit(solution)/shard_map/ppermute | solution.py:33
  34.8 9.2 %collective-permute-start.3 = (bf16[20,5120]{1,0:T(8,128)(2,1)S(1)}, bf16[20,5120]{1,0:T(8,128)(2,1)S(1)}, u32[]{:S(2)}, u32[]{:S(2)}) collective-permute-start(bf16[20,5120]{1,0:T(8,128)(2,1)S(1)} %held.15.refs_0_), channel_id=1, source_target_pairs={{3,0},{0,1},{1,2},{2,3},{7,4},{4,5},{5,6},{6,7},{11,8},{8,9},{9,10... | collective-permute-start | bytes 614408 | tf_op jit(solution)/shard_map/ppermute | solution.py:33
  34.8 9.2 %collective-permute-start.4 = (bf16[20,5120]{1,0:T(8,128)(2,1)S(1)}, bf16[20,5120]{1,0:T(8,128)(2,1)S(1)}, u32[]{:S(2)}, u32[]{:S(2)}) collective-permute-start(bf16[20,5120]{1,0:T(8,128)(2,1)S(1)} %held.15.refs_0_), channel_id=1, source_target_pairs={{2,0},{3,1},{0,2},{1,3},{6,4},{7,5},{4,6},{5,7},{10,8},{11,9},{8,1... | collective-permute-start | bytes 614408 | tf_op jit(solution)/shard_map/ppermute | solution.py:33
  36.4 7.6 %collective-permute-start.6 = (bf16[20,5120]{1,0:T(8,128)(2,1)S(1)}, bf16[20,5120]{1,0:T(8,128)(2,1)S(1)}, u32[]{:S(2)}, u32[]{:S(2)}) collective-permute-start(bf16[20,5120]{1,0:T(8,128)(2,1)S(1)} %collective-permute-done.5.refs_1_), channel_id=1, source_target_pairs={{8,0},{16,8},{24,16},{32,24},{40,32},{48,40},{56,48},{0,56},{9,1},... | collective-permute-start | bytes 614408 | tf_op jit(solution)/shard_map/ppermute | solution.py:33
  37.9 8.3 %collective-permute-start.8 = (bf16[20,5120]{1,0:T(8,128)(2,1)S(1)}, bf16[20,5120]{1,0:T(8,128)(2,1)S(1)}, u32[]{:S(2)}, u32[]{:S(2)}) collective-permute-start(bf16[20,5120]{1,0:T(8,128)(2,1)S(1)} %collective-permute-done.7.refs_3_.refs_2_), channel_id=1, source_target_pairs={{56,0},{0,8},{8,16},{16,24},{24,32},{32,40},{40,48},{48,56},{57,1}... | collective-permute-start | bytes 614408 | tf_op jit(solution)/shard_map/ppermute | solution.py:33
  46.2 9.1 %collective-permute-start.9 = (bf16[20,5120]{1,0:T(8,128)(2,1)S(1)}, bf16[20,5120]{1,0:T(8,128)(2,1)S(1)}, u32[]{:S(2)}, u32[]{:S(2)}) collective-permute-start(bf16[20,5120]{1,0:T(8,128)(2,1)S(1)} %get-tuple-element.19.refs_2_), channel_id=1, source_target_pairs={{8,0},{16,8},{24,16},{32,24},{40,32},{48,40},{56,48},{0,56},{9,1},... | collective-permute-start | bytes 614408 | tf_op jit(solution)/shard_map/ppermute | solution.py:33
  46.2 9.8 %collective-permute-start.10 = (bf16[20,5120]{1,0:T(8,128)(2,1)S(1)}, bf16[20,5120]{1,0:T(8,128)(2,1)S(1)}, u32[]{:S(2)}, u32[]{:S(2)}) collective-permute-start(bf16[20,5120]{1,0:T(8,128)(2,1)S(1)} %get-tuple-element.19.refs_2_), channel_id=1, source_target_pairs={{16,0},{24,8},{32,16},{40,24},{48,32},{56,40},{0,48},{8,56},{17,1}... | collective-permute-start | bytes 614408 | tf_op jit(solution)/shard_map/ppermute | solution.py:33
  46.2 19.7 %copy-start.2 = (f32[1,112,5120]{2,1,0:T(8,128)S(1)}, f32[1,112,5120]{2,1,0:T(8,128)}, u32[]{:S(2)}) copy-start(f32[1,112,5120]{2,1,0:T(8,128)} %param.13) | copy-start | bytes 6881284
  46.2 9.8 %collective-permute-start.11 = (bf16[20,5120]{1,0:T(8,128)(2,1)S(1)}, bf16[20,5120]{1,0:T(8,128)(2,1)S(1)}, u32[]{:S(2)}, u32[]{:S(2)}) collective-permute-start(bf16[20,5120]{1,0:T(8,128)(2,1)S(1)} %get-tuple-element.20.refs_2_), channel_id=1, source_target_pairs={{56,0},{0,8},{8,16},{16,24},{24,32},{32,40},{40,48},{48,56},{57,1}... | collective-permute-start | bytes 614408 | tf_op jit(solution)/shard_map/ppermute | solution.py:33
  56.3 29.9 %collective-permute-start.12 = (bf16[80,5120]{1,0:T(8,128)(2,1)S(1)}, bf16[80,5120]{1,0:T(8,128)(2,1)S(1)}, u32[]{:S(2)}, u32[]{:S(2)}) collective-permute-start(bf16[80,5120]{1,0:T(8,128)(2,1)S(1)} %stacked.3.refs_0_), channel_id=1, source_target_pairs={{8,0},{16,8},{24,16},{32,24},{40,32},{48,40},{56,48},{0,56},{9,1},... | collective-permute-start | bytes 2457608 | tf_op jit(solution)/shard_map/ppermute | solution.py:33
  63.3 22.8 %collective-permute-start.13 = (bf16[80,5120]{1,0:T(8,128)(2,1)S(1)}, bf16[80,5120]{1,0:T(8,128)(2,1)S(1)}, u32[]{:S(2)}, u32[]{:S(2)}) collective-permute-start(bf16[80,5120]{1,0:T(8,128)(2,1)S(1)} %stacked.3.refs_0_), channel_id=1, source_target_pairs={{56,0},{0,8},{8,16},{16,24},{24,32},{32,40},{40,48},{48,56},{57,1}... | collective-permute-start | bytes 2457608 | tf_op jit(solution)/shard_map/ppermute | solution.py:33
  63.6 22.5 %collective-permute-start.14 = (bf16[80,5120]{1,0:T(8,128)(2,1)S(1)}, bf16[80,5120]{1,0:T(8,128)(2,1)S(1)}, u32[]{:S(2)}, u32[]{:S(2)}) collective-permute-start(bf16[80,5120]{1,0:T(8,128)(2,1)S(1)} %stacked.5.refs_0_), channel_id=1, source_target_pairs={{1,0},{2,1},{3,2},{0,3},{5,4},{6,5},{7,6},{4,7},{9,8},{10,9},{11,1... | collective-permute-start | bytes 2457608 | tf_op jit(solution)/shard_map/ppermute | solution.py:33
  65.9 20.2 %collective-permute-start.15 = (bf16[80,5120]{1,0:T(8,128)(2,1)S(1)}, bf16[80,5120]{1,0:T(8,128)(2,1)S(1)}, u32[]{:S(2)}, u32[]{:S(2)}) collective-permute-start(bf16[80,5120]{1,0:T(8,128)(2,1)S(1)} %stacked.5.refs_0_), channel_id=1, source_target_pairs={{3,0},{0,1},{1,2},{2,3},{7,4},{4,5},{5,6},{6,7},{11,8},{8,9},{9,10... | collective-permute-start | bytes 2457608 | tf_op jit(solution)/shard_map/ppermute | solution.py:33
  85.0 18.1 %collective-permute-start.19 = (f32[64,5120]{1,0:T(8,128)S(1)}, f32[64,5120]{1,0:T(8,128)S(1)}, u32[]{:S(2)}, u32[]{:S(2)}) collective-permute-start(f32[64,5120]{1,0:T(8,128)S(1)} %held.20), channel_id=1, source_target_pairs={{128,0},{0,128},{129,1},{1,129},{130,2},{2,130},{131,3},{3,131},{1... | collective-permute-start | bytes 3932168 | tf_op jit(solution)/shard_map/ppermute | solution.py:33
  86.2 11.3 %collective-permute-start.17 = (bf16[80,5120]{1,0:T(8,128)(2,1)S(1)}, bf16[80,5120]{1,0:T(8,128)(2,1)S(1)}, u32[]{:S(2)}, u32[]{:S(2)}) collective-permute-start(bf16[80,5120]{1,0:T(8,128)(2,1)S(1)} %get-tuple-element.21.refs_1_), channel_id=1, source_target_pairs={{8,0},{16,8},{24,16},{32,24},{40,32},{48,40},{56,48},{0,56},{9,1},... | collective-permute-start | bytes 2457608 | tf_op jit(solution)/shard_map/ppermute | solution.py:33
  86.3 12.5 %collective-permute-start.18 = (bf16[80,5120]{1,0:T(8,128)(2,1)S(1)}, bf16[80,5120]{1,0:T(8,128)(2,1)S(1)}, u32[]{:S(2)}, u32[]{:S(2)}) collective-permute-start(bf16[80,5120]{1,0:T(8,128)(2,1)S(1)} %get-tuple-element.22.refs_2_.refs_8_), channel_id=1, source_target_pairs={{56,0},{0,8},{8,16},{16,24},{24,32},{32,40},{40,48},{48,56},{57,1}... | collective-permute-start | bytes 2457608 | tf_op jit(solution)/shard_map/ppermute | solution.py:33
  87.7 12.3 %collective-permute-start.20 = (bf16[80,5120]{1,0:T(8,128)(2,1)S(1)}, bf16[80,5120]{1,0:T(8,128)(2,1)S(1)}, u32[]{:S(2)}, u32[]{:S(2)}) collective-permute-start(bf16[80,5120]{1,0:T(8,128)(2,1)S(1)} %held.21.refs_1_), channel_id=1, source_target_pairs={{1,0},{2,1},{3,2},{0,3},{5,4},{6,5},{7,6},{4,7},{9,8},{10,9},{11,1... | collective-permute-start | bytes 2457608 | tf_op jit(solution)/shard_map/ppermute | solution.py:33
  90.8 12.4 %collective-permute-start.21 = (bf16[80,5120]{1,0:T(8,128)(2,1)S(1)}, bf16[80,5120]{1,0:T(8,128)(2,1)S(1)}, u32[]{:S(2)}, u32[]{:S(2)}) collective-permute-start(bf16[80,5120]{1,0:T(8,128)(2,1)S(1)} %held.21.refs_1_), channel_id=1, source_target_pairs={{3,0},{0,1},{1,2},{2,3},{7,4},{4,5},{5,6},{6,7},{11,8},{8,9},{9,10... | collective-permute-start | bytes 2457608 | tf_op jit(solution)/shard_map/ppermute | solution.py:33
  103.2 6.1 %collective-permute-start.24 = (bf16[336,5120]{1,0:T(8,128)(2,1)S(1)}, bf16[336,5120]{1,0:T(8,128)(2,1)S(1)}, u32[]{:S(2)}, u32[]{:S(2)}) collective-permute-start(bf16[336,5120]{1,0:T(8,128)(2,1)S(1)} %held.24.refs_6_.refs_2_.refs_9_.refs_11_), channel_id=1, source_target_pairs={{64,0},{0,64},{65,1},{1,65},{66,2},{2,66},{67,3},{3,67},{68,4},{4,... | collective-permute-start | bytes 10321928 | tf_op jit(solution)/shard_map/ppermute | solution.py:33
  103.8 20.6 %collective-permute-start.26 = (bf16[80,5120]{1,0:T(8,128)(2,1)S(1)}, bf16[80,5120]{1,0:T(8,128)(2,1)S(1)}, u32[]{:S(2)}, u32[]{:S(2)}) collective-permute-start(bf16[80,5120]{1,0:T(8,128)(2,1)S(1)} %collective-permute-done.21.refs_4_.refs_5_), channel_id=1, source_target_pairs={{3,0},{0,1},{1,2},{2,3},{7,4},{4,5},{5,6},{6,7},{11,8},{8,9},{9,10... | collective-permute-start | bytes 2457608 | tf_op jit(solution)/shard_map/ppermute | solution.py:33
  103.9 20.5 %collective-permute-start.22 = (bf16[80,5120]{1,0:T(8,128)(2,1)S(1)}, bf16[80,5120]{1,0:T(8,128)(2,1)S(1)}, u32[]{:S(2)}, u32[]{:S(2)}) collective-permute-start(bf16[80,5120]{1,0:T(8,128)(2,1)S(1)} %get-tuple-element.23.refs_1_.refs_2_), channel_id=1, source_target_pairs={{8,0},{16,8},{24,16},{32,24},{40,32},{48,40},{56,48},{0,56},{9,1},... | collective-permute-start | bytes 2457608 | tf_op jit(solution)/shard_map/ppermute | solution.py:33
  105.3 20.2 %collective-permute-start.23 = (bf16[80,5120]{1,0:T(8,128)(2,1)S(1)}, bf16[80,5120]{1,0:T(8,128)(2,1)S(1)}, u32[]{:S(2)}, u32[]{:S(2)}) collective-permute-start(bf16[80,5120]{1,0:T(8,128)(2,1)S(1)} %get-tuple-element.24.refs_2_.refs_7_), channel_id=1, source_target_pairs={{56,0},{0,8},{8,16},{16,24},{24,32},{32,40},{40,48},{48,56},{57,1}... | collective-permute-start | bytes 2457608 | tf_op jit(solution)/shard_map/ppermute | solution.py:33
  105.5 20.0 %collective-permute-start.25 = (bf16[80,5120]{1,0:T(8,128)(2,1)S(1)}, bf16[80,5120]{1,0:T(8,128)(2,1)S(1)}, u32[]{:S(2)}, u32[]{:S(2)}) collective-permute-start(bf16[80,5120]{1,0:T(8,128)(2,1)S(1)} %held.23.refs_2_), channel_id=1, source_target_pairs={{1,0},{2,1},{3,2},{0,3},{5,4},{6,5},{7,6},{4,7},{9,8},{10,9},{11,1... | collective-permute-start | bytes 2457608 | tf_op jit(solution)/shard_map/ppermute | solution.py:33
  109.2 26.2 %collective-permute-start.29 = (f32[56,5120]{1,0:T(8,128)S(1)}, f32[56,5120]{1,0:T(8,128)S(1)}, u32[]{:S(2)}, u32[]{:S(2)}) collective-permute-start(f32[56,5120]{1,0:T(8,128)S(1)} %held.26), channel_id=1, source_target_pairs={{128,0},{0,128},{129,1},{1,129},{130,2},{2,130},{131,3},{3,131},{1... | collective-permute-start | bytes 3440648 | tf_op jit(solution)/shard_map/ppermute | solution.py:33
  125.5 11.1 %collective-permute-start.27 = (bf16[48,5120]{1,0:T(8,128)(2,1)S(1)}, bf16[48,5120]{1,0:T(8,128)(2,1)S(1)}, u32[]{:S(2)}, u32[]{:S(2)}) collective-permute-start(bf16[48,5120]{1,0:T(8,128)(2,1)S(1)} %slice.23), channel_id=1, source_target_pairs={{8,0},{16,8},{24,16},{32,24},{40,32},{48,40},{56,48},{0,56},{9,1},... | collective-permute-start | bytes 1474568 | tf_op jit(solution)/shard_map/ppermute | solution.py:33
  126.9 8.6 %collective-permute-start.28 = (bf16[32,5120]{1,0:T(8,128)(2,1)S(1)}, bf16[32,5120]{1,0:T(8,128)(2,1)S(1)}, u32[]{:S(2)}, u32[]{:S(2)}) collective-permute-start(bf16[32,5120]{1,0:T(8,128)(2,1)S(1)} %slice.24), channel_id=1, source_target_pairs={{56,0},{0,8},{8,16},{16,24},{24,32},{32,40},{40,48},{48,56},{57,1}... | collective-permute-start | bytes 983048 | tf_op jit(solution)/shard_map/ppermute | solution.py:33
  145.7 7.0 %collective-permute-start.30 = (f32[112,5120]{1,0:T(8,128)S(1)}, f32[112,5120]{1,0:T(8,128)S(1)}, u32[]{:S(2)}, u32[]{:S(2)}) collective-permute-start(f32[112,5120]{1,0:T(8,128)S(1)} %get-tuple-element.28), channel_id=1, source_target_pairs={{64,0},{0,64},{65,1},{1,65},{66,2},{2,66},{67,3},{3,67},{68,4},{4,... | collective-permute-start | bytes 6881288 | tf_op jit(solution)/shard_map/ppermute | solution.py:33
  150.3 58.7 %collective-permute-start.33 = (f32[120,5120]{1,0:T(8,128)}, f32[120,5120]{1,0:T(8,128)}, u32[]{:S(2)}, u32[]{:S(2)}) collective-permute-start(f32[120,5120]{1,0:T(8,128)} %held.29), channel_id=1, source_target_pairs={{64,0},{0,64},{65,1},{1,65},{66,2},{2,66},{67,3},{3,67},{68,4},{4,... | collective-permute-start | bytes 7372808 | tf_op jit(solution)/shard_map/ppermute | solution.py:33
  155.2 53.8 %collective-permute-start.34 = (f32[112,5120]{1,0:T(8,128)}, f32[112,5120]{1,0:T(8,128)}, u32[]{:S(2)}, u32[]{:S(2)}) collective-permute-start(f32[112,5120]{1,0:T(8,128)} %get-tuple-element.35.refs_5_), channel_id=1, source_target_pairs={{64,4},{4,64},{65,5},{5,65},{66,6},{6,66},{67,7},{7,67},{72,12},{1... | collective-permute-start | bytes 6881288 | tf_op jit(solution)/shard_map/ppermute | solution.py:43
  166.9 42.1 %copy-start = (f32[64,5120]{1,0:T(8,128)}, f32[64,5120]{1,0:T(8,128)S(1)}, u32[]{:S(2)}) copy-start(f32[64,5120]{1,0:T(8,128)S(1)} %get-tuple-element.29.refs_0_) | copy-start | bytes 3932164
  166.9 42.1 %copy-start.1 = (f32[56,5120]{1,0:T(8,128)}, f32[56,5120]{1,0:T(8,128)S(1)}, u32[]{:S(2)}) copy-start(f32[56,5120]{1,0:T(8,128)S(1)} %get-tuple-element.30.refs_1_) | copy-start | bytes 3440644
  166.9 42.0 %collective-permute-start.31 = (f32[64,5120]{1,0:T(8,128)S(1)}, f32[64,5120]{1,0:T(8,128)}, u32[]{:S(2)}, u32[]{:S(2)}) collective-permute-start(f32[64,5120]{1,0:T(8,128)S(1)} %get-tuple-element.29.refs_0_), channel_id=1, source_target_pairs={{64,0},{0,64},{65,1},{1,65},{66,2},{2,66},{67,3},{3,67},{68,4},{4,... | collective-permute-start | bytes 3932168 | tf_op jit(solution)/shard_map/ppermute | solution.py:33
  167.0 41.9 %collective-permute-start.32 = (f32[56,5120]{1,0:T(8,128)S(1)}, f32[56,5120]{1,0:T(8,128)}, u32[]{:S(2)}, u32[]{:S(2)}) collective-permute-start(f32[56,5120]{1,0:T(8,128)S(1)} %get-tuple-element.30.refs_1_), channel_id=1, source_target_pairs={{64,0},{0,64},{65,1},{1,65},{66,2},{2,66},{67,3},{3,67},{68,4},{4,... | collective-permute-start | bytes 3440648 | tf_op jit(solution)/shard_map/ppermute | solution.py:33

commit v10 on v9

--- a/solution.py
+++ b/solution.py
@@ -41,6 +41,18 @@
         if stay or core != x_hi
     ]
     return lax.ppermute(value, ("core", "x_hi"), pairs)
+
+
+def summed(value):
+    crossing = [(2 * (1 - x_hi) + core, 2 * core + x_hi) for core in range(2) for x_hi in range(2)]
+    value = transposed(value) + lax.ppermute(value, ("core", "x_hi"), crossing)
+    for axis in ("y", "z"):
+        reach = 1
+        while reach < SIZES[axis]:
+            pairs = [(place ^ reach, place) for place in range(SIZES[axis])]
+            value = value + lax.ppermute(value, axis, pairs)
+            reach *= 2
+    return value
 
 
 def held(value, *ready):
@@ -303,7 +315,7 @@
             pltpu.SemaphoreType.DMA((2, blocks)),
             pltpu.SemaphoreType.DMA((blocks,)),
         ],
-        compiler_params=params_of(56),
+        compiler_params=params_of(16),
         name="updated",
     )(factor, kept_weight, which, numerator, *more)
 
@@ -320,58 +332,57 @@
     rows_in = held(rows_in, rows_grad, weights)
     near = [rows_in] + [shifted(rows_in, "y", steps) for steps in (1, 3, 2)]
     ring = {0: rows_grad, 1: shifted(rows_grad, "z", 1), 7: shifted(rows_grad, "z", 7)}
-    mine = transposed(held(weights, ring[1], ring[7]))
+    mine = transposed(held(weights, rows_grad))
     ring[2], ring[6] = shifted(ring[1], "z", 1), shifted(ring[7], "z", 7)
     ring[2], ring[6] = held((ring[2], ring[6]), *near[1:])
     ring[3], ring[5] = shifted(ring[2], "z", 1), shifted(ring[6], "z", 7)
     ring[4] = shifted(ring[2], "z", 2)
-    near[3] = held(near[3], ring[3], ring[4], ring[5])
+    stale = jnp.concatenate([stale_num[0], jnp.broadcast_to(stale_weight, (8, D))], axis=0)
+    stale_hop = shifted(held(stale, ring[2], ring[6]), "core", 1)
+    near[3] = held(near[3], ring[3], ring[4], ring[5], stale_hop)
     blocks = {0: stacked(near)}
     columns = [stacked([ring[steps] for steps in some]) for some in (range(4), range(4, 8))]
 
     blocks[1], blocks[7] = shifted(blocks[0], "z", 1), shifted(blocks[0], "z", 7)
     following, before = [shifted(columns[0], "y", 1)], [shifted(columns[0], "y", 3)]
-    ready = (columns[1], following[0], before[0], mine)
+    mine = held(mine, columns[0], blocks[0])
+    theirs = shifted(mine, "core", 1)
+    ready = (columns[1], following[0], before[0], theirs)
     blocks[1], blocks[7] = held((blocks[1], blocks[7]), *ready)
 
     blocks[2], blocks[6] = shifted(blocks[1], "z", 1), shifted(blocks[7], "z", 7)
     columns[1] = held(columns[1], blocks[1], blocks[7])
     following.append(shifted(columns[1], "y", 1))
     before.append(shifted(columns[1], "y", 3))
-    stale = jnp.concatenate([stale_num[0], jnp.broadcast_to(stale_weight, (8, D))], axis=0)
-    two_before = [shifted(held(stale[:CUT], mine), "x_lo", 1)]
+    two_before = [shifted(held(stale[:CUT], theirs), "x_lo", 1)]
     ready = (two_before[0], following[1], before[1])
     blocks[2], blocks[6] = held((blocks[2], blocks[6]), *ready)
 
     blocks[3], blocks[5] = shifted(blocks[2], "z", 1), shifted(blocks[6], "z", 7)
     following[0] = held(following[0], blocks[2])
     far = [shifted(following[0], "y", 1), shifted(before[1], "y", 3)]
-    mine = held(mine, blocks[2], blocks[6])
-    theirs = shifted(mine, "core", 1)
     two_before.append(shifted(held(stale[CUT:], two_before[0]), "x_lo", 1))
     hidden_most = hidden_of([*columns, *following, *before], mine, theirs)
     blocks[3], blocks[5] = held((blocks[3], blocks[5]), hidden_most, *far)
 
     cut = 48
     last = [shifted(blocks[3][:cut], "z", 1), shifted(blocks[5][cut:], "z", 7)]
-    hidden_far = held(hidden_of(far, mine, theirs), two_before[1])
+    two_before[0] = held(two_before[0], blocks[3])
+    one_before = [shifted(two_before[0], "core", 1)]
+    hidden_far = held(hidden_of(far, mine, theirs), two_before[1], one_before[0])
     parts = [blocks[steps] for steps in (0, 1, 2, 3)] + last + [blocks[steps] for steps in (5, 6, 7)]
 
     own_grad, other_grad = gate_grads(parts, mine, theirs, hidden_most, hidden_far)
-    two_before = held(tuple(two_before), own_grad)
-    one_before = [shifted(part, "core", 1) for part in two_before]
-    stale_hop = shifted(held(stale, own_grad), "core", 1)
+    two_before[1] = held(two_before[1], own_grad)
+    one_before.append(shifted(two_before[1], "core", 1))
     gate_grad = own_grad + shifted(other_grad, "core", 1)
     norm_sq = jnp.sum(gate_grad * gate_grad)
     returned = transposed(gate_grad, stay=False)
-    for axes in ("z", "y"):
-        norm_sq = lax.psum(norm_sq, axes)
-    x_hi, core = lax.axis_index("x_hi"), lax.axis_index("core")
-    norms = lax.psum(jnp.where(jnp.arange(2) == x_hi, norm_sq, 0.0), ("core", "x_hi"))
-    norm_sq = jnp.where(core == 0, norms[0], norms[1])
+    norm_sq = summed(jnp.reshape(norm_sq, (1,)))[0]
 
     clip_factor = jnp.minimum(1.0, MAX_NORM / jnp.sqrt(norm_sq + eps))
     kept_weight = 0.5 * push_weight
+    core, x_hi = lax.axis_index("core"), lax.axis_index("x_hi")
     which = jnp.where(step[0] % 2 == 1, 0, 1 + core)
     kept_half, new_num, new_weight = updated(
         numerator,

time: 218 us -> 247 us (1.13); the launches traced: 217 us -> 243 us
  waiting for transfers between devices: 79.8 us -> 135 us
  blocking collectives: 37.4 us -> 0 us
  local copies, waits for them, and re-layouts: 2.53 us -> 7.25 us
  between operations: 5.56 us -> 8.68 us
  starting transfers between devices: 60.1 us -> 63 us
    ppermute x31, waiting for transfers between devices: 56 us -> 94.1 us  [shifted(): return lax.ppermute(value, axis, pairs)]
    psum x3 -> x0, blocking collectives: 37.4 us -> none  [the longest x2 23.9 us: shards(): norm_sq = lax.psum(norm_sq, axes)]
    ppermute x0 -> x6, waiting for transfers between devices: none -> 12.7 us  [the longest x5 12.7 us: summed(): value = value + lax.ppermute(value, axis, pairs)]
    unnamed x10 -> x16, local copies, waits for them, and re-layouts: 0.02 us -> 6.77 us
    ppermute x0 -> x6, starting transfers between devices: none -> 6.64 us  [the longest x5 6.54 us: summed(): value = value + lax.ppermute(value, axis, pairs)]
    ppermute x4 -> x5, starting transfers between devices: 23.8 us -> 17.9 us  [transposed(): return lax.ppermute(value, ('core', 'x_hi'), pairs)]
    ppermute x4 -> x5, waiting for transfers between devices: 23.9 us -> 28.4 us  [transposed(): return lax.ppermute(value, ('core', 'x_hi'), pairs)]
  transfers between devices with their start and end apart: 35 -> 42, of which waited for: 19 -> 28; matrix products, arithmetic and copies ran while one was open for 4% -> 1% of each run, Pallas kernels for 4% -> 4%
where the time goes in v10:
time: 247 us; the launch traced here: 243 us
  waiting for transfers between devices  135 us (55%)
  starting transfers between devices  63 us (26%)
  Pallas kernels  23.8 us (10%)
  between operations  8.68 us (4%)
  local copies, waits for them, and re-layouts  7.25 us (3%)
  other arithmetic  4.85 us (2%)
    ppermute x31, waiting for transfers between devices, shifted(): return lax.ppermute(value, axis, pairs)  94.1 us
    ppermute x31, starting transfers between devices, shifted(): return lax.ppermute(value, axis, pairs)  38.4 us
    ppermute x5, waiting for transfers between devices, transposed(): return lax.ppermute(value, ('core', 'x_hi'), pairs)  28.4 us
    ppermute x5, starting transfers between devices, transposed(): return lax.ppermute(value, ('core', 'x_hi'), pairs)  17.9 us
    ppermute x5, waiting for transfers between devices, summed(): value = value + lax.ppermute(value, axis, pairs)  12.7 us
    pallas_call x1, Pallas kernels, gate_grads(): pl.pallas_call(grad_kernel, grid=(D // BLOCK,), in_specs=[pl.BlockSpec((p...  9.01 us
    pallas_call x2, Pallas kernels, hidden_of(): pl.pallas_call(hidden_kernel, grid=(D // BLOCK,), in_specs=[pl.BlockSpec(...  8.72 us
    unnamed x16, local copies, waits for them, and re-layouts  6.77 us
  transfers between devices with their start and end apart: 42, of which 28 were waited for; matrix products, arithmetic and copies ran while one was open for 1% of the time, Pallas kernels for 4%

profile of v10, /device:TPU:1, one launch (start us, length us, event | category | flops | bytes accessed | tf_op | source)
XLA Modules:
  0.0 242.7 jit_solution(6159370635487714322)
XLA Ops:
  0.7 6.2 %collective-permute-start.1 = (bf16[20,5120]{1,0:T(8,128)(2,1)}, bf16[20,5120]{1,0:T(8,128)(2,1)S(1)}, u32[]{:S(2)}, u32[]{:S(2)}) collective-permute-start(bf16[20,5120]{1,0:T(8,128)(2,1)} %bitcast.29), channel_id=1, source_target_pairs={{0,0},{64,4},{4,64},{68,68},{1,1},{65,5},{5,65},{69,69},{2,2},{66,... | collective-permute-start | bytes 614408 | tf_op jit(solution)/shard_map/ppermute | solution.py:43
  6.8 1.9 collective-permute-start
  9.4 1.8 divide_convert_fusion
  11.5 4.5 %collective-permute-done.refs_0_ = bf16[20,5120]{1,0:T(8,128)(2,1)S(1)} collective-permute-done((bf16[20,5120]{1,0:T(8,128)(2,1)}, bf16[20,5120]{1,0:T(8,128)(2,1)S(1)}, u32[]{:S(2)}, u32[]{:S(2)}) %collective-permute-start) | collective-permute-done | bytes 204832 | tf_op jit(solution)/shard_map/ppermute | solution.py:43
  16.1 2.7 %collective-permute-start.17 = (bf16[336,5120]{1,0:T(8,128)(2,1)S(1)}, bf16[336,5120]{1,0:T(8,128)(2,1)S(1)}, u32[]{:S(2)}, u32[]{:S(2)}) collective-permute-start(bf16[336,5120]{1,0:T(8,128)(2,1)S(1)} %held.20), channel_id=1, source_target_pairs={{0,0},{64,4},{4,64},{68,68},{1,1},{65,5},{5,65},{69,69},{2,2},{66,... | collective-permute-start | bytes 10321928 | tf_op jit(solution)/shard_map/ppermute | solution.py:43
  18.8 2.8 %collective-permute-start.2 = (bf16[20,5120]{1,0:T(8,128)(2,1)S(1)}, bf16[20,5120]{1,0:T(8,128)(2,1)S(1)}, u32[]{:S(2)}, u32[]{:S(2)}) collective-permute-start(bf16[20,5120]{1,0:T(8,128)(2,1)S(1)} %held.16.refs_0_), channel_id=1, source_target_pairs={{1,0},{2,1},{3,2},{0,3},{5,4},{6,5},{7,6},{4,7},{9,8},{10,9},{11,1... | collective-permute-start | bytes 614408 | tf_op jit(solution)/shard_map/ppermute | solution.py:33
  21.6 5.6 %collective-permute-start.5 = (bf16[20,5120]{1,0:T(8,128)(2,1)S(1)}, bf16[20,5120]{1,0:T(8,128)(2,1)S(1)}, u32[]{:S(2)}, u32[]{:S(2)}) collective-permute-start(bf16[20,5120]{1,0:T(8,128)(2,1)S(1)} %collective-permute-done.1.refs_1_.refs_0_), channel_id=1, source_target_pairs={{8,0},{16,8},{24,16},{32,24},{40,32},{48,40},{56,48},{0,56},{9,1},... | collective-permute-start | bytes 614408 | tf_op jit(solution)/shard_map/ppermute | solution.py:33
  27.4 1.7 collective-permute-start.4
  29.1 2.5 %collective-permute-done.5.refs_1_ = bf16[20,5120]{1,0:T(8,128)(2,1)S(1)} collective-permute-done((bf16[20,5120]{1,0:T(8,128)(2,1)S(1)}, bf16[20,5120]{1,0:T(8,128)(2,1)S(1)}, u32[]{:S(2)}, u32[]{:S(2)}) %collective-permute-start.5) | collective-permute-done | bytes 204832 | tf_op jit(solution)/shard_map/ppermute | solution.py:33
  31.6 3.1 %collective-permute-start.6 = (bf16[20,5120]{1,0:T(8,128)(2,1)S(1)}, bf16[20,5120]{1,0:T(8,128)(2,1)S(1)}, u32[]{:S(2)}, u32[]{:S(2)}) collective-permute-start(bf16[20,5120]{1,0:T(8,128)(2,1)S(1)} %collective-permute-done.5.refs_1_), channel_id=1, source_target_pairs={{8,0},{16,8},{24,16},{32,24},{40,32},{48,40},{56,48},{0,56},{9,1},... | collective-permute-start | bytes 614408 | tf_op jit(solution)/shard_map/ppermute | solution.py:33
  36.1 1.8 collective-permute-done.6.refs_0_
  37.9 3.4 %collective-permute-done.8.refs_1_ = bf16[20,5120]{1,0:T(8,128)(2,1)S(1)} collective-permute-done((bf16[20,5120]{1,0:T(8,128)(2,1)S(1)}, bf16[20,5120]{1,0:T(8,128)(2,1)S(1)}, u32[]{:S(2)}, u32[]{:S(2)}) %collective-permute-start.8) | collective-permute-done | bytes 204832 | tf_op jit(solution)/shard_map/ppermute | solution.py:33
  41.4 1.4 collective-permute-start.11
  42.8 5.5 %collective-permute-done.9.refs_1_.refs_3_ = bf16[20,5120]{1,0:T(8,128)(2,1)S(1)} collective-permute-done((bf16[20,5120]{1,0:T(8,128)(2,1)S(1)}, bf16[20,5120]{1,0:T(8,128)(2,1)S(1)}, u32[]{:S(2)}, u32[]{:S(2)}) %collective-permute-start.9) | collective-permute-done | bytes 204832 | tf_op jit(solution)/shard_map/ppermute | solution.py:33
  48.7 8.7 %collective-permute-done.10.refs_2_.refs_0_ = bf16[20,5120]{1,0:T(8,128)(2,1)S(1)} collective-permute-done((bf16[20,5120]{1,0:T(8,128)(2,1)S(1)}, bf16[20,5120]{1,0:T(8,128)(2,1)S(1)}, u32[]{:S(2)}, u32[]{:S(2)}) %collective-permute-start.10) | collective-permute-done | bytes 204832 | tf_op jit(solution)/shard_map/ppermute | solution.py:33
  57.7 1.1 copy-done
  58.8 0.6 collective-permute-done.17.refs_0_
  59.4 0.7 collective-permute-start.18
  60.2 2.0 collective-permute-start.15
  62.2 5.6 %collective-permute-start.13 = (bf16[80,5120]{1,0:T(8,128)(2,1)S(1)}, bf16[80,5120]{1,0:T(8,128)(2,1)S(1)}, u32[]{:S(2)}, u32[]{:S(2)}) collective-permute-start(bf16[80,5120]{1,0:T(8,128)(2,1)S(1)} %stacked.3.refs_2_.refs_0_), channel_id=1, source_target_pairs={{8,0},{16,8},{24,16},{32,24},{40,32},{48,40},{56,48},{0,56},{9,1},... | collective-permute-start | bytes 2457608 | tf_op jit(solution)/shard_map/ppermute | solution.py:33
  67.9 0.7 collective-permute-start.21
  68.9 11.1 %collective-permute-done.15.refs_3_.refs_0_ = bf16[80,5120]{1,0:T(8,128)(2,1)S(1)} collective-permute-done((bf16[80,5120]{1,0:T(8,128)(2,1)S(1)}, bf16[80,5120]{1,0:T(8,128)(2,1)S(1)}, u32[]{:S(2)}, u32[]{:S(2)}) %collective-permute-start.15) | collective-permute-done | bytes 819232 | tf_op jit(solution)/shard_map/ppermute | solution.py:33
  80.0 2.3 collective-permute-done.16.refs_4_
  82.4 2.2 collective-permute-done.13.refs_0_
  84.5 3.1 %collective-permute-done.14.refs_1_ = bf16[80,5120]{1,0:T(8,128)(2,1)S(1)} collective-permute-done((bf16[80,5120]{1,0:T(8,128)(2,1)S(1)}, bf16[80,5120]{1,0:T(8,128)(2,1)S(1)}, u32[]{:S(2)}, u32[]{:S(2)}) %collective-permute-start.14) | collective-permute-done | bytes 819232 | tf_op jit(solution)/shard_map/ppermute | solution.py:33
  87.6 2.7 %collective-permute-start.22 = (bf16[80,5120]{1,0:T(8,128)(2,1)S(1)}, bf16[80,5120]{1,0:T(8,128)(2,1)S(1)}, u32[]{:S(2)}, u32[]{:S(2)}) collective-permute-start(bf16[80,5120]{1,0:T(8,128)(2,1)S(1)} %held.24.refs_1_), channel_id=1, source_target_pairs={{1,0},{2,1},{3,2},{0,3},{5,4},{6,5},{7,6},{4,7},{9,8},{10,9},{11,1... | collective-permute-start | bytes 2457608 | tf_op jit(solution)/shard_map/ppermute | solution.py:33
  90.3 0.4 collective-permute-start.19
  90.7 1.1 collective-permute-start.20
  91.8 14.8 %collective-permute-done.23.refs_4_.refs_5_ = bf16[80,5120]{1,0:T(8,128)(2,1)S(1)} collective-permute-done((bf16[80,5120]{1,0:T(8,128)(2,1)S(1)}, bf16[80,5120]{1,0:T(8,128)(2,1)S(1)}, u32[]{:S(2)}, u32[]{:S(2)}) %collective-permute-start.23) | collective-permute-done | bytes 819232 | tf_op jit(solution)/shard_map/ppermute | solution.py:33
  106.6 0.9 collective-permute-done.19.refs_0_
  107.5 1.6 collective-permute-done.20.refs_1_
  109.5 0.8 collective-permute-start.26
  110.3 1.1 collective-permute-start.25
  111.5 6.1 %hidden.2.refs_2_.refs_13_ = f32[480,256]{1,0:T(8,128)S(1)} custom-call(bf16[80,5120]{1,0:T(8,128)(2,1)S(1)} %stacked.5.refs_1_.refs_0_, bf16[80,5120]{1,0:T(8,128)(2,1)S(1)} %held.24.refs_1_, bf16[80,5120]{1,0:T(8,128)(2,1)S(1)} %held.26.refs_2_, bf16[80,5120]{1,0:T(8,128)(2,1)S(1)} %collective-permute-done.22.refs_3_, ...), custom_call_target="tpu_custom_call" | custom-call | flops 1 | bytes 1 | tf_op jit(solution)/shard_map/hidden/pallas_call | solution.py:149
  117.6 7.1 %collective-permute-done.27.refs_4_.refs_1_ = bf16[80,5120]{1,0:T(8,128)(2,1)S(1)} collective-permute-done((bf16[80,5120]{1,0:T(8,128)(2,1)S(1)}, bf16[80,5120]{1,0:T(8,128)(2,1)S(1)}, u32[]{:S(2)}, u32[]{:S(2)}) %collective-permute-start.27) | collective-permute-done | bytes 819232 | tf_op jit(solution)/shard_map/ppermute | solution.py:33
  124.6 1.2 collective-permute-done.26.refs_3_.refs_0_
  125.8 1.4 collective-permute-done.25.refs_1_
  127.2 5.0 %collective-permute-start.31 = (f32[64,5120]{1,0:T(8,128)S(1)}, f32[64,5120]{1,0:T(8,128)S(1)}, u32[]{:S(2)}, u32[]{:S(2)}) collective-permute-start(f32[64,5120]{1,0:T(8,128)S(1)} %held.29.refs_0_), channel_id=1, source_target_pairs={{64,0},{0,64},{65,1},{1,65},{66,2},{2,66},{67,3},{3,67},{68,4},{4,... | collective-permute-start | bytes 3932168 | tf_op jit(solution)/shard_map/ppermute | solution.py:33
  132.1 0.6 collective-permute-start.30
  132.9 1.7 collective-permute-start.29
  134.6 2.6 %hidden.3.refs_0_ = f32[160,256]{1,0:T(8,128)S(1)} custom-call(bf16[80,5120]{1,0:T(8,128)(2,1)S(1)} %collective-permute-done.26.refs_3_.refs_0_, bf16[80,5120]{1,0:T(8,128)(2,1)S(1)} %collective-permute-done.27.refs_4_.refs_1_, bf16[336,5120]{1,0:T(8,128)(2,1)S(1)} %held.21.refs_6_.refs_2_.refs_9_.refs_11_, ...), custom_call_target="tpu_custom_call" | custom-call | flops 1 | bytes 1 | tf_op jit(solution)/shard_map/hidden/pallas_call | solution.py:149
  137.3 21.8 %collective-permute-done.30.refs_1_.refs_0_ = f32[56,5120]{1,0:T(8,128)S(1)} collective-permute-done((f32[56,5120]{1,0:T(8,128)S(1)}, f32[56,5120]{1,0:T(8,128)S(1)}, u32[]{:S(2)}, u32[]{:S(2)}) %collective-permute-start.30) | collective-permute-done | bytes 1146912 | tf_op jit(solution)/shard_map/ppermute | solution.py:33
  159.0 1.0 copy-done.3
  160.1 9.0 %gate_grads.1 = (f32[112,5120]{1,0:T(8,128)S(1)}, f32[112,5120]{1,0:T(8,128)S(1)}) custom-call(bf16[80,5120]{1,0:T(8,128)(2,1)S(1)} %stacked.3.refs_2_.refs_0_, bf16[80,5120]{1,0:T(8,128)(2,1)S(1)} %get-tuple-element.19.refs_1_, bf16[80,5120]{1,0:T(8,128)(2,1)S(1)} %get-tuple-element.21.refs_1_.refs_2_, ...), custom_call_target="tpu_custom_call" | custom-call | flops 1 | bytes 1 | tf_op jit(solution)/shard_map/gate_grads/pallas_call | solution.py:217
  169.1 0.9 collective-permute-start.32
  170.0 4.1 %collective-permute-done.32 = f32[112,5120]{1,0:T(8,128)S(1)} collective-permute-done((f32[112,5120]{1,0:T(8,128)S(1)}, f32[112,5120]{1,0:T(8,128)S(1)}, u32[]{:S(2)}, u32[]{:S(2)}) %collective-permute-start.32) | collective-permute-done | bytes 2293792 | tf_op jit(solution)/shard_map/ppermute | solution.py:33
  174.0 2.7 %multiply_reduce_fusion = (f32[]{:T(128)}, f32[112,5120]{1,0:T(8,128)}) fusion(f32[112,5120]{1,0:T(8,128)S(1)} %get-tuple-element.25.refs_1_, f32[112,5120]{1,0:T(8,128)S(1)} %collective-permute-done.32), kind=kLoop, calls=%fused_computation.1 | loop fusion | flops 1720319 | bytes 6881284 | tf_op jit(solution)/shard_map/reduce_sum | solution.py:379
  176.7 4.1 %collective-permute-start.41 = (f32[112,5120]{1,0:T(8,128)}, f32[112,5120]{1,0:T(8,128)}, u32[]{:S(2)}, u32[]{:S(2)}) collective-permute-start(f32[112,5120]{1,0:T(8,128)} %get-tuple-element.31.refs_5_), channel_id=1, source_target_pairs={{64,4},{4,64},{65,5},{5,65},{66,6},{6,66},{67,7},{7,67},{72,12},{1... | collective-permute-start | bytes 6881288 | tf_op jit(solution)/shard_map/ppermute | solution.py:43
  181.8 2.9 %collective-permute-start.33 = (f32[1]{0:T(128)}, f32[1]{0:T(128)}, u32[]{:S(2)}, u32[]{:S(2)}) collective-permute-start(f32[1]{0:T(128)} %bitcast.8), channel_id=1, source_target_pairs={{0,0},{64,4},{4,64},{68,68},{1,1},{65,5},{5,65},{69,69},{2,2},{66,... | collective-permute-start | bytes 20 | tf_op jit(solution)/shard_map/ppermute | solution.py:43
  184.8 23.2 %collective-permute-done.33 = f32[1]{0:T(128)} collective-permute-done((f32[1]{0:T(128)}, f32[1]{0:T(128)}, u32[]{:S(2)}, u32[]{:S(2)}) %collective-permute-start.33) | collective-permute-done | bytes 36 | tf_op jit(solution)/shard_map/ppermute | solution.py:43
  209.4 1.5 collective-permute-start.35
  210.9 1.1 collective-permute-done.35
  212.6 0.9 collective-permute-start.36
  213.4 3.2 %collective-permute-done.36 = f32[1]{0:T(128)} collective-permute-done((f32[1]{0:T(128)}, f32[1]{0:T(128)}, u32[]{:S(2)}, u32[]{:S(2)}) %collective-permute-start.36) | collective-permute-done | bytes 36 | tf_op jit(solution)/shard_map/ppermute | solution.py:53
  217.3 0.8 collective-permute-start.37
  218.1 1.8 collective-permute-done.37
  220.5 0.8 collective-permute-start.38
  221.3 2.7 %collective-permute-done.38 = f32[1]{0:T(128)} collective-permute-done((f32[1]{0:T(128)}, f32[1]{0:T(128)}, u32[]{:S(2)}, u32[]{:S(2)}) %collective-permute-start.38) | collective-permute-done | bytes 36 | tf_op jit(solution)/shard_map/ppermute | solution.py:53
  224.6 2.5 %collective-permute-start.39 = (f32[1]{0:T(128)}, f32[1]{0:T(128)}, u32[]{:S(2)}, u32[]{:S(2)}) collective-permute-start(f32[1]{0:T(128)} %add.47), channel_id=1, source_target_pairs={{32,0},{40,8},{48,16},{56,24},{0,32},{8,40},{16,48},{24,56},{33,1}... | collective-permute-start | bytes 20 | tf_op jit(solution)/shard_map/ppermute | solution.py:53
  227.2 4.0 %collective-permute-done.39 = f32[1]{0:T(128)} collective-permute-done((f32[1]{0:T(128)}, f32[1]{0:T(128)}, u32[]{:S(2)}, u32[]{:S(2)}) %collective-permute-start.39) | collective-permute-done | bytes 36 | tf_op jit(solution)/shard_map/ppermute | solution.py:53
  231.8 1.7 copy-done.1
  233.5 1.6 copy-done.2
  235.2 1.3 copy-done.4
  236.5 5.1 %updated.1 = (f32[112,5120]{1,0:T(8,128)}, f32[112,5120]{1,0:T(8,128)}, f32[1]{0:T(128)}) custom-call(f32[1]{0:T(128)} %bitcast.10.factor, f32[1]{0:T(128)} %mul.11.kept_weight, s32[2]{0:T(128)S(1)} %pad_add_fusion.which, f32[112,5120]{1,0:T(8,128)S(1)} %bitcast.24, f32[64,5120]{1,0:T(8,128)S(1)} %held.29.refs_0_, f32[56,5120]{1,0:T(8,128)S(1)} %held.31.refs_1_, ...), custom_call_target="tpu_custom_call" | custom-call | tf_op jit(solution)/shard_map/updated/pallas_call | solution.py:302
  (68 shorter events, 3.2 us)
Async XLA Ops:
  0.6 10.6 %copy-start.7 = (bf16[112,5120]{1,0:T(8,128)(2,1)S(1)}, bf16[112,5120]{1,0:T(8,128)(2,1)}, u32[]{:S(2)}) copy-start(bf16[112,5120]{1,0:T(8,128)(2,1)} %param.15) | copy-start | bytes 3440644
  0.6 10.6 %copy-start.6 = (bf16[112,5120]{1,0:T(8,128)(2,1)S(1)}, bf16[112,5120]{1,0:T(8,128)(2,1)}, u32[]{:S(2)}) copy-start(bf16[112,5120]{1,0:T(8,128)(2,1)} %param.16) | copy-start | bytes 3440644
  0.7 10.9 %collective-permute-start.1 = (bf16[20,5120]{1,0:T(8,128)(2,1)}, bf16[20,5120]{1,0:T(8,128)(2,1)S(1)}, u32[]{:S(2)}, u32[]{:S(2)}) collective-permute-start(bf16[20,5120]{1,0:T(8,128)(2,1)} %bitcast.29), channel_id=1, source_target_pairs={{0,0},{64,4},{4,64},{68,68},{1,1},{65,5},{5,65},{69,69},{2,2},{66,... | collective-permute-start | bytes 614408 | tf_op jit(solution)/shard_map/ppermute | solution.py:43
  6.8 9.2 %collective-permute-start = (bf16[20,5120]{1,0:T(8,128)(2,1)}, bf16[20,5120]{1,0:T(8,128)(2,1)S(1)}, u32[]{:S(2)}, u32[]{:S(2)}) collective-permute-start(bf16[20,5120]{1,0:T(8,128)(2,1)} %bitcast.30), channel_id=1, source_target_pairs={{0,0},{64,4},{4,64},{68,68},{1,1},{65,5},{5,65},{69,69},{2,2},{66,... | collective-permute-start | bytes 614408 | tf_op jit(solution)/shard_map/ppermute | solution.py:43
  16.1 19.6 %copy-start.5 = (f32[1,112,5120]{2,1,0:T(8,128)S(1)}, f32[1,112,5120]{2,1,0:T(8,128)}, u32[]{:S(2)}) copy-start(f32[1,112,5120]{2,1,0:T(8,128)} %param.13) | copy-start | bytes 6881284
  16.1 43.4 %collective-permute-start.17 = (bf16[336,5120]{1,0:T(8,128)(2,1)S(1)}, bf16[336,5120]{1,0:T(8,128)(2,1)S(1)}, u32[]{:S(2)}, u32[]{:S(2)}) collective-permute-start(bf16[336,5120]{1,0:T(8,128)(2,1)S(1)} %held.20), channel_id=1, source_target_pairs={{0,0},{64,4},{4,64},{68,68},{1,1},{65,5},{5,65},{69,69},{2,2},{66,... | collective-permute-start | bytes 10321928 | tf_op jit(solution)/shard_map/ppermute | solution.py:43
  18.8 8.6 %collective-permute-start.2 = (bf16[20,5120]{1,0:T(8,128)(2,1)S(1)}, bf16[20,5120]{1,0:T(8,128)(2,1)S(1)}, u32[]{:S(2)}, u32[]{:S(2)}) collective-permute-start(bf16[20,5120]{1,0:T(8,128)(2,1)S(1)} %held.16.refs_0_), channel_id=1, source_target_pairs={{1,0},{2,1},{3,2},{0,3},{5,4},{6,5},{7,6},{4,7},{9,8},{10,9},{11,1... | collective-permute-start | bytes 614408 | tf_op jit(solution)/shard_map/ppermute | solution.py:33
  21.6 10.0 %collective-permute-start.5 = (bf16[20,5120]{1,0:T(8,128)(2,1)S(1)}, bf16[20,5120]{1,0:T(8,128)(2,1)S(1)}, u32[]{:S(2)}, u32[]{:S(2)}) collective-permute-start(bf16[20,5120]{1,0:T(8,128)(2,1)S(1)} %collective-permute-done.1.refs_1_.refs_0_), channel_id=1, source_target_pairs={{8,0},{16,8},{24,16},{32,24},{40,32},{48,40},{56,48},{0,56},{9,1},... | collective-permute-start | bytes 614408 | tf_op jit(solution)/shard_map/ppermute | solution.py:33
  27.2 7.8 %collective-permute-start.7 = (bf16[20,5120]{1,0:T(8,128)(2,1)S(1)}, bf16[20,5120]{1,0:T(8,128)(2,1)S(1)}, u32[]{:S(2)}, u32[]{:S(2)}) collective-permute-start(bf16[20,5120]{1,0:T(8,128)(2,1)S(1)} %collective-permute-done.1.refs_1_.refs_0_), channel_id=1, source_target_pairs={{56,0},{0,8},{8,16},{16,24},{24,32},{32,40},{40,48},{48,56},{57,1}... | collective-permute-start | bytes 614408 | tf_op jit(solution)/shard_map/ppermute | solution.py:33
  27.2 8.9 %collective-permute-start.3 = (bf16[20,5120]{1,0:T(8,128)(2,1)S(1)}, bf16[20,5120]{1,0:T(8,128)(2,1)S(1)}, u32[]{:S(2)}, u32[]{:S(2)}) collective-permute-start(bf16[20,5120]{1,0:T(8,128)(2,1)S(1)} %held.16.refs_0_), channel_id=1, source_target_pairs={{3,0},{0,1},{1,2},{2,3},{7,4},{4,5},{5,6},{6,7},{11,8},{8,9},{9,10... | collective-permute-start | bytes 614408 | tf_op jit(solution)/shard_map/ppermute | solution.py:33
  27.4 8.7 %collective-permute-start.4 = (bf16[20,5120]{1,0:T(8,128)(2,1)S(1)}, bf16[20,5120]{1,0:T(8,128)(2,1)S(1)}, u32[]{:S(2)}, u32[]{:S(2)}) collective-permute-start(bf16[20,5120]{1,0:T(8,128)(2,1)S(1)} %held.16.refs_0_), channel_id=1, source_target_pairs={{2,0},{3,1},{0,2},{1,3},{6,4},{7,5},{4,6},{5,7},{10,8},{11,9},{8,1... | collective-permute-start | bytes 614408 | tf_op jit(solution)/shard_map/ppermute | solution.py:33
  31.6 6.3 %collective-permute-start.6 = (bf16[20,5120]{1,0:T(8,128)(2,1)S(1)}, bf16[20,5120]{1,0:T(8,128)(2,1)S(1)}, u32[]{:S(2)}, u32[]{:S(2)}) collective-permute-start(bf16[20,5120]{1,0:T(8,128)(2,1)S(1)} %collective-permute-done.5.refs_1_), channel_id=1, source_target_pairs={{8,0},{16,8},{24,16},{32,24},{40,32},{48,40},{56,48},{0,56},{9,1},... | collective-permute-start | bytes 614408 | tf_op jit(solution)/shard_map/ppermute | solution.py:33
  35.0 6.3 %collective-permute-start.8 = (bf16[20,5120]{1,0:T(8,128)(2,1)S(1)}, bf16[20,5120]{1,0:T(8,128)(2,1)S(1)}, u32[]{:S(2)}, u32[]{:S(2)}) collective-permute-start(bf16[20,5120]{1,0:T(8,128)(2,1)S(1)} %collective-permute-done.7.refs_3_), channel_id=1, source_target_pairs={{56,0},{0,8},{8,16},{16,24},{24,32},{32,40},{40,48},{48,56},{57,1}... | collective-permute-start | bytes 614408 | tf_op jit(solution)/shard_map/ppermute | solution.py:33
  41.3 16.1 %collective-permute-start.12 = (f32[120,5120]{1,0:T(8,128)S(1)}, f32[120,5120]{1,0:T(8,128)S(1)}, u32[]{:S(2)}, u32[]{:S(2)}) collective-permute-start(f32[120,5120]{1,0:T(8,128)S(1)} %held.18), channel_id=1, source_target_pairs={{64,0},{0,64},{65,1},{1,65},{66,2},{2,66},{67,3},{3,67},{68,4},{4,... | collective-permute-start | bytes 7372808 | tf_op jit(solution)/shard_map/ppermute | solution.py:33
  41.3 7.0 %collective-permute-start.9 = (bf16[20,5120]{1,0:T(8,128)(2,1)S(1)}, bf16[20,5120]{1,0:T(8,128)(2,1)S(1)}, u32[]{:S(2)}, u32[]{:S(2)}) collective-permute-start(bf16[20,5120]{1,0:T(8,128)(2,1)S(1)} %get-tuple-element.17.refs_1_.refs_2_), channel_id=1, source_target_pairs={{8,0},{16,8},{24,16},{32,24},{40,32},{48,40},{56,48},{0,56},{9,1},... | collective-permute-start | bytes 614408 | tf_op jit(solution)/shard_map/ppermute | solution.py:33
  41.3 16.0 %collective-permute-start.10 = (bf16[20,5120]{1,0:T(8,128)(2,1)S(1)}, bf16[20,5120]{1,0:T(8,128)(2,1)S(1)}, u32[]{:S(2)}, u32[]{:S(2)}) collective-permute-start(bf16[20,5120]{1,0:T(8,128)(2,1)S(1)} %get-tuple-element.17.refs_1_.refs_2_), channel_id=1, source_target_pairs={{16,0},{24,8},{32,16},{40,24},{48,32},{56,40},{0,48},{8,56},{17,1}... | collective-permute-start | bytes 614408 | tf_op jit(solution)/shard_map/ppermute | solution.py:33
  41.4 16.0 %collective-permute-start.11 = (bf16[20,5120]{1,0:T(8,128)(2,1)S(1)}, bf16[20,5120]{1,0:T(8,128)(2,1)S(1)}, u32[]{:S(2)}, u32[]{:S(2)}) collective-permute-start(bf16[20,5120]{1,0:T(8,128)(2,1)S(1)} %get-tuple-element.18.refs_2_), channel_id=1, source_target_pairs={{56,0},{0,8},{8,16},{16,24},{24,32},{32,40},{40,48},{48,56},{57,1}... | collective-permute-start | bytes 614408 | tf_op jit(solution)/shard_map/ppermute | solution.py:33
  57.4 1.4 copy-start
  59.4 8.4 %collective-permute-start.18 = (bf16[336,5120]{1,0:T(8,128)(2,1)S(1)}, bf16[336,5120]{1,0:T(8,128)(2,1)S(1)}, u32[]{:S(2)}, u32[]{:S(2)}) collective-permute-start(bf16[336,5120]{1,0:T(8,128)(2,1)S(1)} %held.21.refs_6_.refs_2_.refs_9_.refs_11_), channel_id=1, source_target_pairs={{64,0},{0,64},{65,1},{1,65},{66,2},{2,66},{67,3},{3,67},{68,4},{4,... | collective-permute-start | bytes 10321928 | tf_op jit(solution)/shard_map/ppermute | solution.py:33
  60.2 19.9 %collective-permute-start.15 = (bf16[80,5120]{1,0:T(8,128)(2,1)S(1)}, bf16[80,5120]{1,0:T(8,128)(2,1)S(1)}, u32[]{:S(2)}, u32[]{:S(2)}) collective-permute-start(bf16[80,5120]{1,0:T(8,128)(2,1)S(1)} %stacked.5.refs_1_.refs_0_), channel_id=1, source_target_pairs={{1,0},{2,1},{3,2},{0,3},{5,4},{6,5},{7,6},{4,7},{9,8},{10,9},{11,1... | collective-permute-start | bytes 2457608 | tf_op jit(solution)/shard_map/ppermute | solution.py:33
  62.2 20.2 %collective-permute-start.16 = (bf16[80,5120]{1,0:T(8,128)(2,1)S(1)}, bf16[80,5120]{1,0:T(8,128)(2,1)S(1)}, u32[]{:S(2)}, u32[]{:S(2)}) collective-permute-start(bf16[80,5120]{1,0:T(8,128)(2,1)S(1)} %stacked.5.refs_1_.refs_0_), channel_id=1, source_target_pairs={{3,0},{0,1},{1,2},{2,3},{7,4},{4,5},{5,6},{6,7},{11,8},{8,9},{9,10... | collective-permute-start | bytes 2457608 | tf_op jit(solution)/shard_map/ppermute | solution.py:33
  62.2 22.4 %collective-permute-start.13 = (bf16[80,5120]{1,0:T(8,128)(2,1)S(1)}, bf16[80,5120]{1,0:T(8,128)(2,1)S(1)}, u32[]{:S(2)}, u32[]{:S(2)}) collective-permute-start(bf16[80,5120]{1,0:T(8,128)(2,1)S(1)} %stacked.3.refs_2_.refs_0_), channel_id=1, source_target_pairs={{8,0},{16,8},{24,16},{32,24},{40,32},{48,40},{56,48},{0,56},{9,1},... | collective-permute-start | bytes 2457608 | tf_op jit(solution)/shard_map/ppermute | solution.py:33
  67.8 19.9 %collective-permute-start.14 = (bf16[80,5120]{1,0:T(8,128)(2,1)S(1)}, bf16[80,5120]{1,0:T(8,128)(2,1)S(1)}, u32[]{:S(2)}, u32[]{:S(2)}) collective-permute-start(bf16[80,5120]{1,0:T(8,128)(2,1)S(1)} %stacked.3.refs_2_.refs_0_), channel_id=1, source_target_pairs={{56,0},{0,8},{8,16},{16,24},{24,32},{32,40},{40,48},{48,56},{57,1}... | collective-permute-start | bytes 2457608 | tf_op jit(solution)/shard_map/ppermute | solution.py:33
  67.9 41.3 %collective-permute-start.21 = (f32[64,5120]{1,0:T(8,128)S(1)}, f32[64,5120]{1,0:T(8,128)S(1)}, u32[]{:S(2)}, u32[]{:S(2)}) collective-permute-start(f32[64,5120]{1,0:T(8,128)S(1)} %held.23), channel_id=1, source_target_pairs={{128,0},{0,128},{129,1},{1,129},{130,2},{2,130},{131,3},{3,131},{1... | collective-permute-start | bytes 3932168 | tf_op jit(solution)/shard_map/ppermute | solution.py:33
  87.6 19.0 %collective-permute-start.23 = (bf16[80,5120]{1,0:T(8,128)(2,1)S(1)}, bf16[80,5120]{1,0:T(8,128)(2,1)S(1)}, u32[]{:S(2)}, u32[]{:S(2)}) collective-permute-start(bf16[80,5120]{1,0:T(8,128)(2,1)S(1)} %held.24.refs_1_), channel_id=1, source_target_pairs={{3,0},{0,1},{1,2},{2,3},{7,4},{4,5},{5,6},{6,7},{11,8},{8,9},{9,10... | collective-permute-start | bytes 2457608 | tf_op jit(solution)/shard_map/ppermute | solution.py:33
  87.6 19.0 %collective-permute-start.22 = (bf16[80,5120]{1,0:T(8,128)(2,1)S(1)}, bf16[80,5120]{1,0:T(8,128)(2,1)S(1)}, u32[]{:S(2)}, u32[]{:S(2)}) collective-permute-start(bf16[80,5120]{1,0:T(8,128)(2,1)S(1)} %held.24.refs_1_), channel_id=1, source_target_pairs={{1,0},{2,1},{3,2},{0,3},{5,4},{6,5},{7,6},{4,7},{9,8},{10,9},{11,1... | collective-permute-start | bytes 2457608 | tf_op jit(solution)/shard_map/ppermute | solution.py:33
  90.3 17.2 %collective-permute-start.19 = (bf16[80,5120]{1,0:T(8,128)(2,1)S(1)}, bf16[80,5120]{1,0:T(8,128)(2,1)S(1)}, u32[]{:S(2)}, u32[]{:S(2)}) collective-permute-start(bf16[80,5120]{1,0:T(8,128)(2,1)S(1)} %get-tuple-element.19.refs_1_), channel_id=1, source_target_pairs={{8,0},{16,8},{24,16},{32,24},{40,32},{48,40},{56,48},{0,56},{9,1},... | collective-permute-start | bytes 2457608 | tf_op jit(solution)/shard_map/ppermute | solution.py:33
  90.7 18.4 %collective-permute-start.20 = (bf16[80,5120]{1,0:T(8,128)(2,1)S(1)}, bf16[80,5120]{1,0:T(8,128)(2,1)S(1)}, u32[]{:S(2)}, u32[]{:S(2)}) collective-permute-start(bf16[80,5120]{1,0:T(8,128)(2,1)S(1)} %get-tuple-element.20.refs_2_.refs_8_), channel_id=1, source_target_pairs={{56,0},{0,8},{8,16},{16,24},{24,32},{32,40},{40,48},{48,56},{57,1}... | collective-permute-start | bytes 2457608 | tf_op jit(solution)/shard_map/ppermute | solution.py:33
  106.6 18.0 %collective-permute-start.27 = (bf16[80,5120]{1,0:T(8,128)(2,1)S(1)}, bf16[80,5120]{1,0:T(8,128)(2,1)S(1)}, u32[]{:S(2)}, u32[]{:S(2)}) collective-permute-start(bf16[80,5120]{1,0:T(8,128)(2,1)S(1)} %collective-permute-done.23.refs_4_.refs_5_), channel_id=1, source_target_pairs={{3,0},{0,1},{1,2},{2,3},{7,4},{4,5},{5,6},{6,7},{11,8},{8,9},{9,10... | collective-permute-start | bytes 2457608 | tf_op jit(solution)/shard_map/ppermute | solution.py:33
  109.1 16.7 %collective-permute-start.24 = (bf16[80,5120]{1,0:T(8,128)(2,1)S(1)}, bf16[80,5120]{1,0:T(8,128)(2,1)S(1)}, u32[]{:S(2)}, u32[]{:S(2)}) collective-permute-start(bf16[80,5120]{1,0:T(8,128)(2,1)S(1)} %get-tuple-element.21.refs_1_.refs_2_), channel_id=1, source_target_pairs={{8,0},{16,8},{24,16},{32,24},{40,32},{48,40},{56,48},{0,56},{9,1},... | collective-permute-start | bytes 2457608 | tf_op jit(solution)/shard_map/ppermute | solution.py:33
  109.5 16.3 %collective-permute-start.26 = (bf16[80,5120]{1,0:T(8,128)(2,1)S(1)}, bf16[80,5120]{1,0:T(8,128)(2,1)S(1)}, u32[]{:S(2)}, u32[]{:S(2)}) collective-permute-start(bf16[80,5120]{1,0:T(8,128)(2,1)S(1)} %held.26.refs_2_), channel_id=1, source_target_pairs={{1,0},{2,1},{3,2},{0,3},{5,4},{6,5},{7,6},{4,7},{9,8},{10,9},{11,1... | collective-permute-start | bytes 2457608 | tf_op jit(solution)/shard_map/ppermute | solution.py:33
  110.3 16.9 %collective-permute-start.25 = (bf16[80,5120]{1,0:T(8,128)(2,1)S(1)}, bf16[80,5120]{1,0:T(8,128)(2,1)S(1)}, u32[]{:S(2)}, u32[]{:S(2)}) collective-permute-start(bf16[80,5120]{1,0:T(8,128)(2,1)S(1)} %get-tuple-element.22.refs_7_), channel_id=1, source_target_pairs={{56,0},{0,8},{8,16},{16,24},{24,32},{32,40},{40,48},{48,56},{57,1}... | collective-permute-start | bytes 2457608 | tf_op jit(solution)/shard_map/ppermute | solution.py:33
  127.2 31.9 %collective-permute-start.31 = (f32[64,5120]{1,0:T(8,128)S(1)}, f32[64,5120]{1,0:T(8,128)S(1)}, u32[]{:S(2)}, u32[]{:S(2)}) collective-permute-start(f32[64,5120]{1,0:T(8,128)S(1)} %held.29.refs_0_), channel_id=1, source_target_pairs={{64,0},{0,64},{65,1},{1,65},{66,2},{2,66},{67,3},{3,67},{68,4},{4,... | collective-permute-start | bytes 3932168 | tf_op jit(solution)/shard_map/ppermute | solution.py:33
  132.1 26.9 %collective-permute-start.30 = (f32[56,5120]{1,0:T(8,128)S(1)}, f32[56,5120]{1,0:T(8,128)S(1)}, u32[]{:S(2)}, u32[]{:S(2)}) collective-permute-start(f32[56,5120]{1,0:T(8,128)S(1)} %held.28), channel_id=1, source_target_pairs={{128,0},{0,128},{129,1},{1,129},{130,2},{2,130},{131,3},{3,131},{1... | collective-permute-start | bytes 3440648 | tf_op jit(solution)/shard_map/ppermute | solution.py:33
  132.8 27.3 %collective-permute-start.28 = (bf16[48,5120]{1,0:T(8,128)(2,1)S(1)}, bf16[48,5120]{1,0:T(8,128)(2,1)S(1)}, u32[]{:S(2)}, u32[]{:S(2)}) collective-permute-start(bf16[48,5120]{1,0:T(8,128)(2,1)S(1)} %slice.17), channel_id=1, source_target_pairs={{8,0},{16,8},{24,16},{32,24},{40,32},{48,40},{56,48},{0,56},{9,1},... | collective-permute-start | bytes 1474568 | tf_op jit(solution)/shard_map/ppermute | solution.py:33
  132.9 26.1 %collective-permute-start.29 = (bf16[32,5120]{1,0:T(8,128)(2,1)S(1)}, bf16[32,5120]{1,0:T(8,128)(2,1)S(1)}, u32[]{:S(2)}, u32[]{:S(2)}) collective-permute-start(bf16[32,5120]{1,0:T(8,128)(2,1)S(1)} %slice.18), channel_id=1, source_target_pairs={{56,0},{0,8},{8,16},{16,24},{24,32},{32,40},{40,48},{48,56},{57,1}... | collective-permute-start | bytes 983048 | tf_op jit(solution)/shard_map/ppermute | solution.py:33
  159.0 1.1 copy-start.3
  169.1 4.9 %collective-permute-start.32 = (f32[112,5120]{1,0:T(8,128)S(1)}, f32[112,5120]{1,0:T(8,128)S(1)}, u32[]{:S(2)}, u32[]{:S(2)}) collective-permute-start(f32[112,5120]{1,0:T(8,128)S(1)} %get-tuple-element.26), channel_id=1, source_target_pairs={{64,0},{0,64},{65,1},{1,65},{66,2},{2,66},{67,3},{3,67},{68,4},{4,... | collective-permute-start | bytes 6881288 | tf_op jit(solution)/shard_map/ppermute | solution.py:33
  176.7 55.1 %collective-permute-start.41 = (f32[112,5120]{1,0:T(8,128)}, f32[112,5120]{1,0:T(8,128)}, u32[]{:S(2)}, u32[]{:S(2)}) collective-permute-start(f32[112,5120]{1,0:T(8,128)} %get-tuple-element.31.refs_5_), channel_id=1, source_target_pairs={{64,4},{4,64},{65,5},{5,65},{66,6},{6,66},{67,7},{7,67},{72,12},{1... | collective-permute-start | bytes 6881288 | tf_op jit(solution)/shard_map/ppermute | solution.py:43
  180.9 50.9 %collective-permute-start.40 = (f32[56,5120]{1,0:T(8,128)S(1)}, f32[56,5120]{1,0:T(8,128)}, u32[]{:S(2)}, u32[]{:S(2)}) collective-permute-start(f32[56,5120]{1,0:T(8,128)S(1)} %held.31.refs_1_), channel_id=1, source_target_pairs={{64,0},{0,64},{65,1},{1,65},{66,2},{2,66},{67,3},{3,67},{68,4},{4,... | collective-permute-start | bytes 3440648 | tf_op jit(solution)/shard_map/ppermute | solution.py:33
  181.8 26.2 %collective-permute-start.33 = (f32[1]{0:T(128)}, f32[1]{0:T(128)}, u32[]{:S(2)}, u32[]{:S(2)}) collective-permute-start(f32[1]{0:T(128)} %bitcast.8), channel_id=1, source_target_pairs={{0,0},{64,4},{4,64},{68,68},{1,1},{65,5},{5,65},{69,69},{2,2},{66,... | collective-permute-start | bytes 20 | tf_op jit(solution)/shard_map/ppermute | solution.py:43
  184.7 23.3 %collective-permute-start.34 = (f32[1]{0:T(128)}, f32[1]{0:T(128)}, u32[]{:S(2)}, u32[]{:S(2)}) collective-permute-start(f32[1]{0:T(128)} %bitcast.8), channel_id=1, source_target_pairs={{64,0},{0,4},{68,64},{4,68},{65,1},{1,5},{69,65},{5,69},{66,2},{2,... | collective-permute-start | bytes 20 | tf_op jit(solution)/shard_map/ppermute | solution.py:48
  209.4 2.6 %collective-permute-start.35 = (f32[1]{0:T(128)}, f32[1]{0:T(128)}, u32[]{:S(2)}, u32[]{:S(2)}) collective-permute-start(f32[1]{0:T(128)} %add.43), channel_id=1, source_target_pairs={{1,0},{0,1},{3,2},{2,3},{5,4},{4,5},{7,6},{6,7},{9,8},{8,9},{11,10... | collective-permute-start | bytes 20 | tf_op jit(solution)/shard_map/ppermute | solution.py:53
  212.6 4.1 %collective-permute-start.36 = (f32[1]{0:T(128)}, f32[1]{0:T(128)}, u32[]{:S(2)}, u32[]{:S(2)}) collective-permute-start(f32[1]{0:T(128)} %add.44), channel_id=1, source_target_pairs={{2,0},{3,1},{0,2},{1,3},{6,4},{7,5},{4,6},{5,7},{10,8},{11,9},{8,1... | collective-permute-start | bytes 20 | tf_op jit(solution)/shard_map/ppermute | solution.py:53
  217.3 2.6 %collective-permute-start.37 = (f32[1]{0:T(128)}, f32[1]{0:T(128)}, u32[]{:S(2)}, u32[]{:S(2)}) collective-permute-start(f32[1]{0:T(128)} %add.45), channel_id=1, source_target_pairs={{8,0},{0,8},{24,16},{16,24},{40,32},{32,40},{56,48},{48,56},{9,1},... | collective-permute-start | bytes 20 | tf_op jit(solution)/shard_map/ppermute | solution.py:53
  220.5 3.5 %collective-permute-start.38 = (f32[1]{0:T(128)}, f32[1]{0:T(128)}, u32[]{:S(2)}, u32[]{:S(2)}) collective-permute-start(f32[1]{0:T(128)} %add.46), channel_id=1, source_target_pairs={{16,0},{24,8},{0,16},{8,24},{48,32},{56,40},{32,48},{40,56},{17,1}... | collective-permute-start | bytes 20 | tf_op jit(solution)/shard_map/ppermute | solution.py:53
  224.6 6.5 %collective-permute-start.39 = (f32[1]{0:T(128)}, f32[1]{0:T(128)}, u32[]{:S(2)}, u32[]{:S(2)}) collective-permute-start(f32[1]{0:T(128)} %add.47), channel_id=1, source_target_pairs={{32,0},{40,8},{48,16},{56,24},{0,32},{8,40},{16,48},{24,56},{33,1}... | collective-permute-start | bytes 20 | tf_op jit(solution)/shard_map/ppermute | solution.py:53
  231.8 1.7 copy-start.1
  233.5 1.6 copy-start.2
  235.2 1.3 copy-start.4

commit v11 on v9

--- a/solution.py
+++ b/solution.py
@@ -22,7 +22,7 @@
 
 ROWS = 112
 HALF = 128
-CUT = 64
+CUT = 88
 NO_COST = pl.CostEstimate(flops=1, bytes_accessed=1, transcendentals=0)
 BLOCK = 1024
 
@@ -40,6 +40,11 @@
         for x_hi in range(2)
         if stay or core != x_hi
     ]
+    return lax.ppermute(value, ("core", "x_hi"), pairs)
+
+
+def crossed(value):
+    pairs = [(2 * (1 - x_hi) + core, 2 * core + x_hi) for core in range(2) for x_hi in range(2)]
     return lax.ppermute(value, ("core", "x_hi"), pairs)
 
 
@@ -303,7 +308,7 @@
             pltpu.SemaphoreType.DMA((2, blocks)),
             pltpu.SemaphoreType.DMA((blocks,)),
         ],
-        compiler_params=params_of(56),
+        compiler_params=params_of(16),
         name="updated",
     )(factor, kept_weight, which, numerator, *more)
 
@@ -320,7 +325,7 @@
     rows_in = held(rows_in, rows_grad, weights)
     near = [rows_in] + [shifted(rows_in, "y", steps) for steps in (1, 3, 2)]
     ring = {0: rows_grad, 1: shifted(rows_grad, "z", 1), 7: shifted(rows_grad, "z", 7)}
-    mine = transposed(held(weights, ring[1], ring[7]))
+    mine = transposed(held(weights, rows_grad))
     ring[2], ring[6] = shifted(ring[1], "z", 1), shifted(ring[7], "z", 7)
     ring[2], ring[6] = held((ring[2], ring[6]), *near[1:])
     ring[3], ring[5] = shifted(ring[2], "z", 1), shifted(ring[6], "z", 7)
@@ -331,47 +336,47 @@
 
     blocks[1], blocks[7] = shifted(blocks[0], "z", 1), shifted(blocks[0], "z", 7)
     following, before = [shifted(columns[0], "y", 1)], [shifted(columns[0], "y", 3)]
-    ready = (columns[1], following[0], before[0], mine)
-    blocks[1], blocks[7] = held((blocks[1], blocks[7]), *ready)
+    blocks[1], blocks[7] = held((blocks[1], blocks[7]), columns[1], following[0], before[0])
 
     blocks[2], blocks[6] = shifted(blocks[1], "z", 1), shifted(blocks[7], "z", 7)
     columns[1] = held(columns[1], blocks[1], blocks[7])
     following.append(shifted(columns[1], "y", 1))
     before.append(shifted(columns[1], "y", 3))
-    stale = jnp.concatenate([stale_num[0], jnp.broadcast_to(stale_weight, (8, D))], axis=0)
-    two_before = [shifted(held(stale[:CUT], mine), "x_lo", 1)]
-    ready = (two_before[0], following[1], before[1])
-    blocks[2], blocks[6] = held((blocks[2], blocks[6]), *ready)
+    mine = held(mine, blocks[1], blocks[7])
+    theirs = shifted(mine, "core", 1)
+    blocks[2], blocks[6] = held((blocks[2], blocks[6]), theirs, following[1], before[1])
 
     blocks[3], blocks[5] = shifted(blocks[2], "z", 1), shifted(blocks[6], "z", 7)
     following[0] = held(following[0], blocks[2])
     far = [shifted(following[0], "y", 1), shifted(before[1], "y", 3)]
-    mine = held(mine, blocks[2], blocks[6])
-    theirs = shifted(mine, "core", 1)
-    two_before.append(shifted(held(stale[CUT:], two_before[0]), "x_lo", 1))
+    stale = jnp.concatenate([stale_num[0], jnp.broadcast_to(stale_weight, (8, D))], axis=0)
+    two_before = [shifted(held(stale[:CUT], theirs), "x_lo", 1)]
     hidden_most = hidden_of([*columns, *following, *before], mine, theirs)
-    blocks[3], blocks[5] = held((blocks[3], blocks[5]), hidden_most, *far)
+    ready = (two_before[0], hidden_most, *far)
+    blocks[3], blocks[5] = held((blocks[3], blocks[5]), *ready)
 
     cut = 48
     last = [shifted(blocks[3][:cut], "z", 1), shifted(blocks[5][cut:], "z", 7)]
-    hidden_far = held(hidden_of(far, mine, theirs), two_before[1])
+    two_before.append(shifted(held(stale[CUT:], two_before[0]), "x_lo", 1))
+    two_before[0] = held(two_before[0], blocks[3])
+    one_before = [shifted(two_before[0], "core", 1)]
+    hidden_far = held(hidden_of(far, mine, theirs), one_before[0])
     parts = [blocks[steps] for steps in (0, 1, 2, 3)] + last + [blocks[steps] for steps in (5, 6, 7)]
 
     own_grad, other_grad = gate_grads(parts, mine, theirs, hidden_most, hidden_far)
-    two_before = held(tuple(two_before), own_grad)
-    one_before = [shifted(part, "core", 1) for part in two_before]
     stale_hop = shifted(held(stale, own_grad), "core", 1)
     gate_grad = own_grad + shifted(other_grad, "core", 1)
     norm_sq = jnp.sum(gate_grad * gate_grad)
     returned = transposed(gate_grad, stay=False)
-    for axes in ("z", "y"):
-        norm_sq = lax.psum(norm_sq, axes)
-    x_hi, core = lax.axis_index("x_hi"), lax.axis_index("core")
-    norms = lax.psum(jnp.where(jnp.arange(2) == x_hi, norm_sq, 0.0), ("core", "x_hi"))
-    norm_sq = jnp.where(core == 0, norms[0], norms[1])
+    norm_sq = lax.psum(norm_sq, "z")
+    two_before[1] = held(two_before[1], jnp.reshape(norm_sq, (1,)))
+    one_before.append(shifted(two_before[1], "core", 1))
+    norm_sq = lax.psum(norm_sq, "y")
+    norm_sq = transposed(norm_sq) + crossed(norm_sq)
 
     clip_factor = jnp.minimum(1.0, MAX_NORM / jnp.sqrt(norm_sq + eps))
     kept_weight = 0.5 * push_weight
+    core, x_hi = lax.axis_index("core"), lax.axis_index("x_hi")
     which = jnp.where(step[0] % 2 == 1, 0, 1 + core)
     kept_half, new_num, new_weight = updated(
         numerator,

time: 218 us -> 237 us (1.087)
  waiting for transfers between devices: 79.8 us -> 116 us
  blocking collectives: 37.4 us -> 20.1 us
  local copies, waits for them, and re-layouts: 2.53 us -> 6.46 us
    ppermute x31, waiting for transfers between devices: 56 us -> 108 us  [shifted(): return lax.ppermute(value, axis, pairs)]
    ppermute x4 -> x5, waiting for transfers between devices: 23.9 us -> 5.87 us  [transposed(): return lax.ppermute(value, ('core', 'x_hi'), pairs)]
    psum x3 -> x2, blocking collectives: 37.4 us -> 20.1 us  [the longest x1 12.8 us: shards(): norm_sq = lax.psum(norm_sq, 'z')]
    unnamed x10 -> x12, local copies, waits for them, and re-layouts: 0.02 us -> 4.51 us
    ppermute x0 -> x1, waiting for transfers between devices: none -> 2.77 us  [crossed(): return lax.ppermute(value, ('core', 'x_hi'), pairs)]
    ppermute x4 -> x5, starting transfers between devices: 23.8 us -> 23.6 us  [transposed(): return lax.ppermute(value, ('core', 'x_hi'), pairs)]
  transfers between devices with their start and end apart: 35 -> 37, of which waited for: 19 -> 26; matrix products, arithmetic and copies ran while one was open for 4% -> 3% of each run, Pallas kernels for 4% -> 4%
where the time goes in v11:
time: 237 us
  waiting for transfers between devices  116 us (49%)
  starting transfers between devices  59.1 us (25%)
  Pallas kernels  24.6 us (10%)
  blocking collectives  20.1 us (8%)
  local copies, waits for them, and re-layouts  6.46 us (3%)
  between operations  5.54 us (2%)
  other arithmetic  4.71 us (2%)
    ppermute x31, waiting for transfers between devices, shifted(): return lax.ppermute(value, axis, pairs)  108 us
    ppermute x31, starting transfers between devices, shifted(): return lax.ppermute(value, axis, pairs)  35.4 us
    ppermute x5, starting transfers between devices, transposed(): return lax.ppermute(value, ('core', 'x_hi'), pairs)  23.6 us
    psum x1, blocking collectives, shards(): norm_sq = lax.psum(norm_sq, 'z')  12.8 us
    pallas_call x1, Pallas kernels, gate_grads(): pl.pallas_call(grad_kernel, grid=(D // BLOCK,), in_specs=[pl.BlockSpec((p...  9 us
    pallas_call x2, Pallas kernels, hidden_of(): pl.pallas_call(hidden_kernel, grid=(D // BLOCK,), in_specs=[pl.BlockSpec(...  8.72 us
    psum x1, blocking collectives, shards(): norm_sq = lax.psum(norm_sq, 'y')  7.33 us
    ppermute x5, waiting for transfers between devices, transposed(): return lax.ppermute(value, ('core', 'x_hi'), pairs)  5.87 us
  transfers between devices with their start and end apart: 37, of which 26 were waited for; matrix products, arithmetic and copies ran while one was open for 3% of the time, Pallas kernels for 4%

profile of v11, /device:TPU:1, one launch (start us, length us, event | category | flops | bytes accessed | tf_op | source)
XLA Modules:
  0.0 236.6 jit_solution(15870260298369638341)
XLA Ops:
  0.7 6.2 %collective-permute-start.1 = (bf16[20,5120]{1,0:T(8,128)(2,1)}, bf16[20,5120]{1,0:T(8,128)(2,1)S(1)}, u32[]{:S(2)}, u32[]{:S(2)}) collective-permute-start(bf16[20,5120]{1,0:T(8,128)(2,1)} %bitcast.28), channel_id=1, source_target_pairs={{0,0},{64,4},{4,64},{68,68},{1,1},{65,5},{5,65},{69,69},{2,2},{66,... | collective-permute-start | bytes 614408 | tf_op jit(solution)/shard_map/ppermute | solution.py:43
  6.8 1.9 collective-permute-start
  9.4 1.8 divide_convert_fusion
  11.3 0.3 pad_maximum_fusion.refs_2_.refs_0_
  11.5 4.5 %collective-permute-done.refs_0_ = bf16[20,5120]{1,0:T(8,128)(2,1)S(1)} collective-permute-done((bf16[20,5120]{1,0:T(8,128)(2,1)}, bf16[20,5120]{1,0:T(8,128)(2,1)S(1)}, u32[]{:S(2)}, u32[]{:S(2)}) %collective-permute-start) | collective-permute-done | bytes 204832 | tf_op jit(solution)/shard_map/ppermute | solution.py:43
  16.1 2.6 %collective-permute-start.18 = (bf16[336,5120]{1,0:T(8,128)(2,1)S(1)}, bf16[336,5120]{1,0:T(8,128)(2,1)S(1)}, u32[]{:S(2)}, u32[]{:S(2)}) collective-permute-start(bf16[336,5120]{1,0:T(8,128)(2,1)S(1)} %held.20), channel_id=1, source_target_pairs={{0,0},{64,4},{4,64},{68,68},{1,1},{65,5},{5,65},{69,69},{2,2},{66,... | collective-permute-start | bytes 10321928 | tf_op jit(solution)/shard_map/ppermute | solution.py:43
  18.7 2.8 %collective-permute-start.2 = (bf16[20,5120]{1,0:T(8,128)(2,1)S(1)}, bf16[20,5120]{1,0:T(8,128)(2,1)S(1)}, u32[]{:S(2)}, u32[]{:S(2)}) collective-permute-start(bf16[20,5120]{1,0:T(8,128)(2,1)S(1)} %held.16.refs_0_), channel_id=1, source_target_pairs={{1,0},{2,1},{3,2},{0,3},{5,4},{6,5},{7,6},{4,7},{9,8},{10,9},{11,1... | collective-permute-start | bytes 614408 | tf_op jit(solution)/shard_map/ppermute | solution.py:33
  21.5 5.6 %collective-permute-start.5 = (bf16[20,5120]{1,0:T(8,128)(2,1)S(1)}, bf16[20,5120]{1,0:T(8,128)(2,1)S(1)}, u32[]{:S(2)}, u32[]{:S(2)}) collective-permute-start(bf16[20,5120]{1,0:T(8,128)(2,1)S(1)} %collective-permute-done.1.refs_1_.refs_0_), channel_id=1, source_target_pairs={{8,0},{16,8},{24,16},{32,24},{40,32},{48,40},{56,48},{0,56},{9,1},... | collective-permute-start | bytes 614408 | tf_op jit(solution)/shard_map/ppermute | solution.py:33
  27.3 1.7 collective-permute-start.4
  29.0 2.5 %collective-permute-done.5.refs_1_ = bf16[20,5120]{1,0:T(8,128)(2,1)S(1)} collective-permute-done((bf16[20,5120]{1,0:T(8,128)(2,1)S(1)}, bf16[20,5120]{1,0:T(8,128)(2,1)S(1)}, u32[]{:S(2)}, u32[]{:S(2)}) %collective-permute-start.5) | collective-permute-done | bytes 204832 | tf_op jit(solution)/shard_map/ppermute | solution.py:33
  31.5 3.1 %collective-permute-start.6 = (bf16[20,5120]{1,0:T(8,128)(2,1)S(1)}, bf16[20,5120]{1,0:T(8,128)(2,1)S(1)}, u32[]{:S(2)}, u32[]{:S(2)}) collective-permute-start(bf16[20,5120]{1,0:T(8,128)(2,1)S(1)} %collective-permute-done.5.refs_1_), channel_id=1, source_target_pairs={{8,0},{16,8},{24,16},{32,24},{40,32},{48,40},{56,48},{0,56},{9,1},... | collective-permute-start | bytes 614408 | tf_op jit(solution)/shard_map/ppermute | solution.py:33
  34.6 0.3 collective-permute-done.7.refs_3_
  34.9 1.1 collective-permute-done.3.refs_3_.refs_2_
  36.0 7.0 %collective-permute-done.6.refs_0_ = bf16[20,5120]{1,0:T(8,128)(2,1)S(1)} collective-permute-done((bf16[20,5120]{1,0:T(8,128)(2,1)S(1)}, bf16[20,5120]{1,0:T(8,128)(2,1)S(1)}, u32[]{:S(2)}, u32[]{:S(2)}) %collective-permute-start.6) | collective-permute-done | bytes 204832 | tf_op jit(solution)/shard_map/ppermute | solution.py:33
  42.9 1.0 collective-permute-done.8.refs_1_
  43.9 2.2 collective-permute-start.9
  46.1 1.1 collective-permute-start.11
  47.2 6.1 %collective-permute-done.10.refs_2_.refs_0_ = bf16[20,5120]{1,0:T(8,128)(2,1)S(1)} collective-permute-done((bf16[20,5120]{1,0:T(8,128)(2,1)S(1)}, bf16[20,5120]{1,0:T(8,128)(2,1)S(1)}, u32[]{:S(2)}, u32[]{:S(2)}) %collective-permute-start.10) | collective-permute-done | bytes 204832 | tf_op jit(solution)/shard_map/ppermute | solution.py:33
  53.3 6.5 %collective-permute-done.9.refs_1_.refs_3_ = bf16[20,5120]{1,0:T(8,128)(2,1)S(1)} collective-permute-done((bf16[20,5120]{1,0:T(8,128)(2,1)S(1)}, bf16[20,5120]{1,0:T(8,128)(2,1)S(1)}, u32[]{:S(2)}, u32[]{:S(2)}) %collective-permute-start.9) | collective-permute-done | bytes 204832 | tf_op jit(solution)/shard_map/ppermute | solution.py:33
  59.8 0.3 stacked.3.refs_0_
  60.2 1.5 collective-permute-start.13
  61.7 0.3 stacked.5.refs_0_
  62.1 1.8 collective-permute-start.15
  63.9 0.3 stacked.4.refs_2_.refs_0_
  64.2 8.9 %collective-permute-done.12.refs_0_ = bf16[80,5120]{1,0:T(8,128)(2,1)S(1)} collective-permute-done((bf16[80,5120]{1,0:T(8,128)(2,1)S(1)}, bf16[80,5120]{1,0:T(8,128)(2,1)S(1)}, u32[]{:S(2)}, u32[]{:S(2)}) %collective-permute-start.12) | collective-permute-done | bytes 819232 | tf_op jit(solution)/shard_map/ppermute | solution.py:33
  73.2 0.4 collective-permute-done.14.refs_3_.refs_0_
  73.5 2.2 collective-permute-done.15.refs_4_
  76.0 1.4 copy-done.3
  77.5 4.6 %collective-permute-done.19.refs_2_.refs_1_.refs_7_.refs_3_.refs_10_.refs_12_ = bf16[336,5120]{1,0:T(8,128)(2,1)S(1)} collective-permute-done((bf16[336,5120]{1,0:T(8,128)(2,1)S(1)}, bf16[336,5120]{1,0:T(8,128)(2,1)S(1)}, u32[]{:S(2)}, u32[]{:S(2)}) %collective-permute-start.19) | collective-permute-done | bytes 3440672 | tf_op jit(solution)/shard_map/ppermute | solution.py:33
  82.1 1.9 collective-permute-start.24
  84.0 2.7 %collective-permute-start.20 = (bf16[80,5120]{1,0:T(8,128)(2,1)S(1)}, bf16[80,5120]{1,0:T(8,128)(2,1)S(1)}, u32[]{:S(2)}, u32[]{:S(2)}) collective-permute-start(bf16[80,5120]{1,0:T(8,128)(2,1)S(1)} %held.22.refs_1_), channel_id=1, source_target_pairs={{1,0},{2,1},{3,2},{0,3},{5,4},{6,5},{7,6},{4,7},{9,8},{10,9},{11,1... | collective-permute-start | bytes 2457608 | tf_op jit(solution)/shard_map/ppermute | solution.py:33
  86.6 3.0 %collective-permute-start.16 = (bf16[80,5120]{1,0:T(8,128)(2,1)S(1)}, bf16[80,5120]{1,0:T(8,128)(2,1)S(1)}, u32[]{:S(2)}, u32[]{:S(2)}) collective-permute-start(bf16[80,5120]{1,0:T(8,128)(2,1)S(1)} %get-tuple-element.19.refs_1_), channel_id=1, source_target_pairs={{8,0},{16,8},{24,16},{32,24},{40,32},{48,40},{56,48},{0,56},{9,1},... | collective-permute-start | bytes 2457608 | tf_op jit(solution)/shard_map/ppermute | solution.py:33
  89.6 15.0 %collective-permute-done.21.refs_4_.refs_5_ = bf16[80,5120]{1,0:T(8,128)(2,1)S(1)} collective-permute-done((bf16[80,5120]{1,0:T(8,128)(2,1)S(1)}, bf16[80,5120]{1,0:T(8,128)(2,1)S(1)}, u32[]{:S(2)}, u32[]{:S(2)}) %collective-permute-start.21) | collective-permute-done | bytes 819232 | tf_op jit(solution)/shard_map/ppermute | solution.py:33
  104.6 1.6 collective-permute-done.16.refs_0_
  106.1 3.1 %collective-permute-done.17.refs_1_ = bf16[80,5120]{1,0:T(8,128)(2,1)S(1)} collective-permute-done((bf16[80,5120]{1,0:T(8,128)(2,1)S(1)}, bf16[80,5120]{1,0:T(8,128)(2,1)S(1)}, u32[]{:S(2)}, u32[]{:S(2)}) %collective-permute-start.17) | collective-permute-done | bytes 819232 | tf_op jit(solution)/shard_map/ppermute | solution.py:33
  109.3 0.3 collective-permute-start.22
  109.6 0.7 collective-permute-start.25
  110.3 0.7 collective-permute-start.23
  111.7 6.1 %hidden.2.refs_3_.refs_13_ = f32[480,256]{1,0:T(8,128)S(1)} custom-call(bf16[80,5120]{1,0:T(8,128)(2,1)S(1)} %stacked.5.refs_0_, bf16[80,5120]{1,0:T(8,128)(2,1)S(1)} %held.22.refs_1_, bf16[80,5120]{1,0:T(8,128)(2,1)S(1)} %held.25.refs_2_, bf16[80,5120]{1,0:T(8,128)(2,1)S(1)} %collective-permute-done.20.refs_3_, ...), custom_call_target="tpu_custom_call" | custom-call | flops 1 | bytes 1 | tf_op jit(solution)/shard_map/hidden/pallas_call | solution.py:142
  117.8 5.7 %collective-permute-done.24.refs_2_.refs_0_.refs_1_ = f32[88,5120]{1,0:T(8,128)S(1)} collective-permute-done((f32[88,5120]{1,0:T(8,128)S(1)}, f32[88,5120]{1,0:T(8,128)S(1)}, u32[]{:S(2)}, u32[]{:S(2)}) %collective-permute-start.24) | collective-permute-done | bytes 1802272 | tf_op jit(solution)/shard_map/ppermute | solution.py:33
  123.5 0.7 collective-permute-done.26.refs_5_.refs_1_
  124.2 2.9 %collective-permute-done.25.refs_4_.refs_0_ = bf16[80,5120]{1,0:T(8,128)(2,1)S(1)} collective-permute-done((bf16[80,5120]{1,0:T(8,128)(2,1)S(1)}, bf16[80,5120]{1,0:T(8,128)(2,1)S(1)}, u32[]{:S(2)}, u32[]{:S(2)}) %collective-permute-start.25) | collective-permute-done | bytes 819232 | tf_op jit(solution)/shard_map/ppermute | solution.py:33
  127.1 2.0 collective-permute-done.23.refs_1_
  129.1 3.0 %collective-permute-start.29 = (f32[88,5120]{1,0:T(8,128)S(1)}, f32[88,5120]{1,0:T(8,128)S(1)}, u32[]{:S(2)}, u32[]{:S(2)}) collective-permute-start(f32[88,5120]{1,0:T(8,128)S(1)} %held.27.refs_0_), channel_id=1, source_target_pairs={{64,0},{0,64},{65,1},{1,65},{66,2},{2,66},{67,3},{3,67},{68,4},{4,... | collective-permute-start | bytes 5406728 | tf_op jit(solution)/shard_map/ppermute | solution.py:33
  132.3 1.5 collective-permute-start.28
  133.9 2.6 %hidden.3.refs_0_ = f32[160,256]{1,0:T(8,128)S(1)} custom-call(bf16[80,5120]{1,0:T(8,128)(2,1)S(1)} %collective-permute-done.25.refs_4_.refs_0_, bf16[80,5120]{1,0:T(8,128)(2,1)S(1)} %collective-permute-done.26.refs_5_.refs_1_, bf16[336,5120]{1,0:T(8,128)(2,1)S(1)} %held.21.refs_6_.refs_2_.refs_9_.refs_11_, ...), custom_call_target="tpu_custom_call" | custom-call | flops 1 | bytes 1 | tf_op jit(solution)/shard_map/hidden/pallas_call | solution.py:142
  136.5 6.4 %collective-permute-done.28.refs_5_ = bf16[32,5120]{1,0:T(8,128)(2,1)S(1)} collective-permute-done((bf16[32,5120]{1,0:T(8,128)(2,1)S(1)}, bf16[32,5120]{1,0:T(8,128)(2,1)S(1)}, u32[]{:S(2)}, u32[]{:S(2)}) %collective-permute-start.28) | collective-permute-done | bytes 327712 | tf_op jit(solution)/shard_map/ppermute | solution.py:33
  143.0 2.2 collective-permute-done.27.refs_4_
  145.1 9.0 %gate_grads.1 = (f32[112,5120]{1,0:T(8,128)S(1)}, f32[112,5120]{1,0:T(8,128)S(1)}) custom-call(bf16[80,5120]{1,0:T(8,128)(2,1)S(1)} %stacked.3.refs_0_, bf16[80,5120]{1,0:T(8,128)(2,1)S(1)} %get-tuple-element.19.refs_1_, bf16[80,5120]{1,0:T(8,128)(2,1)S(1)} %get-tuple-element.21.refs_1_.refs_2_, bf16[80,5120]{1,0:T(8,128)(2,1)S(1)} %get-tuple-element.23.refs_1_.refs_3_, ...), custom_call_target="tpu_custom_call" | custom-call | flops 1 | bytes 1 | tf_op jit(solution)/shard_map/gate_grads/pallas_call | solution.py:210
  154.2 1.1 collective-permute-start.30
  155.2 1.7 concatenate.7.refs_0_
  157.0 2.3 collective-permute-done.30
  159.3 2.5 %multiply_reduce_fusion = (f32[]{:T(128)}, f32[112,5120]{1,0:T(8,128)}) fusion(f32[112,5120]{1,0:T(8,128)S(1)} %get-tuple-element.25.refs_1_, f32[112,5120]{1,0:T(8,128)S(1)} %collective-permute-done.30), kind=kLoop, calls=%fused_computation.1 | loop fusion | flops 1720319 | bytes 6881284 | tf_op jit(solution)/shard_map/reduce_sum | solution.py:369
  161.9 6.1 %collective-permute-start.36 = (f32[112,5120]{1,0:T(8,128)}, f32[112,5120]{1,0:T(8,128)}, u32[]{:S(2)}, u32[]{:S(2)}) collective-permute-start(f32[112,5120]{1,0:T(8,128)} %get-tuple-element.31.refs_5_), channel_id=1, source_target_pairs={{64,4},{4,64},{65,5},{5,65},{66,6},{6,66},{67,7},{7,67},{72,12},{1... | collective-permute-start | bytes 6881288 | tf_op jit(solution)/shard_map/ppermute | solution.py:43
  168.1 12.8 %psum.14 = f32[]{:T(128)} all-reduce(f32[]{:T(128)} %get-tuple-element.30), channel_id=1, replica_groups=mesh['x_lo'=2,'core'=2,'z'=8,'x_hi'=2,'y'=4] {'z'}, use_global_device_ids=true, to_apply=%region_1.2 | all-reduce | flops 1 | bytes 8 | tf_op jit(solution)/shard_map/psum | solution.py:371
  180.9 24.9 %collective-permute-done.33.refs_0_ = f32[32,5120]{1,0:T(8,128)S(1)} collective-permute-done((f32[32,5120]{1,0:T(8,128)S(1)}, f32[32,5120]{1,0:T(8,128)S(1)}, u32[]{:S(2)}, u32[]{:S(2)}) %collective-permute-start.33) | collective-permute-done | bytes 655392 | tf_op jit(solution)/shard_map/ppermute | solution.py:33
  205.8 0.6 held.30.refs_1_
  207.4 7.3 %psum.15 = f32[]{:T(128)} all-reduce(f32[]{:T(128)} %psum.14), channel_id=1, replica_groups=mesh['x_lo'=2,'core'=2,'z'=8,'x_hi'=2,'y'=4] {'y'}, use_global_device_ids=true, to_apply=%region_2.3 | all-reduce | flops 1 | bytes 8 | tf_op jit(solution)/shard_map/psum | solution.py:374
  214.7 6.8 %collective-permute-start.31 = (f32[]{:T(128)}, f32[]{:T(128)}, u32[]{:S(2)}, u32[]{:S(2)}) collective-permute-start(f32[]{:T(128)} %psum.15), channel_id=1, source_target_pairs={{0,0},{64,4},{4,64},{68,68},{1,1},{65,5},{5,65},{69,69},{2,2},{66,... | collective-permute-start | bytes 20 | tf_op jit(solution)/shard_map/ppermute | solution.py:43
  221.6 1.3 collective-permute-done.31
  223.0 2.8 %collective-permute-done.32 = f32[]{:T(128)} collective-permute-done((f32[]{:T(128)}, f32[]{:T(128)}, u32[]{:S(2)}, u32[]{:S(2)}) %collective-permute-start.32) | collective-permute-done | bytes 36 | tf_op jit(solution)/shard_map/ppermute | solution.py:48
  227.2 1.6 copy-done
  228.8 1.5 copy-done.2
  230.3 5.2 %updated.1 = (f32[112,5120]{1,0:T(8,128)}, f32[112,5120]{1,0:T(8,128)}, f32[1]{0:T(128)}) custom-call(f32[1]{0:T(128)} %bitcast.6.factor, f32[1]{0:T(128)} %mul.11.kept_weight, s32[2]{0:T(128)S(1)} %pad_add_fusion.which, f32[112,5120]{1,0:T(8,128)S(1)} %bitcast.23, f32[88,5120]{1,0:T(8,128)S(1)} %held.27.refs_0_, f32[32,5120]{1,0:T(8,128)S(1)} %held.30.refs_1_, ...), custom_call_target="tpu_custom_call" | custom-call | tf_op jit(solution)/shard_map/updated/pallas_call | solution.py:295
  (56 shorter events, 1.4 us)
Async XLA Ops:
  0.6 10.6 %copy-start.5 = (bf16[112,5120]{1,0:T(8,128)(2,1)S(1)}, bf16[112,5120]{1,0:T(8,128)(2,1)}, u32[]{:S(2)}) copy-start(bf16[112,5120]{1,0:T(8,128)(2,1)} %param.15) | copy-start | bytes 3440644
  0.6 10.6 %copy-start.4 = (bf16[112,5120]{1,0:T(8,128)(2,1)S(1)}, bf16[112,5120]{1,0:T(8,128)(2,1)}, u32[]{:S(2)}) copy-start(bf16[112,5120]{1,0:T(8,128)(2,1)} %param.16) | copy-start | bytes 3440644
  0.7 10.9 %collective-permute-start.1 = (bf16[20,5120]{1,0:T(8,128)(2,1)}, bf16[20,5120]{1,0:T(8,128)(2,1)S(1)}, u32[]{:S(2)}, u32[]{:S(2)}) collective-permute-start(bf16[20,5120]{1,0:T(8,128)(2,1)} %bitcast.28), channel_id=1, source_target_pairs={{0,0},{64,4},{4,64},{68,68},{1,1},{65,5},{5,65},{69,69},{2,2},{66,... | collective-permute-start | bytes 614408 | tf_op jit(solution)/shard_map/ppermute | solution.py:43
  6.8 9.2 %collective-permute-start = (bf16[20,5120]{1,0:T(8,128)(2,1)}, bf16[20,5120]{1,0:T(8,128)(2,1)S(1)}, u32[]{:S(2)}, u32[]{:S(2)}) collective-permute-start(bf16[20,5120]{1,0:T(8,128)(2,1)} %bitcast.29), channel_id=1, source_target_pairs={{0,0},{64,4},{4,64},{68,68},{1,1},{65,5},{5,65},{69,69},{2,2},{66,... | collective-permute-start | bytes 614408 | tf_op jit(solution)/shard_map/ppermute | solution.py:43
  16.1 59.7 %collective-permute-start.18 = (bf16[336,5120]{1,0:T(8,128)(2,1)S(1)}, bf16[336,5120]{1,0:T(8,128)(2,1)S(1)}, u32[]{:S(2)}, u32[]{:S(2)}) collective-permute-start(bf16[336,5120]{1,0:T(8,128)(2,1)S(1)} %held.20), channel_id=1, source_target_pairs={{0,0},{64,4},{4,64},{68,68},{1,1},{65,5},{5,65},{69,69},{2,2},{66,... | collective-permute-start | bytes 10321928 | tf_op jit(solution)/shard_map/ppermute | solution.py:43
  18.7 8.6 %collective-permute-start.2 = (bf16[20,5120]{1,0:T(8,128)(2,1)S(1)}, bf16[20,5120]{1,0:T(8,128)(2,1)S(1)}, u32[]{:S(2)}, u32[]{:S(2)}) collective-permute-start(bf16[20,5120]{1,0:T(8,128)(2,1)S(1)} %held.16.refs_0_), channel_id=1, source_target_pairs={{1,0},{2,1},{3,2},{0,3},{5,4},{6,5},{7,6},{4,7},{9,8},{10,9},{11,1... | collective-permute-start | bytes 614408 | tf_op jit(solution)/shard_map/ppermute | solution.py:33
  21.5 10.0 %collective-permute-start.5 = (bf16[20,5120]{1,0:T(8,128)(2,1)S(1)}, bf16[20,5120]{1,0:T(8,128)(2,1)S(1)}, u32[]{:S(2)}, u32[]{:S(2)}) collective-permute-start(bf16[20,5120]{1,0:T(8,128)(2,1)S(1)} %collective-permute-done.1.refs_1_.refs_0_), channel_id=1, source_target_pairs={{8,0},{16,8},{24,16},{32,24},{40,32},{48,40},{56,48},{0,56},{9,1},... | collective-permute-start | bytes 614408 | tf_op jit(solution)/shard_map/ppermute | solution.py:33
  27.1 7.8 %collective-permute-start.7 = (bf16[20,5120]{1,0:T(8,128)(2,1)S(1)}, bf16[20,5120]{1,0:T(8,128)(2,1)S(1)}, u32[]{:S(2)}, u32[]{:S(2)}) collective-permute-start(bf16[20,5120]{1,0:T(8,128)(2,1)S(1)} %collective-permute-done.1.refs_1_.refs_0_), channel_id=1, source_target_pairs={{56,0},{0,8},{8,16},{16,24},{24,32},{32,40},{40,48},{48,56},{57,1}... | collective-permute-start | bytes 614408 | tf_op jit(solution)/shard_map/ppermute | solution.py:33
  27.1 8.9 %collective-permute-start.3 = (bf16[20,5120]{1,0:T(8,128)(2,1)S(1)}, bf16[20,5120]{1,0:T(8,128)(2,1)S(1)}, u32[]{:S(2)}, u32[]{:S(2)}) collective-permute-start(bf16[20,5120]{1,0:T(8,128)(2,1)S(1)} %held.16.refs_0_), channel_id=1, source_target_pairs={{3,0},{0,1},{1,2},{2,3},{7,4},{4,5},{5,6},{6,7},{11,8},{8,9},{9,10... | collective-permute-start | bytes 614408 | tf_op jit(solution)/shard_map/ppermute | solution.py:33
  27.3 8.7 %collective-permute-start.4 = (bf16[20,5120]{1,0:T(8,128)(2,1)S(1)}, bf16[20,5120]{1,0:T(8,128)(2,1)S(1)}, u32[]{:S(2)}, u32[]{:S(2)}) collective-permute-start(bf16[20,5120]{1,0:T(8,128)(2,1)S(1)} %held.16.refs_0_), channel_id=1, source_target_pairs={{2,0},{3,1},{0,2},{1,3},{6,4},{7,5},{4,6},{5,7},{10,8},{11,9},{8,1... | collective-permute-start | bytes 614408 | tf_op jit(solution)/shard_map/ppermute | solution.py:33
  31.5 11.4 %collective-permute-start.6 = (bf16[20,5120]{1,0:T(8,128)(2,1)S(1)}, bf16[20,5120]{1,0:T(8,128)(2,1)S(1)}, u32[]{:S(2)}, u32[]{:S(2)}) collective-permute-start(bf16[20,5120]{1,0:T(8,128)(2,1)S(1)} %collective-permute-done.5.refs_1_), channel_id=1, source_target_pairs={{8,0},{16,8},{24,16},{32,24},{40,32},{48,40},{56,48},{0,56},{9,1},... | collective-permute-start | bytes 614408 | tf_op jit(solution)/shard_map/ppermute | solution.py:33
  34.9 9.0 %collective-permute-start.8 = (bf16[20,5120]{1,0:T(8,128)(2,1)S(1)}, bf16[20,5120]{1,0:T(8,128)(2,1)S(1)}, u32[]{:S(2)}, u32[]{:S(2)}) collective-permute-start(bf16[20,5120]{1,0:T(8,128)(2,1)S(1)} %collective-permute-done.7.refs_3_), channel_id=1, source_target_pairs={{56,0},{0,8},{8,16},{16,24},{24,32},{32,40},{40,48},{48,56},{57,1}... | collective-permute-start | bytes 614408 | tf_op jit(solution)/shard_map/ppermute | solution.py:33
  43.9 9.4 %collective-permute-start.10 = (bf16[20,5120]{1,0:T(8,128)(2,1)S(1)}, bf16[20,5120]{1,0:T(8,128)(2,1)S(1)}, u32[]{:S(2)}, u32[]{:S(2)}) collective-permute-start(bf16[20,5120]{1,0:T(8,128)(2,1)S(1)} %get-tuple-element.17.refs_2_), channel_id=1, source_target_pairs={{16,0},{24,8},{32,16},{40,24},{48,32},{56,40},{0,48},{8,56},{17,1}... | collective-permute-start | bytes 614408 | tf_op jit(solution)/shard_map/ppermute | solution.py:33
  43.9 15.9 %collective-permute-start.9 = (bf16[20,5120]{1,0:T(8,128)(2,1)S(1)}, bf16[20,5120]{1,0:T(8,128)(2,1)S(1)}, u32[]{:S(2)}, u32[]{:S(2)}) collective-permute-start(bf16[20,5120]{1,0:T(8,128)(2,1)S(1)} %get-tuple-element.17.refs_2_), channel_id=1, source_target_pairs={{8,0},{16,8},{24,16},{32,24},{40,32},{48,40},{56,48},{0,56},{9,1},... | collective-permute-start | bytes 614408 | tf_op jit(solution)/shard_map/ppermute | solution.py:33
  46.1 13.7 %collective-permute-start.11 = (bf16[20,5120]{1,0:T(8,128)(2,1)S(1)}, bf16[20,5120]{1,0:T(8,128)(2,1)S(1)}, u32[]{:S(2)}, u32[]{:S(2)}) collective-permute-start(bf16[20,5120]{1,0:T(8,128)(2,1)S(1)} %get-tuple-element.18.refs_2_), channel_id=1, source_target_pairs={{56,0},{0,8},{8,16},{16,24},{24,32},{32,40},{40,48},{48,56},{57,1}... | collective-permute-start | bytes 614408 | tf_op jit(solution)/shard_map/ppermute | solution.py:33
  60.2 13.0 %collective-permute-start.12 = (bf16[80,5120]{1,0:T(8,128)(2,1)S(1)}, bf16[80,5120]{1,0:T(8,128)(2,1)S(1)}, u32[]{:S(2)}, u32[]{:S(2)}) collective-permute-start(bf16[80,5120]{1,0:T(8,128)(2,1)S(1)} %stacked.3.refs_0_), channel_id=1, source_target_pairs={{8,0},{16,8},{24,16},{32,24},{40,32},{48,40},{56,48},{0,56},{9,1},... | collective-permute-start | bytes 2457608 | tf_op jit(solution)/shard_map/ppermute | solution.py:33
  60.2 12.9 %collective-permute-start.13 = (bf16[80,5120]{1,0:T(8,128)(2,1)S(1)}, bf16[80,5120]{1,0:T(8,128)(2,1)S(1)}, u32[]{:S(2)}, u32[]{:S(2)}) collective-permute-start(bf16[80,5120]{1,0:T(8,128)(2,1)S(1)} %stacked.3.refs_0_), channel_id=1, source_target_pairs={{56,0},{0,8},{8,16},{16,24},{24,32},{32,40},{40,48},{48,56},{57,1}... | collective-permute-start | bytes 2457608 | tf_op jit(solution)/shard_map/ppermute | solution.py:33
  62.0 11.5 %collective-permute-start.14 = (bf16[80,5120]{1,0:T(8,128)(2,1)S(1)}, bf16[80,5120]{1,0:T(8,128)(2,1)S(1)}, u32[]{:S(2)}, u32[]{:S(2)}) collective-permute-start(bf16[80,5120]{1,0:T(8,128)(2,1)S(1)} %stacked.5.refs_0_), channel_id=1, source_target_pairs={{1,0},{2,1},{3,2},{0,3},{5,4},{6,5},{7,6},{4,7},{9,8},{10,9},{11,1... | collective-permute-start | bytes 2457608 | tf_op jit(solution)/shard_map/ppermute | solution.py:33
  62.1 13.6 %collective-permute-start.15 = (bf16[80,5120]{1,0:T(8,128)(2,1)S(1)}, bf16[80,5120]{1,0:T(8,128)(2,1)S(1)}, u32[]{:S(2)}, u32[]{:S(2)}) collective-permute-start(bf16[80,5120]{1,0:T(8,128)(2,1)S(1)} %stacked.5.refs_0_), channel_id=1, source_target_pairs={{3,0},{0,1},{1,2},{2,3},{7,4},{4,5},{5,6},{6,7},{11,8},{8,9},{9,10... | collective-permute-start | bytes 2457608 | tf_op jit(solution)/shard_map/ppermute | solution.py:33
  75.8 1.6 copy-start.3
  75.8 6.3 %collective-permute-start.19 = (bf16[336,5120]{1,0:T(8,128)(2,1)S(1)}, bf16[336,5120]{1,0:T(8,128)(2,1)S(1)}, u32[]{:S(2)}, u32[]{:S(2)}) collective-permute-start(bf16[336,5120]{1,0:T(8,128)(2,1)S(1)} %held.21.refs_6_.refs_2_.refs_9_.refs_11_), channel_id=1, source_target_pairs={{64,0},{0,64},{65,1},{1,65},{66,2},{2,66},{67,3},{3,67},{68,4},{4,... | collective-permute-start | bytes 10321928 | tf_op jit(solution)/shard_map/ppermute | solution.py:33
  82.1 41.4 %collective-permute-start.24 = (f32[88,5120]{1,0:T(8,128)S(1)}, f32[88,5120]{1,0:T(8,128)S(1)}, u32[]{:S(2)}, u32[]{:S(2)}) collective-permute-start(f32[88,5120]{1,0:T(8,128)S(1)} %held.24), channel_id=1, source_target_pairs={{128,0},{0,128},{129,1},{1,129},{130,2},{2,130},{131,3},{3,131},{1... | collective-permute-start | bytes 5406728 | tf_op jit(solution)/shard_map/ppermute | solution.py:33
  84.0 20.6 %collective-permute-start.21 = (bf16[80,5120]{1,0:T(8,128)(2,1)S(1)}, bf16[80,5120]{1,0:T(8,128)(2,1)S(1)}, u32[]{:S(2)}, u32[]{:S(2)}) collective-permute-start(bf16[80,5120]{1,0:T(8,128)(2,1)S(1)} %held.22.refs_1_), channel_id=1, source_target_pairs={{3,0},{0,1},{1,2},{2,3},{7,4},{4,5},{5,6},{6,7},{11,8},{8,9},{9,10... | collective-permute-start | bytes 2457608 | tf_op jit(solution)/shard_map/ppermute | solution.py:33
  84.0 20.6 %collective-permute-start.20 = (bf16[80,5120]{1,0:T(8,128)(2,1)S(1)}, bf16[80,5120]{1,0:T(8,128)(2,1)S(1)}, u32[]{:S(2)}, u32[]{:S(2)}) collective-permute-start(bf16[80,5120]{1,0:T(8,128)(2,1)S(1)} %held.22.refs_1_), channel_id=1, source_target_pairs={{1,0},{2,1},{3,2},{0,3},{5,4},{6,5},{7,6},{4,7},{9,8},{10,9},{11,1... | collective-permute-start | bytes 2457608 | tf_op jit(solution)/shard_map/ppermute | solution.py:33
  86.6 19.5 %collective-permute-start.16 = (bf16[80,5120]{1,0:T(8,128)(2,1)S(1)}, bf16[80,5120]{1,0:T(8,128)(2,1)S(1)}, u32[]{:S(2)}, u32[]{:S(2)}) collective-permute-start(bf16[80,5120]{1,0:T(8,128)(2,1)S(1)} %get-tuple-element.19.refs_1_), channel_id=1, source_target_pairs={{8,0},{16,8},{24,16},{32,24},{40,32},{48,40},{56,48},{0,56},{9,1},... | collective-permute-start | bytes 2457608 | tf_op jit(solution)/shard_map/ppermute | solution.py:33
  89.6 19.7 %collective-permute-start.17 = (bf16[80,5120]{1,0:T(8,128)(2,1)S(1)}, bf16[80,5120]{1,0:T(8,128)(2,1)S(1)}, u32[]{:S(2)}, u32[]{:S(2)}) collective-permute-start(bf16[80,5120]{1,0:T(8,128)(2,1)S(1)} %get-tuple-element.20.refs_2_.refs_8_), channel_id=1, source_target_pairs={{56,0},{0,8},{8,16},{16,24},{24,32},{32,40},{40,48},{48,56},{57,1}... | collective-permute-start | bytes 2457608 | tf_op jit(solution)/shard_map/ppermute | solution.py:33
  104.6 19.7 %collective-permute-start.26 = (bf16[80,5120]{1,0:T(8,128)(2,1)S(1)}, bf16[80,5120]{1,0:T(8,128)(2,1)S(1)}, u32[]{:S(2)}, u32[]{:S(2)}) collective-permute-start(bf16[80,5120]{1,0:T(8,128)(2,1)S(1)} %collective-permute-done.21.refs_4_.refs_5_), channel_id=1, source_target_pairs={{3,0},{0,1},{1,2},{2,3},{7,4},{4,5},{5,6},{6,7},{11,8},{8,9},{9,10... | collective-permute-start | bytes 2457608 | tf_op jit(solution)/shard_map/ppermute | solution.py:33
  109.3 17.8 %collective-permute-start.22 = (bf16[80,5120]{1,0:T(8,128)(2,1)S(1)}, bf16[80,5120]{1,0:T(8,128)(2,1)S(1)}, u32[]{:S(2)}, u32[]{:S(2)}) collective-permute-start(bf16[80,5120]{1,0:T(8,128)(2,1)S(1)} %get-tuple-element.21.refs_1_.refs_2_), channel_id=1, source_target_pairs={{8,0},{16,8},{24,16},{32,24},{40,32},{48,40},{56,48},{0,56},{9,1},... | collective-permute-start | bytes 2457608 | tf_op jit(solution)/shard_map/ppermute | solution.py:33
  109.6 17.5 %collective-permute-start.25 = (bf16[80,5120]{1,0:T(8,128)(2,1)S(1)}, bf16[80,5120]{1,0:T(8,128)(2,1)S(1)}, u32[]{:S(2)}, u32[]{:S(2)}) collective-permute-start(bf16[80,5120]{1,0:T(8,128)(2,1)S(1)} %held.25.refs_2_), channel_id=1, source_target_pairs={{1,0},{2,1},{3,2},{0,3},{5,4},{6,5},{7,6},{4,7},{9,8},{10,9},{11,1... | collective-permute-start | bytes 2457608 | tf_op jit(solution)/shard_map/ppermute | solution.py:33
  110.3 18.8 %collective-permute-start.23 = (bf16[80,5120]{1,0:T(8,128)(2,1)S(1)}, bf16[80,5120]{1,0:T(8,128)(2,1)S(1)}, u32[]{:S(2)}, u32[]{:S(2)}) collective-permute-start(bf16[80,5120]{1,0:T(8,128)(2,1)S(1)} %get-tuple-element.22.refs_7_), channel_id=1, source_target_pairs={{56,0},{0,8},{8,16},{16,24},{24,32},{32,40},{40,48},{48,56},{57,1}... | collective-permute-start | bytes 2457608 | tf_op jit(solution)/shard_map/ppermute | solution.py:33
  129.1 7.3 %collective-permute-start.29 = (f32[88,5120]{1,0:T(8,128)S(1)}, f32[88,5120]{1,0:T(8,128)S(1)}, u32[]{:S(2)}, u32[]{:S(2)}) collective-permute-start(f32[88,5120]{1,0:T(8,128)S(1)} %held.27.refs_0_), channel_id=1, source_target_pairs={{64,0},{0,64},{65,1},{1,65},{66,2},{2,66},{67,3},{3,67},{68,4},{4,... | collective-permute-start | bytes 5406728 | tf_op jit(solution)/shard_map/ppermute | solution.py:33
  132.2 12.9 %collective-permute-start.27 = (bf16[48,5120]{1,0:T(8,128)(2,1)S(1)}, bf16[48,5120]{1,0:T(8,128)(2,1)S(1)}, u32[]{:S(2)}, u32[]{:S(2)}) collective-permute-start(bf16[48,5120]{1,0:T(8,128)(2,1)S(1)} %slice.17), channel_id=1, source_target_pairs={{8,0},{16,8},{24,16},{32,24},{40,32},{48,40},{56,48},{0,56},{9,1},... | collective-permute-start | bytes 1474568 | tf_op jit(solution)/shard_map/ppermute | solution.py:33
  132.3 10.6 %collective-permute-start.28 = (bf16[32,5120]{1,0:T(8,128)(2,1)S(1)}, bf16[32,5120]{1,0:T(8,128)(2,1)S(1)}, u32[]{:S(2)}, u32[]{:S(2)}) collective-permute-start(bf16[32,5120]{1,0:T(8,128)(2,1)S(1)} %slice.18), channel_id=1, source_target_pairs={{56,0},{0,8},{8,16},{16,24},{24,32},{32,40},{40,48},{48,56},{57,1}... | collective-permute-start | bytes 983048 | tf_op jit(solution)/shard_map/ppermute | solution.py:33
  136.5 17.7 %copy-start.1 = (f32[88,5120]{1,0:T(8,128)}, f32[88,5120]{1,0:T(8,128)S(1)}, u32[]{:S(2)}) copy-start(f32[88,5120]{1,0:T(8,128)S(1)} %collective-permute-done.29.refs_1_.refs_2_) | copy-start | bytes 5406724
  154.2 5.2 %collective-permute-start.30 = (f32[112,5120]{1,0:T(8,128)S(1)}, f32[112,5120]{1,0:T(8,128)S(1)}, u32[]{:S(2)}, u32[]{:S(2)}) collective-permute-start(f32[112,5120]{1,0:T(8,128)S(1)} %get-tuple-element.26), channel_id=1, source_target_pairs={{64,0},{0,64},{65,1},{1,65},{66,2},{2,66},{67,3},{3,67},{68,4},{4,... | collective-permute-start | bytes 6881288 | tf_op jit(solution)/shard_map/ppermute | solution.py:33
  157.0 70.2 %collective-permute-start.35 = (f32[120,5120]{1,0:T(8,128)}, f32[120,5120]{1,0:T(8,128)}, u32[]{:S(2)}, u32[]{:S(2)}) collective-permute-start(f32[120,5120]{1,0:T(8,128)} %held.31), channel_id=1, source_target_pairs={{64,0},{0,64},{65,1},{1,65},{66,2},{2,66},{67,3},{3,67},{68,4},{4,... | collective-permute-start | bytes 7372808 | tf_op jit(solution)/shard_map/ppermute | solution.py:33
  161.9 65.3 %collective-permute-start.36 = (f32[112,5120]{1,0:T(8,128)}, f32[112,5120]{1,0:T(8,128)}, u32[]{:S(2)}, u32[]{:S(2)}) collective-permute-start(f32[112,5120]{1,0:T(8,128)} %get-tuple-element.31.refs_5_), channel_id=1, source_target_pairs={{64,4},{4,64},{65,5},{5,65},{66,6},{6,66},{67,7},{7,67},{72,12},{1... | collective-permute-start | bytes 6881288 | tf_op jit(solution)/shard_map/ppermute | solution.py:43
  168.0 37.8 %collective-permute-start.33 = (f32[32,5120]{1,0:T(8,128)S(1)}, f32[32,5120]{1,0:T(8,128)S(1)}, u32[]{:S(2)}, u32[]{:S(2)}) collective-permute-start(f32[32,5120]{1,0:T(8,128)S(1)} %held.29), channel_id=1, source_target_pairs={{128,0},{0,128},{129,1},{1,129},{130,2},{2,130},{131,3},{3,131},{1... | collective-permute-start | bytes 1966088 | tf_op jit(solution)/shard_map/ppermute | solution.py:33
  206.5 20.7 %collective-permute-start.34 = (f32[32,5120]{1,0:T(8,128)S(1)}, f32[32,5120]{1,0:T(8,128)S(1)}, u32[]{:S(2)}, u32[]{:S(2)}) collective-permute-start(f32[32,5120]{1,0:T(8,128)S(1)} %held.30.refs_1_), channel_id=1, source_target_pairs={{64,0},{0,64},{65,1},{1,65},{66,2},{2,66},{67,3},{3,67},{68,4},{4,... | collective-permute-start | bytes 1966088 | tf_op jit(solution)/shard_map/ppermute | solution.py:33
  214.7 8.2 %collective-permute-start.31 = (f32[]{:T(128)}, f32[]{:T(128)}, u32[]{:S(2)}, u32[]{:S(2)}) collective-permute-start(f32[]{:T(128)} %psum.15), channel_id=1, source_target_pairs={{0,0},{64,4},{4,64},{68,68},{1,1},{65,5},{5,65},{69,69},{2,2},{66,... | collective-permute-start | bytes 20 | tf_op jit(solution)/shard_map/ppermute | solution.py:43
  221.5 4.2 %collective-permute-start.32 = (f32[]{:T(128)}, f32[]{:T(128)}, u32[]{:S(2)}, u32[]{:S(2)}) collective-permute-start(f32[]{:T(128)} %psum.15), channel_id=1, source_target_pairs={{64,0},{0,4},{68,64},{4,68},{65,1},{1,5},{69,65},{5,69},{66,2},{2,... | collective-permute-start | bytes 20 | tf_op jit(solution)/shard_map/ppermute | solution.py:48
  227.2 1.6 copy-start
  228.8 1.5 copy-start.2

commit v12 on v11

--- a/solution.py
+++ b/solution.py
@@ -22,7 +22,7 @@
 
 ROWS = 112
 HALF = 128
-CUT = 88
+CUT = 64
 NO_COST = pl.CostEstimate(flops=1, bytes_accessed=1, transcendentals=0)
 BLOCK = 1024
 
@@ -33,14 +33,21 @@
     return lax.ppermute(value, axis, pairs)
 
 
-def transposed(value, stay=True):
-    pairs = [
-        (2 * x_hi + core, 2 * core + x_hi)
-        for core in range(2)
-        for x_hi in range(2)
-        if stay or core != x_hi
-    ]
-    return lax.ppermute(value, ("core", "x_hi"), pairs)
+def transposed(value, axis=None, steps=0, stay=True):
+    names = [name for name in SIZES if name in ("core", "x_hi", axis)]
+    sizes = [SIZES[name] for name in names]
+    pairs = []
+    for place in np.ndindex(*sizes):
+        here = dict(zip(names, place))
+        there = dict(here, core=here["x_hi"], x_hi=here["core"])
+        if axis is not None:
+            there[axis] = (there[axis] + steps) % SIZES[axis]
+        source, target = (
+            int(np.ravel_multi_index([one[name] for name in names], sizes)) for one in (there, here)
+        )
+        if stay or here["core"] != here["x_hi"]:
+            pairs.append((source, target))
+    return lax.ppermute(value, tuple(names), pairs)
 
 
 def crossed(value):
@@ -321,13 +328,12 @@
 
     params = (numerator / push_weight[0]).astype(jnp.bfloat16)
     weights = jnp.concatenate([params, up_weight, down_weight], axis=0)
-    rows_in, rows_grad = transposed(tokens[0]), transposed(cotangent[0])
-    rows_in = held(rows_in, rows_grad, weights)
-    near = [rows_in] + [shifted(rows_in, "y", steps) for steps in (1, 3, 2)]
-    ring = {0: rows_grad, 1: shifted(rows_grad, "z", 1), 7: shifted(rows_grad, "z", 7)}
-    mine = transposed(held(weights, rows_grad))
+    ring = {steps: transposed(cotangent[0], "z", steps) for steps in (0, 1, 7)}
+    rows_in = held(tokens[0], *ring.values(), weights)
+    near = [transposed(rows_in, "y", steps) for steps in (0, 1, 3, 2)]
+    mine = transposed(held(weights, *near))
     ring[2], ring[6] = shifted(ring[1], "z", 1), shifted(ring[7], "z", 7)
-    ring[2], ring[6] = held((ring[2], ring[6]), *near[1:])
+    ring[2], ring[6] = held((ring[2], ring[6]), *near)
     ring[3], ring[5] = shifted(ring[2], "z", 1), shifted(ring[6], "z", 7)
     ring[4] = shifted(ring[2], "z", 2)
     near[3] = held(near[3], ring[3], ring[4], ring[5])
@@ -358,20 +364,18 @@
     cut = 48
     last = [shifted(blocks[3][:cut], "z", 1), shifted(blocks[5][cut:], "z", 7)]
     two_before.append(shifted(held(stale[CUT:], two_before[0]), "x_lo", 1))
-    two_before[0] = held(two_before[0], blocks[3])
-    one_before = [shifted(two_before[0], "core", 1)]
-    hidden_far = held(hidden_of(far, mine, theirs), one_before[0])
+    hidden_far = held(hidden_of(far, mine, theirs), two_before[1])
     parts = [blocks[steps] for steps in (0, 1, 2, 3)] + last + [blocks[steps] for steps in (5, 6, 7)]
 
     own_grad, other_grad = gate_grads(parts, mine, theirs, hidden_most, hidden_far)
+    two_before = held(tuple(two_before), own_grad)
+    one_before = [shifted(part, "core", 1) for part in two_before]
     stale_hop = shifted(held(stale, own_grad), "core", 1)
     gate_grad = own_grad + shifted(other_grad, "core", 1)
     norm_sq = jnp.sum(gate_grad * gate_grad)
     returned = transposed(gate_grad, stay=False)
-    norm_sq = lax.psum(norm_sq, "z")
-    two_before[1] = held(two_before[1], jnp.reshape(norm_sq, (1,)))
-    one_before.append(shifted(two_before[1], "core", 1))
-    norm_sq = lax.psum(norm_sq, "y")
+    for axes in ("z", "y"):
+        norm_sq = lax.psum(norm_sq, axes)
     norm_sq = transposed(norm_sq) + crossed(norm_sq)
 
     clip_factor = jnp.minimum(1.0, MAX_NORM / jnp.sqrt(norm_sq + eps))

time: 237 us -> 218 us (0.920)
  waiting for transfers between devices: 116 us -> 92.9 us
  starting transfers between devices: 59.1 us -> 64.4 us
    ppermute x31 -> x26, waiting for transfers between devices: 108 us -> 72.4 us  [shifted(): return lax.ppermute(value, axis, pairs)]
    ppermute x5 -> x10, starting transfers between devices: 23.6 us -> 40.5 us  [transposed(): return lax.ppermute(value, tuple(names), pairs)]
    ppermute x31 -> x26, starting transfers between devices: 35.4 us -> 23.9 us  [shifted(): return lax.ppermute(value, axis, pairs)]
    ppermute x5 -> x10, waiting for transfers between devices: 5.87 us -> 16.3 us  [transposed(): return lax.ppermute(value, tuple(names), pairs)]
  transfers between devices with their start and end apart: 37 -> 37, of which waited for: 26 -> 20; matrix products, arithmetic and copies ran while one was open for 3% -> 3% of each run, Pallas kernels for 4% -> 4%
where the time goes in v12:
time: 218 us; the launch traced here: 217 us
  waiting for transfers between devices  92.9 us (43%)
  starting transfers between devices  64.4 us (30%)
  Pallas kernels  24 us (11%)
  blocking collectives  20.9 us (10%)
  between operations  5.5 us (3%)
  other arithmetic  4.7 us (2%)
  local copies, waits for them, and re-layouts  4.67 us (2%)
    ppermute x26, waiting for transfers between devices, shifted(): return lax.ppermute(value, axis, pairs)  72.4 us
    ppermute x10, starting transfers between devices, transposed(): return lax.ppermute(value, tuple(names), pairs)  40.5 us
    ppermute x26, starting transfers between devices, shifted(): return lax.ppermute(value, axis, pairs)  23.9 us
    psum x2, blocking collectives, shards(): norm_sq = lax.psum(norm_sq, axes)  20.9 us
    ppermute x10, waiting for transfers between devices, transposed(): return lax.ppermute(value, tuple(names), pairs)  16.3 us
    pallas_call x1, Pallas kernels, gate_grads(): pl.pallas_call(grad_kernel, grid=(D // BLOCK,), in_specs=[pl.BlockSpec((p...  9.03 us
    pallas_call x2, Pallas kernels, hidden_of(): pl.pallas_call(hidden_kernel, grid=(D // BLOCK,), in_specs=[pl.BlockSpec(...  8.72 us
    pallas_call x1, Pallas kernels, updated(): pl.pallas_call(updated_kernel, grid=(blocks,), in_specs=[scalar, scalar,...  5.22 us
  transfers between devices with their start and end apart: 37, of which 20 were waited for; matrix products, arithmetic and copies ran while one was open for 3% of the time, Pallas kernels for 4%

profile of v12, /device:TPU:1, one launch (start us, length us, event | category | flops | bytes accessed | tf_op | source)
XLA Modules:
  0.0 217.0 jit_solution(10850365921523407198)
XLA Ops:
  0.7 1.1 copy.57
  1.7 6.0 %collective-permute-start = (bf16[20,5120]{1,0:T(8,128)(2,1)}, bf16[20,5120]{1,0:T(8,128)(2,1)S(1)}, u32[]{:S(2)}, u32[]{:S(2)}) collective-permute-start(bf16[20,5120]{1,0:T(8,128)(2,1)} %bitcast.28), channel_id=1, source_target_pairs={{0,0},{64,4},{8,8},{72,12},{16,16},{80,20},{24,24},{88,28},{32,32}... | collective-permute-start | bytes 614408 | tf_op jit(solution)/shard_map/ppermute | solution.py:50
  7.8 5.4 %collective-permute-start.1 = (bf16[20,5120]{1,0:T(8,128)(2,1)}, bf16[20,5120]{1,0:T(8,128)(2,1)S(1)}, u32[]{:S(2)}, u32[]{:S(2)}) collective-permute-start(bf16[20,5120]{1,0:T(8,128)(2,1)} %bitcast.29), channel_id=1, source_target_pairs={{8,0},{72,4},{16,8},{80,12},{24,16},{88,20},{32,24},{96,28},{40,32... | collective-permute-start | bytes 614408 | tf_op jit(solution)/shard_map/ppermute | solution.py:50
  13.8 1.8 divide_convert_fusion
  15.7 0.3 pad_maximum_fusion.refs_4_.refs_0_
  16.0 1.0 collective-permute-done.1.refs_2_.refs_1_
  17.0 5.6 %collective-permute-done.2.refs_3_ = bf16[20,5120]{1,0:T(8,128)(2,1)S(1)} collective-permute-done((bf16[20,5120]{1,0:T(8,128)(2,1)}, bf16[20,5120]{1,0:T(8,128)(2,1)S(1)}, u32[]{:S(2)}, u32[]{:S(2)}) %collective-permute-start.2) | collective-permute-done | bytes 204832 | tf_op jit(solution)/shard_map/ppermute | solution.py:50
  22.6 5.1 %collective-permute-start.3 = (bf16[20,5120]{1,0:T(8,128)(2,1)S(1)}, bf16[20,5120]{1,0:T(8,128)(2,1)S(1)}, u32[]{:S(2)}, u32[]{:S(2)}) collective-permute-start(bf16[20,5120]{1,0:T(8,128)(2,1)S(1)} %held.15), channel_id=1, source_target_pairs={{0,0},{1,1},{2,2},{3,3},{64,4},{65,5},{66,6},{67,7},{4,64},{5,65},... | collective-permute-start | bytes 614408 | tf_op jit(solution)/shard_map/ppermute | solution.py:50
  27.8 2.5 %collective-permute-start.4 = (bf16[20,5120]{1,0:T(8,128)(2,1)S(1)}, bf16[20,5120]{1,0:T(8,128)(2,1)S(1)}, u32[]{:S(2)}, u32[]{:S(2)}) collective-permute-start(bf16[20,5120]{1,0:T(8,128)(2,1)S(1)} %held.15), channel_id=1, source_target_pairs={{1,0},{2,1},{3,2},{0,3},{65,4},{66,5},{67,6},{64,7},{5,64},{6,65},... | collective-permute-start | bytes 614408 | tf_op jit(solution)/shard_map/ppermute | solution.py:50
  30.3 1.7 collective-permute-start.5
  32.0 2.6 %collective-permute-start.6 = (bf16[20,5120]{1,0:T(8,128)(2,1)S(1)}, bf16[20,5120]{1,0:T(8,128)(2,1)S(1)}, u32[]{:S(2)}, u32[]{:S(2)}) collective-permute-start(bf16[20,5120]{1,0:T(8,128)(2,1)S(1)} %held.15), channel_id=1, source_target_pairs={{2,0},{3,1},{0,2},{1,3},{66,4},{67,5},{64,6},{65,7},{6,64},{7,65},... | collective-permute-start | bytes 614408 | tf_op jit(solution)/shard_map/ppermute | solution.py:50
  34.6 1.2 collective-permute-done.4.refs_3_.refs_1_.refs_2_
  35.9 4.5 %collective-permute-done.5.refs_4_.refs_2_.refs_3_ = bf16[20,5120]{1,0:T(8,128)(2,1)S(1)} collective-permute-done((bf16[20,5120]{1,0:T(8,128)(2,1)S(1)}, bf16[20,5120]{1,0:T(8,128)(2,1)S(1)}, u32[]{:S(2)}, u32[]{:S(2)}) %collective-permute-start.5) | collective-permute-done | bytes 204832 | tf_op jit(solution)/shard_map/ppermute | solution.py:50
  40.3 2.5 %collective-permute-done.6.refs_5_.refs_0_.refs_4_ = bf16[20,5120]{1,0:T(8,128)(2,1)S(1)} collective-permute-done((bf16[20,5120]{1,0:T(8,128)(2,1)S(1)}, bf16[20,5120]{1,0:T(8,128)(2,1)S(1)}, u32[]{:S(2)}, u32[]{:S(2)}) %collective-permute-start.6) | collective-permute-done | bytes 204832 | tf_op jit(solution)/shard_map/ppermute | solution.py:50
  42.9 4.4 %collective-permute-start.18 = (bf16[336,5120]{1,0:T(8,128)(2,1)S(1)}, bf16[336,5120]{1,0:T(8,128)(2,1)S(1)}, u32[]{:S(2)}, u32[]{:S(2)}) collective-permute-start(bf16[336,5120]{1,0:T(8,128)(2,1)S(1)} %held.19), channel_id=1, source_target_pairs={{0,0},{64,4},{4,64},{68,68},{1,1},{65,5},{5,65},{69,69},{2,2},{66,... | collective-permute-start | bytes 10321928 | tf_op jit(solution)/shard_map/ppermute | solution.py:50
  47.3 0.2 collective-permute-start.7
  47.5 1.4 collective-permute-start.8
  48.9 5.7 %collective-permute-done.7.refs_0_ = bf16[20,5120]{1,0:T(8,128)(2,1)S(1)} collective-permute-done((bf16[20,5120]{1,0:T(8,128)(2,1)S(1)}, bf16[20,5120]{1,0:T(8,128)(2,1)S(1)}, u32[]{:S(2)}, u32[]{:S(2)}) %collective-permute-start.7) | collective-permute-done | bytes 204832 | tf_op jit(solution)/shard_map/ppermute | solution.py:33
  54.5 0.6 collective-permute-start.9
  55.1 1.3 collective-permute-start.11
  56.4 4.8 %collective-permute-done.9.refs_1_.refs_3_ = bf16[20,5120]{1,0:T(8,128)(2,1)S(1)} collective-permute-done((bf16[20,5120]{1,0:T(8,128)(2,1)S(1)}, bf16[20,5120]{1,0:T(8,128)(2,1)S(1)}, u32[]{:S(2)}, u32[]{:S(2)}) %collective-permute-start.9) | collective-permute-done | bytes 204832 | tf_op jit(solution)/shard_map/ppermute | solution.py:33
  61.2 8.0 %collective-permute-done.10.refs_2_.refs_0_ = bf16[20,5120]{1,0:T(8,128)(2,1)S(1)} collective-permute-done((bf16[20,5120]{1,0:T(8,128)(2,1)S(1)}, bf16[20,5120]{1,0:T(8,128)(2,1)S(1)}, u32[]{:S(2)}, u32[]{:S(2)}) %collective-permute-start.10) | collective-permute-done | bytes 204832 | tf_op jit(solution)/shard_map/ppermute | solution.py:33
  69.2 0.3 stacked.3.refs_0_
  69.6 1.9 collective-permute-start.12
  71.5 0.3 stacked.5.refs_0_
  71.8 2.6 %collective-permute-start.14 = (bf16[80,5120]{1,0:T(8,128)(2,1)S(1)}, bf16[80,5120]{1,0:T(8,128)(2,1)S(1)}, u32[]{:S(2)}, u32[]{:S(2)}) collective-permute-start(bf16[80,5120]{1,0:T(8,128)(2,1)S(1)} %stacked.5.refs_0_), channel_id=1, source_target_pairs={{1,0},{2,1},{3,2},{0,3},{5,4},{6,5},{7,6},{4,7},{9,8},{10,9},{11,1... | collective-permute-start | bytes 2457608 | tf_op jit(solution)/shard_map/ppermute | solution.py:33
  74.4 0.3 stacked.4.refs_2_.refs_0_
  74.7 7.7 %collective-permute-done.12.refs_0_ = bf16[80,5120]{1,0:T(8,128)(2,1)S(1)} collective-permute-done((bf16[80,5120]{1,0:T(8,128)(2,1)S(1)}, bf16[80,5120]{1,0:T(8,128)(2,1)S(1)}, u32[]{:S(2)}, u32[]{:S(2)}) %collective-permute-start.12) | collective-permute-done | bytes 819232 | tf_op jit(solution)/shard_map/ppermute | solution.py:33
  82.4 1.4 collective-permute-done.13.refs_1_
  83.9 2.9 %collective-permute-done.15.refs_4_ = bf16[80,5120]{1,0:T(8,128)(2,1)S(1)} collective-permute-done((bf16[80,5120]{1,0:T(8,128)(2,1)S(1)}, bf16[80,5120]{1,0:T(8,128)(2,1)S(1)}, u32[]{:S(2)}, u32[]{:S(2)}) %collective-permute-start.15) | collective-permute-done | bytes 819232 | tf_op jit(solution)/shard_map/ppermute | solution.py:33
  86.8 0.3 collective-permute-start.19
  87.1 2.7 %collective-permute-start.16 = (bf16[80,5120]{1,0:T(8,128)(2,1)S(1)}, bf16[80,5120]{1,0:T(8,128)(2,1)S(1)}, u32[]{:S(2)}, u32[]{:S(2)}) collective-permute-start(bf16[80,5120]{1,0:T(8,128)(2,1)S(1)} %get-tuple-element.21.refs_1_), channel_id=1, source_target_pairs={{8,0},{16,8},{24,16},{32,24},{40,32},{48,40},{56,48},{0,56},{9,1},... | collective-permute-start | bytes 2457608 | tf_op jit(solution)/shard_map/ppermute | solution.py:33
  89.8 0.3 collective-permute-start.20
  90.2 1.1 collective-permute-start.21
  91.3 0.1 slice_bitcast_fusion.refs_0_
  91.4 1.8 collective-permute-done.19.refs_2_.refs_1_.refs_7_.refs_3_.refs_10_.refs_12_
  93.2 0.7 collective-permute-start.24
  94.5 15.3 %collective-permute-done.21.refs_4_.refs_5_ = bf16[80,5120]{1,0:T(8,128)(2,1)S(1)} collective-permute-done((bf16[80,5120]{1,0:T(8,128)(2,1)S(1)}, bf16[80,5120]{1,0:T(8,128)(2,1)S(1)}, u32[]{:S(2)}, u32[]{:S(2)}) %collective-permute-start.21) | collective-permute-done | bytes 819232 | tf_op jit(solution)/shard_map/ppermute | solution.py:33
  109.8 0.3 collective-permute-start.26
  110.1 2.4 %collective-permute-start.22 = (bf16[80,5120]{1,0:T(8,128)(2,1)S(1)}, bf16[80,5120]{1,0:T(8,128)(2,1)S(1)}, u32[]{:S(2)}, u32[]{:S(2)}) collective-permute-start(bf16[80,5120]{1,0:T(8,128)(2,1)S(1)} %get-tuple-element.23.refs_1_.refs_2_), channel_id=1, source_target_pairs={{8,0},{16,8},{24,16},{32,24},{40,32},{48,40},{56,48},{0,56},{9,1},... | collective-permute-start | bytes 2457608 | tf_op jit(solution)/shard_map/ppermute | solution.py:33
  112.6 2.4 %collective-permute-start.25 = (bf16[80,5120]{1,0:T(8,128)(2,1)S(1)}, bf16[80,5120]{1,0:T(8,128)(2,1)S(1)}, u32[]{:S(2)}, u32[]{:S(2)}) collective-permute-start(bf16[80,5120]{1,0:T(8,128)(2,1)S(1)} %held.24.refs_2_), channel_id=1, source_target_pairs={{1,0},{2,1},{3,2},{0,3},{5,4},{6,5},{7,6},{4,7},{9,8},{10,9},{11,1... | collective-permute-start | bytes 2457608 | tf_op jit(solution)/shard_map/ppermute | solution.py:33
  115.1 8.3 %collective-permute-done.24.refs_2_.refs_1_.refs_0_ = f32[64,5120]{1,0:T(8,128)S(1)} collective-permute-done((f32[64,5120]{1,0:T(8,128)S(1)}, f32[64,5120]{1,0:T(8,128)S(1)}, u32[]{:S(2)}, u32[]{:S(2)}) %collective-permute-start.24) | collective-permute-done | bytes 1310752 | tf_op jit(solution)/shard_map/ppermute | solution.py:33
  123.4 0.7 collective-permute-start.29
  124.1 6.1 %hidden.2.refs_3_.refs_13_ = f32[480,256]{1,0:T(8,128)S(1)} custom-call(bf16[80,5120]{1,0:T(8,128)(2,1)S(1)} %stacked.5.refs_0_, bf16[80,5120]{1,0:T(8,128)(2,1)S(1)} %held.21.refs_1_, bf16[80,5120]{1,0:T(8,128)(2,1)S(1)} %held.24.refs_2_, bf16[80,5120]{1,0:T(8,128)(2,1)S(1)} %collective-permute-done.20.refs_3_, ...), custom_call_target="tpu_custom_call" | custom-call | flops 1 | bytes 1 | tf_op jit(solution)/shard_map/hidden/pallas_call | solution.py:149
  130.2 0.6 collective-permute-done.23.refs_1_
  130.8 2.2 %collective-permute-start.27 = (bf16[48,5120]{1,0:T(8,128)(2,1)S(1)}, bf16[48,5120]{1,0:T(8,128)(2,1)S(1)}, u32[]{:S(2)}, u32[]{:S(2)}) collective-permute-start(bf16[48,5120]{1,0:T(8,128)(2,1)S(1)} %slice.17), channel_id=1, source_target_pairs={{8,0},{16,8},{24,16},{32,24},{40,32},{48,40},{56,48},{0,56},{9,1},... | collective-permute-start | bytes 1474568 | tf_op jit(solution)/shard_map/ppermute | solution.py:33
  133.0 0.1 collective-permute-start.28
  133.1 2.6 %hidden.3.refs_0_ = f32[160,256]{1,0:T(8,128)S(1)} custom-call(bf16[80,5120]{1,0:T(8,128)(2,1)S(1)} %collective-permute-done.25.refs_4_.refs_0_, bf16[80,5120]{1,0:T(8,128)(2,1)S(1)} %collective-permute-done.26.refs_5_.refs_1_, bf16[336,5120]{1,0:T(8,128)(2,1)S(1)} %held.20.refs_6_.refs_2_.refs_9_.refs_11_, ...), custom_call_target="tpu_custom_call" | custom-call | flops 1 | bytes 1 | tf_op jit(solution)/shard_map/hidden/pallas_call | solution.py:149
  135.8 13.5 %collective-permute-done.29.refs_1_ = f32[56,5120]{1,0:T(8,128)S(1)} collective-permute-done((f32[56,5120]{1,0:T(8,128)S(1)}, f32[56,5120]{1,0:T(8,128)S(1)}, u32[]{:S(2)}, u32[]{:S(2)}) %collective-permute-start.29) | collective-permute-done | bytes 1146912 | tf_op jit(solution)/shard_map/ppermute | solution.py:33
  149.2 9.0 %gate_grads.1 = (f32[112,5120]{1,0:T(8,128)S(1)}, f32[112,5120]{1,0:T(8,128)S(1)}) custom-call(bf16[80,5120]{1,0:T(8,128)(2,1)S(1)} %stacked.3.refs_0_, bf16[80,5120]{1,0:T(8,128)(2,1)S(1)} %get-tuple-element.21.refs_1_, bf16[80,5120]{1,0:T(8,128)(2,1)S(1)} %get-tuple-element.23.refs_1_.refs_2_, bf16[80,5120]{1,0:T(8,128)(2,1)S(1)} %get-tuple-element.25.refs_3_, ...), custom_call_target="tpu_custom_call" | custom-call | flops 1 | bytes 1 | tf_op jit(solution)/shard_map/gate_grads/pallas_call | solution.py:217
  158.2 2.2 collective-permute-start.30
  160.4 1.7 concatenate.7.refs_0_
  162.1 2.3 %collective-permute-done.30 = f32[112,5120]{1,0:T(8,128)S(1)} collective-permute-done((f32[112,5120]{1,0:T(8,128)S(1)}, f32[112,5120]{1,0:T(8,128)S(1)}, u32[]{:S(2)}, u32[]{:S(2)}) %collective-permute-start.30) | collective-permute-done | bytes 2293792 | tf_op jit(solution)/shard_map/ppermute | solution.py:33
  164.5 2.5 %multiply_reduce_fusion = (f32[]{:T(128)}, f32[112,5120]{1,0:T(8,128)}) fusion(f32[112,5120]{1,0:T(8,128)S(1)} %get-tuple-element.27.refs_2_.refs_1_, f32[112,5120]{1,0:T(8,128)S(1)} %collective-permute-done.30), kind=kLoop, calls=%fused_computation.1 | loop fusion | flops 1720319 | bytes 6881284 | tf_op jit(solution)/shard_map/reduce_sum | solution.py:375
  167.0 5.3 %collective-permute-start.36 = (f32[112,5120]{1,0:T(8,128)}, f32[112,5120]{1,0:T(8,128)}, u32[]{:S(2)}, u32[]{:S(2)}) collective-permute-start(f32[112,5120]{1,0:T(8,128)} %get-tuple-element.35.refs_5_), channel_id=1, source_target_pairs={{64,4},{4,64},{65,5},{5,65},{66,6},{6,66},{67,7},{7,67},{72,12},{1... | collective-permute-start | bytes 6881288 | tf_op jit(solution)/shard_map/ppermute | solution.py:50
  172.3 0.1 collective-permute-start.33
  172.4 0.5 collective-permute-start.34
  173.8 14.3 %psum.14 = f32[]{:T(128)} all-reduce(f32[]{:T(128)} %get-tuple-element.34), channel_id=1, replica_groups=mesh['x_lo'=2,'core'=2,'z'=8,'x_hi'=2,'y'=4] {'z'}, use_global_device_ids=true, to_apply=%region_1.2 | all-reduce | flops 1 | bytes 8 | tf_op jit(solution)/shard_map/psum | solution.py:378
  188.0 6.6 %psum.15 = f32[]{:T(128)} all-reduce(f32[]{:T(128)} %psum.14), channel_id=1, replica_groups=mesh['x_lo'=2,'core'=2,'z'=8,'x_hi'=2,'y'=4] {'y'}, use_global_device_ids=true, to_apply=%region_2.3 | all-reduce | flops 1 | bytes 8 | tf_op jit(solution)/shard_map/psum | solution.py:378
  194.6 7.4 %collective-permute-start.31 = (f32[]{:T(128)}, f32[]{:T(128)}, u32[]{:S(2)}, u32[]{:S(2)}) collective-permute-start(f32[]{:T(128)} %psum.15), channel_id=1, source_target_pairs={{0,0},{64,4},{4,64},{68,68},{1,1},{65,5},{5,65},{69,69},{2,2},{66,... | collective-permute-start | bytes 20 | tf_op jit(solution)/shard_map/ppermute | solution.py:50
  202.0 1.4 collective-permute-done.31
  203.5 4.1 %collective-permute-done.32 = f32[]{:T(128)} collective-permute-done((f32[]{:T(128)}, f32[]{:T(128)}, u32[]{:S(2)}, u32[]{:S(2)}) %collective-permute-start.32) | collective-permute-done | bytes 36 | tf_op jit(solution)/shard_map/ppermute | solution.py:55
  209.0 1.6 copy-done
  210.7 5.2 %updated.1 = (f32[112,5120]{1,0:T(8,128)}, f32[112,5120]{1,0:T(8,128)}, f32[1]{0:T(128)}) custom-call(f32[1]{0:T(128)} %bitcast.8.factor, f32[1]{0:T(128)} %mul.11.kept_weight, s32[2]{0:T(128)S(1)} %pad_add_fusion.which, f32[112,5120]{1,0:T(8,128)S(1)} %bitcast.22, f32[64,5120]{1,0:T(8,128)S(1)} %get-tuple-element.29.refs_0_, ...), custom_call_target="tpu_custom_call" | custom-call | tf_op jit(solution)/shard_map/updated/pallas_call | solution.py:302
  (52 shorter events, 0.4 us)
Async XLA Ops:
  0.6 15.0 %copy-start.3 = (bf16[112,5120]{1,0:T(8,128)(2,1)S(1)}, bf16[112,5120]{1,0:T(8,128)(2,1)}, u32[]{:S(2)}) copy-start(bf16[112,5120]{1,0:T(8,128)(2,1)} %param.15) | copy-start | bytes 3440644
  0.6 15.0 %copy-start.2 = (bf16[112,5120]{1,0:T(8,128)(2,1)S(1)}, bf16[112,5120]{1,0:T(8,128)(2,1)}, u32[]{:S(2)}) copy-start(bf16[112,5120]{1,0:T(8,128)(2,1)} %param.16) | copy-start | bytes 3440644
  1.7 14.2 %collective-permute-start = (bf16[20,5120]{1,0:T(8,128)(2,1)}, bf16[20,5120]{1,0:T(8,128)(2,1)S(1)}, u32[]{:S(2)}, u32[]{:S(2)}) collective-permute-start(bf16[20,5120]{1,0:T(8,128)(2,1)} %bitcast.28), channel_id=1, source_target_pairs={{0,0},{64,4},{8,8},{72,12},{16,16},{80,20},{24,24},{88,28},{32,32}... | collective-permute-start | bytes 614408 | tf_op jit(solution)/shard_map/ppermute | solution.py:50
  7.8 9.2 %collective-permute-start.1 = (bf16[20,5120]{1,0:T(8,128)(2,1)}, bf16[20,5120]{1,0:T(8,128)(2,1)S(1)}, u32[]{:S(2)}, u32[]{:S(2)}) collective-permute-start(bf16[20,5120]{1,0:T(8,128)(2,1)} %bitcast.29), channel_id=1, source_target_pairs={{8,0},{72,4},{16,8},{80,12},{24,16},{88,20},{32,24},{96,28},{40,32... | collective-permute-start | bytes 614408 | tf_op jit(solution)/shard_map/ppermute | solution.py:50
  13.2 9.4 %collective-permute-start.2 = (bf16[20,5120]{1,0:T(8,128)(2,1)}, bf16[20,5120]{1,0:T(8,128)(2,1)S(1)}, u32[]{:S(2)}, u32[]{:S(2)}) collective-permute-start(bf16[20,5120]{1,0:T(8,128)(2,1)} %bitcast.30), channel_id=1, source_target_pairs={{56,0},{120,4},{0,8},{64,12},{8,16},{72,20},{16,24},{80,28},{24,32... | collective-permute-start | bytes 614408 | tf_op jit(solution)/shard_map/ppermute | solution.py:50
  22.6 12.0 %collective-permute-start.3 = (bf16[20,5120]{1,0:T(8,128)(2,1)S(1)}, bf16[20,5120]{1,0:T(8,128)(2,1)S(1)}, u32[]{:S(2)}, u32[]{:S(2)}) collective-permute-start(bf16[20,5120]{1,0:T(8,128)(2,1)S(1)} %held.15), channel_id=1, source_target_pairs={{0,0},{1,1},{2,2},{3,3},{64,4},{65,5},{66,6},{67,7},{4,64},{5,65},... | collective-permute-start | bytes 614408 | tf_op jit(solution)/shard_map/ppermute | solution.py:50
  27.8 8.1 %collective-permute-start.4 = (bf16[20,5120]{1,0:T(8,128)(2,1)S(1)}, bf16[20,5120]{1,0:T(8,128)(2,1)S(1)}, u32[]{:S(2)}, u32[]{:S(2)}) collective-permute-start(bf16[20,5120]{1,0:T(8,128)(2,1)S(1)} %held.15), channel_id=1, source_target_pairs={{1,0},{2,1},{3,2},{0,3},{65,4},{66,5},{67,6},{64,7},{5,64},{6,65},... | collective-permute-start | bytes 614408 | tf_op jit(solution)/shard_map/ppermute | solution.py:50
  30.3 10.0 %collective-permute-start.5 = (bf16[20,5120]{1,0:T(8,128)(2,1)S(1)}, bf16[20,5120]{1,0:T(8,128)(2,1)S(1)}, u32[]{:S(2)}, u32[]{:S(2)}) collective-permute-start(bf16[20,5120]{1,0:T(8,128)(2,1)S(1)} %held.15), channel_id=1, source_target_pairs={{3,0},{0,1},{1,2},{2,3},{67,4},{64,5},{65,6},{66,7},{7,64},{4,65},... | collective-permute-start | bytes 614408 | tf_op jit(solution)/shard_map/ppermute | solution.py:50
  32.0 10.9 %collective-permute-start.6 = (bf16[20,5120]{1,0:T(8,128)(2,1)S(1)}, bf16[20,5120]{1,0:T(8,128)(2,1)S(1)}, u32[]{:S(2)}, u32[]{:S(2)}) collective-permute-start(bf16[20,5120]{1,0:T(8,128)(2,1)S(1)} %held.15), channel_id=1, source_target_pairs={{2,0},{3,1},{0,2},{1,3},{66,4},{67,5},{64,6},{65,7},{6,64},{7,65},... | collective-permute-start | bytes 614408 | tf_op jit(solution)/shard_map/ppermute | solution.py:50
  42.9 43.9 %collective-permute-start.18 = (bf16[336,5120]{1,0:T(8,128)(2,1)S(1)}, bf16[336,5120]{1,0:T(8,128)(2,1)S(1)}, u32[]{:S(2)}, u32[]{:S(2)}) collective-permute-start(bf16[336,5120]{1,0:T(8,128)(2,1)S(1)} %held.19), channel_id=1, source_target_pairs={{0,0},{64,4},{4,64},{68,68},{1,1},{65,5},{5,65},{69,69},{2,2},{66,... | collective-permute-start | bytes 10321928 | tf_op jit(solution)/shard_map/ppermute | solution.py:50
  47.3 7.2 %collective-permute-start.7 = (bf16[20,5120]{1,0:T(8,128)(2,1)S(1)}, bf16[20,5120]{1,0:T(8,128)(2,1)S(1)}, u32[]{:S(2)}, u32[]{:S(2)}) collective-permute-start(bf16[20,5120]{1,0:T(8,128)(2,1)S(1)} %collective-permute-done.1.refs_2_.refs_1_), channel_id=1, source_target_pairs={{8,0},{16,8},{24,16},{32,24},{40,32},{48,40},{56,48},{0,56},{9,1},... | collective-permute-start | bytes 614408 | tf_op jit(solution)/shard_map/ppermute | solution.py:33
  47.5 7.1 %collective-permute-start.8 = (bf16[20,5120]{1,0:T(8,128)(2,1)S(1)}, bf16[20,5120]{1,0:T(8,128)(2,1)S(1)}, u32[]{:S(2)}, u32[]{:S(2)}) collective-permute-start(bf16[20,5120]{1,0:T(8,128)(2,1)S(1)} %collective-permute-done.2.refs_3_), channel_id=1, source_target_pairs={{56,0},{0,8},{8,16},{16,24},{24,32},{32,40},{40,48},{48,56},{57,1}... | collective-permute-start | bytes 614408 | tf_op jit(solution)/shard_map/ppermute | solution.py:33
  54.5 6.6 %collective-permute-start.9 = (bf16[20,5120]{1,0:T(8,128)(2,1)S(1)}, bf16[20,5120]{1,0:T(8,128)(2,1)S(1)}, u32[]{:S(2)}, u32[]{:S(2)}) collective-permute-start(bf16[20,5120]{1,0:T(8,128)(2,1)S(1)} %get-tuple-element.19.refs_2_), channel_id=1, source_target_pairs={{8,0},{16,8},{24,16},{32,24},{40,32},{48,40},{56,48},{0,56},{9,1},... | collective-permute-start | bytes 614408 | tf_op jit(solution)/shard_map/ppermute | solution.py:33
  55.1 14.1 %collective-permute-start.10 = (bf16[20,5120]{1,0:T(8,128)(2,1)S(1)}, bf16[20,5120]{1,0:T(8,128)(2,1)S(1)}, u32[]{:S(2)}, u32[]{:S(2)}) collective-permute-start(bf16[20,5120]{1,0:T(8,128)(2,1)S(1)} %get-tuple-element.19.refs_2_), channel_id=1, source_target_pairs={{16,0},{24,8},{32,16},{40,24},{48,32},{56,40},{0,48},{8,56},{17,1}... | collective-permute-start | bytes 614408 | tf_op jit(solution)/shard_map/ppermute | solution.py:33
  55.1 14.1 %collective-permute-start.11 = (bf16[20,5120]{1,0:T(8,128)(2,1)S(1)}, bf16[20,5120]{1,0:T(8,128)(2,1)S(1)}, u32[]{:S(2)}, u32[]{:S(2)}) collective-permute-start(bf16[20,5120]{1,0:T(8,128)(2,1)S(1)} %get-tuple-element.20.refs_2_), channel_id=1, source_target_pairs={{56,0},{0,8},{8,16},{16,24},{24,32},{32,40},{40,48},{48,56},{57,1}... | collective-permute-start | bytes 614408 | tf_op jit(solution)/shard_map/ppermute | solution.py:33
  69.6 12.8 %collective-permute-start.12 = (bf16[80,5120]{1,0:T(8,128)(2,1)S(1)}, bf16[80,5120]{1,0:T(8,128)(2,1)S(1)}, u32[]{:S(2)}, u32[]{:S(2)}) collective-permute-start(bf16[80,5120]{1,0:T(8,128)(2,1)S(1)} %stacked.3.refs_0_), channel_id=1, source_target_pairs={{8,0},{16,8},{24,16},{32,24},{40,32},{48,40},{56,48},{0,56},{9,1},... | collective-permute-start | bytes 2457608 | tf_op jit(solution)/shard_map/ppermute | solution.py:33
  71.5 12.4 %collective-permute-start.13 = (bf16[80,5120]{1,0:T(8,128)(2,1)S(1)}, bf16[80,5120]{1,0:T(8,128)(2,1)S(1)}, u32[]{:S(2)}, u32[]{:S(2)}) collective-permute-start(bf16[80,5120]{1,0:T(8,128)(2,1)S(1)} %stacked.3.refs_0_), channel_id=1, source_target_pairs={{56,0},{0,8},{8,16},{16,24},{24,32},{32,40},{40,48},{48,56},{57,1}... | collective-permute-start | bytes 2457608 | tf_op jit(solution)/shard_map/ppermute | solution.py:33
  71.8 12.1 %collective-permute-start.14 = (bf16[80,5120]{1,0:T(8,128)(2,1)S(1)}, bf16[80,5120]{1,0:T(8,128)(2,1)S(1)}, u32[]{:S(2)}, u32[]{:S(2)}) collective-permute-start(bf16[80,5120]{1,0:T(8,128)(2,1)S(1)} %stacked.5.refs_0_), channel_id=1, source_target_pairs={{1,0},{2,1},{3,2},{0,3},{5,4},{6,5},{7,6},{4,7},{9,8},{10,9},{11,1... | collective-permute-start | bytes 2457608 | tf_op jit(solution)/shard_map/ppermute | solution.py:33
  74.4 12.4 %collective-permute-start.15 = (bf16[80,5120]{1,0:T(8,128)(2,1)S(1)}, bf16[80,5120]{1,0:T(8,128)(2,1)S(1)}, u32[]{:S(2)}, u32[]{:S(2)}) collective-permute-start(bf16[80,5120]{1,0:T(8,128)(2,1)S(1)} %stacked.5.refs_0_), channel_id=1, source_target_pairs={{3,0},{0,1},{1,2},{2,3},{7,4},{4,5},{5,6},{6,7},{11,8},{8,9},{9,10... | collective-permute-start | bytes 2457608 | tf_op jit(solution)/shard_map/ppermute | solution.py:33
  86.8 4.5 %copy-start.1 = (f32[1,112,5120]{2,1,0:T(8,128)S(1)}, f32[1,112,5120]{2,1,0:T(8,128)}, u32[]{:S(2)}) copy-start(f32[1,112,5120]{2,1,0:T(8,128)} %param.13) | copy-start | bytes 6881284
  86.8 6.3 %collective-permute-start.19 = (bf16[336,5120]{1,0:T(8,128)(2,1)S(1)}, bf16[336,5120]{1,0:T(8,128)(2,1)S(1)}, u32[]{:S(2)}, u32[]{:S(2)}) collective-permute-start(bf16[336,5120]{1,0:T(8,128)(2,1)S(1)} %held.20.refs_6_.refs_2_.refs_9_.refs_11_), channel_id=1, source_target_pairs={{64,0},{0,64},{65,1},{1,65},{66,2},{2,66},{67,3},{3,67},{68,4},{4,... | collective-permute-start | bytes 10321928 | tf_op jit(solution)/shard_map/ppermute | solution.py:33
  87.1 23.0 %collective-permute-start.16 = (bf16[80,5120]{1,0:T(8,128)(2,1)S(1)}, bf16[80,5120]{1,0:T(8,128)(2,1)S(1)}, u32[]{:S(2)}, u32[]{:S(2)}) collective-permute-start(bf16[80,5120]{1,0:T(8,128)(2,1)S(1)} %get-tuple-element.21.refs_1_), channel_id=1, source_target_pairs={{8,0},{16,8},{24,16},{32,24},{40,32},{48,40},{56,48},{0,56},{9,1},... | collective-permute-start | bytes 2457608 | tf_op jit(solution)/shard_map/ppermute | solution.py:33
  89.8 20.3 %collective-permute-start.17 = (bf16[80,5120]{1,0:T(8,128)(2,1)S(1)}, bf16[80,5120]{1,0:T(8,128)(2,1)S(1)}, u32[]{:S(2)}, u32[]{:S(2)}) collective-permute-start(bf16[80,5120]{1,0:T(8,128)(2,1)S(1)} %get-tuple-element.22.refs_2_.refs_8_), channel_id=1, source_target_pairs={{56,0},{0,8},{8,16},{16,24},{24,32},{32,40},{40,48},{48,56},{57,1}... | collective-permute-start | bytes 2457608 | tf_op jit(solution)/shard_map/ppermute | solution.py:33
  89.8 20.3 %collective-permute-start.20 = (bf16[80,5120]{1,0:T(8,128)(2,1)S(1)}, bf16[80,5120]{1,0:T(8,128)(2,1)S(1)}, u32[]{:S(2)}, u32[]{:S(2)}) collective-permute-start(bf16[80,5120]{1,0:T(8,128)(2,1)S(1)} %held.21.refs_1_), channel_id=1, source_target_pairs={{1,0},{2,1},{3,2},{0,3},{5,4},{6,5},{7,6},{4,7},{9,8},{10,9},{11,1... | collective-permute-start | bytes 2457608 | tf_op jit(solution)/shard_map/ppermute | solution.py:33
  90.2 19.6 %collective-permute-start.21 = (bf16[80,5120]{1,0:T(8,128)(2,1)S(1)}, bf16[80,5120]{1,0:T(8,128)(2,1)S(1)}, u32[]{:S(2)}, u32[]{:S(2)}) collective-permute-start(bf16[80,5120]{1,0:T(8,128)(2,1)S(1)} %held.21.refs_1_), channel_id=1, source_target_pairs={{3,0},{0,1},{1,2},{2,3},{7,4},{4,5},{5,6},{6,7},{11,8},{8,9},{9,10... | collective-permute-start | bytes 2457608 | tf_op jit(solution)/shard_map/ppermute | solution.py:33
  93.2 30.2 %collective-permute-start.24 = (f32[64,5120]{1,0:T(8,128)S(1)}, f32[64,5120]{1,0:T(8,128)S(1)}, u32[]{:S(2)}, u32[]{:S(2)}) collective-permute-start(f32[64,5120]{1,0:T(8,128)S(1)} %held.23), channel_id=1, source_target_pairs={{128,0},{0,128},{129,1},{1,129},{130,2},{2,130},{131,3},{3,131},{1... | collective-permute-start | bytes 3932168 | tf_op jit(solution)/shard_map/ppermute | solution.py:33
  109.8 20.4 %collective-permute-start.26 = (bf16[80,5120]{1,0:T(8,128)(2,1)S(1)}, bf16[80,5120]{1,0:T(8,128)(2,1)S(1)}, u32[]{:S(2)}, u32[]{:S(2)}) collective-permute-start(bf16[80,5120]{1,0:T(8,128)(2,1)S(1)} %collective-permute-done.21.refs_4_.refs_5_), channel_id=1, source_target_pairs={{3,0},{0,1},{1,2},{2,3},{7,4},{4,5},{5,6},{6,7},{11,8},{8,9},{9,10... | collective-permute-start | bytes 2457608 | tf_op jit(solution)/shard_map/ppermute | solution.py:33
  110.1 20.0 %collective-permute-start.22 = (bf16[80,5120]{1,0:T(8,128)(2,1)S(1)}, bf16[80,5120]{1,0:T(8,128)(2,1)S(1)}, u32[]{:S(2)}, u32[]{:S(2)}) collective-permute-start(bf16[80,5120]{1,0:T(8,128)(2,1)S(1)} %get-tuple-element.23.refs_1_.refs_2_), channel_id=1, source_target_pairs={{8,0},{16,8},{24,16},{32,24},{40,32},{48,40},{56,48},{0,56},{9,1},... | collective-permute-start | bytes 2457608 | tf_op jit(solution)/shard_map/ppermute | solution.py:33
  112.5 18.2 %collective-permute-start.23 = (bf16[80,5120]{1,0:T(8,128)(2,1)S(1)}, bf16[80,5120]{1,0:T(8,128)(2,1)S(1)}, u32[]{:S(2)}, u32[]{:S(2)}) collective-permute-start(bf16[80,5120]{1,0:T(8,128)(2,1)S(1)} %get-tuple-element.24.refs_7_), channel_id=1, source_target_pairs={{56,0},{0,8},{8,16},{16,24},{24,32},{32,40},{40,48},{48,56},{57,1}... | collective-permute-start | bytes 2457608 | tf_op jit(solution)/shard_map/ppermute | solution.py:33
  112.6 18.2 %collective-permute-start.25 = (bf16[80,5120]{1,0:T(8,128)(2,1)S(1)}, bf16[80,5120]{1,0:T(8,128)(2,1)S(1)}, u32[]{:S(2)}, u32[]{:S(2)}) collective-permute-start(bf16[80,5120]{1,0:T(8,128)(2,1)S(1)} %held.24.refs_2_), channel_id=1, source_target_pairs={{1,0},{2,1},{3,2},{0,3},{5,4},{6,5},{7,6},{4,7},{9,8},{10,9},{11,1... | collective-permute-start | bytes 2457608 | tf_op jit(solution)/shard_map/ppermute | solution.py:33
  123.4 25.8 %collective-permute-start.29 = (f32[56,5120]{1,0:T(8,128)S(1)}, f32[56,5120]{1,0:T(8,128)S(1)}, u32[]{:S(2)}, u32[]{:S(2)}) collective-permute-start(f32[56,5120]{1,0:T(8,128)S(1)} %held.26), channel_id=1, source_target_pairs={{128,0},{0,128},{129,1},{1,129},{130,2},{2,130},{131,3},{3,131},{1... | collective-permute-start | bytes 3440648 | tf_op jit(solution)/shard_map/ppermute | solution.py:33
  130.8 18.4 %collective-permute-start.27 = (bf16[48,5120]{1,0:T(8,128)(2,1)S(1)}, bf16[48,5120]{1,0:T(8,128)(2,1)S(1)}, u32[]{:S(2)}, u32[]{:S(2)}) collective-permute-start(bf16[48,5120]{1,0:T(8,128)(2,1)S(1)} %slice.17), channel_id=1, source_target_pairs={{8,0},{16,8},{24,16},{32,24},{40,32},{48,40},{56,48},{0,56},{9,1},... | collective-permute-start | bytes 1474568 | tf_op jit(solution)/shard_map/ppermute | solution.py:33
  133.0 16.2 %collective-permute-start.28 = (bf16[32,5120]{1,0:T(8,128)(2,1)S(1)}, bf16[32,5120]{1,0:T(8,128)(2,1)S(1)}, u32[]{:S(2)}, u32[]{:S(2)}) collective-permute-start(bf16[32,5120]{1,0:T(8,128)(2,1)S(1)} %slice.18), channel_id=1, source_target_pairs={{56,0},{0,8},{8,16},{16,24},{24,32},{32,40},{40,48},{48,56},{57,1}... | collective-permute-start | bytes 983048 | tf_op jit(solution)/shard_map/ppermute | solution.py:33
  158.2 6.2 %collective-permute-start.30 = (f32[112,5120]{1,0:T(8,128)S(1)}, f32[112,5120]{1,0:T(8,128)S(1)}, u32[]{:S(2)}, u32[]{:S(2)}) collective-permute-start(f32[112,5120]{1,0:T(8,128)S(1)} %get-tuple-element.28), channel_id=1, source_target_pairs={{64,0},{0,64},{65,1},{1,65},{66,2},{2,66},{67,3},{3,67},{68,4},{4,... | collective-permute-start | bytes 6881288 | tf_op jit(solution)/shard_map/ppermute | solution.py:33
  162.1 46.9 %collective-permute-start.35 = (f32[120,5120]{1,0:T(8,128)}, f32[120,5120]{1,0:T(8,128)}, u32[]{:S(2)}, u32[]{:S(2)}) collective-permute-start(f32[120,5120]{1,0:T(8,128)} %held.29), channel_id=1, source_target_pairs={{64,0},{0,64},{65,1},{1,65},{66,2},{2,66},{67,3},{3,67},{68,4},{4,... | collective-permute-start | bytes 7372808 | tf_op jit(solution)/shard_map/ppermute | solution.py:33
  167.0 42.0 %collective-permute-start.36 = (f32[112,5120]{1,0:T(8,128)}, f32[112,5120]{1,0:T(8,128)}, u32[]{:S(2)}, u32[]{:S(2)}) collective-permute-start(f32[112,5120]{1,0:T(8,128)} %get-tuple-element.35.refs_5_), channel_id=1, source_target_pairs={{64,4},{4,64},{65,5},{5,65},{66,6},{6,66},{67,7},{7,67},{72,12},{1... | collective-permute-start | bytes 6881288 | tf_op jit(solution)/shard_map/ppermute | solution.py:50
  172.3 36.7 %collective-permute-start.33 = (f32[64,5120]{1,0:T(8,128)S(1)}, f32[64,5120]{1,0:T(8,128)}, u32[]{:S(2)}, u32[]{:S(2)}) collective-permute-start(f32[64,5120]{1,0:T(8,128)S(1)} %get-tuple-element.29.refs_0_), channel_id=1, source_target_pairs={{64,0},{0,64},{65,1},{1,65},{66,2},{2,66},{67,3},{3,67},{68,4},{4,... | collective-permute-start | bytes 3932168 | tf_op jit(solution)/shard_map/ppermute | solution.py:33
  172.4 36.6 %collective-permute-start.34 = (f32[56,5120]{1,0:T(8,128)S(1)}, f32[56,5120]{1,0:T(8,128)}, u32[]{:S(2)}, u32[]{:S(2)}) collective-permute-start(f32[56,5120]{1,0:T(8,128)S(1)} %get-tuple-element.30.refs_1_), channel_id=1, source_target_pairs={{64,0},{0,64},{65,1},{1,65},{66,2},{2,66},{67,3},{3,67},{68,4},{4,... | collective-permute-start | bytes 3440648 | tf_op jit(solution)/shard_map/ppermute | solution.py:33
  194.6 8.8 %collective-permute-start.31 = (f32[]{:T(128)}, f32[]{:T(128)}, u32[]{:S(2)}, u32[]{:S(2)}) collective-permute-start(f32[]{:T(128)} %psum.15), channel_id=1, source_target_pairs={{0,0},{64,4},{4,64},{68,68},{1,1},{65,5},{5,65},{69,69},{2,2},{66,... | collective-permute-start | bytes 20 | tf_op jit(solution)/shard_map/ppermute | solution.py:50
  203.5 4.1 %collective-permute-start.32 = (f32[]{:T(128)}, f32[]{:T(128)}, u32[]{:S(2)}, u32[]{:S(2)}) collective-permute-start(f32[]{:T(128)} %psum.15), channel_id=1, source_target_pairs={{64,0},{0,4},{68,64},{4,68},{65,1},{1,5},{69,65},{5,69},{66,2},{2,... | collective-permute-start | bytes 20 | tf_op jit(solution)/shard_map/ppermute | solution.py:55
  209.0 1.6 copy-start

commit v13 on v9

--- a/solution.py
+++ b/solution.py
@@ -40,6 +40,11 @@
         for x_hi in range(2)
         if stay or core != x_hi
     ]
+    return lax.ppermute(value, ("core", "x_hi"), pairs)
+
+
+def crossed(value):
+    pairs = [(2 * (1 - x_hi) + core, 2 * core + x_hi) for core in range(2) for x_hi in range(2)]
     return lax.ppermute(value, ("core", "x_hi"), pairs)
 
 
@@ -303,7 +308,7 @@
             pltpu.SemaphoreType.DMA((2, blocks)),
             pltpu.SemaphoreType.DMA((blocks,)),
         ],
-        compiler_params=params_of(56),
+        compiler_params=params_of(16),
         name="updated",
     )(factor, kept_weight, which, numerator, *more)
 
@@ -320,7 +325,7 @@
     rows_in = held(rows_in, rows_grad, weights)
     near = [rows_in] + [shifted(rows_in, "y", steps) for steps in (1, 3, 2)]
     ring = {0: rows_grad, 1: shifted(rows_grad, "z", 1), 7: shifted(rows_grad, "z", 7)}
-    mine = transposed(held(weights, ring[1], ring[7]))
+    mine = transposed(held(weights, rows_grad))
     ring[2], ring[6] = shifted(ring[1], "z", 1), shifted(ring[7], "z", 7)
     ring[2], ring[6] = held((ring[2], ring[6]), *near[1:])
     ring[3], ring[5] = shifted(ring[2], "z", 1), shifted(ring[6], "z", 7)
@@ -366,12 +371,11 @@
     returned = transposed(gate_grad, stay=False)
     for axes in ("z", "y"):
         norm_sq = lax.psum(norm_sq, axes)
-    x_hi, core = lax.axis_index("x_hi"), lax.axis_index("core")
-    norms = lax.psum(jnp.where(jnp.arange(2) == x_hi, norm_sq, 0.0), ("core", "x_hi"))
-    norm_sq = jnp.where(core == 0, norms[0], norms[1])
+    norm_sq = transposed(norm_sq) + crossed(norm_sq)
 
     clip_factor = jnp.minimum(1.0, MAX_NORM / jnp.sqrt(norm_sq + eps))
     kept_weight = 0.5 * push_weight
+    core, x_hi = lax.axis_index("core"), lax.axis_index("x_hi")
     which = jnp.where(step[0] % 2 == 1, 0, 1 + core)
     kept_half, new_num, new_weight = updated(
         numerator,

time: 218 us -> 210 us (0.963)
  starting transfers between devices: 60.1 us -> 74.9 us
  blocking collectives: 37.4 us -> 23.6 us
  waiting for transfers between devices: 79.8 us -> 73.2 us
    ppermute x4 -> x5, waiting for transfers between devices: 23.9 us -> 9.88 us  [transposed(): return lax.ppermute(value, ('core', 'x_hi'), pairs)]
    psum x1 -> x0, blocking collectives: 13.6 us -> none  [shards(): lax.psum(jnp.where(jnp.arange(2) == x_hi, norm_sq, 0.0), ('core', 'x_hi'))]
    ppermute x4 -> x5, starting transfers between devices: 23.8 us -> 32.4 us  [transposed(): return lax.ppermute(value, ('core', 'x_hi'), pairs)]
    ppermute x31, starting transfers between devices: 36.3 us -> 42.6 us  [shifted(): return lax.ppermute(value, axis, pairs)]
    ppermute x0 -> x1, waiting for transfers between devices: none -> 4.13 us  [crossed(): return lax.ppermute(value, ('core', 'x_hi'), pairs)]
    ppermute x31, waiting for transfers between devices: 56 us -> 59.1 us  [shifted(): return lax.ppermute(value, axis, pairs)]
  transfers between devices with their start and end apart: 35 -> 37, of which waited for: 19 -> 24; matrix products, arithmetic and copies ran while one was open for 4% -> 3% of each run, Pallas kernels for 4% -> 5%
where the time goes in v13:
time: 210 us; the launch traced here: 209 us
  starting transfers between devices  74.9 us (36%)
  waiting for transfers between devices  73.2 us (35%)
  Pallas kernels  23.9 us (11%)
  blocking collectives  23.6 us (11%)
  between operations  5.5 us (3%)
  other arithmetic  4.7 us (2%)
  local copies, waits for them, and re-layouts  3.58 us (2%)
    ppermute x31, waiting for transfers between devices, shifted(): return lax.ppermute(value, axis, pairs)  59.1 us
    ppermute x31, starting transfers between devices, shifted(): return lax.ppermute(value, axis, pairs)  42.6 us
    ppermute x5, starting transfers between devices, transposed(): return lax.ppermute(value, ('core', 'x_hi'), pairs)  32.4 us
    psum x2, blocking collectives, shards(): norm_sq = lax.psum(norm_sq, axes)  23.6 us
    ppermute x5, waiting for transfers between devices, transposed(): return lax.ppermute(value, ('core', 'x_hi'), pairs)  9.88 us
    pallas_call x1, Pallas kernels, gate_grads(): pl.pallas_call(grad_kernel, grid=(D // BLOCK,), in_specs=[pl.BlockSpec((p...  9 us
    pallas_call x2, Pallas kernels, hidden_of(): pl.pallas_call(hidden_kernel, grid=(D // BLOCK,), in_specs=[pl.BlockSpec(...  8.72 us
    pallas_call x1, Pallas kernels, updated(): pl.pallas_call(updated_kernel, grid=(blocks,), in_specs=[scalar, scalar,...  5.22 us
  transfers between devices with their start and end apart: 37, of which 24 were waited for; matrix products, arithmetic and copies ran while one was open for 3% of the time, Pallas kernels for 5%

profile of v13, /device:TPU:1, one launch (start us, length us, event | category | flops | bytes accessed | tf_op | source)
XLA Modules:
  0.0 209.4 jit_solution(13879062293025912483)
XLA Ops:
  0.7 6.2 %collective-permute-start = (bf16[20,5120]{1,0:T(8,128)(2,1)}, bf16[20,5120]{1,0:T(8,128)(2,1)S(1)}, u32[]{:S(2)}, u32[]{:S(2)}) collective-permute-start(bf16[20,5120]{1,0:T(8,128)(2,1)} %bitcast.27), channel_id=1, source_target_pairs={{0,0},{64,4},{4,64},{68,68},{1,1},{65,5},{5,65},{69,69},{2,2},{66,... | collective-permute-start | bytes 614408 | tf_op jit(solution)/shard_map/ppermute | solution.py:43
  6.8 1.9 collective-permute-start.1
  9.4 1.8 divide_convert_fusion
  11.3 0.3 pad_maximum_fusion.refs_2_.refs_0_
  11.5 4.5 %collective-permute-done.1.refs_1_.refs_0_ = bf16[20,5120]{1,0:T(8,128)(2,1)S(1)} collective-permute-done((bf16[20,5120]{1,0:T(8,128)(2,1)}, bf16[20,5120]{1,0:T(8,128)(2,1)S(1)}, u32[]{:S(2)}, u32[]{:S(2)}) %collective-permute-start.1) | collective-permute-done | bytes 204832 | tf_op jit(solution)/shard_map/ppermute | solution.py:43
  16.1 2.6 %collective-permute-start.16 = (bf16[336,5120]{1,0:T(8,128)(2,1)S(1)}, bf16[336,5120]{1,0:T(8,128)(2,1)S(1)}, u32[]{:S(2)}, u32[]{:S(2)}) collective-permute-start(bf16[336,5120]{1,0:T(8,128)(2,1)S(1)} %held.18), channel_id=1, source_target_pairs={{0,0},{64,4},{4,64},{68,68},{1,1},{65,5},{5,65},{69,69},{2,2},{66,... | collective-permute-start | bytes 10321928 | tf_op jit(solution)/shard_map/ppermute | solution.py:43
  18.7 2.8 %collective-permute-start.2 = (bf16[20,5120]{1,0:T(8,128)(2,1)S(1)}, bf16[20,5120]{1,0:T(8,128)(2,1)S(1)}, u32[]{:S(2)}, u32[]{:S(2)}) collective-permute-start(bf16[20,5120]{1,0:T(8,128)(2,1)S(1)} %held.15.refs_0_), channel_id=1, source_target_pairs={{1,0},{2,1},{3,2},{0,3},{5,4},{6,5},{7,6},{4,7},{9,8},{10,9},{11,1... | collective-permute-start | bytes 614408 | tf_op jit(solution)/shard_map/ppermute | solution.py:33
  21.5 5.6 %collective-permute-start.5 = (bf16[20,5120]{1,0:T(8,128)(2,1)S(1)}, bf16[20,5120]{1,0:T(8,128)(2,1)S(1)}, u32[]{:S(2)}, u32[]{:S(2)}) collective-permute-start(bf16[20,5120]{1,0:T(8,128)(2,1)S(1)} %collective-permute-done.1.refs_1_.refs_0_), channel_id=1, source_target_pairs={{8,0},{16,8},{24,16},{32,24},{40,32},{48,40},{56,48},{0,56},{9,1},... | collective-permute-start | bytes 614408 | tf_op jit(solution)/shard_map/ppermute | solution.py:33
  27.1 0.2 collective-permute-done.2.refs_2_.refs_1_
  27.3 1.7 collective-permute-start.4
  29.0 2.5 %collective-permute-done.5.refs_1_ = bf16[20,5120]{1,0:T(8,128)(2,1)S(1)} collective-permute-done((bf16[20,5120]{1,0:T(8,128)(2,1)S(1)}, bf16[20,5120]{1,0:T(8,128)(2,1)S(1)}, u32[]{:S(2)}, u32[]{:S(2)}) %collective-permute-start.5) | collective-permute-done | bytes 204832 | tf_op jit(solution)/shard_map/ppermute | solution.py:33
  31.5 3.1 %collective-permute-start.6 = (bf16[20,5120]{1,0:T(8,128)(2,1)S(1)}, bf16[20,5120]{1,0:T(8,128)(2,1)S(1)}, u32[]{:S(2)}, u32[]{:S(2)}) collective-permute-start(bf16[20,5120]{1,0:T(8,128)(2,1)S(1)} %collective-permute-done.5.refs_1_), channel_id=1, source_target_pairs={{8,0},{16,8},{24,16},{32,24},{40,32},{48,40},{56,48},{0,56},{9,1},... | collective-permute-start | bytes 614408 | tf_op jit(solution)/shard_map/ppermute | solution.py:33
  34.6 0.3 collective-permute-done.7.refs_3_
  34.9 1.1 collective-permute-done.3.refs_3_.refs_2_
  36.0 4.3 %collective-permute-done.6.refs_0_ = bf16[20,5120]{1,0:T(8,128)(2,1)S(1)} collective-permute-done((bf16[20,5120]{1,0:T(8,128)(2,1)S(1)}, bf16[20,5120]{1,0:T(8,128)(2,1)S(1)}, u32[]{:S(2)}, u32[]{:S(2)}) %collective-permute-start.6) | collective-permute-done | bytes 204832 | tf_op jit(solution)/shard_map/ppermute | solution.py:33
  40.3 3.6 %collective-permute-done.8.refs_1_ = bf16[20,5120]{1,0:T(8,128)(2,1)S(1)} collective-permute-done((bf16[20,5120]{1,0:T(8,128)(2,1)S(1)}, bf16[20,5120]{1,0:T(8,128)(2,1)S(1)}, u32[]{:S(2)}, u32[]{:S(2)}) %collective-permute-start.8) | collective-permute-done | bytes 204832 | tf_op jit(solution)/shard_map/ppermute | solution.py:33
  43.9 1.5 collective-permute-start.11
  45.4 5.8 %collective-permute-done.9.refs_1_.refs_3_ = bf16[20,5120]{1,0:T(8,128)(2,1)S(1)} collective-permute-done((bf16[20,5120]{1,0:T(8,128)(2,1)S(1)}, bf16[20,5120]{1,0:T(8,128)(2,1)S(1)}, u32[]{:S(2)}, u32[]{:S(2)}) %collective-permute-start.9) | collective-permute-done | bytes 204832 | tf_op jit(solution)/shard_map/ppermute | solution.py:33
  51.2 1.4 collective-permute-done.10.refs_2_.refs_0_
  52.7 0.3 stacked.3.refs_0_
  53.0 6.7 %collective-permute-start.12 = (bf16[80,5120]{1,0:T(8,128)(2,1)S(1)}, bf16[80,5120]{1,0:T(8,128)(2,1)S(1)}, u32[]{:S(2)}, u32[]{:S(2)}) collective-permute-start(bf16[80,5120]{1,0:T(8,128)(2,1)S(1)} %stacked.3.refs_0_), channel_id=1, source_target_pairs={{8,0},{16,8},{24,16},{32,24},{40,32},{48,40},{56,48},{0,56},{9,1},... | collective-permute-start | bytes 2457608 | tf_op jit(solution)/shard_map/ppermute | solution.py:33
  59.7 0.3 stacked.5.refs_0_
  60.1 0.1 collective-permute-start.14
  60.1 1.5 collective-permute-start.15
  61.6 0.1 slice_bitcast_fusion.refs_0_
  61.7 3.9 %collective-permute-done.16.refs_5_.refs_1_.refs_0_ = bf16[336,5120]{1,0:T(8,128)(2,1)S(1)} collective-permute-done((bf16[336,5120]{1,0:T(8,128)(2,1)S(1)}, bf16[336,5120]{1,0:T(8,128)(2,1)S(1)}, u32[]{:S(2)}, u32[]{:S(2)}) %collective-permute-start.16) | collective-permute-done | bytes 3440672 | tf_op jit(solution)/shard_map/ppermute | solution.py:43
  65.6 1.2 collective-permute-start.19
  66.8 0.3 stacked.4.refs_2_.refs_0_
  67.2 5.4 %collective-permute-done.12.refs_0_ = bf16[80,5120]{1,0:T(8,128)(2,1)S(1)} collective-permute-done((bf16[80,5120]{1,0:T(8,128)(2,1)S(1)}, bf16[80,5120]{1,0:T(8,128)(2,1)S(1)}, u32[]{:S(2)}, u32[]{:S(2)}) %collective-permute-start.12) | collective-permute-done | bytes 819232 | tf_op jit(solution)/shard_map/ppermute | solution.py:33
  72.6 0.4 collective-permute-done.15.refs_4_
  73.0 3.2 %collective-permute-start.17 = (bf16[80,5120]{1,0:T(8,128)(2,1)S(1)}, bf16[80,5120]{1,0:T(8,128)(2,1)S(1)}, u32[]{:S(2)}, u32[]{:S(2)}) collective-permute-start(bf16[80,5120]{1,0:T(8,128)(2,1)S(1)} %get-tuple-element.21.refs_1_), channel_id=1, source_target_pairs={{8,0},{16,8},{24,16},{32,24},{40,32},{48,40},{56,48},{0,56},{9,1},... | collective-permute-start | bytes 2457608 | tf_op jit(solution)/shard_map/ppermute | solution.py:33
  76.1 4.3 %collective-permute-start.20 = (bf16[80,5120]{1,0:T(8,128)(2,1)S(1)}, bf16[80,5120]{1,0:T(8,128)(2,1)S(1)}, u32[]{:S(2)}, u32[]{:S(2)}) collective-permute-start(bf16[80,5120]{1,0:T(8,128)(2,1)S(1)} %held.21.refs_1_), channel_id=1, source_target_pairs={{1,0},{2,1},{3,2},{0,3},{5,4},{6,5},{7,6},{4,7},{9,8},{10,9},{11,1... | collective-permute-start | bytes 2457608 | tf_op jit(solution)/shard_map/ppermute | solution.py:33
  80.5 8.9 %collective-permute-done.17.refs_0_ = bf16[80,5120]{1,0:T(8,128)(2,1)S(1)} collective-permute-done((bf16[80,5120]{1,0:T(8,128)(2,1)S(1)}, bf16[80,5120]{1,0:T(8,128)(2,1)S(1)}, u32[]{:S(2)}, u32[]{:S(2)}) %collective-permute-start.17) | collective-permute-done | bytes 819232 | tf_op jit(solution)/shard_map/ppermute | solution.py:33
  89.3 1.3 collective-permute-done.18.refs_1_
  90.6 0.7 collective-permute-done.20.refs_3_
  91.4 2.7 %collective-permute-done.21.refs_4_.refs_5_ = bf16[80,5120]{1,0:T(8,128)(2,1)S(1)} collective-permute-done((bf16[80,5120]{1,0:T(8,128)(2,1)S(1)}, bf16[80,5120]{1,0:T(8,128)(2,1)S(1)}, u32[]{:S(2)}, u32[]{:S(2)}) %collective-permute-start.21) | collective-permute-done | bytes 819232 | tf_op jit(solution)/shard_map/ppermute | solution.py:33
  94.7 0.1 collective-permute-start.26
  94.8 3.0 %collective-permute-start.22 = (bf16[80,5120]{1,0:T(8,128)(2,1)S(1)}, bf16[80,5120]{1,0:T(8,128)(2,1)S(1)}, u32[]{:S(2)}, u32[]{:S(2)}) collective-permute-start(bf16[80,5120]{1,0:T(8,128)(2,1)S(1)} %get-tuple-element.23.refs_1_.refs_2_), channel_id=1, source_target_pairs={{8,0},{16,8},{24,16},{32,24},{40,32},{48,40},{56,48},{0,56},{9,1},... | collective-permute-start | bytes 2457608 | tf_op jit(solution)/shard_map/ppermute | solution.py:33
  97.8 2.6 %collective-permute-start.25 = (bf16[80,5120]{1,0:T(8,128)(2,1)S(1)}, bf16[80,5120]{1,0:T(8,128)(2,1)S(1)}, u32[]{:S(2)}, u32[]{:S(2)}) collective-permute-start(bf16[80,5120]{1,0:T(8,128)(2,1)S(1)} %held.23.refs_2_), channel_id=1, source_target_pairs={{1,0},{2,1},{3,2},{0,3},{5,4},{6,5},{7,6},{4,7},{9,8},{10,9},{11,1... | collective-permute-start | bytes 2457608 | tf_op jit(solution)/shard_map/ppermute | solution.py:33
  100.5 0.1 collective-permute-start.29
  100.6 6.1 %hidden.2.refs_2_.refs_13_ = f32[480,256]{1,0:T(8,128)S(1)} custom-call(bf16[80,5120]{1,0:T(8,128)(2,1)S(1)} %stacked.5.refs_0_, bf16[80,5120]{1,0:T(8,128)(2,1)S(1)} %held.21.refs_1_, bf16[80,5120]{1,0:T(8,128)(2,1)S(1)} %held.23.refs_2_, bf16[80,5120]{1,0:T(8,128)(2,1)S(1)} %collective-permute-done.20.refs_3_, ...), custom_call_target="tpu_custom_call" | custom-call | flops 1 | bytes 1 | tf_op jit(solution)/shard_map/hidden/pallas_call | solution.py:142
  106.7 8.6 %collective-permute-done.26.refs_4_.refs_1_ = bf16[80,5120]{1,0:T(8,128)(2,1)S(1)} collective-permute-done((bf16[80,5120]{1,0:T(8,128)(2,1)S(1)}, bf16[80,5120]{1,0:T(8,128)(2,1)S(1)}, u32[]{:S(2)}, u32[]{:S(2)}) %collective-permute-start.26) | collective-permute-done | bytes 819232 | tf_op jit(solution)/shard_map/ppermute | solution.py:33
  115.3 2.7 %collective-permute-done.23.refs_1_ = bf16[80,5120]{1,0:T(8,128)(2,1)S(1)} collective-permute-done((bf16[80,5120]{1,0:T(8,128)(2,1)S(1)}, bf16[80,5120]{1,0:T(8,128)(2,1)S(1)}, u32[]{:S(2)}, u32[]{:S(2)}) %collective-permute-start.23) | collective-permute-done | bytes 819232 | tf_op jit(solution)/shard_map/ppermute | solution.py:33
  118.1 1.3 collective-permute-start.27
  119.4 0.3 collective-permute-start.28
  119.7 2.6 %hidden.3.refs_0_ = f32[160,256]{1,0:T(8,128)S(1)} custom-call(bf16[80,5120]{1,0:T(8,128)(2,1)S(1)} %collective-permute-done.25.refs_3_.refs_0_, bf16[80,5120]{1,0:T(8,128)(2,1)S(1)} %collective-permute-done.26.refs_4_.refs_1_, bf16[336,5120]{1,0:T(8,128)(2,1)S(1)} %held.24.refs_6_.refs_2_.refs_9_.refs_11_, ...), custom_call_target="tpu_custom_call" | custom-call | flops 1 | bytes 1 | tf_op jit(solution)/shard_map/hidden/pallas_call | solution.py:142
  122.3 3.7 %collective-permute-done.29.refs_1_ = f32[56,5120]{1,0:T(8,128)S(1)} collective-permute-done((f32[56,5120]{1,0:T(8,128)S(1)}, f32[56,5120]{1,0:T(8,128)S(1)}, u32[]{:S(2)}, u32[]{:S(2)}) %collective-permute-start.29) | collective-permute-done | bytes 1146912 | tf_op jit(solution)/shard_map/ppermute | solution.py:33
  126.0 1.3 collective-permute-done.28.refs_5_
  127.4 1.8 collective-permute-done.27.refs_4_
  129.2 9.0 %gate_grads.1 = (f32[112,5120]{1,0:T(8,128)S(1)}, f32[112,5120]{1,0:T(8,128)S(1)}) custom-call(bf16[80,5120]{1,0:T(8,128)(2,1)S(1)} %stacked.3.refs_0_, bf16[80,5120]{1,0:T(8,128)(2,1)S(1)} %get-tuple-element.21.refs_1_, bf16[80,5120]{1,0:T(8,128)(2,1)S(1)} %get-tuple-element.23.refs_1_.refs_2_, bf16[80,5120]{1,0:T(8,128)(2,1)S(1)} %get-tuple-element.25.refs_3_, ...), custom_call_target="tpu_custom_call" | custom-call | flops 1 | bytes 1 | tf_op jit(solution)/shard_map/gate_grads/pallas_call | solution.py:210
  138.2 2.9 %collective-permute-start.30 = (f32[112,5120]{1,0:T(8,128)S(1)}, f32[112,5120]{1,0:T(8,128)S(1)}, u32[]{:S(2)}, u32[]{:S(2)}) collective-permute-start(f32[112,5120]{1,0:T(8,128)S(1)} %get-tuple-element.28), channel_id=1, source_target_pairs={{64,0},{0,64},{65,1},{1,65},{66,2},{2,66},{67,3},{3,67},{68,4},{4,... | collective-permute-start | bytes 6881288 | tf_op jit(solution)/shard_map/ppermute | solution.py:33
  141.1 1.7 concatenate.7.refs_0_
  142.8 2.3 %collective-permute-done.30 = f32[112,5120]{1,0:T(8,128)S(1)} collective-permute-done((f32[112,5120]{1,0:T(8,128)S(1)}, f32[112,5120]{1,0:T(8,128)S(1)}, u32[]{:S(2)}, u32[]{:S(2)}) %collective-permute-start.30) | collective-permute-done | bytes 2293792 | tf_op jit(solution)/shard_map/ppermute | solution.py:33
  145.2 2.5 %multiply_reduce_fusion = (f32[]{:T(128)}, f32[112,5120]{1,0:T(8,128)}) fusion(f32[112,5120]{1,0:T(8,128)S(1)} %get-tuple-element.27.refs_2_.refs_1_, f32[112,5120]{1,0:T(8,128)S(1)} %collective-permute-done.30), kind=kLoop, calls=%fused_computation.1 | loop fusion | flops 1720319 | bytes 6881284 | tf_op jit(solution)/shard_map/reduce_sum | solution.py:370
  147.7 14.0 %collective-permute-start.36 = (f32[112,5120]{1,0:T(8,128)}, f32[112,5120]{1,0:T(8,128)}, u32[]{:S(2)}, u32[]{:S(2)}) collective-permute-start(f32[112,5120]{1,0:T(8,128)} %get-tuple-element.35.refs_5_), channel_id=1, source_target_pairs={{64,4},{4,64},{65,5},{5,65},{66,6},{6,66},{67,7},{7,67},{72,12},{1... | collective-permute-start | bytes 6881288 | tf_op jit(solution)/shard_map/ppermute | solution.py:43
  161.7 0.1 collective-permute-start.33
  161.8 0.5 collective-permute-start.34
  163.2 13.7 %psum.14 = f32[]{:T(128)} all-reduce(f32[]{:T(128)} %get-tuple-element.34), channel_id=1, replica_groups=mesh['x_lo'=2,'core'=2,'z'=8,'x_hi'=2,'y'=4] {'z'}, use_global_device_ids=true, to_apply=%region_1.2 | all-reduce | flops 1 | bytes 8 | tf_op jit(solution)/shard_map/psum | solution.py:373
  176.8 10.0 %psum.15 = f32[]{:T(128)} all-reduce(f32[]{:T(128)} %psum.14), channel_id=1, replica_groups=mesh['x_lo'=2,'core'=2,'z'=8,'x_hi'=2,'y'=4] {'y'}, use_global_device_ids=true, to_apply=%region_2.3 | all-reduce | flops 1 | bytes 8 | tf_op jit(solution)/shard_map/psum | solution.py:373
  186.8 7.7 %collective-permute-start.31 = (f32[]{:T(128)}, f32[]{:T(128)}, u32[]{:S(2)}, u32[]{:S(2)}) collective-permute-start(f32[]{:T(128)} %psum.15), channel_id=1, source_target_pairs={{0,0},{64,4},{4,64},{68,68},{1,1},{65,5},{5,65},{69,69},{2,2},{66,... | collective-permute-start | bytes 20 | tf_op jit(solution)/shard_map/ppermute | solution.py:43
  194.4 1.4 collective-permute-done.31
  195.9 4.1 %collective-permute-done.32 = f32[]{:T(128)} collective-permute-done((f32[]{:T(128)}, f32[]{:T(128)}, u32[]{:S(2)}, u32[]{:S(2)}) %collective-permute-start.32) | collective-permute-done | bytes 36 | tf_op jit(solution)/shard_map/ppermute | solution.py:48
  201.4 1.6 copy-done
  203.1 5.2 %updated.1 = (f32[112,5120]{1,0:T(8,128)}, f32[112,5120]{1,0:T(8,128)}, f32[1]{0:T(128)}) custom-call(f32[1]{0:T(128)} %bitcast.8.factor, f32[1]{0:T(128)} %mul.11.kept_weight, s32[2]{0:T(128)S(1)} %pad_add_fusion.which, f32[112,5120]{1,0:T(8,128)S(1)} %bitcast.22, f32[64,5120]{1,0:T(8,128)S(1)} %get-tuple-element.29.refs_0_, ...), custom_call_target="tpu_custom_call" | custom-call | tf_op jit(solution)/shard_map/updated/pallas_call | solution.py:295
  (51 shorter events, 0.3 us)
Async XLA Ops:
  0.6 10.6 %copy-start.2 = (bf16[112,5120]{1,0:T(8,128)(2,1)S(1)}, bf16[112,5120]{1,0:T(8,128)(2,1)}, u32[]{:S(2)}) copy-start(bf16[112,5120]{1,0:T(8,128)(2,1)} %param.16) | copy-start | bytes 3440644
  0.6 10.6 %copy-start.3 = (bf16[112,5120]{1,0:T(8,128)(2,1)S(1)}, bf16[112,5120]{1,0:T(8,128)(2,1)}, u32[]{:S(2)}) copy-start(bf16[112,5120]{1,0:T(8,128)(2,1)} %param.15) | copy-start | bytes 3440644
  0.7 10.9 %collective-permute-start = (bf16[20,5120]{1,0:T(8,128)(2,1)}, bf16[20,5120]{1,0:T(8,128)(2,1)S(1)}, u32[]{:S(2)}, u32[]{:S(2)}) collective-permute-start(bf16[20,5120]{1,0:T(8,128)(2,1)} %bitcast.27), channel_id=1, source_target_pairs={{0,0},{64,4},{4,64},{68,68},{1,1},{65,5},{5,65},{69,69},{2,2},{66,... | collective-permute-start | bytes 614408 | tf_op jit(solution)/shard_map/ppermute | solution.py:43
  6.8 9.2 %collective-permute-start.1 = (bf16[20,5120]{1,0:T(8,128)(2,1)}, bf16[20,5120]{1,0:T(8,128)(2,1)S(1)}, u32[]{:S(2)}, u32[]{:S(2)}) collective-permute-start(bf16[20,5120]{1,0:T(8,128)(2,1)} %bitcast.28), channel_id=1, source_target_pairs={{0,0},{64,4},{4,64},{68,68},{1,1},{65,5},{5,65},{69,69},{2,2},{66,... | collective-permute-start | bytes 614408 | tf_op jit(solution)/shard_map/ppermute | solution.py:43
  16.1 49.5 %collective-permute-start.16 = (bf16[336,5120]{1,0:T(8,128)(2,1)S(1)}, bf16[336,5120]{1,0:T(8,128)(2,1)S(1)}, u32[]{:S(2)}, u32[]{:S(2)}) collective-permute-start(bf16[336,5120]{1,0:T(8,128)(2,1)S(1)} %held.18), channel_id=1, source_target_pairs={{0,0},{64,4},{4,64},{68,68},{1,1},{65,5},{5,65},{69,69},{2,2},{66,... | collective-permute-start | bytes 10321928 | tf_op jit(solution)/shard_map/ppermute | solution.py:43
  18.7 8.6 %collective-permute-start.2 = (bf16[20,5120]{1,0:T(8,128)(2,1)S(1)}, bf16[20,5120]{1,0:T(8,128)(2,1)S(1)}, u32[]{:S(2)}, u32[]{:S(2)}) collective-permute-start(bf16[20,5120]{1,0:T(8,128)(2,1)S(1)} %held.15.refs_0_), channel_id=1, source_target_pairs={{1,0},{2,1},{3,2},{0,3},{5,4},{6,5},{7,6},{4,7},{9,8},{10,9},{11,1... | collective-permute-start | bytes 614408 | tf_op jit(solution)/shard_map/ppermute | solution.py:33
  21.5 10.0 %collective-permute-start.5 = (bf16[20,5120]{1,0:T(8,128)(2,1)S(1)}, bf16[20,5120]{1,0:T(8,128)(2,1)S(1)}, u32[]{:S(2)}, u32[]{:S(2)}) collective-permute-start(bf16[20,5120]{1,0:T(8,128)(2,1)S(1)} %collective-permute-done.1.refs_1_.refs_0_), channel_id=1, source_target_pairs={{8,0},{16,8},{24,16},{32,24},{40,32},{48,40},{56,48},{0,56},{9,1},... | collective-permute-start | bytes 614408 | tf_op jit(solution)/shard_map/ppermute | solution.py:33
  27.1 7.8 %collective-permute-start.7 = (bf16[20,5120]{1,0:T(8,128)(2,1)S(1)}, bf16[20,5120]{1,0:T(8,128)(2,1)S(1)}, u32[]{:S(2)}, u32[]{:S(2)}) collective-permute-start(bf16[20,5120]{1,0:T(8,128)(2,1)S(1)} %collective-permute-done.1.refs_1_.refs_0_), channel_id=1, source_target_pairs={{56,0},{0,8},{8,16},{16,24},{24,32},{32,40},{40,48},{48,56},{57,1}... | collective-permute-start | bytes 614408 | tf_op jit(solution)/shard_map/ppermute | solution.py:33
  27.1 8.9 %collective-permute-start.3 = (bf16[20,5120]{1,0:T(8,128)(2,1)S(1)}, bf16[20,5120]{1,0:T(8,128)(2,1)S(1)}, u32[]{:S(2)}, u32[]{:S(2)}) collective-permute-start(bf16[20,5120]{1,0:T(8,128)(2,1)S(1)} %held.15.refs_0_), channel_id=1, source_target_pairs={{3,0},{0,1},{1,2},{2,3},{7,4},{4,5},{5,6},{6,7},{11,8},{8,9},{9,10... | collective-permute-start | bytes 614408 | tf_op jit(solution)/shard_map/ppermute | solution.py:33
  27.3 8.7 %collective-permute-start.4 = (bf16[20,5120]{1,0:T(8,128)(2,1)S(1)}, bf16[20,5120]{1,0:T(8,128)(2,1)S(1)}, u32[]{:S(2)}, u32[]{:S(2)}) collective-permute-start(bf16[20,5120]{1,0:T(8,128)(2,1)S(1)} %held.15.refs_0_), channel_id=1, source_target_pairs={{2,0},{3,1},{0,2},{1,3},{6,4},{7,5},{4,6},{5,7},{10,8},{11,9},{8,1... | collective-permute-start | bytes 614408 | tf_op jit(solution)/shard_map/ppermute | solution.py:33
  31.5 8.8 %collective-permute-start.6 = (bf16[20,5120]{1,0:T(8,128)(2,1)S(1)}, bf16[20,5120]{1,0:T(8,128)(2,1)S(1)}, u32[]{:S(2)}, u32[]{:S(2)}) collective-permute-start(bf16[20,5120]{1,0:T(8,128)(2,1)S(1)} %collective-permute-done.5.refs_1_), channel_id=1, source_target_pairs={{8,0},{16,8},{24,16},{32,24},{40,32},{48,40},{56,48},{0,56},{9,1},... | collective-permute-start | bytes 614408 | tf_op jit(solution)/shard_map/ppermute | solution.py:33
  34.9 9.0 %collective-permute-start.8 = (bf16[20,5120]{1,0:T(8,128)(2,1)S(1)}, bf16[20,5120]{1,0:T(8,128)(2,1)S(1)}, u32[]{:S(2)}, u32[]{:S(2)}) collective-permute-start(bf16[20,5120]{1,0:T(8,128)(2,1)S(1)} %collective-permute-done.7.refs_3_), channel_id=1, source_target_pairs={{56,0},{0,8},{8,16},{16,24},{24,32},{32,40},{40,48},{48,56},{57,1}... | collective-permute-start | bytes 614408 | tf_op jit(solution)/shard_map/ppermute | solution.py:33
  43.9 7.3 %collective-permute-start.9 = (bf16[20,5120]{1,0:T(8,128)(2,1)S(1)}, bf16[20,5120]{1,0:T(8,128)(2,1)S(1)}, u32[]{:S(2)}, u32[]{:S(2)}) collective-permute-start(bf16[20,5120]{1,0:T(8,128)(2,1)S(1)} %get-tuple-element.19.refs_2_), channel_id=1, source_target_pairs={{8,0},{16,8},{24,16},{32,24},{40,32},{48,40},{56,48},{0,56},{9,1},... | collective-permute-start | bytes 614408 | tf_op jit(solution)/shard_map/ppermute | solution.py:33
  43.9 8.7 %collective-permute-start.10 = (bf16[20,5120]{1,0:T(8,128)(2,1)S(1)}, bf16[20,5120]{1,0:T(8,128)(2,1)S(1)}, u32[]{:S(2)}, u32[]{:S(2)}) collective-permute-start(bf16[20,5120]{1,0:T(8,128)(2,1)S(1)} %get-tuple-element.19.refs_2_), channel_id=1, source_target_pairs={{16,0},{24,8},{32,16},{40,24},{48,32},{56,40},{0,48},{8,56},{17,1}... | collective-permute-start | bytes 614408 | tf_op jit(solution)/shard_map/ppermute | solution.py:33
  43.9 17.7 %copy-start.1 = (f32[1,112,5120]{2,1,0:T(8,128)S(1)}, f32[1,112,5120]{2,1,0:T(8,128)}, u32[]{:S(2)}) copy-start(f32[1,112,5120]{2,1,0:T(8,128)} %param.13) | copy-start | bytes 6881284
  43.9 8.7 %collective-permute-start.11 = (bf16[20,5120]{1,0:T(8,128)(2,1)S(1)}, bf16[20,5120]{1,0:T(8,128)(2,1)S(1)}, u32[]{:S(2)}, u32[]{:S(2)}) collective-permute-start(bf16[20,5120]{1,0:T(8,128)(2,1)S(1)} %get-tuple-element.20.refs_2_), channel_id=1, source_target_pairs={{56,0},{0,8},{8,16},{16,24},{24,32},{32,40},{40,48},{48,56},{57,1}... | collective-permute-start | bytes 614408 | tf_op jit(solution)/shard_map/ppermute | solution.py:33
  53.0 19.6 %collective-permute-start.12 = (bf16[80,5120]{1,0:T(8,128)(2,1)S(1)}, bf16[80,5120]{1,0:T(8,128)(2,1)S(1)}, u32[]{:S(2)}, u32[]{:S(2)}) collective-permute-start(bf16[80,5120]{1,0:T(8,128)(2,1)S(1)} %stacked.3.refs_0_), channel_id=1, source_target_pairs={{8,0},{16,8},{24,16},{32,24},{40,32},{48,40},{56,48},{0,56},{9,1},... | collective-permute-start | bytes 2457608 | tf_op jit(solution)/shard_map/ppermute | solution.py:33
  59.7 12.9 %collective-permute-start.13 = (bf16[80,5120]{1,0:T(8,128)(2,1)S(1)}, bf16[80,5120]{1,0:T(8,128)(2,1)S(1)}, u32[]{:S(2)}, u32[]{:S(2)}) collective-permute-start(bf16[80,5120]{1,0:T(8,128)(2,1)S(1)} %stacked.3.refs_0_), channel_id=1, source_target_pairs={{56,0},{0,8},{8,16},{16,24},{24,32},{32,40},{40,48},{48,56},{57,1}... | collective-permute-start | bytes 2457608 | tf_op jit(solution)/shard_map/ppermute | solution.py:33
  60.1 12.5 %collective-permute-start.14 = (bf16[80,5120]{1,0:T(8,128)(2,1)S(1)}, bf16[80,5120]{1,0:T(8,128)(2,1)S(1)}, u32[]{:S(2)}, u32[]{:S(2)}) collective-permute-start(bf16[80,5120]{1,0:T(8,128)(2,1)S(1)} %stacked.5.refs_0_), channel_id=1, source_target_pairs={{1,0},{2,1},{3,2},{0,3},{5,4},{6,5},{7,6},{4,7},{9,8},{10,9},{11,1... | collective-permute-start | bytes 2457608 | tf_op jit(solution)/shard_map/ppermute | solution.py:33
  60.1 12.8 %collective-permute-start.15 = (bf16[80,5120]{1,0:T(8,128)(2,1)S(1)}, bf16[80,5120]{1,0:T(8,128)(2,1)S(1)}, u32[]{:S(2)}, u32[]{:S(2)}) collective-permute-start(bf16[80,5120]{1,0:T(8,128)(2,1)S(1)} %stacked.5.refs_0_), channel_id=1, source_target_pairs={{3,0},{0,1},{1,2},{2,3},{7,4},{4,5},{5,6},{6,7},{11,8},{8,9},{9,10... | collective-permute-start | bytes 2457608 | tf_op jit(solution)/shard_map/ppermute | solution.py:33
  65.6 28.5 %collective-permute-start.19 = (f32[64,5120]{1,0:T(8,128)S(1)}, f32[64,5120]{1,0:T(8,128)S(1)}, u32[]{:S(2)}, u32[]{:S(2)}) collective-permute-start(f32[64,5120]{1,0:T(8,128)S(1)} %held.20), channel_id=1, source_target_pairs={{128,0},{0,128},{129,1},{1,129},{130,2},{2,130},{131,3},{3,131},{1... | collective-permute-start | bytes 3932168 | tf_op jit(solution)/shard_map/ppermute | solution.py:33
  73.0 16.4 %collective-permute-start.17 = (bf16[80,5120]{1,0:T(8,128)(2,1)S(1)}, bf16[80,5120]{1,0:T(8,128)(2,1)S(1)}, u32[]{:S(2)}, u32[]{:S(2)}) collective-permute-start(bf16[80,5120]{1,0:T(8,128)(2,1)S(1)} %get-tuple-element.21.refs_1_), channel_id=1, source_target_pairs={{8,0},{16,8},{24,16},{32,24},{40,32},{48,40},{56,48},{0,56},{9,1},... | collective-permute-start | bytes 2457608 | tf_op jit(solution)/shard_map/ppermute | solution.py:33
  76.1 14.5 %collective-permute-start.18 = (bf16[80,5120]{1,0:T(8,128)(2,1)S(1)}, bf16[80,5120]{1,0:T(8,128)(2,1)S(1)}, u32[]{:S(2)}, u32[]{:S(2)}) collective-permute-start(bf16[80,5120]{1,0:T(8,128)(2,1)S(1)} %get-tuple-element.22.refs_2_.refs_8_), channel_id=1, source_target_pairs={{56,0},{0,8},{8,16},{16,24},{24,32},{32,40},{40,48},{48,56},{57,1}... | collective-permute-start | bytes 2457608 | tf_op jit(solution)/shard_map/ppermute | solution.py:33
  76.1 15.2 %collective-permute-start.20 = (bf16[80,5120]{1,0:T(8,128)(2,1)S(1)}, bf16[80,5120]{1,0:T(8,128)(2,1)S(1)}, u32[]{:S(2)}, u32[]{:S(2)}) collective-permute-start(bf16[80,5120]{1,0:T(8,128)(2,1)S(1)} %held.21.refs_1_), channel_id=1, source_target_pairs={{1,0},{2,1},{3,2},{0,3},{5,4},{6,5},{7,6},{4,7},{9,8},{10,9},{11,1... | collective-permute-start | bytes 2457608 | tf_op jit(solution)/shard_map/ppermute | solution.py:33
  80.5 13.6 %collective-permute-start.21 = (bf16[80,5120]{1,0:T(8,128)(2,1)S(1)}, bf16[80,5120]{1,0:T(8,128)(2,1)S(1)}, u32[]{:S(2)}, u32[]{:S(2)}) collective-permute-start(bf16[80,5120]{1,0:T(8,128)(2,1)S(1)} %held.21.refs_1_), channel_id=1, source_target_pairs={{3,0},{0,1},{1,2},{2,3},{7,4},{4,5},{5,6},{6,7},{11,8},{8,9},{9,10... | collective-permute-start | bytes 2457608 | tf_op jit(solution)/shard_map/ppermute | solution.py:33
  94.1 6.5 %collective-permute-start.24 = (bf16[336,5120]{1,0:T(8,128)(2,1)S(1)}, bf16[336,5120]{1,0:T(8,128)(2,1)S(1)}, u32[]{:S(2)}, u32[]{:S(2)}) collective-permute-start(bf16[336,5120]{1,0:T(8,128)(2,1)S(1)} %held.24.refs_6_.refs_2_.refs_9_.refs_11_), channel_id=1, source_target_pairs={{64,0},{0,64},{65,1},{1,65},{66,2},{2,66},{67,3},{3,67},{68,4},{4,... | collective-permute-start | bytes 10321928 | tf_op jit(solution)/shard_map/ppermute | solution.py:33
  94.7 20.6 %collective-permute-start.26 = (bf16[80,5120]{1,0:T(8,128)(2,1)S(1)}, bf16[80,5120]{1,0:T(8,128)(2,1)S(1)}, u32[]{:S(2)}, u32[]{:S(2)}) collective-permute-start(bf16[80,5120]{1,0:T(8,128)(2,1)S(1)} %collective-permute-done.21.refs_4_.refs_5_), channel_id=1, source_target_pairs={{3,0},{0,1},{1,2},{2,3},{7,4},{4,5},{5,6},{6,7},{11,8},{8,9},{9,10... | collective-permute-start | bytes 2457608 | tf_op jit(solution)/shard_map/ppermute | solution.py:33
  94.8 20.5 %collective-permute-start.22 = (bf16[80,5120]{1,0:T(8,128)(2,1)S(1)}, bf16[80,5120]{1,0:T(8,128)(2,1)S(1)}, u32[]{:S(2)}, u32[]{:S(2)}) collective-permute-start(bf16[80,5120]{1,0:T(8,128)(2,1)S(1)} %get-tuple-element.23.refs_1_.refs_2_), channel_id=1, source_target_pairs={{8,0},{16,8},{24,16},{32,24},{40,32},{48,40},{56,48},{0,56},{9,1},... | collective-permute-start | bytes 2457608 | tf_op jit(solution)/shard_map/ppermute | solution.py:33
  97.8 20.2 %collective-permute-start.23 = (bf16[80,5120]{1,0:T(8,128)(2,1)S(1)}, bf16[80,5120]{1,0:T(8,128)(2,1)S(1)}, u32[]{:S(2)}, u32[]{:S(2)}) collective-permute-start(bf16[80,5120]{1,0:T(8,128)(2,1)S(1)} %get-tuple-element.24.refs_2_.refs_7_), channel_id=1, source_target_pairs={{56,0},{0,8},{8,16},{16,24},{24,32},{32,40},{40,48},{48,56},{57,1}... | collective-permute-start | bytes 2457608 | tf_op jit(solution)/shard_map/ppermute | solution.py:33
  97.8 20.2 %collective-permute-start.25 = (bf16[80,5120]{1,0:T(8,128)(2,1)S(1)}, bf16[80,5120]{1,0:T(8,128)(2,1)S(1)}, u32[]{:S(2)}, u32[]{:S(2)}) collective-permute-start(bf16[80,5120]{1,0:T(8,128)(2,1)S(1)} %held.23.refs_2_), channel_id=1, source_target_pairs={{1,0},{2,1},{3,2},{0,3},{5,4},{6,5},{7,6},{4,7},{9,8},{10,9},{11,1... | collective-permute-start | bytes 2457608 | tf_op jit(solution)/shard_map/ppermute | solution.py:33
  100.5 25.5 %collective-permute-start.29 = (f32[56,5120]{1,0:T(8,128)S(1)}, f32[56,5120]{1,0:T(8,128)S(1)}, u32[]{:S(2)}, u32[]{:S(2)}) collective-permute-start(f32[56,5120]{1,0:T(8,128)S(1)} %held.26), channel_id=1, source_target_pairs={{128,0},{0,128},{129,1},{1,129},{130,2},{2,130},{131,3},{3,131},{1... | collective-permute-start | bytes 3440648 | tf_op jit(solution)/shard_map/ppermute | solution.py:33
  118.1 11.1 %collective-permute-start.27 = (bf16[48,5120]{1,0:T(8,128)(2,1)S(1)}, bf16[48,5120]{1,0:T(8,128)(2,1)S(1)}, u32[]{:S(2)}, u32[]{:S(2)}) collective-permute-start(bf16[48,5120]{1,0:T(8,128)(2,1)S(1)} %slice.17), channel_id=1, source_target_pairs={{8,0},{16,8},{24,16},{32,24},{40,32},{48,40},{56,48},{0,56},{9,1},... | collective-permute-start | bytes 1474568 | tf_op jit(solution)/shard_map/ppermute | solution.py:33
  119.4 7.9 %collective-permute-start.28 = (bf16[32,5120]{1,0:T(8,128)(2,1)S(1)}, bf16[32,5120]{1,0:T(8,128)(2,1)S(1)}, u32[]{:S(2)}, u32[]{:S(2)}) collective-permute-start(bf16[32,5120]{1,0:T(8,128)(2,1)S(1)} %slice.18), channel_id=1, source_target_pairs={{56,0},{0,8},{8,16},{16,24},{24,32},{32,40},{40,48},{48,56},{57,1}... | collective-permute-start | bytes 983048 | tf_op jit(solution)/shard_map/ppermute | solution.py:33
  138.2 7.0 %collective-permute-start.30 = (f32[112,5120]{1,0:T(8,128)S(1)}, f32[112,5120]{1,0:T(8,128)S(1)}, u32[]{:S(2)}, u32[]{:S(2)}) collective-permute-start(f32[112,5120]{1,0:T(8,128)S(1)} %get-tuple-element.28), channel_id=1, source_target_pairs={{64,0},{0,64},{65,1},{1,65},{66,2},{2,66},{67,3},{3,67},{68,4},{4,... | collective-permute-start | bytes 6881288 | tf_op jit(solution)/shard_map/ppermute | solution.py:33
  142.8 58.6 %collective-permute-start.35 = (f32[120,5120]{1,0:T(8,128)}, f32[120,5120]{1,0:T(8,128)}, u32[]{:S(2)}, u32[]{:S(2)}) collective-permute-start(f32[120,5120]{1,0:T(8,128)} %held.29), channel_id=1, source_target_pairs={{64,0},{0,64},{65,1},{1,65},{66,2},{2,66},{67,3},{3,67},{68,4},{4,... | collective-permute-start | bytes 7372808 | tf_op jit(solution)/shard_map/ppermute | solution.py:33
  147.7 53.7 %collective-permute-start.36 = (f32[112,5120]{1,0:T(8,128)}, f32[112,5120]{1,0:T(8,128)}, u32[]{:S(2)}, u32[]{:S(2)}) collective-permute-start(f32[112,5120]{1,0:T(8,128)} %get-tuple-element.35.refs_5_), channel_id=1, source_target_pairs={{64,4},{4,64},{65,5},{5,65},{66,6},{6,66},{67,7},{7,67},{72,12},{1... | collective-permute-start | bytes 6881288 | tf_op jit(solution)/shard_map/ppermute | solution.py:43
  161.7 39.7 %collective-permute-start.33 = (f32[64,5120]{1,0:T(8,128)S(1)}, f32[64,5120]{1,0:T(8,128)}, u32[]{:S(2)}, u32[]{:S(2)}) collective-permute-start(f32[64,5120]{1,0:T(8,128)S(1)} %get-tuple-element.29.refs_0_), channel_id=1, source_target_pairs={{64,0},{0,64},{65,1},{1,65},{66,2},{2,66},{67,3},{3,67},{68,4},{4,... | collective-permute-start | bytes 3932168 | tf_op jit(solution)/shard_map/ppermute | solution.py:33
  161.8 39.6 %collective-permute-start.34 = (f32[56,5120]{1,0:T(8,128)S(1)}, f32[56,5120]{1,0:T(8,128)}, u32[]{:S(2)}, u32[]{:S(2)}) collective-permute-start(f32[56,5120]{1,0:T(8,128)S(1)} %get-tuple-element.30.refs_1_), channel_id=1, source_target_pairs={{64,0},{0,64},{65,1},{1,65},{66,2},{2,66},{67,3},{3,67},{68,4},{4,... | collective-permute-start | bytes 3440648 | tf_op jit(solution)/shard_map/ppermute | solution.py:33
  186.8 9.1 %collective-permute-start.31 = (f32[]{:T(128)}, f32[]{:T(128)}, u32[]{:S(2)}, u32[]{:S(2)}) collective-permute-start(f32[]{:T(128)} %psum.15), channel_id=1, source_target_pairs={{0,0},{64,4},{4,64},{68,68},{1,1},{65,5},{5,65},{69,69},{2,2},{66,... | collective-permute-start | bytes 20 | tf_op jit(solution)/shard_map/ppermute | solution.py:43
  195.9 4.1 %collective-permute-start.32 = (f32[]{:T(128)}, f32[]{:T(128)}, u32[]{:S(2)}, u32[]{:S(2)}) collective-permute-start(f32[]{:T(128)} %psum.15), channel_id=1, source_target_pairs={{64,0},{0,4},{68,64},{4,68},{65,1},{1,5},{69,65},{5,69},{66,2},{2,... | collective-permute-start | bytes 20 | tf_op jit(solution)/shard_map/ppermute | solution.py:48
  201.4 1.6 copy-start

commit v14 on v13

--- a/solution.py
+++ b/solution.py
@@ -24,7 +24,7 @@
 HALF = 128
 CUT = 64
 NO_COST = pl.CostEstimate(flops=1, bytes_accessed=1, transcendentals=0)
-BLOCK = 1024
+BLOCK = 1280
 
 
 def shifted(value, axis, steps):
@@ -224,7 +224,7 @@
             pltpu.VMEM((2 * HALF, BLOCK), jnp.bfloat16),
             pltpu.VMEM((2 * HALF, BLOCK), jnp.bfloat16),
         ],
-        compiler_params=params_of(36),
+        compiler_params=params_of(30),
         cost_estimate=NO_COST,
         name="gate_grads",
     )(*parts, mine, theirs, mine, theirs, hidden_most, hidden_far)

time: 210 us -> 209 us (level)
  no operation moved by 1% of the time
where the time goes in v14:
time: 209 us; the launch traced here: 208 us
  starting transfers between devices  75 us (36%)
  waiting for transfers between devices  73.5 us (35%)
  blocking collectives  23.6 us (11%)
  Pallas kernels  22.5 us (11%)
  between operations  5.5 us (3%)
  other arithmetic  4.7 us (2%)
  local copies, waits for them, and re-layouts  3.58 us (2%)
    ppermute x31, waiting for transfers between devices, shifted(): return lax.ppermute(value, axis, pairs)  59.4 us
    ppermute x31, starting transfers between devices, shifted(): return lax.ppermute(value, axis, pairs)  42.6 us
    ppermute x5, starting transfers between devices, transposed(): return lax.ppermute(value, ('core', 'x_hi'), pairs)  32.4 us
    psum x2, blocking collectives, shards(): norm_sq = lax.psum(norm_sq, axes)  23.6 us
    ppermute x5, waiting for transfers between devices, transposed(): return lax.ppermute(value, ('core', 'x_hi'), pairs)  9.88 us
    pallas_call x1, Pallas kernels, gate_grads(): pl.pallas_call(grad_kernel, grid=(D // BLOCK,), in_specs=[pl.BlockSpec((p...  8.44 us
    pallas_call x2, Pallas kernels, hidden_of(): pl.pallas_call(hidden_kernel, grid=(D // BLOCK,), in_specs=[pl.BlockSpec(...  8.42 us
    pallas_call x1, Pallas kernels, updated(): pl.pallas_call(updated_kernel, grid=(blocks,), in_specs=[scalar, scalar,...  4.66 us
  transfers between devices with their start and end apart: 37, of which 24 were waited for; matrix products, arithmetic and copies ran while one was open for 3% of the time, Pallas kernels for 5%

profile of v14, /device:TPU:1, one launch (start us, length us, event | category | flops | bytes accessed | tf_op | source)
XLA Modules:
  0.0 208.3 jit_solution(1629019755209745129)
XLA Ops:
  0.7 6.2 %collective-permute-start = (bf16[20,5120]{1,0:T(8,128)(2,1)}, bf16[20,5120]{1,0:T(8,128)(2,1)S(1)}, u32[]{:S(2)}, u32[]{:S(2)}) collective-permute-start(bf16[20,5120]{1,0:T(8,128)(2,1)} %bitcast.27), channel_id=1, source_target_pairs={{0,0},{64,4},{4,64},{68,68},{1,1},{65,5},{5,65},{69,69},{2,2},{66,... | collective-permute-start | bytes 614408 | tf_op jit(solution)/shard_map/ppermute | solution.py:43
  6.8 1.9 collective-permute-start.1
  9.4 1.8 divide_convert_fusion
  11.3 0.3 pad_maximum_fusion.refs_2_.refs_0_
  11.5 4.5 %collective-permute-done.1.refs_1_.refs_0_ = bf16[20,5120]{1,0:T(8,128)(2,1)S(1)} collective-permute-done((bf16[20,5120]{1,0:T(8,128)(2,1)}, bf16[20,5120]{1,0:T(8,128)(2,1)S(1)}, u32[]{:S(2)}, u32[]{:S(2)}) %collective-permute-start.1) | collective-permute-done | bytes 204832 | tf_op jit(solution)/shard_map/ppermute | solution.py:43
  16.1 2.6 %collective-permute-start.16 = (bf16[336,5120]{1,0:T(8,128)(2,1)S(1)}, bf16[336,5120]{1,0:T(8,128)(2,1)S(1)}, u32[]{:S(2)}, u32[]{:S(2)}) collective-permute-start(bf16[336,5120]{1,0:T(8,128)(2,1)S(1)} %held.18), channel_id=1, source_target_pairs={{0,0},{64,4},{4,64},{68,68},{1,1},{65,5},{5,65},{69,69},{2,2},{66,... | collective-permute-start | bytes 10321928 | tf_op jit(solution)/shard_map/ppermute | solution.py:43
  18.7 2.8 %collective-permute-start.2 = (bf16[20,5120]{1,0:T(8,128)(2,1)S(1)}, bf16[20,5120]{1,0:T(8,128)(2,1)S(1)}, u32[]{:S(2)}, u32[]{:S(2)}) collective-permute-start(bf16[20,5120]{1,0:T(8,128)(2,1)S(1)} %held.15.refs_0_), channel_id=1, source_target_pairs={{1,0},{2,1},{3,2},{0,3},{5,4},{6,5},{7,6},{4,7},{9,8},{10,9},{11,1... | collective-permute-start | bytes 614408 | tf_op jit(solution)/shard_map/ppermute | solution.py:33
  21.5 5.6 %collective-permute-start.5 = (bf16[20,5120]{1,0:T(8,128)(2,1)S(1)}, bf16[20,5120]{1,0:T(8,128)(2,1)S(1)}, u32[]{:S(2)}, u32[]{:S(2)}) collective-permute-start(bf16[20,5120]{1,0:T(8,128)(2,1)S(1)} %collective-permute-done.1.refs_1_.refs_0_), channel_id=1, source_target_pairs={{8,0},{16,8},{24,16},{32,24},{40,32},{48,40},{56,48},{0,56},{9,1},... | collective-permute-start | bytes 614408 | tf_op jit(solution)/shard_map/ppermute | solution.py:33
  27.1 0.2 collective-permute-done.2.refs_2_.refs_1_
  27.3 1.7 collective-permute-start.4
  29.0 2.5 %collective-permute-done.5.refs_1_ = bf16[20,5120]{1,0:T(8,128)(2,1)S(1)} collective-permute-done((bf16[20,5120]{1,0:T(8,128)(2,1)S(1)}, bf16[20,5120]{1,0:T(8,128)(2,1)S(1)}, u32[]{:S(2)}, u32[]{:S(2)}) %collective-permute-start.5) | collective-permute-done | bytes 204832 | tf_op jit(solution)/shard_map/ppermute | solution.py:33
  31.5 3.1 %collective-permute-start.6 = (bf16[20,5120]{1,0:T(8,128)(2,1)S(1)}, bf16[20,5120]{1,0:T(8,128)(2,1)S(1)}, u32[]{:S(2)}, u32[]{:S(2)}) collective-permute-start(bf16[20,5120]{1,0:T(8,128)(2,1)S(1)} %collective-permute-done.5.refs_1_), channel_id=1, source_target_pairs={{8,0},{16,8},{24,16},{32,24},{40,32},{48,40},{56,48},{0,56},{9,1},... | collective-permute-start | bytes 614408 | tf_op jit(solution)/shard_map/ppermute | solution.py:33
  34.6 0.3 collective-permute-done.7.refs_3_
  34.9 1.1 collective-permute-done.3.refs_3_.refs_2_
  36.0 4.3 %collective-permute-done.6.refs_0_ = bf16[20,5120]{1,0:T(8,128)(2,1)S(1)} collective-permute-done((bf16[20,5120]{1,0:T(8,128)(2,1)S(1)}, bf16[20,5120]{1,0:T(8,128)(2,1)S(1)}, u32[]{:S(2)}, u32[]{:S(2)}) %collective-permute-start.6) | collective-permute-done | bytes 204832 | tf_op jit(solution)/shard_map/ppermute | solution.py:33
  40.3 3.6 %collective-permute-done.8.refs_1_ = bf16[20,5120]{1,0:T(8,128)(2,1)S(1)} collective-permute-done((bf16[20,5120]{1,0:T(8,128)(2,1)S(1)}, bf16[20,5120]{1,0:T(8,128)(2,1)S(1)}, u32[]{:S(2)}, u32[]{:S(2)}) %collective-permute-start.8) | collective-permute-done | bytes 204832 | tf_op jit(solution)/shard_map/ppermute | solution.py:33
  43.9 1.5 collective-permute-start.11
  45.4 5.8 %collective-permute-done.9.refs_1_.refs_3_ = bf16[20,5120]{1,0:T(8,128)(2,1)S(1)} collective-permute-done((bf16[20,5120]{1,0:T(8,128)(2,1)S(1)}, bf16[20,5120]{1,0:T(8,128)(2,1)S(1)}, u32[]{:S(2)}, u32[]{:S(2)}) %collective-permute-start.9) | collective-permute-done | bytes 204832 | tf_op jit(solution)/shard_map/ppermute | solution.py:33
  51.2 1.4 collective-permute-done.10.refs_2_.refs_0_
  52.7 0.3 stacked.3.refs_0_
  53.0 6.7 %collective-permute-start.12 = (bf16[80,5120]{1,0:T(8,128)(2,1)S(1)}, bf16[80,5120]{1,0:T(8,128)(2,1)S(1)}, u32[]{:S(2)}, u32[]{:S(2)}) collective-permute-start(bf16[80,5120]{1,0:T(8,128)(2,1)S(1)} %stacked.3.refs_0_), channel_id=1, source_target_pairs={{8,0},{16,8},{24,16},{32,24},{40,32},{48,40},{56,48},{0,56},{9,1},... | collective-permute-start | bytes 2457608 | tf_op jit(solution)/shard_map/ppermute | solution.py:33
  59.7 0.3 stacked.5.refs_0_
  60.1 0.1 collective-permute-start.14
  60.1 1.5 collective-permute-start.15
  61.6 0.1 slice_bitcast_fusion.refs_0_
  61.7 3.9 %collective-permute-done.16.refs_5_.refs_1_.refs_0_ = bf16[336,5120]{1,0:T(8,128)(2,1)S(1)} collective-permute-done((bf16[336,5120]{1,0:T(8,128)(2,1)S(1)}, bf16[336,5120]{1,0:T(8,128)(2,1)S(1)}, u32[]{:S(2)}, u32[]{:S(2)}) %collective-permute-start.16) | collective-permute-done | bytes 3440672 | tf_op jit(solution)/shard_map/ppermute | solution.py:43
  65.6 1.2 collective-permute-start.19
  66.8 0.3 stacked.4.refs_2_.refs_0_
  67.2 5.4 %collective-permute-done.12.refs_0_ = bf16[80,5120]{1,0:T(8,128)(2,1)S(1)} collective-permute-done((bf16[80,5120]{1,0:T(8,128)(2,1)S(1)}, bf16[80,5120]{1,0:T(8,128)(2,1)S(1)}, u32[]{:S(2)}, u32[]{:S(2)}) %collective-permute-start.12) | collective-permute-done | bytes 819232 | tf_op jit(solution)/shard_map/ppermute | solution.py:33
  72.6 0.4 collective-permute-done.15.refs_4_
  73.0 3.2 %collective-permute-start.17 = (bf16[80,5120]{1,0:T(8,128)(2,1)S(1)}, bf16[80,5120]{1,0:T(8,128)(2,1)S(1)}, u32[]{:S(2)}, u32[]{:S(2)}) collective-permute-start(bf16[80,5120]{1,0:T(8,128)(2,1)S(1)} %get-tuple-element.21.refs_1_), channel_id=1, source_target_pairs={{8,0},{16,8},{24,16},{32,24},{40,32},{48,40},{56,48},{0,56},{9,1},... | collective-permute-start | bytes 2457608 | tf_op jit(solution)/shard_map/ppermute | solution.py:33
  76.1 4.3 %collective-permute-start.20 = (bf16[80,5120]{1,0:T(8,128)(2,1)S(1)}, bf16[80,5120]{1,0:T(8,128)(2,1)S(1)}, u32[]{:S(2)}, u32[]{:S(2)}) collective-permute-start(bf16[80,5120]{1,0:T(8,128)(2,1)S(1)} %held.21.refs_1_), channel_id=1, source_target_pairs={{1,0},{2,1},{3,2},{0,3},{5,4},{6,5},{7,6},{4,7},{9,8},{10,9},{11,1... | collective-permute-start | bytes 2457608 | tf_op jit(solution)/shard_map/ppermute | solution.py:33
  80.5 8.9 %collective-permute-done.17.refs_0_ = bf16[80,5120]{1,0:T(8,128)(2,1)S(1)} collective-permute-done((bf16[80,5120]{1,0:T(8,128)(2,1)S(1)}, bf16[80,5120]{1,0:T(8,128)(2,1)S(1)}, u32[]{:S(2)}, u32[]{:S(2)}) %collective-permute-start.17) | collective-permute-done | bytes 819232 | tf_op jit(solution)/shard_map/ppermute | solution.py:33
  89.3 1.3 collective-permute-done.18.refs_1_
  90.6 0.7 collective-permute-done.20.refs_3_
  91.4 2.7 %collective-permute-done.21.refs_4_.refs_5_ = bf16[80,5120]{1,0:T(8,128)(2,1)S(1)} collective-permute-done((bf16[80,5120]{1,0:T(8,128)(2,1)S(1)}, bf16[80,5120]{1,0:T(8,128)(2,1)S(1)}, u32[]{:S(2)}, u32[]{:S(2)}) %collective-permute-start.21) | collective-permute-done | bytes 819232 | tf_op jit(solution)/shard_map/ppermute | solution.py:33
  94.7 0.1 collective-permute-start.26
  94.8 3.0 %collective-permute-start.22 = (bf16[80,5120]{1,0:T(8,128)(2,1)S(1)}, bf16[80,5120]{1,0:T(8,128)(2,1)S(1)}, u32[]{:S(2)}, u32[]{:S(2)}) collective-permute-start(bf16[80,5120]{1,0:T(8,128)(2,1)S(1)} %get-tuple-element.23.refs_1_.refs_2_), channel_id=1, source_target_pairs={{8,0},{16,8},{24,16},{32,24},{40,32},{48,40},{56,48},{0,56},{9,1},... | collective-permute-start | bytes 2457608 | tf_op jit(solution)/shard_map/ppermute | solution.py:33
  97.8 2.6 %collective-permute-start.25 = (bf16[80,5120]{1,0:T(8,128)(2,1)S(1)}, bf16[80,5120]{1,0:T(8,128)(2,1)S(1)}, u32[]{:S(2)}, u32[]{:S(2)}) collective-permute-start(bf16[80,5120]{1,0:T(8,128)(2,1)S(1)} %held.23.refs_2_), channel_id=1, source_target_pairs={{1,0},{2,1},{3,2},{0,3},{5,4},{6,5},{7,6},{4,7},{9,8},{10,9},{11,1... | collective-permute-start | bytes 2457608 | tf_op jit(solution)/shard_map/ppermute | solution.py:33
  100.5 0.1 collective-permute-start.29
  100.6 6.0 %hidden.2.refs_2_.refs_13_ = f32[480,256]{1,0:T(8,128)S(1)} custom-call(bf16[80,5120]{1,0:T(8,128)(2,1)S(1)} %stacked.5.refs_0_, bf16[80,5120]{1,0:T(8,128)(2,1)S(1)} %held.21.refs_1_, bf16[80,5120]{1,0:T(8,128)(2,1)S(1)} %held.23.refs_2_, bf16[80,5120]{1,0:T(8,128)(2,1)S(1)} %collective-permute-done.20.refs_3_, ...), custom_call_target="tpu_custom_call" | custom-call | flops 1 | bytes 1 | tf_op jit(solution)/shard_map/hidden/pallas_call | solution.py:142
  106.6 8.7 %collective-permute-done.26.refs_4_.refs_1_ = bf16[80,5120]{1,0:T(8,128)(2,1)S(1)} collective-permute-done((bf16[80,5120]{1,0:T(8,128)(2,1)S(1)}, bf16[80,5120]{1,0:T(8,128)(2,1)S(1)}, u32[]{:S(2)}, u32[]{:S(2)}) %collective-permute-start.26) | collective-permute-done | bytes 819232 | tf_op jit(solution)/shard_map/ppermute | solution.py:33
  115.3 2.7 %collective-permute-done.23.refs_1_ = bf16[80,5120]{1,0:T(8,128)(2,1)S(1)} collective-permute-done((bf16[80,5120]{1,0:T(8,128)(2,1)S(1)}, bf16[80,5120]{1,0:T(8,128)(2,1)S(1)}, u32[]{:S(2)}, u32[]{:S(2)}) %collective-permute-start.23) | collective-permute-done | bytes 819232 | tf_op jit(solution)/shard_map/ppermute | solution.py:33
  118.1 1.3 collective-permute-start.27
  119.4 0.3 collective-permute-start.28
  119.7 2.5 %hidden.3.refs_0_ = f32[160,256]{1,0:T(8,128)S(1)} custom-call(bf16[80,5120]{1,0:T(8,128)(2,1)S(1)} %collective-permute-done.25.refs_3_.refs_0_, bf16[80,5120]{1,0:T(8,128)(2,1)S(1)} %collective-permute-done.26.refs_4_.refs_1_, bf16[336,5120]{1,0:T(8,128)(2,1)S(1)} %held.24.refs_6_.refs_2_.refs_9_.refs_11_, ...), custom_call_target="tpu_custom_call" | custom-call | flops 1 | bytes 1 | tf_op jit(solution)/shard_map/hidden/pallas_call | solution.py:142
  122.2 3.8 %collective-permute-done.29.refs_1_ = f32[56,5120]{1,0:T(8,128)S(1)} collective-permute-done((f32[56,5120]{1,0:T(8,128)S(1)}, f32[56,5120]{1,0:T(8,128)S(1)}, u32[]{:S(2)}, u32[]{:S(2)}) %collective-permute-start.29) | collective-permute-done | bytes 1146912 | tf_op jit(solution)/shard_map/ppermute | solution.py:33
  126.0 1.3 collective-permute-done.28.refs_5_
  127.4 1.8 collective-permute-done.27.refs_4_
  129.2 8.4 %gate_grads.1 = (f32[112,5120]{1,0:T(8,128)S(1)}, f32[112,5120]{1,0:T(8,128)S(1)}) custom-call(bf16[80,5120]{1,0:T(8,128)(2,1)S(1)} %stacked.3.refs_0_, bf16[80,5120]{1,0:T(8,128)(2,1)S(1)} %get-tuple-element.21.refs_1_, bf16[80,5120]{1,0:T(8,128)(2,1)S(1)} %get-tuple-element.23.refs_1_.refs_2_, bf16[80,5120]{1,0:T(8,128)(2,1)S(1)} %get-tuple-element.25.refs_3_, ...), custom_call_target="tpu_custom_call" | custom-call | flops 1 | bytes 1 | tf_op jit(solution)/shard_map/gate_grads/pallas_call | solution.py:210
  137.6 2.9 %collective-permute-start.30 = (f32[112,5120]{1,0:T(8,128)S(1)}, f32[112,5120]{1,0:T(8,128)S(1)}, u32[]{:S(2)}, u32[]{:S(2)}) collective-permute-start(f32[112,5120]{1,0:T(8,128)S(1)} %get-tuple-element.28), channel_id=1, source_target_pairs={{64,0},{0,64},{65,1},{1,65},{66,2},{2,66},{67,3},{3,67},{68,4},{4,... | collective-permute-start | bytes 6881288 | tf_op jit(solution)/shard_map/ppermute | solution.py:33
  140.5 1.7 concatenate.7.refs_0_
  142.3 2.3 %collective-permute-done.30 = f32[112,5120]{1,0:T(8,128)S(1)} collective-permute-done((f32[112,5120]{1,0:T(8,128)S(1)}, f32[112,5120]{1,0:T(8,128)S(1)}, u32[]{:S(2)}, u32[]{:S(2)}) %collective-permute-start.30) | collective-permute-done | bytes 2293792 | tf_op jit(solution)/shard_map/ppermute | solution.py:33
  144.6 2.5 %multiply_reduce_fusion = (f32[]{:T(128)}, f32[112,5120]{1,0:T(8,128)}) fusion(f32[112,5120]{1,0:T(8,128)S(1)} %get-tuple-element.27.refs_2_.refs_1_, f32[112,5120]{1,0:T(8,128)S(1)} %collective-permute-done.30), kind=kLoop, calls=%fused_computation.1 | loop fusion | flops 1720319 | bytes 6881284 | tf_op jit(solution)/shard_map/reduce_sum | solution.py:370
  147.1 14.0 %collective-permute-start.36 = (f32[112,5120]{1,0:T(8,128)}, f32[112,5120]{1,0:T(8,128)}, u32[]{:S(2)}, u32[]{:S(2)}) collective-permute-start(f32[112,5120]{1,0:T(8,128)} %get-tuple-element.35.refs_5_), channel_id=1, source_target_pairs={{64,4},{4,64},{65,5},{5,65},{66,6},{6,66},{67,7},{7,67},{72,12},{1... | collective-permute-start | bytes 6881288 | tf_op jit(solution)/shard_map/ppermute | solution.py:43
  161.2 0.1 collective-permute-start.33
  161.3 0.5 collective-permute-start.34
  162.6 13.6 %psum.14 = f32[]{:T(128)} all-reduce(f32[]{:T(128)} %get-tuple-element.34), channel_id=1, replica_groups=mesh['x_lo'=2,'core'=2,'z'=8,'x_hi'=2,'y'=4] {'z'}, use_global_device_ids=true, to_apply=%region_1.2 | all-reduce | flops 1 | bytes 8 | tf_op jit(solution)/shard_map/psum | solution.py:373
  176.2 10.0 %psum.15 = f32[]{:T(128)} all-reduce(f32[]{:T(128)} %psum.14), channel_id=1, replica_groups=mesh['x_lo'=2,'core'=2,'z'=8,'x_hi'=2,'y'=4] {'y'}, use_global_device_ids=true, to_apply=%region_2.3 | all-reduce | flops 1 | bytes 8 | tf_op jit(solution)/shard_map/psum | solution.py:373
  186.2 7.7 %collective-permute-start.31 = (f32[]{:T(128)}, f32[]{:T(128)}, u32[]{:S(2)}, u32[]{:S(2)}) collective-permute-start(f32[]{:T(128)} %psum.15), channel_id=1, source_target_pairs={{0,0},{64,4},{4,64},{68,68},{1,1},{65,5},{5,65},{69,69},{2,2},{66,... | collective-permute-start | bytes 20 | tf_op jit(solution)/shard_map/ppermute | solution.py:43
  193.9 1.4 collective-permute-done.31
  195.3 4.1 %collective-permute-done.32 = f32[]{:T(128)} collective-permute-done((f32[]{:T(128)}, f32[]{:T(128)}, u32[]{:S(2)}, u32[]{:S(2)}) %collective-permute-start.32) | collective-permute-done | bytes 36 | tf_op jit(solution)/shard_map/ppermute | solution.py:48
  200.9 1.6 copy-done
  202.5 4.7 %updated.1 = (f32[112,5120]{1,0:T(8,128)}, f32[112,5120]{1,0:T(8,128)}, f32[1]{0:T(128)}) custom-call(f32[1]{0:T(128)} %bitcast.8.factor, f32[1]{0:T(128)} %mul.11.kept_weight, s32[2]{0:T(128)S(1)} %pad_add_fusion.which, f32[112,5120]{1,0:T(8,128)S(1)} %bitcast.22, f32[64,5120]{1,0:T(8,128)S(1)} %get-tuple-element.29.refs_0_, ...), custom_call_target="tpu_custom_call" | custom-call | tf_op jit(solution)/shard_map/updated/pallas_call | solution.py:295
  (51 shorter events, 0.3 us)
Async XLA Ops:
  0.6 10.6 %copy-start.2 = (bf16[112,5120]{1,0:T(8,128)(2,1)S(1)}, bf16[112,5120]{1,0:T(8,128)(2,1)}, u32[]{:S(2)}) copy-start(bf16[112,5120]{1,0:T(8,128)(2,1)} %param.16) | copy-start | bytes 3440644
  0.6 10.6 %copy-start.3 = (bf16[112,5120]{1,0:T(8,128)(2,1)S(1)}, bf16[112,5120]{1,0:T(8,128)(2,1)}, u32[]{:S(2)}) copy-start(bf16[112,5120]{1,0:T(8,128)(2,1)} %param.15) | copy-start | bytes 3440644
  0.7 10.9 %collective-permute-start = (bf16[20,5120]{1,0:T(8,128)(2,1)}, bf16[20,5120]{1,0:T(8,128)(2,1)S(1)}, u32[]{:S(2)}, u32[]{:S(2)}) collective-permute-start(bf16[20,5120]{1,0:T(8,128)(2,1)} %bitcast.27), channel_id=1, source_target_pairs={{0,0},{64,4},{4,64},{68,68},{1,1},{65,5},{5,65},{69,69},{2,2},{66,... | collective-permute-start | bytes 614408 | tf_op jit(solution)/shard_map/ppermute | solution.py:43
  6.8 9.2 %collective-permute-start.1 = (bf16[20,5120]{1,0:T(8,128)(2,1)}, bf16[20,5120]{1,0:T(8,128)(2,1)S(1)}, u32[]{:S(2)}, u32[]{:S(2)}) collective-permute-start(bf16[20,5120]{1,0:T(8,128)(2,1)} %bitcast.28), channel_id=1, source_target_pairs={{0,0},{64,4},{4,64},{68,68},{1,1},{65,5},{5,65},{69,69},{2,2},{66,... | collective-permute-start | bytes 614408 | tf_op jit(solution)/shard_map/ppermute | solution.py:43
  16.1 49.5 %collective-permute-start.16 = (bf16[336,5120]{1,0:T(8,128)(2,1)S(1)}, bf16[336,5120]{1,0:T(8,128)(2,1)S(1)}, u32[]{:S(2)}, u32[]{:S(2)}) collective-permute-start(bf16[336,5120]{1,0:T(8,128)(2,1)S(1)} %held.18), channel_id=1, source_target_pairs={{0,0},{64,4},{4,64},{68,68},{1,1},{65,5},{5,65},{69,69},{2,2},{66,... | collective-permute-start | bytes 10321928 | tf_op jit(solution)/shard_map/ppermute | solution.py:43
  18.7 8.6 %collective-permute-start.2 = (bf16[20,5120]{1,0:T(8,128)(2,1)S(1)}, bf16[20,5120]{1,0:T(8,128)(2,1)S(1)}, u32[]{:S(2)}, u32[]{:S(2)}) collective-permute-start(bf16[20,5120]{1,0:T(8,128)(2,1)S(1)} %held.15.refs_0_), channel_id=1, source_target_pairs={{1,0},{2,1},{3,2},{0,3},{5,4},{6,5},{7,6},{4,7},{9,8},{10,9},{11,1... | collective-permute-start | bytes 614408 | tf_op jit(solution)/shard_map/ppermute | solution.py:33
  21.5 10.0 %collective-permute-start.5 = (bf16[20,5120]{1,0:T(8,128)(2,1)S(1)}, bf16[20,5120]{1,0:T(8,128)(2,1)S(1)}, u32[]{:S(2)}, u32[]{:S(2)}) collective-permute-start(bf16[20,5120]{1,0:T(8,128)(2,1)S(1)} %collective-permute-done.1.refs_1_.refs_0_), channel_id=1, source_target_pairs={{8,0},{16,8},{24,16},{32,24},{40,32},{48,40},{56,48},{0,56},{9,1},... | collective-permute-start | bytes 614408 | tf_op jit(solution)/shard_map/ppermute | solution.py:33
  27.1 7.8 %collective-permute-start.7 = (bf16[20,5120]{1,0:T(8,128)(2,1)S(1)}, bf16[20,5120]{1,0:T(8,128)(2,1)S(1)}, u32[]{:S(2)}, u32[]{:S(2)}) collective-permute-start(bf16[20,5120]{1,0:T(8,128)(2,1)S(1)} %collective-permute-done.1.refs_1_.refs_0_), channel_id=1, source_target_pairs={{56,0},{0,8},{8,16},{16,24},{24,32},{32,40},{40,48},{48,56},{57,1}... | collective-permute-start | bytes 614408 | tf_op jit(solution)/shard_map/ppermute | solution.py:33
  27.1 8.9 %collective-permute-start.3 = (bf16[20,5120]{1,0:T(8,128)(2,1)S(1)}, bf16[20,5120]{1,0:T(8,128)(2,1)S(1)}, u32[]{:S(2)}, u32[]{:S(2)}) collective-permute-start(bf16[20,5120]{1,0:T(8,128)(2,1)S(1)} %held.15.refs_0_), channel_id=1, source_target_pairs={{3,0},{0,1},{1,2},{2,3},{7,4},{4,5},{5,6},{6,7},{11,8},{8,9},{9,10... | collective-permute-start | bytes 614408 | tf_op jit(solution)/shard_map/ppermute | solution.py:33
  27.3 8.7 %collective-permute-start.4 = (bf16[20,5120]{1,0:T(8,128)(2,1)S(1)}, bf16[20,5120]{1,0:T(8,128)(2,1)S(1)}, u32[]{:S(2)}, u32[]{:S(2)}) collective-permute-start(bf16[20,5120]{1,0:T(8,128)(2,1)S(1)} %held.15.refs_0_), channel_id=1, source_target_pairs={{2,0},{3,1},{0,2},{1,3},{6,4},{7,5},{4,6},{5,7},{10,8},{11,9},{8,1... | collective-permute-start | bytes 614408 | tf_op jit(solution)/shard_map/ppermute | solution.py:33
  31.5 8.8 %collective-permute-start.6 = (bf16[20,5120]{1,0:T(8,128)(2,1)S(1)}, bf16[20,5120]{1,0:T(8,128)(2,1)S(1)}, u32[]{:S(2)}, u32[]{:S(2)}) collective-permute-start(bf16[20,5120]{1,0:T(8,128)(2,1)S(1)} %collective-permute-done.5.refs_1_), channel_id=1, source_target_pairs={{8,0},{16,8},{24,16},{32,24},{40,32},{48,40},{56,48},{0,56},{9,1},... | collective-permute-start | bytes 614408 | tf_op jit(solution)/shard_map/ppermute | solution.py:33
  34.9 9.0 %collective-permute-start.8 = (bf16[20,5120]{1,0:T(8,128)(2,1)S(1)}, bf16[20,5120]{1,0:T(8,128)(2,1)S(1)}, u32[]{:S(2)}, u32[]{:S(2)}) collective-permute-start(bf16[20,5120]{1,0:T(8,128)(2,1)S(1)} %collective-permute-done.7.refs_3_), channel_id=1, source_target_pairs={{56,0},{0,8},{8,16},{16,24},{24,32},{32,40},{40,48},{48,56},{57,1}... | collective-permute-start | bytes 614408 | tf_op jit(solution)/shard_map/ppermute | solution.py:33
  43.9 7.3 %collective-permute-start.9 = (bf16[20,5120]{1,0:T(8,128)(2,1)S(1)}, bf16[20,5120]{1,0:T(8,128)(2,1)S(1)}, u32[]{:S(2)}, u32[]{:S(2)}) collective-permute-start(bf16[20,5120]{1,0:T(8,128)(2,1)S(1)} %get-tuple-element.19.refs_2_), channel_id=1, source_target_pairs={{8,0},{16,8},{24,16},{32,24},{40,32},{48,40},{56,48},{0,56},{9,1},... | collective-permute-start | bytes 614408 | tf_op jit(solution)/shard_map/ppermute | solution.py:33
  43.9 8.7 %collective-permute-start.10 = (bf16[20,5120]{1,0:T(8,128)(2,1)S(1)}, bf16[20,5120]{1,0:T(8,128)(2,1)S(1)}, u32[]{:S(2)}, u32[]{:S(2)}) collective-permute-start(bf16[20,5120]{1,0:T(8,128)(2,1)S(1)} %get-tuple-element.19.refs_2_), channel_id=1, source_target_pairs={{16,0},{24,8},{32,16},{40,24},{48,32},{56,40},{0,48},{8,56},{17,1}... | collective-permute-start | bytes 614408 | tf_op jit(solution)/shard_map/ppermute | solution.py:33
  43.9 17.7 %copy-start.1 = (f32[1,112,5120]{2,1,0:T(8,128)S(1)}, f32[1,112,5120]{2,1,0:T(8,128)}, u32[]{:S(2)}) copy-start(f32[1,112,5120]{2,1,0:T(8,128)} %param.13) | copy-start | bytes 6881284
  43.9 8.7 %collective-permute-start.11 = (bf16[20,5120]{1,0:T(8,128)(2,1)S(1)}, bf16[20,5120]{1,0:T(8,128)(2,1)S(1)}, u32[]{:S(2)}, u32[]{:S(2)}) collective-permute-start(bf16[20,5120]{1,0:T(8,128)(2,1)S(1)} %get-tuple-element.20.refs_2_), channel_id=1, source_target_pairs={{56,0},{0,8},{8,16},{16,24},{24,32},{32,40},{40,48},{48,56},{57,1}... | collective-permute-start | bytes 614408 | tf_op jit(solution)/shard_map/ppermute | solution.py:33
  53.0 19.6 %collective-permute-start.12 = (bf16[80,5120]{1,0:T(8,128)(2,1)S(1)}, bf16[80,5120]{1,0:T(8,128)(2,1)S(1)}, u32[]{:S(2)}, u32[]{:S(2)}) collective-permute-start(bf16[80,5120]{1,0:T(8,128)(2,1)S(1)} %stacked.3.refs_0_), channel_id=1, source_target_pairs={{8,0},{16,8},{24,16},{32,24},{40,32},{48,40},{56,48},{0,56},{9,1},... | collective-permute-start | bytes 2457608 | tf_op jit(solution)/shard_map/ppermute | solution.py:33
  59.7 12.9 %collective-permute-start.13 = (bf16[80,5120]{1,0:T(8,128)(2,1)S(1)}, bf16[80,5120]{1,0:T(8,128)(2,1)S(1)}, u32[]{:S(2)}, u32[]{:S(2)}) collective-permute-start(bf16[80,5120]{1,0:T(8,128)(2,1)S(1)} %stacked.3.refs_0_), channel_id=1, source_target_pairs={{56,0},{0,8},{8,16},{16,24},{24,32},{32,40},{40,48},{48,56},{57,1}... | collective-permute-start | bytes 2457608 | tf_op jit(solution)/shard_map/ppermute | solution.py:33
  60.1 12.5 %collective-permute-start.14 = (bf16[80,5120]{1,0:T(8,128)(2,1)S(1)}, bf16[80,5120]{1,0:T(8,128)(2,1)S(1)}, u32[]{:S(2)}, u32[]{:S(2)}) collective-permute-start(bf16[80,5120]{1,0:T(8,128)(2,1)S(1)} %stacked.5.refs_0_), channel_id=1, source_target_pairs={{1,0},{2,1},{3,2},{0,3},{5,4},{6,5},{7,6},{4,7},{9,8},{10,9},{11,1... | collective-permute-start | bytes 2457608 | tf_op jit(solution)/shard_map/ppermute | solution.py:33
  60.1 12.8 %collective-permute-start.15 = (bf16[80,5120]{1,0:T(8,128)(2,1)S(1)}, bf16[80,5120]{1,0:T(8,128)(2,1)S(1)}, u32[]{:S(2)}, u32[]{:S(2)}) collective-permute-start(bf16[80,5120]{1,0:T(8,128)(2,1)S(1)} %stacked.5.refs_0_), channel_id=1, source_target_pairs={{3,0},{0,1},{1,2},{2,3},{7,4},{4,5},{5,6},{6,7},{11,8},{8,9},{9,10... | collective-permute-start | bytes 2457608 | tf_op jit(solution)/shard_map/ppermute | solution.py:33
  65.6 28.5 %collective-permute-start.19 = (f32[64,5120]{1,0:T(8,128)S(1)}, f32[64,5120]{1,0:T(8,128)S(1)}, u32[]{:S(2)}, u32[]{:S(2)}) collective-permute-start(f32[64,5120]{1,0:T(8,128)S(1)} %held.20), channel_id=1, source_target_pairs={{128,0},{0,128},{129,1},{1,129},{130,2},{2,130},{131,3},{3,131},{1... | collective-permute-start | bytes 3932168 | tf_op jit(solution)/shard_map/ppermute | solution.py:33
  73.0 16.4 %collective-permute-start.17 = (bf16[80,5120]{1,0:T(8,128)(2,1)S(1)}, bf16[80,5120]{1,0:T(8,128)(2,1)S(1)}, u32[]{:S(2)}, u32[]{:S(2)}) collective-permute-start(bf16[80,5120]{1,0:T(8,128)(2,1)S(1)} %get-tuple-element.21.refs_1_), channel_id=1, source_target_pairs={{8,0},{16,8},{24,16},{32,24},{40,32},{48,40},{56,48},{0,56},{9,1},... | collective-permute-start | bytes 2457608 | tf_op jit(solution)/shard_map/ppermute | solution.py:33
  76.1 14.5 %collective-permute-start.18 = (bf16[80,5120]{1,0:T(8,128)(2,1)S(1)}, bf16[80,5120]{1,0:T(8,128)(2,1)S(1)}, u32[]{:S(2)}, u32[]{:S(2)}) collective-permute-start(bf16[80,5120]{1,0:T(8,128)(2,1)S(1)} %get-tuple-element.22.refs_2_.refs_8_), channel_id=1, source_target_pairs={{56,0},{0,8},{8,16},{16,24},{24,32},{32,40},{40,48},{48,56},{57,1}... | collective-permute-start | bytes 2457608 | tf_op jit(solution)/shard_map/ppermute | solution.py:33
  76.1 15.2 %collective-permute-start.20 = (bf16[80,5120]{1,0:T(8,128)(2,1)S(1)}, bf16[80,5120]{1,0:T(8,128)(2,1)S(1)}, u32[]{:S(2)}, u32[]{:S(2)}) collective-permute-start(bf16[80,5120]{1,0:T(8,128)(2,1)S(1)} %held.21.refs_1_), channel_id=1, source_target_pairs={{1,0},{2,1},{3,2},{0,3},{5,4},{6,5},{7,6},{4,7},{9,8},{10,9},{11,1... | collective-permute-start | bytes 2457608 | tf_op jit(solution)/shard_map/ppermute | solution.py:33
  80.5 13.6 %collective-permute-start.21 = (bf16[80,5120]{1,0:T(8,128)(2,1)S(1)}, bf16[80,5120]{1,0:T(8,128)(2,1)S(1)}, u32[]{:S(2)}, u32[]{:S(2)}) collective-permute-start(bf16[80,5120]{1,0:T(8,128)(2,1)S(1)} %held.21.refs_1_), channel_id=1, source_target_pairs={{3,0},{0,1},{1,2},{2,3},{7,4},{4,5},{5,6},{6,7},{11,8},{8,9},{9,10... | collective-permute-start | bytes 2457608 | tf_op jit(solution)/shard_map/ppermute | solution.py:33
  94.1 6.5 %collective-permute-start.24 = (bf16[336,5120]{1,0:T(8,128)(2,1)S(1)}, bf16[336,5120]{1,0:T(8,128)(2,1)S(1)}, u32[]{:S(2)}, u32[]{:S(2)}) collective-permute-start(bf16[336,5120]{1,0:T(8,128)(2,1)S(1)} %held.24.refs_6_.refs_2_.refs_9_.refs_11_), channel_id=1, source_target_pairs={{64,0},{0,64},{65,1},{1,65},{66,2},{2,66},{67,3},{3,67},{68,4},{4,... | collective-permute-start | bytes 10321928 | tf_op jit(solution)/shard_map/ppermute | solution.py:33
  94.7 20.6 %collective-permute-start.26 = (bf16[80,5120]{1,0:T(8,128)(2,1)S(1)}, bf16[80,5120]{1,0:T(8,128)(2,1)S(1)}, u32[]{:S(2)}, u32[]{:S(2)}) collective-permute-start(bf16[80,5120]{1,0:T(8,128)(2,1)S(1)} %collective-permute-done.21.refs_4_.refs_5_), channel_id=1, source_target_pairs={{3,0},{0,1},{1,2},{2,3},{7,4},{4,5},{5,6},{6,7},{11,8},{8,9},{9,10... | collective-permute-start | bytes 2457608 | tf_op jit(solution)/shard_map/ppermute | solution.py:33
  94.8 20.5 %collective-permute-start.22 = (bf16[80,5120]{1,0:T(8,128)(2,1)S(1)}, bf16[80,5120]{1,0:T(8,128)(2,1)S(1)}, u32[]{:S(2)}, u32[]{:S(2)}) collective-permute-start(bf16[80,5120]{1,0:T(8,128)(2,1)S(1)} %get-tuple-element.23.refs_1_.refs_2_), channel_id=1, source_target_pairs={{8,0},{16,8},{24,16},{32,24},{40,32},{48,40},{56,48},{0,56},{9,1},... | collective-permute-start | bytes 2457608 | tf_op jit(solution)/shard_map/ppermute | solution.py:33
  97.8 20.2 %collective-permute-start.23 = (bf16[80,5120]{1,0:T(8,128)(2,1)S(1)}, bf16[80,5120]{1,0:T(8,128)(2,1)S(1)}, u32[]{:S(2)}, u32[]{:S(2)}) collective-permute-start(bf16[80,5120]{1,0:T(8,128)(2,1)S(1)} %get-tuple-element.24.refs_2_.refs_7_), channel_id=1, source_target_pairs={{56,0},{0,8},{8,16},{16,24},{24,32},{32,40},{40,48},{48,56},{57,1}... | collective-permute-start | bytes 2457608 | tf_op jit(solution)/shard_map/ppermute | solution.py:33
  97.8 20.2 %collective-permute-start.25 = (bf16[80,5120]{1,0:T(8,128)(2,1)S(1)}, bf16[80,5120]{1,0:T(8,128)(2,1)S(1)}, u32[]{:S(2)}, u32[]{:S(2)}) collective-permute-start(bf16[80,5120]{1,0:T(8,128)(2,1)S(1)} %held.23.refs_2_), channel_id=1, source_target_pairs={{1,0},{2,1},{3,2},{0,3},{5,4},{6,5},{7,6},{4,7},{9,8},{10,9},{11,1... | collective-permute-start | bytes 2457608 | tf_op jit(solution)/shard_map/ppermute | solution.py:33
  100.5 25.5 %collective-permute-start.29 = (f32[56,5120]{1,0:T(8,128)S(1)}, f32[56,5120]{1,0:T(8,128)S(1)}, u32[]{:S(2)}, u32[]{:S(2)}) collective-permute-start(f32[56,5120]{1,0:T(8,128)S(1)} %held.26), channel_id=1, source_target_pairs={{128,0},{0,128},{129,1},{1,129},{130,2},{2,130},{131,3},{3,131},{1... | collective-permute-start | bytes 3440648 | tf_op jit(solution)/shard_map/ppermute | solution.py:33
  118.1 11.1 %collective-permute-start.27 = (bf16[48,5120]{1,0:T(8,128)(2,1)S(1)}, bf16[48,5120]{1,0:T(8,128)(2,1)S(1)}, u32[]{:S(2)}, u32[]{:S(2)}) collective-permute-start(bf16[48,5120]{1,0:T(8,128)(2,1)S(1)} %slice.17), channel_id=1, source_target_pairs={{8,0},{16,8},{24,16},{32,24},{40,32},{48,40},{56,48},{0,56},{9,1},... | collective-permute-start | bytes 1474568 | tf_op jit(solution)/shard_map/ppermute | solution.py:33
  119.4 7.9 %collective-permute-start.28 = (bf16[32,5120]{1,0:T(8,128)(2,1)S(1)}, bf16[32,5120]{1,0:T(8,128)(2,1)S(1)}, u32[]{:S(2)}, u32[]{:S(2)}) collective-permute-start(bf16[32,5120]{1,0:T(8,128)(2,1)S(1)} %slice.18), channel_id=1, source_target_pairs={{56,0},{0,8},{8,16},{16,24},{24,32},{32,40},{40,48},{48,56},{57,1}... | collective-permute-start | bytes 983048 | tf_op jit(solution)/shard_map/ppermute | solution.py:33
  137.6 7.0 %collective-permute-start.30 = (f32[112,5120]{1,0:T(8,128)S(1)}, f32[112,5120]{1,0:T(8,128)S(1)}, u32[]{:S(2)}, u32[]{:S(2)}) collective-permute-start(f32[112,5120]{1,0:T(8,128)S(1)} %get-tuple-element.28), channel_id=1, source_target_pairs={{64,0},{0,64},{65,1},{1,65},{66,2},{2,66},{67,3},{3,67},{68,4},{4,... | collective-permute-start | bytes 6881288 | tf_op jit(solution)/shard_map/ppermute | solution.py:33
  142.2 58.6 %collective-permute-start.35 = (f32[120,5120]{1,0:T(8,128)}, f32[120,5120]{1,0:T(8,128)}, u32[]{:S(2)}, u32[]{:S(2)}) collective-permute-start(f32[120,5120]{1,0:T(8,128)} %held.29), channel_id=1, source_target_pairs={{64,0},{0,64},{65,1},{1,65},{66,2},{2,66},{67,3},{3,67},{68,4},{4,... | collective-permute-start | bytes 7372808 | tf_op jit(solution)/shard_map/ppermute | solution.py:33
  147.1 53.7 %collective-permute-start.36 = (f32[112,5120]{1,0:T(8,128)}, f32[112,5120]{1,0:T(8,128)}, u32[]{:S(2)}, u32[]{:S(2)}) collective-permute-start(f32[112,5120]{1,0:T(8,128)} %get-tuple-element.35.refs_5_), channel_id=1, source_target_pairs={{64,4},{4,64},{65,5},{5,65},{66,6},{6,66},{67,7},{7,67},{72,12},{1... | collective-permute-start | bytes 6881288 | tf_op jit(solution)/shard_map/ppermute | solution.py:43
  161.2 39.7 %collective-permute-start.33 = (f32[64,5120]{1,0:T(8,128)S(1)}, f32[64,5120]{1,0:T(8,128)}, u32[]{:S(2)}, u32[]{:S(2)}) collective-permute-start(f32[64,5120]{1,0:T(8,128)S(1)} %get-tuple-element.29.refs_0_), channel_id=1, source_target_pairs={{64,0},{0,64},{65,1},{1,65},{66,2},{2,66},{67,3},{3,67},{68,4},{4,... | collective-permute-start | bytes 3932168 | tf_op jit(solution)/shard_map/ppermute | solution.py:33
  161.3 39.6 %collective-permute-start.34 = (f32[56,5120]{1,0:T(8,128)S(1)}, f32[56,5120]{1,0:T(8,128)}, u32[]{:S(2)}, u32[]{:S(2)}) collective-permute-start(f32[56,5120]{1,0:T(8,128)S(1)} %get-tuple-element.30.refs_1_), channel_id=1, source_target_pairs={{64,0},{0,64},{65,1},{1,65},{66,2},{2,66},{67,3},{3,67},{68,4},{4,... | collective-permute-start | bytes 3440648 | tf_op jit(solution)/shard_map/ppermute | solution.py:33
  186.2 9.1 %collective-permute-start.31 = (f32[]{:T(128)}, f32[]{:T(128)}, u32[]{:S(2)}, u32[]{:S(2)}) collective-permute-start(f32[]{:T(128)} %psum.15), channel_id=1, source_target_pairs={{0,0},{64,4},{4,64},{68,68},{1,1},{65,5},{5,65},{69,69},{2,2},{66,... | collective-permute-start | bytes 20 | tf_op jit(solution)/shard_map/ppermute | solution.py:43
  195.3 4.1 %collective-permute-start.32 = (f32[]{:T(128)}, f32[]{:T(128)}, u32[]{:S(2)}, u32[]{:S(2)}) collective-permute-start(f32[]{:T(128)} %psum.15), channel_id=1, source_target_pairs={{64,0},{0,4},{68,64},{4,68},{65,1},{1,5},{69,65},{5,69},{66,2},{2,... | collective-permute-start | bytes 20 | tf_op jit(solution)/shard_map/ppermute | solution.py:48
  200.9 1.6 copy-start
